TPU v7x, 32 devices: a whole 2x2x4 slice. The times are simulated.
32 devices in a mesh: ctx: 8 (over z, core), wt: 4 (over y, x).
Axes of the slice: x: 2, y: 2, z: 4, core: 2. Of those that a mesh axis runs over, the one named last changes fastest.
Arguments:
- hidden: bfloat16 [4, 2048, 1536], P('wt', 'ctx'), may hold values from -6 to 6
- segment_ids: int32 [4, 2048], P('wt'), may hold values from 0 to 2, as said below
- routes: int32 [4, 2048, 6], P('wt', 'ctx'), may hold values from 0 to 63, all different within a row; in each aligned block of 256 rows (0 to 255, 256 to 511, ..., all dimensions but the last counted through in order) at most 40 rows name the same one
- gates: float32 [4, 2048, 6], P('wt', 'ctx'), may hold values from 0.08 to 0.25
- cotangent: bfloat16 [4, 2048, 1536], P('wt', 'ctx'), may hold values from -6 to 6
- norm_one_gain: bfloat16 [1536], P('wt'), may hold values from 0.25 to 1.75
- w_query: bfloat16 [1536, 1536], P('wt'), may hold values from -0.3125 to 0.3125
- w_key: bfloat16 [1536, 512], P('wt'), may hold values from -0.15625 to 0.15625
- w_value: bfloat16 [1536, 512], P('wt'), may hold values from -0.15625 to 0.15625
- w_out: bfloat16 [1536, 1536], P('wt'), may hold values from -0.75 to 0.75
- norm_two_gain: bfloat16 [1536], P('wt'), may hold values from 0.25 to 1.75
- shared_gate: bfloat16 [1536, 1024], P('wt'), may hold values from -0.15625 to 0.15625
- shared_up: bfloat16 [1536, 1024], P('wt'), may hold values from -0.15625 to 0.15625
- shared_down: bfloat16 [1024, 1536], P('wt'), may hold values from -0.1875 to 0.1875
- expert_gate: bfloat16 [64, 1536, 512], P('ctx', 'wt'), may hold values from -0.15625 to 0.15625
- expert_up: bfloat16 [64, 1536, 512], P('ctx', 'wt'), may hold values from -0.15625 to 0.15625
- expert_down: bfloat16 [64, 512, 1536], P('ctx', None, 'wt'), may hold values from -0.25 to 0.25
Outputs:
- output: bfloat16 [4, 2048, 1536], P('wt', 'ctx')
- grad_hidden: float32 [4, 2048, 1536], P('wt', 'ctx')
- grad_norm_one_gain: float32 [1536], P('wt')
- grad_w_query: float32 [1536, 1536], P('wt')
- grad_w_key: float32 [1536, 512], P('wt')
- grad_w_value: float32 [1536, 512], P('wt')
- grad_w_out: float32 [1536, 1536], P('wt')
- grad_norm_two_gain: float32 [1536], P('wt')
- grad_shared_gate: float32 [1536, 1024], P('wt')
- grad_shared_up: float32 [1536, 1024], P('wt')
- grad_shared_down: float32 [1024, 1536], P('wt')
- grad_expert_gate: float32 [64, 1536, 512], P('ctx', 'wt')
- grad_expert_up: float32 [64, 1536, 512], P('ctx', 'wt')
- grad_expert_down: float32 [64, 512, 1536], P('ctx', None, 'wt')
Inputs may be any that keep to these rules, and one draw needn't show every extreme that they name: `routes`: each row names 6 different experts; of the 256 rows of one device at most 40 name any one expert. `segment_ids`: along each pack the ids never fall; id 0 covers the first 1 to 255 tokens, id 2 the last 1 to 255 tokens, id 1 all others.
All inputs are finite; a program needn't handle non-finite values.
Results may differ from a plain program's by a relative error of at most 0.024.
Values may be sent and summed in bfloat16 or wider, within the bound.
A program may use at most 384 MiB of HBM per device.

v0:
```python
import math

import jax
import jax.numpy as jnp
from jax import lax
from jax.sharding import PartitionSpec as P

HEADS = 12
KV_HEADS = 4
HEAD_DIM = 128
EXPERTS = 64
TOPK = 6
CAP = 40


epsilon = 1e-05
masked_value = -1e30


def inverse_rms(rows):
    return lax.rsqrt(jnp.mean(rows * rows, axis=-1, keepdims=True) + epsilon)


def silu_slope(gate_part):
    sigmoid = jax.nn.sigmoid(gate_part)
    return sigmoid * (1.0 + gate_part * (1.0 - sigmoid))


def slot_table(route_rows):
    flat_routes = route_rows.reshape(-1)
    onehot = (flat_routes[:, None] == jnp.arange(EXPERTS, dtype=jnp.int32)[None, :]).astype(
        jnp.int32
    )
    earlier = jnp.cumsum(onehot, axis=0) - onehot
    return flat_routes * CAP + jnp.sum(earlier * onehot, axis=1)


def block_mask(begin, width, query_pos, query_seg, seg_all):
    key_pos = begin + jnp.arange(width, dtype=jnp.int32)
    key_seg = lax.dynamic_slice_in_dim(seg_all, begin, width)
    return (key_pos[None, :] <= query_pos[:, None]) & (key_seg[None, :] == query_seg[:, None])


def forward_piece(state, piece, grouped, query_pos, query_seg, seg_all, last_query):
    piece_keys, piece_values = piece
    count = piece_keys.shape[0]
    width = math.gcd(count, 512)
    scale = HEAD_DIM ** (-0.5)

    def forward_inner(carry, index):
        begin = index * width

        def forward_compute(current):
            best, total, accum = current
            block_keys = lax.dynamic_slice_in_dim(piece_keys, begin, width).reshape(
                width, KV_HEADS, HEAD_DIM
            )
            block_values = lax.dynamic_slice_in_dim(piece_values, begin, width).reshape(
                width, KV_HEADS, HEAD_DIM
            )
            allowed = block_mask(begin, width, query_pos, query_seg, seg_all)
            scores = (
                jnp.einsum(
                    "qkgd,skd->kgqs", grouped, block_keys, preferred_element_type=jnp.float32
                )
                * scale
            )
            scores = jnp.where(allowed[None, None], scores, masked_value)
            newest = jnp.maximum(best, jnp.max(scores, axis=-1))
            factor = jnp.exp(best - newest)
            weights = jnp.exp(scores - newest[..., None])
            total = total * factor + jnp.sum(weights, axis=-1)
            accum = accum * factor[..., None] + jnp.einsum(
                "kgqs,skd->kgqd",
                weights.astype(jnp.bfloat16),
                block_values,
                preferred_element_type=jnp.float32,
            )
            return (newest, total, accum)

        def forward_keep(current):
            return current

        return (lax.cond(begin <= last_query, forward_compute, forward_keep, carry), None)

    state, _ = lax.scan(forward_inner, state, jnp.arange(count // width, dtype=jnp.int32))
    return state


def backward_piece(
    state,
    piece,
    grouped,
    grad_grouped,
    log_totals,
    deltas,
    query_pos,
    query_seg,
    seg_all,
    last_query,
):
    piece_keys, piece_values = piece
    count = piece_keys.shape[0]
    width = math.gcd(count, 512)
    scale = HEAD_DIM ** (-0.5)
    grad_queries, keys_grad, values_grad = state
    kv_width = piece_keys.shape[1]

    def backward_inner(carry, index):
        begin = index * width

        def backward_compute(current):
            block_keys = lax.dynamic_slice_in_dim(piece_keys, begin, width).reshape(
                width, KV_HEADS, HEAD_DIM
            )
            block_values = lax.dynamic_slice_in_dim(piece_values, begin, width).reshape(
                width, KV_HEADS, HEAD_DIM
            )
            allowed = block_mask(begin, width, query_pos, query_seg, seg_all)
            scores = (
                jnp.einsum(
                    "qkgd,skd->kgqs", grouped, block_keys, preferred_element_type=jnp.float32
                )
                * scale
            )
            scores = jnp.where(allowed[None, None], scores, masked_value)
            probs = jnp.exp(scores - log_totals[..., None])
            grad_probs = jnp.einsum(
                "qkgd,skd->kgqs", grad_grouped, block_values, preferred_element_type=jnp.float32
            )
            grad_scores = (probs * (grad_probs - deltas[..., None])).astype(jnp.bfloat16)
            updated = (
                current
                + jnp.einsum(
                    "kgqs,skd->qkgd", grad_scores, block_keys, preferred_element_type=jnp.float32
                )
                * scale
            )
            key_term = (
                jnp.einsum(
                    "kgqs,qkgd->skd", grad_scores, grouped, preferred_element_type=jnp.float32
                )
                * scale
            )
            value_term = jnp.einsum(
                "kgqs,qkgd->skd",
                probs.astype(jnp.bfloat16),
                grad_grouped,
                preferred_element_type=jnp.float32,
            )
            return (updated, key_term.reshape(width, kv_width), value_term.reshape(width, kv_width))

        def backward_keep(current):
            empty = jnp.zeros((width, kv_width), jnp.float32)
            return (current, empty, empty)

        updated, key_term, value_term = lax.cond(
            begin <= last_query, backward_compute, backward_keep, carry
        )
        return (updated, (key_term, value_term))

    grad_queries, (key_terms, value_terms) = lax.scan(
        backward_inner, grad_queries, jnp.arange(count // width, dtype=jnp.int32)
    )
    keys_grad = key_terms.reshape(count, -1)
    values_grad = value_terms.reshape(count, -1)
    return (grad_queries, keys_grad, values_grad)


def body(
    hidden,
    segment_ids,
    routes,
    gates,
    cotangent,
    norm_one_gain,
    w_query,
    w_key,
    w_value,
    w_out,
    norm_two_gain,
    shared_gate,
    shared_up,
    shared_down,
    expert_gate,
    expert_up,
    expert_down,
):
    (
        gain_one,
        query_weight,
        key_weight,
        value_weight,
        out_weight,
        gain_two,
        gate_weight,
        up_weight,
        down_weight,
    ) = (
        lax.all_gather(norm_one_gain, "wt", axis=0, tiled=True),
        lax.all_gather(w_query, "wt", axis=0, tiled=True),
        lax.all_gather(w_key, "wt", axis=0, tiled=True),
        lax.all_gather(w_value, "wt", axis=0, tiled=True),
        lax.all_gather(w_out, "wt", axis=0, tiled=True),
        lax.all_gather(norm_two_gain, "wt", axis=0, tiled=True),
        lax.all_gather(shared_gate, "wt", axis=0, tiled=True),
        lax.all_gather(shared_up, "wt", axis=0, tiled=True),
        lax.all_gather(shared_down, "wt", axis=0, tiled=True),
    )
    experts_gate, experts_up, experts_down = (
        lax.all_gather(expert_gate, "wt", axis=1, tiled=True),
        lax.all_gather(expert_up, "wt", axis=1, tiled=True),
        lax.all_gather(expert_down, "wt", axis=2, tiled=True),
    )
    inputs = hidden[0].astype(jnp.float32)
    tokens = inputs.shape[0]
    width_model = inputs.shape[1]
    ctx_count = lax.axis_size("ctx")
    offset = lax.axis_index("ctx") * tokens
    query_pos = offset + jnp.arange(tokens, dtype=jnp.int32)
    last_query = offset + tokens - 1
    seg_all = segment_ids[0]
    query_seg = lax.dynamic_slice_in_dim(seg_all, offset, tokens)
    group = HEADS // KV_HEADS
    scale_one = inverse_rms(inputs)
    gain_one_full = gain_one.astype(jnp.float32)
    normed = (inputs * scale_one * gain_one_full).astype(jnp.bfloat16)
    queries = jnp.dot(normed, query_weight, preferred_element_type=jnp.float32).astype(jnp.bfloat16)
    keys = jnp.dot(normed, key_weight, preferred_element_type=jnp.float32).astype(jnp.bfloat16)
    values = jnp.dot(normed, value_weight, preferred_element_type=jnp.float32).astype(jnp.bfloat16)
    grouped = queries.reshape(tokens, KV_HEADS, group, HEAD_DIM)
    start_state = (
        jnp.full((KV_HEADS, group, tokens), masked_value, jnp.float32),
        jnp.zeros((KV_HEADS, group, tokens), jnp.float32),
        jnp.zeros((KV_HEADS, group, tokens, HEAD_DIM), jnp.float32),
    )
    best, total, accum = forward_piece(
        start_state,
        (
            lax.all_gather(keys, "ctx", axis=0, tiled=True),
            lax.all_gather(values, "ctx", axis=0, tiled=True),
        ),
        grouped,
        query_pos,
        query_seg,
        seg_all,
        last_query,
    )
    log_totals = best + jnp.log(total)
    attended_full = jnp.transpose(accum / total[..., None], (2, 0, 1, 3)).reshape(
        tokens, HEADS * HEAD_DIM
    )
    attended = attended_full.astype(jnp.bfloat16)
    middle = inputs + jnp.dot(attended, out_weight, preferred_element_type=jnp.float32)
    scale_two = inverse_rms(middle)
    gain_two_full = gain_two.astype(jnp.float32)
    normed_two = (middle * scale_two * gain_two_full).astype(jnp.bfloat16)
    shared_gate_part = jnp.dot(normed_two, gate_weight, preferred_element_type=jnp.float32)
    shared_up_part = jnp.dot(normed_two, up_weight, preferred_element_type=jnp.float32)
    shared_inner = (jax.nn.silu(shared_gate_part) * shared_up_part).astype(jnp.bfloat16)
    shared_result = jnp.dot(shared_inner, down_weight, preferred_element_type=jnp.float32)
    slots = slot_table(routes[0])
    pairs = tokens * TOPK
    owners = (
        jnp.full((EXPERTS * CAP,), pairs, jnp.int32)
        .at[slots]
        .set(jnp.arange(pairs, dtype=jnp.int32))
    )
    owner_tokens = owners // TOPK
    local_experts = experts_gate.shape[0]
    padded = jnp.concatenate([normed_two, jnp.zeros((1, width_model), jnp.bfloat16)], axis=0)
    dispatch = padded[owner_tokens].reshape(ctx_count, local_experts, CAP, width_model)
    received_rows = lax.all_to_all(dispatch, "ctx", split_axis=0, concat_axis=0, tiled=True)
    gate_part = jnp.einsum(
        "nemd,edf->nemf", received_rows, experts_gate, preferred_element_type=jnp.float32
    )
    up_part = jnp.einsum(
        "nemd,edf->nemf", received_rows, experts_up, preferred_element_type=jnp.float32
    )
    inner_rows = (jax.nn.silu(gate_part) * up_part).astype(jnp.bfloat16)
    result = jnp.einsum(
        "nemf,efd->nemd", inner_rows, experts_down, preferred_element_type=jnp.float32
    ).astype(jnp.bfloat16)
    returned_rows = lax.all_to_all(result, "ctx", split_axis=0, concat_axis=0, tiled=True)
    gate_rows = gates[0]
    picked = (
        returned_rows.reshape(EXPERTS * CAP, width_model)[slots]
        .astype(jnp.float32)
        .reshape(tokens, TOPK, width_model)
    )
    routed = jnp.sum(gate_rows[:, :, None] * picked, axis=1)
    output = (middle + shared_result + routed).astype(jnp.bfloat16)
    grad_rows = cotangent[0]
    grad_out = grad_rows.astype(jnp.float32)
    gate_flat = jnp.concatenate([gate_rows.reshape(-1), jnp.zeros((1,), jnp.float32)])
    grad_padded = jnp.concatenate([grad_out, jnp.zeros((1, width_model), jnp.float32)], axis=0)
    grad_dispatch = (gate_flat[owners][:, None] * grad_padded[owner_tokens]).astype(jnp.bfloat16)
    grad_received = lax.all_to_all(
        grad_dispatch.reshape(ctx_count, local_experts, CAP, width_model),
        "ctx",
        split_axis=0,
        concat_axis=0,
        tiled=True,
    )
    gate_part = jnp.einsum(
        "nemd,edf->nemf", received_rows, experts_gate, preferred_element_type=jnp.float32
    )
    up_part = jnp.einsum(
        "nemd,edf->nemf", received_rows, experts_up, preferred_element_type=jnp.float32
    )
    activated = jax.nn.silu(gate_part)
    inner_rows = (activated * up_part).astype(jnp.bfloat16)
    grad_inner = jnp.einsum(
        "nemd,efd->nemf", grad_received, experts_down, preferred_element_type=jnp.float32
    )
    grad_experts_down = jnp.einsum(
        "nemf,nemd->efd", inner_rows, grad_received, preferred_element_type=jnp.float32
    )
    grad_gate_part = (grad_inner * up_part * silu_slope(gate_part)).astype(jnp.bfloat16)
    grad_up_part = (grad_inner * activated).astype(jnp.bfloat16)
    grad_experts_gate = jnp.einsum(
        "nemd,nemf->edf", received_rows, grad_gate_part, preferred_element_type=jnp.float32
    )
    grad_experts_up = jnp.einsum(
        "nemd,nemf->edf", received_rows, grad_up_part, preferred_element_type=jnp.float32
    )
    grad_sent = jnp.einsum(
        "nemf,edf->nemd", grad_gate_part, experts_gate, preferred_element_type=jnp.float32
    ) + jnp.einsum("nemf,edf->nemd", grad_up_part, experts_up, preferred_element_type=jnp.float32)
    grad_returned = lax.all_to_all(
        grad_sent.astype(jnp.bfloat16), "ctx", split_axis=0, concat_axis=0, tiled=True
    )
    routed_grad = jnp.sum(
        grad_returned.reshape(EXPERTS * CAP, width_model)[slots]
        .astype(jnp.float32)
        .reshape(tokens, TOPK, width_model),
        axis=1,
    )
    sum_experts_gate, sum_experts_up, sum_experts_down = (
        lax.psum_scatter(
            grad_experts_gate.astype(jnp.bfloat16), "wt", scatter_dimension=1, tiled=True
        ).astype(jnp.float32),
        lax.psum_scatter(
            grad_experts_up.astype(jnp.bfloat16), "wt", scatter_dimension=1, tiled=True
        ).astype(jnp.float32),
        lax.psum_scatter(
            grad_experts_down.astype(jnp.bfloat16), "wt", scatter_dimension=2, tiled=True
        ).astype(jnp.float32),
    )
    grad_shared_down = jnp.einsum(
        "tf,td->fd", shared_inner, grad_rows, preferred_element_type=jnp.float32
    )
    grad_shared_inner = jnp.einsum(
        "td,fd->tf", grad_rows, down_weight, preferred_element_type=jnp.float32
    )
    grad_shared_gate_part = (
        grad_shared_inner * shared_up_part * silu_slope(shared_gate_part)
    ).astype(jnp.bfloat16)
    grad_shared_up_part = (grad_shared_inner * jax.nn.silu(shared_gate_part)).astype(jnp.bfloat16)
    grad_shared_gate = jnp.einsum(
        "td,tf->df", normed_two, grad_shared_gate_part, preferred_element_type=jnp.float32
    )
    grad_shared_up = jnp.einsum(
        "td,tf->df", normed_two, grad_shared_up_part, preferred_element_type=jnp.float32
    )
    grad_normed_two = (
        jnp.einsum(
            "tf,df->td", grad_shared_gate_part, gate_weight, preferred_element_type=jnp.float32
        )
        + jnp.einsum(
            "tf,df->td", grad_shared_up_part, up_weight, preferred_element_type=jnp.float32
        )
        + routed_grad
    )
    grad_gain_two = jnp.sum(grad_normed_two * middle * scale_two, axis=0)
    scaled_two = grad_normed_two * gain_two_full
    grad_middle = (
        grad_out
        + scale_two * scaled_two
        - middle * scale_two**3 * jnp.mean(scaled_two * middle, axis=-1, keepdims=True)
    )
    grad_branch = grad_middle.astype(jnp.bfloat16)
    grad_out_weight = jnp.einsum(
        "tq,td->qd", attended, grad_branch, preferred_element_type=jnp.float32
    )
    grad_attended = jnp.einsum(
        "td,qd->tq", grad_branch, out_weight, preferred_element_type=jnp.float32
    ).astype(jnp.bfloat16)
    grad_grouped = grad_attended.reshape(tokens, KV_HEADS, group, HEAD_DIM)
    deltas = jnp.transpose(
        jnp.sum(
            grad_grouped.astype(jnp.float32)
            * attended_full.reshape(tokens, KV_HEADS, group, HEAD_DIM),
            axis=-1,
        ),
        (1, 2, 0),
    )
    pack_len = seg_all.shape[0]
    kv_width = keys.shape[1]
    back_state = (
        jnp.zeros((tokens, KV_HEADS, group, HEAD_DIM), jnp.float32),
        jnp.zeros((pack_len, kv_width), jnp.float32),
        jnp.zeros((pack_len, kv_width), jnp.float32),
    )
    grad_queries_full, keys_terms, values_terms = backward_piece(
        back_state,
        (
            lax.all_gather(keys, "ctx", axis=0, tiled=True),
            lax.all_gather(values, "ctx", axis=0, tiled=True),
        ),
        grouped,
        grad_grouped,
        log_totals,
        deltas,
        query_pos,
        query_seg,
        seg_all,
        last_query,
    )
    grad_keys, grad_values = (
        lax.psum_scatter(
            keys_terms.astype(jnp.bfloat16), "ctx", scatter_dimension=0, tiled=True
        ).astype(jnp.float32),
        lax.psum_scatter(
            values_terms.astype(jnp.bfloat16), "ctx", scatter_dimension=0, tiled=True
        ).astype(jnp.float32),
    )
    grad_queries = grad_queries_full.reshape(tokens, HEADS * HEAD_DIM).astype(jnp.bfloat16)
    grad_keys = grad_keys.astype(jnp.bfloat16)
    grad_values = grad_values.astype(jnp.bfloat16)
    grad_query_weight = jnp.einsum(
        "tc,tq->cq", normed, grad_queries, preferred_element_type=jnp.float32
    )
    grad_key_weight = jnp.einsum("tc,tq->cq", normed, grad_keys, preferred_element_type=jnp.float32)
    grad_value_weight = jnp.einsum(
        "tc,tq->cq", normed, grad_values, preferred_element_type=jnp.float32
    )
    grad_normed = (
        jnp.einsum("tq,cq->tc", grad_queries, query_weight, preferred_element_type=jnp.float32)
        + jnp.einsum("tq,cq->tc", grad_keys, key_weight, preferred_element_type=jnp.float32)
        + jnp.einsum("tq,cq->tc", grad_values, value_weight, preferred_element_type=jnp.float32)
    )
    grad_gain_one = jnp.sum(grad_normed * inputs * scale_one, axis=0)
    scaled_one = grad_normed * gain_one_full
    grad_inputs = (
        grad_middle
        + scale_one * scaled_one
        - inputs * scale_one**3 * jnp.mean(scaled_one * inputs, axis=-1, keepdims=True)
    )
    (
        sum_gain_one,
        sum_query,
        sum_key,
        sum_value,
        sum_out,
        sum_gain_two,
        sum_gate,
        sum_up,
        sum_down,
    ) = (
        lax.psum_scatter(
            grad_gain_one.astype(jnp.bfloat16), "wt", scatter_dimension=0, tiled=True
        ).astype(jnp.float32),
        lax.psum_scatter(
            grad_query_weight.astype(jnp.bfloat16), "wt", scatter_dimension=0, tiled=True
        ).astype(jnp.float32),
        lax.psum_scatter(
            grad_key_weight.astype(jnp.bfloat16), "wt", scatter_dimension=0, tiled=True
        ).astype(jnp.float32),
        lax.psum_scatter(
            grad_value_weight.astype(jnp.bfloat16), "wt", scatter_dimension=0, tiled=True
        ).astype(jnp.float32),
        lax.psum_scatter(
            grad_out_weight.astype(jnp.bfloat16), "wt", scatter_dimension=0, tiled=True
        ).astype(jnp.float32),
        lax.psum_scatter(
            grad_gain_two.astype(jnp.bfloat16), "wt", scatter_dimension=0, tiled=True
        ).astype(jnp.float32),
        lax.psum_scatter(
            grad_shared_gate.astype(jnp.bfloat16), "wt", scatter_dimension=0, tiled=True
        ).astype(jnp.float32),
        lax.psum_scatter(
            grad_shared_up.astype(jnp.bfloat16), "wt", scatter_dimension=0, tiled=True
        ).astype(jnp.float32),
        lax.psum_scatter(
            grad_shared_down.astype(jnp.bfloat16), "wt", scatter_dimension=0, tiled=True
        ).astype(jnp.float32),
    )
    dense_parts = (
        lax.psum(sum_gain_one.astype(jnp.bfloat16), "ctx").astype(jnp.float32),
        lax.psum(sum_query.astype(jnp.bfloat16), "ctx").astype(jnp.float32),
        lax.psum(sum_key.astype(jnp.bfloat16), "ctx").astype(jnp.float32),
        lax.psum(sum_value.astype(jnp.bfloat16), "ctx").astype(jnp.float32),
        lax.psum(sum_out.astype(jnp.bfloat16), "ctx").astype(jnp.float32),
        lax.psum(sum_gain_two.astype(jnp.bfloat16), "ctx").astype(jnp.float32),
        lax.psum(sum_gate.astype(jnp.bfloat16), "ctx").astype(jnp.float32),
        lax.psum(sum_up.astype(jnp.bfloat16), "ctx").astype(jnp.float32),
        lax.psum(sum_down.astype(jnp.bfloat16), "ctx").astype(jnp.float32),
    )
    (
        final_gain_one,
        final_query,
        final_key,
        final_value,
        final_out,
        final_gain_two,
        final_gate,
        final_up,
        final_down,
    ) = dense_parts
    return (
        output[None],
        grad_inputs[None],
        final_gain_one,
        final_query,
        final_key,
        final_value,
        final_out,
        final_gain_two,
        final_gate,
        final_up,
        final_down,
        sum_experts_gate,
        sum_experts_up,
        sum_experts_down,
    )


def solution(mesh):
    placed = (
        P("wt", "ctx", None),
        P("wt", None),
        P("wt", "ctx", None),
        P("wt", "ctx", None),
        P("wt", "ctx", None),
        P("wt"),
        P("wt", None),
        P("wt", None),
        P("wt", None),
        P("wt", None),
        P("wt"),
        P("wt", None),
        P("wt", None),
        P("wt", None),
        P("ctx", "wt", None),
        P("ctx", "wt", None),
        P("ctx", None, "wt"),
    )
    return jax.shard_map(
        body,
        mesh=mesh,
        in_specs=placed,
        out_specs=(
            P("wt", "ctx", None),
            P("wt", "ctx", None),
            P("wt"),
            P("wt", None),
            P("wt", None),
            P("wt", None),
            P("wt", None),
            P("wt"),
            P("wt", None),
            P("wt", None),
            P("wt", None),
            P("ctx", "wt", None),
            P("ctx", "wt", None),
            P("ctx", None, "wt"),
        ),
        check_vma=False,
    )
```

profile of v0, /device:TPU:0, one launch (start us, length us, event | category | flops | bytes accessed | tf_op | source)
XLA Modules:
  0.0 1888.2 jit_solution(5396583043586820675)
XLA Ops:
  21.0 22.6 %all-gather.15.cloned.1.call-done = bf16[1536,512]{1,0:T(8,128)(2,1)} async-done(((bf16[384,512]{1,0:T(8,128)(2,1)}), bf16[1536,512]{1,0:T(8,128)(2,1)}) %all-gather.15.cloned.1.call-update) | async-done | bytes 1572880 | tf_op jit(solution)/shard_map/all_gather | solution.py:202
  46.6 29.8 %all-gather.21.cloned.1.call-done = bf16[1536,512]{1,0:T(8,128)(2,1)} async-done(((bf16[384,512]{1,0:T(8,128)(2,1)}), bf16[1536,512]{1,0:T(8,128)(2,1)}) %all-gather.21.cloned.1.call-update) | async-done | bytes 1572880 | tf_op jit(solution)/shard_map/all_gather | solution.py:203
  90.4 18.1 reduce-window.6
  121.0 17.4 all-gather.23.cloned.1.call-done
  142.4 54.4 %all-gather.19.cloned.1.call-done = bf16[1536,1536]{1,0:T(8,128)(2,1)} async-done(((bf16[384,1536]{1,0:T(8,128)(2,1)}), bf16[1536,1536]{1,0:T(8,128)(2,1)}) %all-gather.19.cloned.1.call-update) | async-done | bytes 4718608 | tf_op jit(solution)/shard_map/all_gather | solution.py:201
  221.5 34.0 %all-gather.25.cloned.1.call-done = bf16[1536,1536]{1,0:T(8,128)(2,1)} async-done(((bf16[384,1536]{1,0:T(8,128)(2,1)}), bf16[1536,1536]{1,0:T(8,128)(2,1)}) %all-gather.25.cloned.1.call-update) | async-done | bytes 4718608 | tf_op jit(solution)/shard_map/all_gather | solution.py:204
  310.4 137.5 %all-to-all-done = bf16[8,8,40,1536]{3,2,1,0:T(8,128)(2,1)} async-done(((bf16[8,8,40,1536]{3,2,1,0:T(8,128)(2,1)}), bf16[8,8,40,1536]{3,2,1,0:T(8,128)(2,1)}, u32[]{:S(2)}, u32[]{:S(2)}) %all-to-all-start) | async-done | bytes 7864352 | tf_op jit(solution)/shard_map/all_to_all | solution.py:273
  466.9 37.4 %all-gather.35.cloned.1.call-done = bf16[8,1536,512]{2,1,0:T(8,128)(2,1)} async-done(((bf16[8,384,512]{2,1,0:T(8,128)(2,1)}), bf16[8,1536,512]{2,1,0:T(8,128)(2,1)}) %all-gather.35.cloned.1.call-update) | async-done | bytes 12582928 | tf_op jit(solution)/shard_map/all_gather | solution.py:212
  517.8 107.7 %all-to-all-done.2 = bf16[8,8,40,1536]{3,2,1,0:T(8,128)(2,1)} async-done(((bf16[8,8,40,1536]{3,2,1,0:T(8,128)(2,1)}), bf16[8,8,40,1536]{3,2,1,0:T(8,128)(2,1)}, u32[]{:S(2)}, u32[]{:S(2)}) %all-to-all-start.2) | async-done | bytes 7864352 | tf_op jit(solution)/shard_map/all_to_all | solution.py:298
  628.6 16.8 fusion.50
  660.6 15.5 fusion.40
  692.7 42.7 %all-gather.29.cloned.1.call-done = bf16[1536,1024]{1,0:T(8,128)(2,1)} async-done(((bf16[384,1024]{1,0:T(8,128)(2,1)}), bf16[1536,1024]{1,0:T(8,128)(2,1)}) %all-gather.29.cloned.1.call-update) | async-done | bytes 3145744 | tf_op jit(solution)/shard_map/all_gather | solution.py:207
  739.2 41.9 %all-gather.31.cloned.1.call-done = bf16[1024,1536]{1,0:T(8,128)(2,1)} async-done(((bf16[256,1536]{1,0:T(8,128)(2,1)}), bf16[1024,1536]{1,0:T(8,128)(2,1)}) %all-gather.31.cloned.1.call-update) | async-done | bytes 3145744 | tf_op jit(solution)/shard_map/all_gather | solution.py:208
  788.5 72.5 %all-to-all-done.3 = bf16[8,8,40,1536]{3,2,1,0:T(8,128)(2,1)} async-done(((bf16[8,8,40,1536]{3,2,1,0:T(8,128)(2,1)}), bf16[8,8,40,1536]{3,2,1,0:T(8,128)(2,1)}, u32[]{:S(2)}, u32[]{:S(2)}) %all-to-all-start.3) | async-done | bytes 7864352 | tf_op jit(solution)/shard_map/all_to_all | solution.py:330
  905.2 31.1 %while.34 = (s32[]{:T(128)}, f32[256,4,3,128]{0,3,2,1:T(8,128)S(1)}, bf16[4,512,512]{2,1,0:T(8,128)(2,1)}, bf16[4,512,512]{2,1,0:T(8,128)(2,1)}, s32[4]{0:T(128)...) while((s32[]{:T(128)}, ...), condition=%wide.region_19.20_spmd.clone, body=%wide.region_16.19_spmd.clone.sunk | while | flops 2030699264 | bytes 46059396 | solution.py:162
  948.0 57.8 %reduce-scatter.15.cloned.1.call-done = bf16[256,512]{1,0:T(8,128)(2,1)} async-done(((bf16[2048,512]{1,0:T(8,128)(2,1)}), bf16[256,512]{1,0:T(8,128)(2,1)}) %reduce-scatter.15.cloned.1.call-update) | async-done | bytes 262160 | tf_op jit(solution)/shard_map/reduce_scatter | solution.py:421
  1008.7 34.3 %reduce-scatter.17.cloned.1.call-done = bf16[256,512]{1,0:T(8,128)(2,1)} async-done(((bf16[2048,512]{1,0:T(8,128)(2,1)}), bf16[256,512]{1,0:T(8,128)(2,1)}) %reduce-scatter.17.cloned.1.call-update) | async-done | bytes 262160 | tf_op jit(solution)/shard_map/reduce_scatter | solution.py:424
  1071.2 17.2 copy.140
  1149.0 171.1 %all-to-all-done.1 = bf16[8,8,40,1536]{3,2,1,0:T(8,128)(2,1)} async-done(((bf16[8,8,40,1536]{3,2,1,0:T(8,128)(2,1)}), bf16[8,8,40,1536]{3,2,1,0:T(8,128)(2,1)}, u32[]{:S(2)}, u32[]{:S(2)}) %all-to-all-start.1) | async-done | bytes 7864352 | tf_op jit(solution)/shard_map/all_to_all | solution.py:284
  1344.6 27.7 %reduce-scatter.25.cloned.1.call-done = bf16[384,1536]{1,0:T(8,128)(2,1)} async-done(((bf16[1536,1536]{1,0:T(8,128)(2,1)}), bf16[384,1536]{1,0:T(8,128)(2,1)}) %reduce-scatter.25.cloned.1.call-update) | async-done | bytes 1179664 | tf_op jit(solution)/shard_map/reduce_scatter | solution.py:473
  1423.0 73.5 %reduce-scatter.37.cloned.1.call-done = bf16[384,4096]{1,0:T(8,128)(2,1)} async-done(((bf16[1536,4096]{1,0:T(8,128)(2,1)}), bf16[384,4096]{1,0:T(8,128)(2,1)}) %reduce-scatter.37.cloned.1.call-update) | async-done | bytes 3145744
  1508.4 111.9 %reduce-scatter.33.cloned.1.call-done = bf16[8,384,512]{2,1,0:T(8,128)(2,1)} async-done(((bf16[8,1536,512]{2,1,0:T(8,128)(2,1)}), bf16[8,384,512]{2,1,0:T(8,128)(2,1)}) %reduce-scatter.33.cloned.1.call-update) | async-done | bytes 3145744 | tf_op jit(solution)/shard_map/reduce_scatter | solution.py:340
  1625.8 118.3 %reduce-scatter.35.cloned.1.call-done = bf16[8,384,512]{2,1,0:T(8,128)(2,1)} async-done(((bf16[8,1536,512]{2,1,0:T(8,128)(2,1)}), bf16[8,384,512]{2,1,0:T(8,128)(2,1)}) %reduce-scatter.35.cloned.1.call-update) | async-done | bytes 3145744 | tf_op jit(solution)/shard_map/reduce_scatter | solution.py:343
  1749.5 120.9 %all-reduce.9.cloned.1.call-done = (bf16[384,1536]{1,0:T(8,128)(2,1)}, bf16[384,512]{1,0:T(8,128)(2,1)}, bf16[384,512]{1,0:T(8,128)(2,1)}, bf16[384,1536]{1,0:T(...) async-done(((bf16[384,1536]{1,0:T(8,128)(2,1)}, bf16[384,512]{1,0:T(8,128)(2,1)}, bf16[384,512]{1,0:T(8,128)(2,1)}, ...) | async-done | bytes 5505040 | tf_op jit(solution)/shard_map/psum | solution.py:491
  (402 shorter events, 520.9 us)
Async XLA Ops:
  8.7 108.4 %all-gather.17.cloned.1.call-start = ((), (), s32[]{:S(2)}) async-start(), calls=%async_computation.17 | async-start | bytes 2359296 | tf_op jit(solution)/shard_map/all_gather | solution.py:240
  79.2 117.6 %all-gather.19.cloned.1.call-start = ((), (), s32[]{:S(2)}) async-start(), calls=%async_computation.18 | async-start | bytes 5898240 | tf_op jit(solution)/shard_map/all_gather | solution.py:201
  79.8 175.8 %all-gather.25.cloned.1.call-start = ((), (), s32[]{:S(2)}) async-start(), calls=%async_computation.21 | async-start | bytes 5898240 | tf_op jit(solution)/shard_map/all_gather | solution.py:204
  80.4 373.1 %all-gather.33.cloned.1.call-start = ((), (), s32[]{:S(2)}) async-start(), calls=%async_computation.25 | async-start | bytes 15728640 | tf_op jit(solution)/shard_map/all_gather | solution.py:211
  81.1 423.2 %all-gather.35.cloned.1.call-start = ((), (), s32[]{:S(2)}) async-start(), calls=%async_computation.26 | async-start | bytes 15728640 | tf_op jit(solution)/shard_map/all_gather | solution.py:212
  270.4 177.6 %all-to-all-start = ((bf16[8,8,40,1536]{3,2,1,0:T(8,128)(2,1)}), bf16[8,8,40,1536]{3,2,1,0:T(8,128)(2,1)}, u32[]{:S(2)}, u32[]{:S(2)}) async-start(bf16[8,8,40,1536]{3,2,1,0:T(8,128)(2,1)} %bitcast.309), calls=%async_computation | async-start | bytes 15728640 | tf_op jit(solution)/shard_map/all_to_all | solution.py:273
  275.3 353.3 %all-gather.37.cloned.1.call-start = ((), (), s32[]{:S(2)}) async-start(), calls=%async_computation.27 | async-start | bytes 15728640 | tf_op jit(solution)/shard_map/all_gather | solution.py:213
  447.9 177.6 %all-to-all-start.2 = ((bf16[8,8,40,1536]{3,2,1,0:T(8,128)(2,1)}), bf16[8,8,40,1536]{3,2,1,0:T(8,128)(2,1)}, u32[]{:S(2)}, u32[]{:S(2)}) async-start(bf16[8,8,40,1536]{3,2,1,0:T(8,128)(2,1)} %multiply_convert_fusion), calls=%async_computation.2 | async-start | bytes 15728640 | tf_op jit(solution)/shard_map/all_to_all | solution.py:298
  452.8 237.0 %all-gather.27.cloned.1.call-start = ((), (), s32[]{:S(2)}) async-start(), calls=%async_computation.22 | async-start | bytes 3932160 | tf_op jit(solution)/shard_map/all_gather | solution.py:206
  683.3 177.7 %all-to-all-start.3 = ((bf16[8,8,40,1536]{3,2,1,0:T(8,128)(2,1)}), bf16[8,8,40,1536]{3,2,1,0:T(8,128)(2,1)}, u32[]{:S(2)}, u32[]{:S(2)}) async-start(bf16[8,8,40,1536]{3,2,1,0:T(8,128)(2,1)} %copy.101), calls=%async_computation.3 | async-start | bytes 15728640 | tf_op jit(solution)/shard_map/all_to_all | solution.py:330
  689.6 316.2 %reduce-scatter.15.cloned.1.call-start = ((), (), s32[]{:S(2)}) async-start(), calls=%async_computation.28 | async-start | bytes 2359296 | tf_op jit(solution)/shard_map/reduce_scatter | solution.py:421
  936.3 106.7 %reduce-scatter.17.cloned.1.call-start = ((), (), s32[]{:S(2)}) async-start(), calls=%async_computation.29 | async-start | bytes 2359296 | tf_op jit(solution)/shard_map/reduce_scatter | solution.py:424
  936.8 407.6 %reduce-scatter.27.cloned.1.call-start = ((), (), s32[]{:S(2)}) async-start(), calls=%async_computation.34 | async-start | bytes 3932160 | tf_op jit(solution)/shard_map/reduce_scatter | solution.py:479
  940.2 404.3 %reduce-scatter.29.cloned.1.call-start = ((), (), s32[]{:S(2)}) async-start(), calls=%async_computation.35 | async-start | bytes 3932160 | tf_op jit(solution)/shard_map/reduce_scatter | solution.py:482
  944.0 400.5 %reduce-scatter.31.cloned.1.call-start = ((), (), s32[]{:S(2)}) async-start(), calls=%async_computation.36 | async-start | bytes 3932160 | tf_op jit(solution)/shard_map/reduce_scatter | solution.py:485
  947.9 396.6 %reduce-scatter.21.cloned.1.call-start = ((), (), s32[]{:S(2)}) async-start(), calls=%async_computation.31 | async-start | bytes 1966080 | tf_op jit(solution)/shard_map/reduce_scatter | solution.py:467
  1008.6 335.9 %reduce-scatter.23.cloned.1.call-start = ((), (), s32[]{:S(2)}) async-start(), calls=%async_computation.32 | async-start | bytes 1966080 | tf_op jit(solution)/shard_map/reduce_scatter | solution.py:470
  1045.8 298.8 %reduce-scatter.19.cloned.1.call-start = ((), (), s32[]{:S(2)}) async-start(), calls=%async_computation.30 | async-start | bytes 5898240 | tf_op jit(solution)/shard_map/reduce_scatter | solution.py:464
  1050.8 321.5 %reduce-scatter.25.cloned.1.call-start = ((), (), s32[]{:S(2)}) async-start(), calls=%async_computation.33 | async-start | bytes 5898240 | tf_op jit(solution)/shard_map/reduce_scatter | solution.py:473
  1056.1 440.4 %reduce-scatter.37.cloned.1.call-start = ((), (), s32[]{:S(2)}) async-start(), calls=%async_computation.39 | async-start | bytes 15728640
  1101.6 518.8 %reduce-scatter.33.cloned.1.call-start = ((), (), s32[]{:S(2)}) async-start(), calls=%async_computation.37 | async-start | bytes 15728640 | tf_op jit(solution)/shard_map/reduce_scatter | solution.py:340
  1115.0 629.0 %reduce-scatter.35.cloned.1.call-start = ((), (), s32[]{:S(2)}) async-start(), calls=%async_computation.38 | async-start | bytes 15728640 | tf_op jit(solution)/shard_map/reduce_scatter | solution.py:343
  1142.2 177.9 %all-to-all-start.1 = ((bf16[8,8,40,1536]{3,2,1,0:T(8,128)(2,1)}), bf16[8,8,40,1536]{3,2,1,0:T(8,128)(2,1)}, u32[]{:S(2)}, u32[]{:S(2)}) async-start(bf16[8,8,40,1536]{3,2,1,0:T(8,128)(2,1)} %copy.98), calls=%async_computation.1 | async-start | bytes 15728640 | tf_op jit(solution)/shard_map/all_to_all | solution.py:284
  1147.4 723.0 %all-reduce.9.cloned.1.call-start = ((), (), s32[]{:S(2)}) async-start(), calls=%async_computation.40 | async-start | bytes 11010048 | tf_op jit(solution)/shard_map/psum | solution.py:491
  (81 other events, 2480.4 us)
Sparse Core Ops, SparseCore 0:
  9.9 33.6 all-gather.14
  45.4 30.9 all-gather.20
  78.6 29.1 all-gather.16
  140.1 56.5 all-gather.18
  198.4 57.0 all-gather.24
  257.4 122.5 all-gather.32
  381.8 122.5 all-gather.34
  506.2 122.3 all-gather.36
  630.3 43.9 all-gather.26
  691.0 44.3 all-gather.28
  737.1 43.9 all-gather.30
  936.4 69.3 reduce-scatter.14
  1008.5 34.4 reduce-scatter.16
  1045.8 42.6 reduce-scatter.26
  1091.3 43.9 reduce-scatter.28
  1138.1 43.9 reduce-scatter.30
  1185.5 30.8 reduce-scatter.20
  1220.0 30.9 reduce-scatter.22
  1254.4 57.0 reduce-scatter.18
  1315.1 57.0 reduce-scatter.24
  1375.4 121.1 reduce-scatter.36
  1499.6 120.6 reduce-scatter.32
  1623.3 120.7 reduce-scatter.34
  1747.0 123.3 all-reduce.8
  (1 shorter events, 28.5 us)
where the time goes:
time: 1900 us; the launch traced here: 1890 us
  waiting for transfers between devices  1320 us (69%)
  matrix products  198 us (10%)
  local copies, waits for them, and re-layouts  194 us (10%)
  other arithmetic  85.8 us (5%)
  blocking collectives  42.4 us (2%)
  starting transfers between devices  22.1 us (1%)
    all_to_all x1, waiting for transfers between devices, body(): lax.all_to_all(result, 'ctx', split_axis=0, concat_axis=0, tiled=True)  171 us
    all_to_all x1, waiting for transfers between devices, body(): lax.all_to_all(dispatch, 'ctx', split_axis=0, concat_axis=0, tiled=True)  138 us
    psum x1, waiting for transfers between devices, body(): lax.psum(sum_query.astype(jnp.bfloat16), 'ctx').astype(jnp.float32)  121 us
    reduce_scatter x1, waiting for transfers between devices, body(): lax.psum_scatter(grad_experts_up.astype(jnp.bfloat16), 'wt', scatter_dime...  118 us
    reduce_scatter x1, waiting for transfers between devices, body(): lax.psum_scatter(grad_experts_gate.astype(jnp.bfloat16), 'wt', scatter_di...  112 us
    all_to_all x1, waiting for transfers between devices, body(): lax.all_to_all(grad_dispatch.reshape(ctx_count, local_experts, CAP, width...  108 us
    unnamed x26, waiting for transfers between devices  80.1 us
    all_to_all x1, waiting for transfers between devices, body(): lax.all_to_all(grad_sent.astype(jnp.bfloat16), 'ctx', split_axis=0, conca...  72.5 us
  transfers between devices with their start and end apart: 29, of which 20 were waited for; matrix products, arithmetic and copies ran while one was open for 20% of the time, Pallas kernels for 0%

commit v1 on v0

v1 whole, which is shorter than its diff:
```python
import functools
import math

import jax
import jax.numpy as jnp
from jax import lax
from jax.experimental import pallas as pl
from jax.experimental.pallas import tpu as pltpu
from jax.sharding import PartitionSpec as P

HEADS = 12
KV_HEADS = 4
HEAD_DIM = 128
EXPERTS = 64
TOPK = 6
CAP = 40


epsilon = 1e-05
masked_value = -1e30


def inverse_rms(rows):
    return lax.rsqrt(jnp.mean(rows * rows, axis=-1, keepdims=True) + epsilon)


def silu_slope(gate_part):
    sigmoid = jax.nn.sigmoid(gate_part)
    return sigmoid * (1.0 + gate_part * (1.0 - sigmoid))


def block_mask(begin, width, query_pos, query_seg, seg_all):
    key_pos = begin + jnp.arange(width, dtype=jnp.int32)
    key_seg = lax.dynamic_slice_in_dim(seg_all, begin, width)
    return (key_pos[None, :] <= query_pos[:, None]) & (key_seg[None, :] == query_seg[:, None])


def forward_piece(state, piece, grouped, query_pos, query_seg, seg_all, last_query):
    piece_keys, piece_values = piece
    count = piece_keys.shape[0]
    width = math.gcd(count, 512)
    scale = HEAD_DIM ** (-0.5)

    def forward_inner(carry, index):
        begin = index * width

        def forward_compute(current):
            best, total, accum = current
            block_keys = lax.dynamic_slice_in_dim(piece_keys, begin, width).reshape(
                width, KV_HEADS, HEAD_DIM
            )
            block_values = lax.dynamic_slice_in_dim(piece_values, begin, width).reshape(
                width, KV_HEADS, HEAD_DIM
            )
            allowed = block_mask(begin, width, query_pos, query_seg, seg_all)
            scores = (
                jnp.einsum(
                    "qkgd,skd->kgqs", grouped, block_keys, preferred_element_type=jnp.float32
                )
                * scale
            )
            scores = jnp.where(allowed[None, None], scores, masked_value)
            newest = jnp.maximum(best, jnp.max(scores, axis=-1))
            factor = jnp.exp(best - newest)
            weights = jnp.exp(scores - newest[..., None])
            total = total * factor + jnp.sum(weights, axis=-1)
            accum = accum * factor[..., None] + jnp.einsum(
                "kgqs,skd->kgqd",
                weights.astype(jnp.bfloat16),
                block_values,
                preferred_element_type=jnp.float32,
            )
            return (newest, total, accum)

        def forward_keep(current):
            return current

        return (lax.cond(begin <= last_query, forward_compute, forward_keep, carry), None)

    state, _ = lax.scan(forward_inner, state, jnp.arange(count // width, dtype=jnp.int32))
    return state


def backward_piece(
    state,
    piece,
    grouped,
    grad_grouped,
    log_totals,
    deltas,
    query_pos,
    query_seg,
    seg_all,
    last_query,
):
    piece_keys, piece_values = piece
    count = piece_keys.shape[0]
    width = math.gcd(count, 512)
    scale = HEAD_DIM ** (-0.5)
    grad_queries, keys_grad, values_grad = state
    kv_width = piece_keys.shape[1]

    def backward_inner(carry, index):
        begin = index * width

        def backward_compute(current):
            block_keys = lax.dynamic_slice_in_dim(piece_keys, begin, width).reshape(
                width, KV_HEADS, HEAD_DIM
            )
            block_values = lax.dynamic_slice_in_dim(piece_values, begin, width).reshape(
                width, KV_HEADS, HEAD_DIM
            )
            allowed = block_mask(begin, width, query_pos, query_seg, seg_all)
            scores = (
                jnp.einsum(
                    "qkgd,skd->kgqs", grouped, block_keys, preferred_element_type=jnp.float32
                )
                * scale
            )
            scores = jnp.where(allowed[None, None], scores, masked_value)
            probs = jnp.exp(scores - log_totals[..., None])
            grad_probs = jnp.einsum(
                "qkgd,skd->kgqs", grad_grouped, block_values, preferred_element_type=jnp.float32
            )
            grad_scores = (probs * (grad_probs - deltas[..., None])).astype(jnp.bfloat16)
            updated = (
                current
                + jnp.einsum(
                    "kgqs,skd->qkgd", grad_scores, block_keys, preferred_element_type=jnp.float32
                )
                * scale
            )
            key_term = (
                jnp.einsum(
                    "kgqs,qkgd->skd", grad_scores, grouped, preferred_element_type=jnp.float32
                )
                * scale
            )
            value_term = jnp.einsum(
                "kgqs,qkgd->skd",
                probs.astype(jnp.bfloat16),
                grad_grouped,
                preferred_element_type=jnp.float32,
            )
            return (updated, key_term.reshape(width, kv_width), value_term.reshape(width, kv_width))

        def backward_keep(current):
            empty = jnp.zeros((width, kv_width), jnp.float32)
            return (current, empty, empty)

        updated, key_term, value_term = lax.cond(
            begin <= last_query, backward_compute, backward_keep, carry
        )
        return (updated, (key_term, value_term))

    grad_queries, (key_terms, value_terms) = lax.scan(
        backward_inner, grad_queries, jnp.arange(count // width, dtype=jnp.int32)
    )
    keys_grad = key_terms.reshape(count, -1)
    values_grad = value_terms.reshape(count, -1)
    return (grad_queries, keys_grad, values_grad)


MESH = pl.DeviceIdType.MESH
WIDE = 56 * 2**20


def flip(index, distance):
    result = index
    bit = 1
    while bit <= distance:
        if distance // bit % 2:
            result = result + bit - 2 * bit * (index // bit % 2)
        bit *= 2
    return result


def remote(src, dst, send_sem, recv_sem, device):
    return pltpu.make_async_remote_copy(
        src_ref=src,
        dst_ref=dst,
        send_sem=send_sem,
        recv_sem=recv_sem,
        device_id=device,
        device_id_type=MESH,
    )


def greet(devices):
    barrier = pltpu.get_barrier_semaphore()
    for device in devices:
        pl.semaphore_signal(barrier, inc=1, device_id=device, device_id_type=MESH)
    pl.semaphore_wait(barrier, len(devices))


class Slabs:
    def __init__(self, count, sources, targets, here, send, recv, near_send, near_recv):
        self.c, self.w = lax.axis_index("ctx"), lax.axis_index("wt")
        self.core = lax.rem(self.c, 2)
        self.near = (flip(self.c, 1), self.w)
        self.peers = [flip(self.w, d) for d in range(1, count)]
        self.pairs = list(zip(sources, targets))
        self.here, self.send, self.recv = here, send, recv
        self.near_send, self.near_recv = near_send, near_recv

    def devices(self):
        return [(self.c, p) for p in self.peers]

    def half(self, source, core):
        rows = source.shape[0] // 2
        return pl.ds(pl.multiple_of(core * rows, 16), rows)

    def push(self, i, s):
        source, target = self.pairs[s]
        part = self.half(source, self.core)
        return remote(
            source.at[part], target.at[self.w, part], self.send.at[s, i], self.recv.at[s, i], (self.c, self.peers[i])
        )

    def arrival(self, i, s):
        source, target = self.pairs[s]
        spot = target.at[self.peers[i], self.half(source, self.core)]
        return remote(spot, spot, self.send.at[s, i], self.recv.at[s, i], (self.c, self.peers[i]))

    def hand(self, i, s, core):
        source, target = self.pairs[s]
        spot = target.at[self.peers[i], self.half(source, core)]
        return remote(spot, spot, self.near_send.at[s, i], self.near_recv.at[s, i], self.near)

    def keep(self, s):
        source, target = self.pairs[s]
        return pltpu.make_async_copy(source, target.at[self.w], self.here.at[s])

    def every(self):
        return [(i, s) for s in range(len(self.pairs)) for i in range(len(self.peers))]

    def start(self):
        for i, s in self.every():
            self.push(i, s).start()
        for s in range(len(self.pairs)):
            self.keep(s).start()

    def relay(self):
        for i, s in self.every():
            self.arrival(i, s).wait_recv()
            self.hand(i, s, self.core).start()

    def finish(self):
        for i, s in self.every():
            self.hand(i, s, 1 - self.core).wait_recv()
            self.hand(i, s, self.core).wait_send()
            self.push(i, s).wait_send()
        for s in range(len(self.pairs)):
            self.keep(s).wait()

    @staticmethod
    def scratch(slabs, count):
        dma = pltpu.SemaphoreType.DMA
        return [dma((slabs,))] + [dma((slabs, count - 1))] * 4

    @staticmethod
    def shapes(slabs, count):
        return tuple(jax.ShapeDtypeStruct((count,) + s.shape, s.dtype) for s in slabs)


def weights_kernel(count, slabs, *refs):
    sources, targets, zero_ref = refs[:slabs], refs[slabs : 2 * slabs], refs[2 * slabs]
    plan = Slabs(count, sources, targets, *refs[2 * slabs + 1 :])
    greet(plan.devices() + [plan.near])
    plan.start()
    zero_ref[...] = jnp.zeros_like(zero_ref)
    plan.relay()
    plan.finish()


def gather_weights(slabs):
    count = lax.axis_size("wt")
    return pl.pallas_call(
        functools.partial(weights_kernel, count, len(slabs)),
        out_shape=Slabs.shapes(slabs, count) + (jax.ShapeDtypeStruct((8, 128), jnp.int32),),
        in_specs=[pl.BlockSpec(memory_space=pl.ANY)] * len(slabs),
        out_specs=(pl.BlockSpec(memory_space=pl.ANY),) * len(slabs)
        + (pl.BlockSpec(memory_space=pltpu.VMEM),),
        scratch_shapes=Slabs.scratch(len(slabs), count),
        compiler_params=pltpu.CompilerParams(
            collective_id=1, has_side_effects=True, vmem_limit_bytes=WIDE
        ),
        cost_estimate=pl.CostEstimate(flops=0, bytes_accessed=150_000_000, transcendentals=0),
        name="gather_weights",
    )(*slabs)


def gather_kernel(chips, downward, paired, count, slabs, rows_ref, *refs):
    sources, out_ref, targets = refs[:slabs], refs[slabs], refs[slabs + 1 : 2 * slabs + 1]
    here, up_send, up_recv, down_send, down_recv, pair_send, pair_recv, near_send, near_recv = refs[
        2 * slabs + 1 : 2 * slabs + 10
    ]
    plan = Slabs(count, sources, targets, *refs[2 * slabs + 10 :]) if slabs else None
    c, w = lax.axis_index("ctx"), lax.axis_index("wt")
    z = c // 2
    core = lax.rem(c, 2)
    side = lax.rem(w, 2) if paired else 0
    near, partner = (flip(c, 1), w), (c, flip(w, 1))
    above = (lax.rem(c + 2, 2 * chips), w)
    below = (lax.rem(c + 2 * chips - 2, 2 * chips), w)
    greet([near, above, below] + ([partner] if paired else []) + (plan.devices() if plan else []))

    def spot(chip, which, parity):
        return out_ref.at[chip, which, parity]

    def lift(chip, source):
        return remote(source, spot(chip, side, core), up_send.at[chip], up_recv.at[chip], above)

    def drop(chip, source):
        return remote(source, spot(chip, side, core), down_send.at[chip], down_recv.at[chip], below)

    def give(chip, source):
        return remote(source, spot(chip, side, core), pair_send.at[chip], pair_recv.at[chip], partner)

    def taken(chip):
        return remote(
            spot(chip, 1 - side, core), spot(chip, 1 - side, core), pair_send.at[chip], pair_recv.at[chip], partner
        )

    def hand(chip, which, source):
        return remote(source, spot(chip, which, core), near_send.at[chip, which], near_recv.at[chip, which], near)

    def handed(chip, which):
        there = spot(chip, which, 1 - core)
        return remote(there, there, near_send.at[chip, which], near_recv.at[chip, which], near)

    def settle_pair(chip):
        taken(chip).wait_recv()
        hand(chip, 1 - side, spot(chip, 1 - side, core)).start()

    keep = pltpu.make_async_copy(rows_ref, spot(z, side, core), here)
    keep.start()
    pl.when(z < chips - 1)(lambda: lift(z, rows_ref).start())
    if downward:
        pl.when(z > 0)(lambda: drop(z, rows_ref).start())
    if paired:
        give(z, rows_ref).start()
    hand(z, side, rows_ref).start()
    if plan:
        plan.start()
    for step in range(1, chips):
        low, high = z - step, z + step

        @pl.when(low >= 0)
        def _():
            lift(low, spot(low, side, core)).wait_recv()
            pl.when(z < chips - 1)(lambda: lift(low, spot(low, side, core)).start())
            if paired:
                give(low, spot(low, side, core)).start()
            hand(low, side, spot(low, side, core)).start()

        if downward:

            @pl.when(high < chips)
            def _():
                drop(high, spot(high, side, core)).wait_recv()
                pl.when(z > 0)(lambda: drop(high, spot(high, side, core)).start())
                if paired:
                    give(high, spot(high, side, core)).start()
                hand(high, side, spot(high, side, core)).start()

        if paired:
            if step == 1:
                settle_pair(z)
            else:
                pl.when(z - step + 1 >= 0)(lambda: settle_pair(z - step + 1))
                pl.when(z + step - 1 < chips)(lambda: settle_pair(z + step - 1))
    if paired:
        pl.when(z - chips + 1 >= 0)(lambda: settle_pair(z - chips + 1))
        pl.when(z + chips - 1 < chips)(lambda: settle_pair(z + chips - 1))
    keep.wait()
    if plan:
        plan.relay()
        plan.finish()

    def finish(chip):
        here_now = spot(chip, side, core)
        pl.when((z < chips - 1) & (chip <= z))(lambda: lift(chip, here_now).wait_send())
        if downward:
            pl.when((z > 0) & (chip >= z))(lambda: drop(chip, here_now).wait_send())
        if paired:
            give(chip, here_now).wait_send()
            for which in range(2):
                hand(chip, which, spot(chip, which, core)).wait_send()
                handed(chip, which).wait_recv()
        else:
            hand(chip, side, here_now).wait_send()
            handed(chip, side).wait_recv()

    for chip in range(chips):
        if downward:
            finish(chip)
        else:
            pl.when(chip <= z)(lambda: finish(chip))


def gather_rows(rows, collective_id, downward, paired, name, slabs=()):
    chips = lax.axis_size("ctx") // 2
    count = lax.axis_size("wt")
    line = pltpu.SemaphoreType.DMA((chips,))
    both = pltpu.SemaphoreType.DMA((chips, 2))
    shape = jax.ShapeDtypeStruct((chips, 2 if paired else 1, 2) + rows.shape, rows.dtype)
    return pl.pallas_call(
        functools.partial(gather_kernel, chips, downward, paired, count, len(slabs)),
        out_shape=(shape,) + Slabs.shapes(slabs, count),
        in_specs=[pl.BlockSpec(memory_space=pl.ANY)] * (1 + len(slabs)),
        out_specs=(pl.BlockSpec(memory_space=pl.ANY),) * (1 + len(slabs)),
        scratch_shapes=[pltpu.SemaphoreType.DMA]
        + [line] * 6
        + [both] * 2
        + (Slabs.scratch(len(slabs), count) if slabs else []),
        compiler_params=pltpu.CompilerParams(
            collective_id=collective_id, has_side_effects=True, vmem_limit_bytes=WIDE
        ),
        cost_estimate=pl.CostEstimate(flops=0, bytes_accessed=250_000_000, transcendentals=0),
        name=name,
    )(rows, *slabs)


def scatter_kernel(chips, upward, paired, pieces, partial_ref, out_ref, own, sib, mate, low_in, high_in, load, near_send, near_recv, pair_send, pair_recv, up_send, up_recv, down_send, down_recv):
    c, w = lax.axis_index("ctx"), lax.axis_index("wt")
    z = c // 2
    core = lax.rem(c, 2)
    side = lax.rem(w, 2) if paired else 0
    sides = 2 if paired else 1
    near, partner = (flip(c, 1), w), (c, flip(w, 1))
    above = (lax.rem(c + 2, 2 * chips), w)
    below = (lax.rem(c + 2 * chips - 2, 2 * chips), w)
    rows = own.shape[2] // pieces
    greet([near, above, below] + ([partner] if paired else []))
    order = []
    for i in range(chips // 2):
        order += [chips - 1 - i, i]
    if chips % 2:
        order.append(chips // 2)
    if not upward:
        order = list(range(chips))

    def wanted(chip, action):
        if upward:
            action()
        else:
            pl.when(chip <= z)(action)

    def fetch(chip, which):
        return pltpu.make_async_copy(
            partial_ref.at[chip, which, core], own.at[chip, which], load.at[chip, which]
        )

    def hand(chip, which):
        return remote(
            partial_ref.at[chip, which, 1 - core],
            sib.at[chip, which],
            near_send.at[chip, which],
            near_recv.at[chip, which],
            near,
        )

    def cut(piece):
        return pl.ds(piece * rows, rows)

    def give(chip, piece):
        return remote(
            own.at[chip, 1 - side, cut(piece)],
            mate.at[chip, cut(piece)],
            pair_send.at[chip, piece],
            pair_recv.at[chip, piece],
            partner,
        )

    def lift(chip, piece):
        return remote(
            own.at[chip, side, cut(piece)],
            low_in.at[chip, cut(piece)],
            up_send.at[chip, piece],
            up_recv.at[chip, piece],
            above,
        )

    def drop(chip, piece):
        return remote(
            own.at[chip, side, cut(piece)],
            high_in.at[chip, cut(piece)],
            down_send.at[chip, piece],
            down_recv.at[chip, piece],
            below,
        )

    def add_into(chip, which, piece, other):
        spot = own.at[chip, which, cut(piece)]
        spot[...] = (spot[...].astype(jnp.float32) + other[...].astype(jnp.float32)).astype(spot.dtype)

    for chip in order:

        def begin(chip=chip):
            for which in range(sides):
                hand(chip, which).start()
                fetch(chip, which).start()

        wanted(chip, begin)

    def meet(chip):
        for which in range(sides):
            fetch(chip, which).wait()
            hand(chip, which).wait_recv()
        for piece in range(pieces):
            if paired:
                add_into(chip, 1 - side, piece, sib.at[chip, 1 - side, cut(piece)])
                give(chip, piece).start()
            add_into(chip, side, piece, sib.at[chip, side, cut(piece)])

    def travel(chip):
        for piece in range(pieces):
            if paired:
                give(chip, piece).wait_recv()
                add_into(chip, side, piece, mate.at[chip, cut(piece)])
            if upward:

                @pl.when(z < chip)
                def _():
                    @pl.when(z > 0)
                    def _():
                        lift(chip, piece).wait_recv()
                        add_into(chip, side, piece, low_in.at[chip, cut(piece)])

                    lift(chip, piece).start()

            @pl.when(z > chip)
            def _():
                @pl.when(z < chips - 1)
                def _():
                    drop(chip, piece).wait_recv()
                    add_into(chip, side, piece, high_in.at[chip, cut(piece)])

                drop(chip, piece).start()

    for i, chip in enumerate(order):
        wanted(chip, lambda: meet(chip))
        if i >= 1:
            wanted(order[i - 1], lambda: travel(order[i - 1]))
    wanted(order[-1], lambda: travel(order[-1]))
    for piece in range(pieces):
        out_ref[cut(piece), :] = own.at[z, side, cut(piece)][...].astype(jnp.float32)
    for piece in range(pieces):
        if upward:

            @pl.when(z > 0)
            def _():
                lift(z, piece).wait_recv()
                out_ref[cut(piece), :] += low_in.at[z, cut(piece)][...].astype(jnp.float32)

        @pl.when(z < chips - 1)
        def _():
            drop(z, piece).wait_recv()
            out_ref[cut(piece), :] += high_in.at[z, cut(piece)][...].astype(jnp.float32)

    def finish(chip):
        for which in range(sides):
            hand(chip, which).wait_send()
        for piece in range(pieces):
            if paired:
                give(chip, piece).wait_send()
            if upward:
                pl.when(z < chip)(lambda: lift(chip, piece).wait_send())
            pl.when(z > chip)(lambda: drop(chip, piece).wait_send())

    for chip in order:
        wanted(chip, lambda: finish(chip))


def scatter_rows(partial, collective_id, upward, paired, name):
    chips, sides, _, tokens, width = partial.shape
    pieces = 2
    dma = pltpu.SemaphoreType.DMA
    block = (tokens, width)
    return pl.pallas_call(
        functools.partial(scatter_kernel, chips, upward, paired, pieces),
        out_shape=jax.ShapeDtypeStruct(block, jnp.float32),
        in_specs=[pl.BlockSpec(memory_space=pl.ANY)],
        out_specs=pl.BlockSpec(memory_space=pltpu.VMEM),
        scratch_shapes=[
            pltpu.VMEM((chips, sides) + block, jnp.bfloat16),
            pltpu.VMEM((chips, sides) + block, jnp.bfloat16),
            pltpu.VMEM((chips if paired else 1,) + block, jnp.bfloat16),
            pltpu.VMEM((chips if upward else 1,) + block, jnp.bfloat16),
            pltpu.VMEM((chips,) + block, jnp.bfloat16),
            dma((chips, 2)),
            dma((chips, 2)),
            dma((chips, 2)),
        ]
        + [dma((chips, pieces))] * 6,
        compiler_params=pltpu.CompilerParams(
            collective_id=collective_id, has_side_effects=True, vmem_limit_bytes=WIDE
        ),
        cost_estimate=pl.CostEstimate(
            flops=0, bytes_accessed=300_000_000 if paired else 150_000_000, transcendentals=0
        ),
        name=name,
    )(partial)


def pick_kernel(scaled, slot_ref, gate_ref, rows_ref, out_ref, scale_ref=None):
    local, depth = out_ref.shape[2], out_ref.shape[3]
    tokens = rows_ref.shape[3]
    place = lax.broadcasted_iota(jnp.int32, (depth, tokens), 0)
    total, weight = None, None
    for core in range(2):
        span = slice(core * tokens, (core + 1) * tokens)
        chosen = [slot_ref[0, 0, e : e + 1, span] == place for e in range(local)]
        ones = jnp.concatenate([c.astype(jnp.float32) for c in chosen], axis=0).astype(jnp.bfloat16)
        rows = rows_ref[0, core, 0] if scaled else rows_ref[0, 0, core]
        term = jnp.dot(ones, rows, preferred_element_type=jnp.float32)
        total = term if total is None else total + term
        if scaled:
            gates = jnp.concatenate(
                [
                    jnp.sum(jnp.where(c, gate_ref[0, 0, e : e + 1, span], 0.0), axis=1, keepdims=True)
                    for e, c in enumerate(chosen)
                ],
                axis=0,
            )
            weight = gates if weight is None else weight + gates
    if scaled:
        total = total * weight
        scale_ref[0, 0] = jnp.broadcast_to(weight, (local * depth, 128)).reshape(local, depth, 128)
    out_ref[0, 0] = total.astype(jnp.bfloat16).reshape(local, depth, total.shape[1])


def pick_rows(rows, slots, gates, scaled):
    chips, sides, local, both = slots.shape
    tokens, width = both // 2, rows.shape[4]
    depth = 2 * CAP
    table = pl.BlockSpec((1, 1, local, both), lambda z, s: (z, s, 0, 0))
    shapes = [jax.ShapeDtypeStruct((chips, sides, local, depth, width), jnp.bfloat16)]
    specs = [pl.BlockSpec((1, 1, local, depth, width), lambda z, s: (z, s, 0, 0, 0))]
    if scaled:
        shapes.append(jax.ShapeDtypeStruct((chips, sides, local, depth, 128), jnp.float32))
        specs.append(pl.BlockSpec((1, 1, local, depth, 128), lambda z, s: (z, s, 0, 0, 0)))
        source = pl.BlockSpec((1, 2, 1, tokens, width), lambda z, s: (z, 0, s, 0, 0))
    else:
        source = pl.BlockSpec((1, 1, 2, tokens, width), lambda z, s: (z, s, 0, 0, 0))
    return pl.pallas_call(
        functools.partial(pick_kernel, scaled),
        grid=(chips, sides),
        out_shape=shapes,
        in_specs=[table, table, source],
        out_specs=specs,
        compiler_params=pltpu.CompilerParams(vmem_limit_bytes=WIDE),
        cost_estimate=pl.CostEstimate(
            flops=4 * chips * sides * local * depth * both * width // 2,
            bytes_accessed=40_000_000,
            transcendentals=0,
        ),
        name="pick_grads" if scaled else "pick_tokens",
    )(slots, gates, rows)


def spread_kernel(slot_ref, rows_ref, out_ref):
    local, depth, width = rows_ref.shape[2:]
    tokens = out_ref.shape[3]
    place = lax.broadcasted_iota(jnp.int32, (depth, tokens), 0)
    rows = rows_ref[0, 0].reshape(local * depth, width)
    for core in range(2):
        span = slice(core * tokens, (core + 1) * tokens)
        ones = jnp.concatenate(
            [(slot_ref[0, 0, e : e + 1, span] == place).astype(jnp.float32) for e in range(local)], axis=0
        ).astype(jnp.bfloat16)
        out_ref[0, 0, core] = lax.dot_general(
            ones, rows, (((0,), (0,)), ((), ())), preferred_element_type=jnp.float32
        ).astype(jnp.bfloat16)


def spread_rows(rows, slots, name):
    chips, sides, local, both = slots.shape
    depth, width = rows.shape[3:]
    tokens = both // 2
    return pl.pallas_call(
        spread_kernel,
        grid=(chips, sides),
        out_shape=jax.ShapeDtypeStruct((chips, sides, 2, tokens, width), jnp.bfloat16),
        in_specs=[
            pl.BlockSpec((1, 1, local, both), lambda z, s: (z, s, 0, 0)),
            pl.BlockSpec((1, 1, local, depth, width), lambda z, s: (z, s, 0, 0, 0)),
        ],
        out_specs=pl.BlockSpec((1, 1, 2, tokens, width), lambda z, s: (z, s, 0, 0, 0)),
        compiler_params=pltpu.CompilerParams(vmem_limit_bytes=WIDE),
        cost_estimate=pl.CostEstimate(
            flops=2 * chips * sides * local * depth * both * width,
            bytes_accessed=40_000_000,
            transcendentals=0,
        ),
        name=name,
    )(slots, rows)


def expert_kernel(blocks, x_ref, g_ref, scale_ref, *refs):
    gate_refs, up_refs, down_refs = refs[:blocks], refs[blocks : 2 * blocks], refs[2 * blocks : 3 * blocks]
    result_ref, back_ref, grad_gate_ref, grad_up_ref, grad_down_ref = refs[3 * blocks :]
    w = lax.axis_index("wt")
    chips, sides, _, depth, width = x_ref.shape
    rows = chips * sides * depth
    part = gate_refs[0].shape[1]
    nn, nt, tn = (((1,), (0,)), ((), ())), (((1,), (1,)), ((), ())), (((0,), (0,)), ((), ()))

    def dot(a, b, dims):
        return lax.dot_general(a, b, dims, preferred_element_type=jnp.float32)

    def columns(ref, q):
        if blocks == 1:
            return ref.at[:, :, 0]
        span = pl.ds(pl.multiple_of(flip(w, q) * part, 128), part)
        return ref.at[:, :, 0, :, span]

    def piece(ref, q):
        return columns(ref, q)[...].reshape(rows, part)

    gate, up, grad_inner = None, None, None
    for q in range(blocks):
        x = piece(x_ref, q)
        more_gate, more_up = dot(x, gate_refs[q][0], nn), dot(x, up_refs[q][0], nn)
        gate, up = (more_gate, more_up) if q == 0 else (gate + more_gate, up + more_up)
    for q in range(blocks):
        more = dot(piece(g_ref, q), down_refs[q][0], nt)
        grad_inner = more if q == 0 else grad_inner + more
    sigmoid = jax.nn.sigmoid(gate)
    activated = gate * sigmoid
    inner = (activated * up).astype(jnp.bfloat16)
    grad_gate = (grad_inner * up * (sigmoid * (1.0 + gate * (1.0 - sigmoid)))).astype(jnp.bfloat16)
    grad_up = (grad_inner * activated).astype(jnp.bfloat16)
    scale = scale_ref[...].reshape(rows, 128)[:, :1]
    for q in range(blocks):
        result = dot(inner, down_refs[q][0], nn) * scale
        columns(result_ref, q)[...] = result.astype(jnp.bfloat16).reshape(chips, sides, depth, part)
        back = dot(grad_gate, gate_refs[q][0], nt) + dot(grad_up, up_refs[q][0], nt)
        columns(back_ref, q)[...] = back.astype(jnp.bfloat16).reshape(chips, sides, depth, part)
        grad_down_ref[q, 0] = dot(inner, piece(g_ref, q), tn).astype(jnp.bfloat16)
        x = piece(x_ref, q)
        grad_gate_ref[q, 0] = dot(x, grad_gate, tn).astype(jnp.bfloat16)
        grad_up_ref[q, 0] = dot(x, grad_up, tn).astype(jnp.bfloat16)


def run_experts(x, g, scale, gates, ups, downs):
    chips, sides, local, depth, width = x.shape
    blocks = len(gates)
    part, inner = gates[0].shape[1:]
    large = chips * sides * depth > 1024
    rows = pl.BlockSpec((chips, sides, 1, depth, width), lambda e: (0, 0, e, 0, 0))
    sources = pl.BlockSpec(
        (chips, sides, 1, depth, width),
        lambda e: (0, 0, e, 0, 0),
        pipeline_mode=pl.Buffered(1 if large else 2),
    )
    scales = pl.BlockSpec((chips, sides, 1, depth, 128), lambda e: (0, 0, e, 0, 0))
    tall = pl.BlockSpec((1, part, inner), lambda e: (e, 0, 0))
    flat = pl.BlockSpec((1, inner, part), lambda e: (e, 0, 0))
    tall_out = pl.BlockSpec((blocks, 1, part, inner), lambda e: (0, e, 0, 0))
    flat_out = pl.BlockSpec((blocks, 1, inner, part), lambda e: (0, e, 0, 0))
    total = chips * sides * local * depth
    return pl.pallas_call(
        functools.partial(expert_kernel, blocks),
        grid=(local,),
        out_shape=(
            jax.ShapeDtypeStruct(x.shape, jnp.bfloat16),
            jax.ShapeDtypeStruct(x.shape, jnp.bfloat16),
            jax.ShapeDtypeStruct((blocks, local, part, inner), jnp.bfloat16),
            jax.ShapeDtypeStruct((blocks, local, part, inner), jnp.bfloat16),
            jax.ShapeDtypeStruct((blocks, local, inner, part), jnp.bfloat16),
        ),
        in_specs=[sources, sources, scales] + [tall] * (2 * blocks) + [flat] * blocks,
        out_specs=(rows, rows, tall_out, tall_out, flat_out),
        compiler_params=pltpu.CompilerParams(vmem_limit_bytes=60 * 2**20),
        cost_estimate=pl.CostEstimate(
            flops=18 * total * width * inner, bytes_accessed=70_000_000, transcendentals=total * inner
        ),
        name="experts",
    )(x, g, scale, *gates, *ups, *downs)


def swap_pairs(value, axis, distance):
    count = lax.axis_size(axis)
    return lax.ppermute(value, axis, [(i, i ^ distance) for i in range(count)])


def own_and_other(stacked, mine):
    return (
        lax.dynamic_index_in_dim(stacked, mine, 0, keepdims=False),
        lax.dynamic_index_in_dim(stacked, 1 - mine, 0, keepdims=False),
    )


def in_order(own, other, mine):
    first = jnp.where(mine == 0, own, other)
    second = jnp.where(mine == 0, other, own)
    return jnp.stack([first, second])


def collect_expert(shard, side, pairs):
    local = shard.shape[0]
    kept, given = own_and_other(shard.reshape((2, local // 2) + shard.shape[1:]), side)
    blocks = [kept, swap_pairs(given, "wt", 1)]
    for d in range(1, pairs):
        blocks += [swap_pairs(blocks[0], "wt", 2 * d), swap_pairs(blocks[1], "wt", 2 * d)]
    return blocks


def settle_blocks(blocks, index, axis):
    stacked = jnp.stack(blocks)
    return jnp.concatenate(
        [
            lax.dynamic_index_in_dim(stacked, jnp.bitwise_xor(j, index), 0, False)
            for j in range(len(blocks))
        ],
        axis=axis,
    )


def split_blocks(whole, index, count, axis):
    parts = jnp.stack(jnp.split(whole, count, axis=axis))
    return jnp.stack(
        [
            lax.dynamic_index_in_dim(parts, jnp.bitwise_xor(q, index), 0, False)
            for q in range(count)
        ]
    )


def scatter_expert(grads, side, pairs):
    total = grads[:2].astype(jnp.float32)
    for d in range(1, pairs):
        total = total + swap_pairs(grads[2 * d : 2 * d + 2], "wt", 2 * d).astype(jnp.float32)
    other = swap_pairs(total[1].astype(jnp.bfloat16), "wt", 1).astype(jnp.float32)
    both = in_order(total[0], other, side)
    return both.reshape((-1,) + both.shape[2:])


def gather_side(rows, side):
    both = in_order(rows, swap_pairs(rows, "wt", 1), side)
    return lax.all_gather(both, "ctx", axis=0)


def body(
    hidden,
    segment_ids,
    routes,
    gates,
    cotangent,
    norm_one_gain,
    w_query,
    w_key,
    w_value,
    w_out,
    norm_two_gain,
    shared_gate,
    shared_up,
    shared_down,
    expert_gate,
    expert_up,
    expert_down,
):
    wt_index = lax.axis_index("wt")
    wt_count = lax.axis_size("wt")
    ctx_count = lax.axis_size("ctx")
    chips = ctx_count // 2
    pairs = wt_count // 2
    tokens, width_model = hidden.shape[1:]
    wide, kv_width = w_query.shape[1], w_key.shape[1]
    shared_width = shared_gate.shape[1]
    slab, gains, zero = gather_weights(
        (
            jnp.concatenate([w_query, w_key, w_value], axis=1),
            jnp.concatenate(
                [
                    norm_one_gain[None],
                    norm_two_gain[None],
                    jnp.zeros((30, norm_one_gain.shape[0]), jnp.bfloat16),
                ]
            ),
        )
    )
    side = lax.rem(wt_index, 2)
    later = side + zero[0, 0]
    slab = slab.reshape(-1, slab.shape[2])
    gain_one, gain_two = gains[:, 0].reshape(-1), gains[:, 1].reshape(-1)
    tables = jnp.concatenate(
        [jnp.swapaxes(routes[0], 0, 1).astype(jnp.float32), jnp.swapaxes(gates[0], 0, 1)], axis=0
    )
    all_tables = gather_side(tables, side)
    gate_blocks = collect_expert(expert_gate, later, pairs)
    up_blocks = collect_expert(expert_up, later, pairs)
    down_blocks = collect_expert(expert_down, later, pairs)
    local = expert_gate.shape[0] // 2
    first_expert = (lax.axis_index("ctx") * 2 + side) * local

    inputs = hidden[0].astype(jnp.float32)
    offset = lax.axis_index("ctx") * tokens
    query_pos = offset + jnp.arange(tokens, dtype=jnp.int32)
    last_query = offset + tokens - 1
    seg_all = segment_ids[0]
    query_seg = lax.dynamic_slice_in_dim(seg_all, offset, tokens)
    group = HEADS // KV_HEADS
    scale_one = inverse_rms(inputs)
    gain_one_full = gain_one.astype(jnp.float32)
    normed = (inputs * scale_one * gain_one_full).astype(jnp.bfloat16)
    projected = jnp.dot(normed, slab, preferred_element_type=jnp.float32).astype(jnp.bfloat16)
    queries = projected[:, :wide]
    both, out_weight, both_weight, down_weight = gather_rows(
        projected[:, wide:],
        2,
        False,
        False,
        "gather_keys",
        (w_out, jnp.concatenate([shared_gate, shared_up], axis=1), shared_down),
    )
    out_weight = out_weight.reshape(-1, out_weight.shape[2])
    both_weight = both_weight.reshape(-1, both_weight.shape[2])
    down_weight = down_weight.reshape(-1, down_weight.shape[2])
    both = both.reshape(-1, 2 * kv_width)
    all_keys, all_values = both[:, :kv_width], both[:, kv_width:]

    table_shape = (chips, 2, 2, 2 * TOPK, tokens)
    ordered_tables = jnp.transpose(all_tables.reshape(table_shape), (0, 2, 3, 1, 4)).reshape(
        chips, 2, 2 * TOPK, 2 * tokens
    )
    experts_here = (first_expert + jnp.arange(local, dtype=jnp.int32)).astype(jnp.float32)
    named = ordered_tables[:, :, None, :TOPK] == experts_here[None, None, :, None, None]
    member = jnp.any(named, axis=3)
    slot_gates = jnp.sum(jnp.where(named, ordered_tables[:, :, None, TOPK:], 0.0), axis=3)
    earlier = (
        jnp.arange(2 * tokens)[:, None] < jnp.arange(2 * tokens)[None, :]
    ).astype(jnp.bfloat16)
    rank = jnp.dot(member.astype(jnp.bfloat16), earlier, preferred_element_type=jnp.float32)
    slots = jnp.where(member, rank.astype(jnp.int32), -1)

    grad_rows = cotangent[0]
    all_grads = gather_side(
        lax.dynamic_index_in_dim(jnp.stack([grad_rows, grad_rows]), later - side, 0, False), side
    ).reshape(chips, 2, 2, tokens, width_model)

    grouped = queries.reshape(tokens, KV_HEADS, group, HEAD_DIM)
    start_state = (
        jnp.full((KV_HEADS, group, tokens), masked_value, jnp.float32),
        jnp.zeros((KV_HEADS, group, tokens), jnp.float32),
        jnp.zeros((KV_HEADS, group, tokens, HEAD_DIM), jnp.float32),
    )
    best, total, accum = forward_piece(
        start_state, (all_keys, all_values), grouped, query_pos, query_seg, seg_all, last_query
    )
    log_totals = best + jnp.log(total)
    attended_full = jnp.transpose(accum / total[..., None], (2, 0, 1, 3)).reshape(
        tokens, HEADS * HEAD_DIM
    )
    attended = attended_full.astype(jnp.bfloat16)
    middle = inputs + jnp.dot(attended, out_weight, preferred_element_type=jnp.float32)
    scale_two = inverse_rms(middle)
    gain_two_full = gain_two.astype(jnp.float32)
    normed_two = (middle * scale_two * gain_two_full).astype(jnp.bfloat16)

    (all_rows,) = gather_rows(normed_two, 3, True, True, "gather_tokens")
    (received_rows,) = pick_rows(all_rows, slots, slot_gates, False)
    grad_received, row_gates = pick_rows(all_grads, slots, slot_gates, True)
    if gate_blocks[0].shape[1] % 128:
        results, backs, grads_gate, grads_up, grads_down = run_experts(
            received_rows,
            grad_received,
            row_gates,
            [settle_blocks(gate_blocks, wt_index, 1)],
            [settle_blocks(up_blocks, wt_index, 1)],
            [settle_blocks(down_blocks, wt_index, 2)],
        )
        grads_gate = split_blocks(grads_gate[0], wt_index, wt_count, 1)
        grads_up = split_blocks(grads_up[0], wt_index, wt_count, 1)
        grads_down = split_blocks(grads_down[0], wt_index, wt_count, 2)
    else:
        results, backs, grads_gate, grads_up, grads_down = run_experts(
            received_rows, grad_received, row_gates, gate_blocks, up_blocks, down_blocks
        )
    sum_experts_gate = scatter_expert(grads_gate, side, pairs)
    sum_experts_up = scatter_expert(grads_up, side, pairs)
    sum_experts_down = scatter_expert(grads_down, side, pairs)
    routed_grad = scatter_rows(
        spread_rows(backs, slots, "spread_grads"), 5, True, True, "scatter_grads"
    )
    routed = scatter_rows(
        spread_rows(results, slots, "spread_results"), 4, True, True, "scatter_results"
    )

    shared_parts = jnp.dot(normed_two, both_weight, preferred_element_type=jnp.float32)
    shared_gate_part, shared_up_part = shared_parts[:, :shared_width], shared_parts[:, shared_width:]
    shared_inner = (jax.nn.silu(shared_gate_part) * shared_up_part).astype(jnp.bfloat16)
    shared_result = jnp.dot(shared_inner, down_weight, preferred_element_type=jnp.float32)
    output = (middle + shared_result + routed).astype(jnp.bfloat16)
    grad_out = grad_rows.astype(jnp.float32)
    grad_shared_down = jnp.einsum(
        "tf,td->fd", shared_inner, grad_rows, preferred_element_type=jnp.float32
    )
    grad_shared_inner = jnp.einsum(
        "td,fd->tf", grad_rows, down_weight, preferred_element_type=jnp.float32
    )
    grad_shared_gate_part = (
        grad_shared_inner * shared_up_part * silu_slope(shared_gate_part)
    ).astype(jnp.bfloat16)
    grad_shared_up_part = (grad_shared_inner * jax.nn.silu(shared_gate_part)).astype(jnp.bfloat16)
    grad_shared_parts = jnp.concatenate([grad_shared_gate_part, grad_shared_up_part], axis=1)
    grad_shared_both = jnp.einsum(
        "td,tf->df", normed_two, grad_shared_parts, preferred_element_type=jnp.float32
    )
    grad_normed_two = (
        jnp.einsum("tf,df->td", grad_shared_parts, both_weight, preferred_element_type=jnp.float32)
        + routed_grad
    )
    grad_gain_two = jnp.sum(grad_normed_two * middle * scale_two, axis=0)
    scaled_two = grad_normed_two * gain_two_full
    grad_middle = (
        grad_out
        + scale_two * scaled_two
        - middle * scale_two**3 * jnp.mean(scaled_two * middle, axis=-1, keepdims=True)
    )
    grad_branch = grad_middle.astype(jnp.bfloat16)
    grad_out_weight = jnp.einsum(
        "tq,td->qd", attended, grad_branch, preferred_element_type=jnp.float32
    )
    grad_attended = jnp.einsum(
        "td,qd->tq", grad_branch, out_weight, preferred_element_type=jnp.float32
    ).astype(jnp.bfloat16)
    grad_grouped = grad_attended.reshape(tokens, KV_HEADS, group, HEAD_DIM)
    deltas = jnp.transpose(
        jnp.sum(
            grad_grouped.astype(jnp.float32)
            * attended_full.reshape(tokens, KV_HEADS, group, HEAD_DIM),
            axis=-1,
        ),
        (1, 2, 0),
    )
    pack_len = seg_all.shape[0]
    back_state = (
        jnp.zeros((tokens, KV_HEADS, group, HEAD_DIM), jnp.float32),
        jnp.zeros((pack_len, kv_width), jnp.float32),
        jnp.zeros((pack_len, kv_width), jnp.float32),
    )
    grad_queries_full, keys_terms, values_terms = backward_piece(
        back_state,
        (all_keys, all_values),
        grouped,
        grad_grouped,
        log_totals,
        deltas,
        query_pos,
        query_seg,
        seg_all,
        last_query,
    )
    grad_both = scatter_rows(
        jnp.concatenate([keys_terms, values_terms], axis=1)
        .astype(jnp.bfloat16)
        .reshape(chips, 1, 2, tokens, 2 * kv_width),
        6,
        False,
        False,
        "scatter_keys",
    ).astype(jnp.bfloat16)
    grad_queries = grad_queries_full.reshape(tokens, HEADS * HEAD_DIM).astype(jnp.bfloat16)
    grad_projected = jnp.concatenate([grad_queries, grad_both], axis=1)
    grad_slab = jnp.einsum("tc,tq->cq", normed, grad_projected, preferred_element_type=jnp.float32)
    grad_normed = jnp.einsum(
        "tq,cq->tc", grad_projected, slab, preferred_element_type=jnp.float32
    )
    grad_gain_one = jnp.sum(grad_normed * inputs * scale_one, axis=0)
    scaled_one = grad_normed * gain_one_full
    grad_inputs = (
        grad_middle
        + scale_one * scaled_one
        - inputs * scale_one**3 * jnp.mean(scaled_one * inputs, axis=-1, keepdims=True)
    )

    def reduced(grad):
        part = lax.psum_scatter(grad.astype(jnp.bfloat16), "wt", scatter_dimension=0, tiled=True)
        return lax.psum(part, "ctx").astype(jnp.float32)

    final_shared = reduced(grad_shared_both)
    final_gate, final_up = final_shared[:, :shared_width], final_shared[:, shared_width:]
    final_down = reduced(grad_shared_down)
    final_out = reduced(grad_out_weight)
    final_slab = reduced(grad_slab)
    final_query = final_slab[:, :wide]
    final_key = final_slab[:, wide : wide + kv_width]
    final_value = final_slab[:, wide + kv_width :]
    final_gains = reduced(jnp.stack([grad_gain_one, grad_gain_two], axis=1))
    final_gain_one, final_gain_two = final_gains[:, 0], final_gains[:, 1]
    return (
        output[None],
        grad_inputs[None],
        final_gain_one,
        final_query,
        final_key,
        final_value,
        final_out,
        final_gain_two,
        final_gate,
        final_up,
        final_down,
        sum_experts_gate,
        sum_experts_up,
        sum_experts_down,
    )


def solution(mesh):
    placed = (
        P("wt", "ctx", None),
        P("wt", None),
        P("wt", "ctx", None),
        P("wt", "ctx", None),
        P("wt", "ctx", None),
        P("wt"),
        P("wt", None),
        P("wt", None),
        P("wt", None),
        P("wt", None),
        P("wt"),
        P("wt", None),
        P("wt", None),
        P("wt", None),
        P("ctx", "wt", None),
        P("ctx", "wt", None),
        P("ctx", None, "wt"),
    )
    return jax.shard_map(
        body,
        mesh=mesh,
        in_specs=placed,
        out_specs=(
            P("wt", "ctx", None),
            P("wt", "ctx", None),
            P("wt"),
            P("wt", None),
            P("wt", None),
            P("wt", None),
            P("wt", None),
            P("wt"),
            P("wt", None),
            P("wt", None),
            P("wt", None),
            P("ctx", "wt", None),
            P("ctx", "wt", None),
            P("ctx", None, "wt"),
        ),
        check_vma=False,
    )
```

time: 1900 us -> 1480 us (0.78)
  waiting for transfers between devices: 1320 us -> 292 us
  Pallas kernels: 0 us -> 841 us
  matrix products: 198 us -> 63.3 us
  local copies, waits for them, and re-layouts: 194 us -> 88.3 us
  blocking collectives: 42.4 us -> 69.4 us
  other arithmetic: 85.8 us -> 60.3 us
    pallas_call x0 -> x11, Pallas kernels: none -> 841 us  [the longest x2 369 us: gather_rows(): pl.pallas_call(functools.partial(gather_kernel, chips, downward, paired,...]
    all_to_all x4 -> x0, waiting for transfers between devices: 489 us -> none  [the longest x1 171 us: body(): lax.all_to_all(result, 'ctx', split_axis=0, concat_axis=0, tiled=True)]
    reduce_scatter x11 -> x4, waiting for transfers between devices: 350 us -> 0.03 us  [reduced(): lax.psum_scatter(grad.astype(jnp.bfloat16), 'wt', scatter_dimension=0, ti...]
    all_gather x12 -> x1, waiting for transfers between devices: 283 us -> 0.01 us  [gather_side(): return lax.all_gather(both, 'ctx', axis=0)]
    ppermute x0 -> x17, waiting for transfers between devices: none -> 216 us  [swap_pairs(): return lax.ppermute(value, axis, [(i, i ^ distance) for i in range(count)])]
    dot_general x24 -> x7, matrix products: 165 us -> 31.9 us  [the longest x1 6.77 us: body(): jnp.einsum('tq,cq->tc', grad_projected, slab, preferred_element_type=jnp....]
    unnamed x26 -> x8, waiting for transfers between devices: 80.1 us -> 0.12 us
    gather x5 -> x0, local copies, waits for them, and re-layouts: 63.7 us -> none  [the longest x1 15.4 us: body(): returned_rows.reshape(EXPERTS * CAP, width_model)[slots].astype(jnp.float32)]
  transfers between devices with their start and end apart: 29 -> 24, of which waited for: 20 -> 7; matrix products, arithmetic and copies ran while one was open for 20% -> 12% of each run, Pallas kernels for 0% -> 53%
where the time goes in v1:
time: 1480 us; the launch traced here: 1460 us
  Pallas kernels  841 us (57%)
  waiting for transfers between devices  292 us (20%)
  local copies, waits for them, and re-layouts  88.3 us (6%)
  blocking collectives  69.4 us (5%)
  matrix products  63.3 us (4%)
  other arithmetic  60.3 us (4%)
  starting transfers between devices  24.6 us (2%)
  between operations  19.6 us (1%)
    pallas_call x2, Pallas kernels, gather_rows(): pl.pallas_call(functools.partial(gather_kernel, chips, downward, paired,...  369 us
    pallas_call x3, Pallas kernels, scatter_rows(): pl.pallas_call(functools.partial(scatter_kernel, chips, upward, paired, p...  297 us
    ppermute x17, waiting for transfers between devices, swap_pairs(): return lax.ppermute(value, axis, [(i, i ^ distance) for i in range(count)])  216 us
    psum x1, waiting for transfers between devices, reduced(): return lax.psum(part, 'ctx').astype(jnp.float32)  75.8 us
    pallas_call x1, Pallas kernels, gather_weights(): pl.pallas_call(functools.partial(weights_kernel, count, len(slabs)), out_...  66.1 us
    pallas_call x1, Pallas kernels, run_experts(): pl.pallas_call(functools.partial(expert_kernel, blocks), grid=(local,), o...  57.9 us
    all_gather x1, blocking collectives, gather_side(): return lax.all_gather(both, 'ctx', axis=0)  47.3 us
  transfers between devices with their start and end apart: 24, of which 7 were waited for; matrix products, arithmetic and copies ran while one was open for 12% of the time, Pallas kernels for 53%

profile of v1, /device:TPU:0, one launch (start us, length us, event | category | flops | bytes accessed | tf_op | source)
XLA Modules:
  0.0 1464.3 jit_solution(14613105225402774344)
XLA Ops:
  13.2 66.1 %gather_weights.1 = (bf16[4,384,2560]{2,1,0:T(8,128)(2,1)}, bf16[4,32,384]{2,1,0:T(8,128)(2,1)}, s32[8,128]{1,0:T(8,128)}) custom-call(bf16[384,2560]{1,0:T(8,128)(2,1)} %pad_maximum_fusion.4.refs_0_, bf16[32,384]{1,0:T(8,128)(2,1)} %maximum_maximum_fusion.refs_1_), custom_call_target="tpu_custom_call" | custom-call | bytes 150000000 | tf_op jit(solution)/shard_map/gather_weights/pallas_call | solution.py:278
  83.4 18.4 %collective-permute-done.1 = bf16[256,1536]{1,0:T(8,128)(2,1)S(1)} collective-permute-done((bf16[256,1536]{1,0:T(8,128)(2,1)S(1)}, bf16[256,1536]{1,0:T(8,128)(2,1)S(1)}, u32[]{:S(2)}, u32[]{:S(2)}) %collective-permute-start.1) | collective-permute-done | bytes 786464 | tf_op jit(solution)/shard_map/ppermute | solution.py:786
  114.4 128.5 %gather_keys.1 = (bf16[4,1,2,256,1024]{4,3,2,1,0:T(8,128)(2,1)}, bf16[4,384,1536]{2,1,0:T(8,128)(2,1)}, bf16[4,384,2048]{2,1,0:T(8,128)(2,1)}, bf16[4,256,1536]{2,1,0:T(8,128)(2,1)}) custom-call(bf16[256,1024]{1,0:T(8,128)(2,1)} %slice.123.rows_ref, bf16[384,1536]{1,0:T(8,128)(2,1)} %refs_0_.1, bf16[384,2048]{1,0:T(8,128)(2,1)} %pad_maximum_fusion.5.refs_1_, ...), custom_call_target="tpu_custom_call" | custom-call | bytes 250000000 | tf_op jit(solution)/shard_map/gather_keys/pallas_call | solution.py:408
  255.0 12.5 while.33
  303.8 240.1 %gather_tokens.1.rows_ref = bf16[4,2,2,256,1536]{4,3,2,1,0:T(8,128)(2,1)} custom-call(bf16[256,1536]{1,0:T(8,128)(2,1)} %copy-done.16), custom_call_target="tpu_custom_call" | custom-call | bytes 250000000 | tf_op jit(solution)/shard_map/gather_tokens/pallas_call | solution.py:408
  548.7 47.3 %all-gather = f32[16,12,256]{2,1,0:T(8,128)S(1)} all-gather(f32[2,12,256]{2,1,0:T(8,128)S(1)} %pad_maximum_fusion.13), channel_id=2, replica_groups=mesh['ctx'=8,'wt'=4] {'ctx'}, dimensions={0}, use_global_device_ids=true | all-gather | bytes 221184 | tf_op jit(solution)/shard_map/all_gather | solution.py:843
  599.9 12.5 pick_tokens.1.x_ref
  612.5 12.6 pick_grads.1
  625.1 23.9 %collective-permute-done.10.refs_11_ = bf16[4,512,384]{2,1,0:T(8,128)(2,1)} collective-permute-done((bf16[4,512,384]{2,1,0:T(8,128)(2,1)}, bf16[4,512,384]{2,1,0:T(8,128)(2,1)}, u32[]{:S(2)}, u32[]{:S(2)}) %collective-permute-start.10) | collective-permute-done | bytes 1572896 | tf_op jit(solution)/shard_map/ppermute | solution.py:786
  649.0 33.7 %collective-permute-done.4.refs_3_ = bf16[4,384,512]{2,1,0:T(8,128)(2,1)} collective-permute-done((bf16[4,384,512]{2,1,0:T(8,128)(2,1)}, bf16[4,384,512]{2,1,0:T(8,128)(2,1)}, u32[]{:S(2)}, u32[]{:S(2)}) %collective-permute-start.4) | collective-permute-done | bytes 1572896 | tf_op jit(solution)/shard_map/ppermute | solution.py:786
  682.7 33.2 %collective-permute-done.7.refs_7_ = bf16[4,384,512]{2,1,0:T(8,128)(2,1)} collective-permute-done((bf16[4,384,512]{2,1,0:T(8,128)(2,1)}, bf16[4,384,512]{2,1,0:T(8,128)(2,1)}, u32[]{:S(2)}, u32[]{:S(2)}) %collective-permute-start.7) | collective-permute-done | bytes 1572896 | tf_op jit(solution)/shard_map/ppermute | solution.py:786
  715.8 57.9 %experts.1 = (bf16[4,2,4,80,1536]{4,3,2,1,0:T(8,128)(2,1)}, bf16[4,2,4,80,1536]{4,3,2,1,0:T(8,128)(2,1)}, bf16[4,4,384,512]{3,2,1,0:T(8,128)(2,1)}, bf16[4,4,384...) custom-call(bf16[4,2,4,80,1536]{4,3,2,1,0:T(8,128)(2,1)} %pick_tokens.1.x_ref, ...), custom_call_target="tpu_custom_call" | custom-call | flops 36238786560 | bytes 70000000 | tf_op jit(solution)/shard_map/experts/pallas_call | solution.py:764
  773.7 13.1 spread_grads.1.partial_ref
  786.8 118.7 %scatter_grads.1 = f32[256,1536]{1,0:T(8,128)} custom-call(bf16[4,2,2,256,1536]{4,3,2,1,0:T(8,128)(2,1)} %spread_grads.1.partial_ref), custom_call_target="tpu_custom_call" | custom-call | bytes 300000000 | tf_op jit(solution)/shard_map/scatter_grads/pallas_call | solution.py:581
  924.7 21.0 %while.34 = (s32[]{:T(128)}, f32[256,4,3,128]{0,3,2,1:T(8,128)S(1)}, bf16[4,512,512]{1,2,0:T(8,128)(2,1)}, bf16[4,512,512]{1,2,0:T(8,128)(2,1)}, s32[4]{0:T(128)...) while((s32[]{:T(128)}, ...), condition=%wide.region_15.16_spmd.clone, body=%wide.region_12.15_spmd.clone.sunk | while | flops 2030699264 | bytes 41865064 | solution.py:156
  926.0 11.3 conditional.7
  958.8 66.8 %scatter_keys.1 = f32[256,1024]{1,0:T(8,128)} custom-call(bf16[4,1,2,256,1024]{4,3,2,1,0:T(8,128)(2,1)} %pad_maximum_fusion.3.partial_ref), custom_call_target="tpu_custom_call" | custom-call | bytes 150000000 | tf_op jit(solution)/shard_map/scatter_keys/pallas_call | solution.py:581
  1057.8 13.2 spread_results.1.partial_ref
  1071.0 111.5 %scatter_results.1 = f32[256,1536]{1,0:T(8,128)} custom-call(bf16[4,2,2,256,1536]{4,3,2,1,0:T(8,128)(2,1)} %spread_results.1.partial_ref), custom_call_target="tpu_custom_call" | custom-call | bytes 300000000 | tf_op jit(solution)/shard_map/scatter_results/pallas_call | solution.py:581
  1187.7 10.6 collective-permute-start.16
  1198.3 45.6 %collective-permute-done.13 = bf16[2,4,384,512]{3,2,1,0:T(8,128)(2,1)} collective-permute-done((bf16[2,4,384,512]{3,2,1,0:T(8,128)(2,1)}, bf16[2,4,384,512]{3,2,1,0:T(8,128)(2,1)}, u32[]{:S(2)}, u32[]{:S(2)}) %collective-permute-start.13) | collective-permute-done | bytes 3145760 | tf_op jit(solution)/shard_map/ppermute | solution.py:786
  1248.2 61.1 %collective-permute-done.11 = bf16[2,4,384,512]{3,2,1,0:T(8,128)(2,1)} collective-permute-done((bf16[2,4,384,512]{3,2,1,0:T(8,128)(2,1)}, bf16[2,4,384,512]{3,2,1,0:T(8,128)(2,1)}, u32[]{:S(2)}, u32[]{:S(2)}) %collective-permute-start.11) | collective-permute-done | bytes 3145760 | tf_op jit(solution)/shard_map/ppermute | solution.py:786
  1321.9 22.1 %psum.35 = bf16[384,2]{0,1:T(2,128)(2,1)S(1)} all-reduce(bf16[384,2]{0,1:T(2,128)(2,1)S(1)} %copy.143), channel_id=1, replica_groups=mesh['ctx'=8,'wt'=4] {'ctx'}, use_global_device_ids=true, to_apply=%region_20.21 | all-reduce | flops 768 | bytes 3072 | tf_op jit(solution)/shard_map/psum | solution.py:1082
  1370.3 75.8 %all-reduce.3.cloned.1.call-done = (bf16[384,2560]{1,0:T(8,128)(2,1)}, bf16[384,1536]{1,0:T(8,128)(2,1)}, bf16[384,2048]{1,0:T(8,128)(2,1)}, bf16[256,1536]{1,0:T(8,128)(2,1)}) async-done(((bf16[384,2560]{1,0:T(8,128)(2,1)}, bf16[384,1536]{1,0:T(8,128)(2,1)}, bf16[384,2048]{1,0:T(8,128)(2,1)}, bf16[256,1536]{1,0:T(8,128)(2,1)}), (bf16[384,2560]{1,0:T(8,128)(2,1)}, bf16[384,1536]{1,0:T(8,128)(2,1)}, ...) | async-done | bytes 5505040 | tf_op jit(solution)/shard_map/psum | solution.py:1082
  (316 shorter events, 233.5 us)
Async XLA Ops:
  8.0 604.5 %all-gather.4.cloned.1.call-start = ((), (), s32[]{:S(2)}) async-start(), calls=%async_computation.9 | async-start | bytes 14155776 | tf_op jit(solution)/shard_map/all_gather | solution.py:843
  82.7 19.1 %collective-permute-start.1 = (bf16[256,1536]{1,0:T(8,128)(2,1)S(1)}, bf16[256,1536]{1,0:T(8,128)(2,1)S(1)}, u32[]{:S(2)}, u32[]{:S(2)}) collective-permute-start(bf16[256,1536]{1,0:T(8,128)(2,1)S(1)} %fusion.61), channel_id=1, source_target_pairs={{0,1},{1,0},{2,3},{3,2},{4,5},{5,4},{6,7},{7,6},{8,9},{9,8},{10,11... | collective-permute-start | bytes 2359304 | tf_op jit(solution)/shard_map/ppermute | solution.py:786
  103.5 1211.8 %reduce-scatter.14.cloned.1.call-start = ((), (), s32[]{:S(2)}) async-start(), calls=%async_computation.8 | async-start | bytes 3932160 | tf_op jit(solution)/shard_map/reduce_scatter | solution.py:1081
  284.6 1030.7 %reduce-scatter.12.cloned.1.call-start = ((), (), s32[]{:S(2)}) async-start(), calls=%async_computation.7 | async-start | bytes 7864320 | tf_op jit(solution)/shard_map/reduce_scatter | solution.py:1081
  290.6 1024.7 %reduce-scatter.10.cloned.1.call-start = ((), (), s32[]{:S(2)}) async-start(), calls=%async_computation.6 | async-start | bytes 5898240 | tf_op jit(solution)/shard_map/reduce_scatter | solution.py:1081
  295.3 249.3 %collective-permute-start.8 = (bf16[4,512,384]{2,1,0:T(8,128)(2,1)}, bf16[4,512,384]{2,1,0:T(8,128)(2,1)}, u32[]{:S(2)}, u32[]{:S(2)}) collective-permute-start(bf16[4,512,384]{2,1,0:T(8,128)(2,1)} %get-tuple-element.490), channel_id=1, source_target_pairs={{0,1},{1,0},{2,3},{3,2},{4,5},{5,4},{6,7},{7,6},{8,9},{9,8},{10,11... | collective-permute-start | bytes 4718600 | tf_op jit(solution)/shard_map/ppermute | solution.py:786
  297.7 248.4 %collective-permute-start.2 = (bf16[4,384,512]{2,1,0:T(8,128)(2,1)}, bf16[4,384,512]{2,1,0:T(8,128)(2,1)}, u32[]{:S(2)}, u32[]{:S(2)}) collective-permute-start(bf16[4,384,512]{2,1,0:T(8,128)(2,1)} %get-tuple-element.494), channel_id=1, source_target_pairs={{0,1},{1,0},{2,3},{3,2},{4,5},{5,4},{6,7},{7,6},{8,9},{9,8},{10,11... | collective-permute-start | bytes 4718600 | tf_op jit(solution)/shard_map/ppermute | solution.py:786
  301.1 245.6 %collective-permute-start.5 = (bf16[4,384,512]{2,1,0:T(8,128)(2,1)}, bf16[4,384,512]{2,1,0:T(8,128)(2,1)}, u32[]{:S(2)}, u32[]{:S(2)}) collective-permute-start(bf16[4,384,512]{2,1,0:T(8,128)(2,1)} %get-tuple-element.492), channel_id=1, source_target_pairs={{0,1},{1,0},{2,3},{3,2},{4,5},{5,4},{6,7},{7,6},{8,9},{9,8},{10,11... | collective-permute-start | bytes 4718600 | tf_op jit(solution)/shard_map/ppermute | solution.py:786
  302.2 246.0 %collective-permute-start.3 = (bf16[4,384,512]{2,1,0:T(8,128)(2,1)}, bf16[4,384,512]{2,1,0:T(8,128)(2,1)}, u32[]{:S(2)}, u32[]{:S(2)}) collective-permute-start(bf16[4,384,512]{2,1,0:T(8,128)(2,1)} %get-tuple-element.495.refs_0_), channel_id=1, source_target_pairs={{0,2},{1,3},{2,0},{3,1},{4,6},{5,7},{6,4},{7,5},{8,10},{9,11},{10,... | collective-permute-start | bytes 4718600 | tf_op jit(solution)/shard_map/ppermute | solution.py:786
  302.8 241.1 %collective-permute-start = (f32[12,256]{1,0:T(8,128)S(1)}, f32[12,256]{1,0:T(8,128)S(1)}, u32[]{:S(2)}, u32[]{:S(2)}) collective-permute-start(f32[12,256]{1,0:T(8,128)S(1)} %pad_maximum_fusion.14), channel_id=1, source_target_pairs={{0,1},{1,0},{2,3},{3,2},{4,5},{5,4},{6,7},{7,6},{8,9},{9,8},{10,11... | collective-permute-start | bytes 36872 | tf_op jit(solution)/shard_map/ppermute | solution.py:786
  543.9 81.1 %collective-permute-start.6 = (bf16[4,384,512]{2,1,0:T(8,128)(2,1)}, bf16[4,384,512]{2,1,0:T(8,128)(2,1)}, u32[]{:S(2)}, u32[]{:S(2)}) collective-permute-start(bf16[4,384,512]{2,1,0:T(8,128)(2,1)} %get-tuple-element.493.refs_4_), channel_id=1, source_target_pairs={{0,2},{1,3},{2,0},{3,1},{4,6},{5,7},{6,4},{7,5},{8,10},{9,11},{10,... | collective-permute-start | bytes 4718600 | tf_op jit(solution)/shard_map/ppermute | solution.py:786
  544.6 80.5 %collective-permute-start.9 = (bf16[4,512,384]{2,1,0:T(8,128)(2,1)}, bf16[4,512,384]{2,1,0:T(8,128)(2,1)}, u32[]{:S(2)}, u32[]{:S(2)}) collective-permute-start(bf16[4,512,384]{2,1,0:T(8,128)(2,1)} %get-tuple-element.491.refs_8_), channel_id=1, source_target_pairs={{0,2},{1,3},{2,0},{3,1},{4,6},{5,7},{6,4},{7,5},{8,10},{9,11},{10,... | collective-permute-start | bytes 4718600 | tf_op jit(solution)/shard_map/ppermute | solution.py:786
  546.2 102.8 %collective-permute-start.10 = (bf16[4,512,384]{2,1,0:T(8,128)(2,1)}, bf16[4,512,384]{2,1,0:T(8,128)(2,1)}, u32[]{:S(2)}, u32[]{:S(2)}) collective-permute-start(bf16[4,512,384]{2,1,0:T(8,128)(2,1)} %collective-permute-done.8.refs_9_), channel_id=1, source_target_pairs={{0,2},{1,3},{2,0},{3,1},{4,6},{5,7},{6,4},{7,5},{8,10},{9,11},{10,... | collective-permute-start | bytes 4718600 | tf_op jit(solution)/shard_map/ppermute | solution.py:786
  546.7 136.0 %collective-permute-start.4 = (bf16[4,384,512]{2,1,0:T(8,128)(2,1)}, bf16[4,384,512]{2,1,0:T(8,128)(2,1)}, u32[]{:S(2)}, u32[]{:S(2)}) collective-permute-start(bf16[4,384,512]{2,1,0:T(8,128)(2,1)} %collective-permute-done.2.refs_1_), channel_id=1, source_target_pairs={{0,2},{1,3},{2,0},{3,1},{4,6},{5,7},{6,4},{7,5},{8,10},{9,11},{10,... | collective-permute-start | bytes 4718600 | tf_op jit(solution)/shard_map/ppermute | solution.py:786
  548.2 167.6 %collective-permute-start.7 = (bf16[4,384,512]{2,1,0:T(8,128)(2,1)}, bf16[4,384,512]{2,1,0:T(8,128)(2,1)}, u32[]{:S(2)}, u32[]{:S(2)}) collective-permute-start(bf16[4,384,512]{2,1,0:T(8,128)(2,1)} %collective-permute-done.5.refs_5_), channel_id=1, source_target_pairs={{0,2},{1,3},{2,0},{3,1},{4,6},{5,7},{6,4},{7,5},{8,10},{9,11},{10,... | collective-permute-start | bytes 4718600 | tf_op jit(solution)/shard_map/ppermute | solution.py:786
  916.4 399.0 %reduce-scatter.8.cloned.1.call-start = ((), (), s32[]{:S(2)}) async-start(), calls=%async_computation.5 | async-start | bytes 9830400 | tf_op jit(solution)/shard_map/reduce_scatter | solution.py:1081
  1034.6 286.3 %reduce-scatter.16.cloned.1.call-start = ((), (), s32[]{:S(2)}) async-start(), calls=%async_computation.10 | async-start | bytes 491520
  1038.7 143.9 %collective-permute-start.15 = (bf16[2,4,512,384]{3,2,1,0:T(8,128)(2,1)}, bf16[2,4,512,384]{3,2,1,0:T(8,128)(2,1)}, u32[]{:S(2)}, u32[]{:S(2)}) collective-permute-start(bf16[2,4,512,384]{3,2,1,0:T(8,128)(2,1)} %slice.120), channel_id=1, source_target_pairs={{0,2},{1,3},{2,0},{3,1},{4,6},{5,7},{6,4},{7,5},{8,10},{9,11},{10,... | collective-permute-start | bytes 9437192 | tf_op jit(solution)/shard_map/ppermute | solution.py:786
  1043.5 200.3 %collective-permute-start.13 = (bf16[2,4,384,512]{3,2,1,0:T(8,128)(2,1)}, bf16[2,4,384,512]{3,2,1,0:T(8,128)(2,1)}, u32[]{:S(2)}, u32[]{:S(2)}) collective-permute-start(bf16[2,4,384,512]{3,2,1,0:T(8,128)(2,1)} %slice.116), channel_id=1, source_target_pairs={{0,2},{1,3},{2,0},{3,1},{4,6},{5,7},{6,4},{7,5},{8,10},{9,11},{10,... | collective-permute-start | bytes 9437192 | tf_op jit(solution)/shard_map/ppermute | solution.py:786
  1048.7 260.6 %collective-permute-start.11 = (bf16[2,4,384,512]{3,2,1,0:T(8,128)(2,1)}, bf16[2,4,384,512]{3,2,1,0:T(8,128)(2,1)}, u32[]{:S(2)}, u32[]{:S(2)}) collective-permute-start(bf16[2,4,384,512]{3,2,1,0:T(8,128)(2,1)} %slice.112), channel_id=1, source_target_pairs={{0,2},{1,3},{2,0},{3,1},{4,6},{5,7},{6,4},{7,5},{8,10},{9,11},{10,... | collective-permute-start | bytes 9437192 | tf_op jit(solution)/shard_map/ppermute | solution.py:786
  1182.5 263.6 %all-reduce.3.cloned.1.call-start = ((), (), s32[]{:S(2)}) async-start(), calls=%async_computation.11 | async-start | bytes 11010048 | tf_op jit(solution)/shard_map/psum | solution.py:1082
  1187.7 157.0 %collective-permute-start.16 = (bf16[4,512,384]{2,1,0:T(8,128)(2,1)}, bf16[4,512,384]{2,1,0:T(8,128)(2,1)}, u32[]{:S(2)}, u32[]{:S(2)}) collective-permute-start(bf16[4,512,384]{2,1,0:T(8,128)(2,1)} %fusion.52), channel_id=1, source_target_pairs={{0,1},{1,0},{2,3},{3,2},{4,5},{5,4},{6,7},{7,6},{8,9},{9,8},{10,11... | collective-permute-start | bytes 4718600 | tf_op jit(solution)/shard_map/ppermute | solution.py:786
  1248.2 102.9 %collective-permute-start.14 = (bf16[4,384,512]{2,1,0:T(8,128)(2,1)}, bf16[4,384,512]{2,1,0:T(8,128)(2,1)}, u32[]{:S(2)}, u32[]{:S(2)}) collective-permute-start(bf16[4,384,512]{2,1,0:T(8,128)(2,1)} %fusion.51), channel_id=1, source_target_pairs={{0,1},{1,0},{2,3},{3,2},{4,5},{5,4},{6,7},{7,6},{8,9},{9,8},{10,11... | collective-permute-start | bytes 4718600 | tf_op jit(solution)/shard_map/ppermute | solution.py:786
  1315.3 35.9 %collective-permute-start.12 = (bf16[4,384,512]{2,1,0:T(8,128)(2,1)}, bf16[4,384,512]{2,1,0:T(8,128)(2,1)}, u32[]{:S(2)}, u32[]{:S(2)}) collective-permute-start(bf16[4,384,512]{2,1,0:T(8,128)(2,1)} %fusion.50), channel_id=1, source_target_pairs={{0,1},{1,0},{2,3},{3,2},{4,5},{5,4},{6,7},{7,6},{8,9},{9,8},{10,11... | collective-permute-start | bytes 4718600 | tf_op jit(solution)/shard_map/ppermute | solution.py:786
  (53 other events, 1529.4 us)
Sparse Core Ops, SparseCore 0:
  103.6 122.1 all-gather.3
  1315.5 130.5 all-reduce.2
Sparse Core Ops, SparseCore 1:
  284.7 104.0 reduce-scatter.13
  391.6 120.6 reduce-scatter.11
  916.5 66.2 reduce-scatter.9
  1034.7 151.9 reduce-scatter.7
  1190.1 38.7 reduce-scatter.15

commit v2 on v1

--- a/solution.py
+++ b/solution.py
@@ -163,6 +163,8 @@
 
 MESH = pl.DeviceIdType.MESH
 WIDE = 56 * 2**20
+LONG = pl.CostEstimate(flops=0, bytes_accessed=2_000_000_000, transcendentals=0)
+CHEAP = pl.CostEstimate(flops=0, bytes_accessed=4096, transcendentals=0)
 
 
 def flip(index, distance):
@@ -285,17 +287,26 @@
         compiler_params=pltpu.CompilerParams(
             collective_id=1, has_side_effects=True, vmem_limit_bytes=WIDE
         ),
-        cost_estimate=pl.CostEstimate(flops=0, bytes_accessed=150_000_000, transcendentals=0),
+        cost_estimate=CHEAP,
         name="gather_weights",
     )(*slabs)
 
 
-def gather_kernel(chips, downward, paired, count, slabs, rows_ref, *refs):
-    sources, out_ref, targets = refs[:slabs], refs[slabs], refs[slabs + 1 : 2 * slabs + 1]
-    here, up_send, up_recv, down_send, down_recv, pair_send, pair_recv, near_send, near_recv = refs[
-        2 * slabs + 1 : 2 * slabs + 10
-    ]
-    plan = Slabs(count, sources, targets, *refs[2 * slabs + 10 :]) if slabs else None
+def gather_kernel(chips, downward, paired, count, slabs, passed, rows_ref, *refs):
+    refs = list(refs)
+
+    def take(number):
+        taken = refs[:number]
+        del refs[:number]
+        return taken
+
+    hops = count // 2 - 1
+    sources, moved = take(slabs), take(passed)
+    (out_ref,), targets, landed, (zero_ref,) = take(1), take(slabs), take(passed * hops), take(1)
+    here, up_send, up_recv, down_send, down_recv, pair_send, pair_recv, near_send, near_recv = take(9)
+    plan = Slabs(count, sources, targets, *take(5)) if slabs else None
+    pass_send, pass_recv = take(2) if passed else (None, None)
+    zero_ref[...] = jnp.zeros_like(zero_ref)
     c, w = lax.axis_index("ctx"), lax.axis_index("wt")
     z = c // 2
     core = lax.rem(c, 2)
@@ -303,7 +314,13 @@
     near, partner = (flip(c, 1), w), (c, flip(w, 1))
     above = (lax.rem(c + 2, 2 * chips), w)
     below = (lax.rem(c + 2 * chips - 2, 2 * chips), w)
-    greet([near, above, below] + ([partner] if paired else []) + (plan.devices() if plan else []))
+    far = [(c, flip(w, 2 * d + 2)) for d in range(hops)]
+    greet([near, above, below] + ([partner] if paired else []) + (plan.devices() if plan else []) + (far if passed else []))
+
+    def onward(i, d):
+        return remote(
+            moved[i], landed[i * hops + d], pass_send.at[i, d], pass_recv.at[i, d], far[d]
+        )
 
     def spot(chip, which, parity):
         return out_ref.at[chip, which, parity]
@@ -343,6 +360,9 @@
     hand(z, side, rows_ref).start()
     if plan:
         plan.start()
+    for d in range(hops):
+        for i in range(passed):
+            onward(i, d).start()
     for step in range(1, chips):
         low, high = z - step, z + step
 
@@ -397,29 +417,38 @@
             finish(chip)
         else:
             pl.when(chip <= z)(lambda: finish(chip))
-
-
-def gather_rows(rows, collective_id, downward, paired, name, slabs=()):
+    for d in range(hops):
+        for i in range(passed):
+            onward(i, d).wait()
+
+
+def gather_rows(rows, collective_id, downward, paired, name, slabs=(), moved=()):
     chips = lax.axis_size("ctx") // 2
     count = lax.axis_size("wt")
+    hops = count // 2 - 1
     line = pltpu.SemaphoreType.DMA((chips,))
     both = pltpu.SemaphoreType.DMA((chips, 2))
     shape = jax.ShapeDtypeStruct((chips, 2 if paired else 1, 2) + rows.shape, rows.dtype)
-    return pl.pallas_call(
-        functools.partial(gather_kernel, chips, downward, paired, count, len(slabs)),
-        out_shape=(shape,) + Slabs.shapes(slabs, count),
-        in_specs=[pl.BlockSpec(memory_space=pl.ANY)] * (1 + len(slabs)),
-        out_specs=(pl.BlockSpec(memory_space=pl.ANY),) * (1 + len(slabs)),
+    landed = tuple(jax.ShapeDtypeStruct(m.shape, m.dtype) for m in moved for _ in range(hops))
+    shapes = (shape,) + Slabs.shapes(slabs, count) + landed
+    *results, zero = pl.pallas_call(
+        functools.partial(gather_kernel, chips, downward, paired, count, len(slabs), len(moved)),
+        out_shape=shapes + (jax.ShapeDtypeStruct((8, 128), jnp.int32),),
+        in_specs=[pl.BlockSpec(memory_space=pl.ANY)] * (1 + len(slabs) + len(moved)),
+        out_specs=(pl.BlockSpec(memory_space=pl.ANY),) * len(shapes)
+        + (pl.BlockSpec(memory_space=pltpu.VMEM),),
         scratch_shapes=[pltpu.SemaphoreType.DMA]
         + [line] * 6
         + [both] * 2
-        + (Slabs.scratch(len(slabs), count) if slabs else []),
+        + (Slabs.scratch(len(slabs), count) if slabs else [])
+        + ([pltpu.SemaphoreType.DMA((len(moved), hops))] * 2 if moved else []),
         compiler_params=pltpu.CompilerParams(
             collective_id=collective_id, has_side_effects=True, vmem_limit_bytes=WIDE
         ),
-        cost_estimate=pl.CostEstimate(flops=0, bytes_accessed=250_000_000, transcendentals=0),
+        cost_estimate=LONG,
         name=name,
-    )(rows, *slabs)
+    )(rows, *slabs, *moved)
+    return results + [zero[0, 0]]
 
 
 def scatter_kernel(chips, upward, paired, pieces, partial_ref, out_ref, own, sib, mate, low_in, high_in, load, near_send, near_recv, pair_send, pair_recv, up_send, up_recv, down_send, down_recv):
@@ -597,9 +626,7 @@
         compiler_params=pltpu.CompilerParams(
             collective_id=collective_id, has_side_effects=True, vmem_limit_bytes=WIDE
         ),
-        cost_estimate=pl.CostEstimate(
-            flops=0, bytes_accessed=300_000_000 if paired else 150_000_000, transcendentals=0
-        ),
+        cost_estimate=LONG,
         name=name,
     )(partial)
 
@@ -651,11 +678,7 @@
         in_specs=[table, table, source],
         out_specs=specs,
         compiler_params=pltpu.CompilerParams(vmem_limit_bytes=WIDE),
-        cost_estimate=pl.CostEstimate(
-            flops=4 * chips * sides * local * depth * both * width // 2,
-            bytes_accessed=40_000_000,
-            transcendentals=0,
-        ),
+        cost_estimate=CHEAP,
         name="pick_grads" if scaled else "pick_tokens",
     )(slots, gates, rows)
 
@@ -689,11 +712,7 @@
         ],
         out_specs=pl.BlockSpec((1, 1, 2, tokens, width), lambda z, s: (z, s, 0, 0, 0)),
         compiler_params=pltpu.CompilerParams(vmem_limit_bytes=WIDE),
-        cost_estimate=pl.CostEstimate(
-            flops=2 * chips * sides * local * depth * both * width,
-            bytes_accessed=40_000_000,
-            transcendentals=0,
-        ),
+        cost_estimate=CHEAP,
         name=name,
     )(slots, rows)
 
@@ -774,9 +793,7 @@
         in_specs=[sources, sources, scales] + [tall] * (2 * blocks) + [flat] * blocks,
         out_specs=(rows, rows, tall_out, tall_out, flat_out),
         compiler_params=pltpu.CompilerParams(vmem_limit_bytes=60 * 2**20),
-        cost_estimate=pl.CostEstimate(
-            flops=18 * total * width * inner, bytes_accessed=70_000_000, transcendentals=total * inner
-        ),
+        cost_estimate=CHEAP,
         name="experts",
     )(x, g, scale, *gates, *ups, *downs)
 
@@ -802,10 +819,7 @@
 def collect_expert(shard, side, pairs):
     local = shard.shape[0]
     kept, given = own_and_other(shard.reshape((2, local // 2) + shard.shape[1:]), side)
-    blocks = [kept, swap_pairs(given, "wt", 1)]
-    for d in range(1, pairs):
-        blocks += [swap_pairs(blocks[0], "wt", 2 * d), swap_pairs(blocks[1], "wt", 2 * d)]
-    return blocks
+    return kept, swap_pairs(given, "wt", 1), [swap_pairs(kept, "wt", 2 * d) for d in range(1, pairs)]
 
 
 def settle_blocks(blocks, index, axis):
@@ -829,10 +843,10 @@
     )
 
 
-def scatter_expert(grads, side, pairs):
+def scatter_expert(grads, arrived, side):
     total = grads[:2].astype(jnp.float32)
-    for d in range(1, pairs):
-        total = total + swap_pairs(grads[2 * d : 2 * d + 2], "wt", 2 * d).astype(jnp.float32)
+    for more in arrived:
+        total = total + more.astype(jnp.float32)
     other = swap_pairs(total[1].astype(jnp.bfloat16), "wt", 1).astype(jnp.float32)
     both = in_order(total[0], other, side)
     return both.reshape((-1,) + both.shape[2:])
@@ -890,9 +904,7 @@
         [jnp.swapaxes(routes[0], 0, 1).astype(jnp.float32), jnp.swapaxes(gates[0], 0, 1)], axis=0
     )
     all_tables = gather_side(tables, side)
-    gate_blocks = collect_expert(expert_gate, later, pairs)
-    up_blocks = collect_expert(expert_up, later, pairs)
-    down_blocks = collect_expert(expert_down, later, pairs)
+    collected = [collect_expert(e, later, pairs) for e in (expert_gate, expert_up, expert_down)]
     local = expert_gate.shape[0] // 2
     first_expert = (lax.axis_index("ctx") * 2 + side) * local
 
@@ -908,7 +920,7 @@
     normed = (inputs * scale_one * gain_one_full).astype(jnp.bfloat16)
     projected = jnp.dot(normed, slab, preferred_element_type=jnp.float32).astype(jnp.bfloat16)
     queries = projected[:, :wide]
-    both, out_weight, both_weight, down_weight = gather_rows(
+    both, out_weight, both_weight, down_weight, zero = gather_rows(
         projected[:, wide:],
         2,
         False,
@@ -938,7 +950,7 @@
 
     grad_rows = cotangent[0]
     all_grads = gather_side(
-        lax.dynamic_index_in_dim(jnp.stack([grad_rows, grad_rows]), later - side, 0, False), side
+        lax.dynamic_index_in_dim(jnp.stack([grad_rows, grad_rows]), zero, 0, False), side
     ).reshape(chips, 2, 2, tokens, width_model)
 
     grouped = queries.reshape(tokens, KV_HEADS, group, HEAD_DIM)
@@ -955,12 +967,24 @@
         tokens, HEADS * HEAD_DIM
     )
     attended = attended_full.astype(jnp.bfloat16)
+    attended, collected = lax.optimization_barrier((attended, collected))
     middle = inputs + jnp.dot(attended, out_weight, preferred_element_type=jnp.float32)
     scale_two = inverse_rms(middle)
     gain_two_full = gain_two.astype(jnp.float32)
     normed_two = (middle * scale_two * gain_two_full).astype(jnp.bfloat16)
 
-    (all_rows,) = gather_rows(normed_two, 3, True, True, "gather_tokens")
+    all_rows, *landed, zero = gather_rows(
+        normed_two, 3, True, True, "gather_tokens", (), [c[1] for c in collected]
+    )
+
+    def blocks_of(i):
+        kept, paired, straight = collected[i]
+        blocks = [kept, paired]
+        for d in range(pairs - 1):
+            blocks += [straight[d], landed[i * (pairs - 1) + d]]
+        return blocks
+
+    gate_blocks, up_blocks, down_blocks = blocks_of(0), blocks_of(1), blocks_of(2)
     (received_rows,) = pick_rows(all_rows, slots, slot_gates, False)
     grad_received, row_gates = pick_rows(all_grads, slots, slot_gates, True)
     if gate_blocks[0].shape[1] % 128:
@@ -979,15 +1003,22 @@
         results, backs, grads_gate, grads_up, grads_down = run_experts(
             received_rows, grad_received, row_gates, gate_blocks, up_blocks, down_blocks
         )
-    sum_experts_gate = scatter_expert(grads_gate, side, pairs)
-    sum_experts_up = scatter_expert(grads_up, side, pairs)
-    sum_experts_down = scatter_expert(grads_down, side, pairs)
+    expert_grads = (grads_gate, grads_up, grads_down)
+    arrived = [
+        [swap_pairs(g[2 * d : 2 * d + 2], "wt", 2 * d) for d in range(1, pairs)] for g in expert_grads
+    ]
     routed_grad = scatter_rows(
         spread_rows(backs, slots, "spread_grads"), 5, True, True, "scatter_grads"
     )
-    routed = scatter_rows(
-        spread_rows(results, slots, "spread_results"), 4, True, True, "scatter_results"
-    )
+    spread = spread_rows(results, slots, "spread_results")
+    partial = lax.psum_scatter(
+        jnp.swapaxes(spread, 1, 2).reshape(ctx_count, 2, tokens, width_model),
+        "ctx",
+        scatter_dimension=0,
+        tiled=True,
+    )[0]
+    kept, given = own_and_other(partial, side)
+    routed = kept.astype(jnp.float32) + swap_pairs(given, "wt", 1).astype(jnp.float32)
 
     shared_parts = jnp.dot(normed_two, both_weight, preferred_element_type=jnp.float32)
     shared_gate_part, shared_up_part = shared_parts[:, :shared_width], shared_parts[:, shared_width:]
@@ -1063,6 +1094,10 @@
         False,
         "scatter_keys",
     ).astype(jnp.bfloat16)
+    grad_both, arrived = lax.optimization_barrier((grad_both, arrived))
+    sum_experts_gate, sum_experts_up, sum_experts_down = [
+        scatter_expert(g, a, side) for g, a in zip(expert_grads, arrived)
+    ]
     grad_queries = grad_queries_full.reshape(tokens, HEADS * HEAD_DIM).astype(jnp.bfloat16)
     grad_projected = jnp.concatenate([grad_queries, grad_both], axis=1)
     grad_slab = jnp.einsum("tc,tq->cq", normed, grad_projected, preferred_element_type=jnp.float32)

time: 1480 us -> 1400 us (0.946)
  Pallas kernels: 841 us -> 621 us
  waiting for transfers between devices: 292 us -> 467 us
  blocking collectives: 69.4 us -> 31.9 us
  local copies, waits for them, and re-layouts: 88.3 us -> 105 us
    pallas_call x3 -> x2, Pallas kernels: 297 us -> 151 us  [scatter_rows(): pl.pallas_call(functools.partial(scatter_kernel, chips, upward, paired, p...]
    reduce_scatter x0 -> x1, waiting for transfers between devices: none -> 134 us  [body(): lax.psum_scatter(jnp.swapaxes(spread, 1, 2).reshape(ctx_count, 2, tokens,...]
    reduce_scatter x4, waiting for transfers between devices: 0.03 us -> 77.3 us  [reduced(): lax.psum_scatter(grad.astype(jnp.bfloat16), 'wt', scatter_dimension=0, ti...]
    pallas_call x2, Pallas kernels: 369 us -> 293 us  [gather_rows(): pl.pallas_call(functools.partial(gather_kernel, chips, downward, paired,...]
    psum x1, waiting for transfers between devices: 75.8 us -> 16.4 us  [reduced(): return lax.psum(part, 'ctx').astype(jnp.float32)]
    all_gather x1, blocking collectives: 47.3 us -> 14.2 us  [gather_side(): return lax.all_gather(both, 'ctx', axis=0)]
    unnamed x8 -> x9, waiting for transfers between devices: 0.12 us -> 25.1 us
    ppermute x17 -> x15, waiting for transfers between devices: 216 us -> 214 us  [swap_pairs(): return lax.ppermute(value, axis, [(i, i ^ distance) for i in range(count)])]
  transfers between devices with their start and end apart: 24 -> 23, of which waited for: 7 -> 12; matrix products, arithmetic and copies ran while one was open for 12% -> 14% of each run, Pallas kernels for 53% -> 30%
where the time goes in v2:
time: 1400 us
  Pallas kernels  621 us (44%)
  waiting for transfers between devices  467 us (33%)
  local copies, waits for them, and re-layouts  105 us (8%)
  other arithmetic  64.8 us (5%)
  matrix products  63.9 us (5%)
  blocking collectives  31.9 us (2%)
  between operations  19.4 us (1%)
  starting transfers between devices  17.1 us (1%)
    pallas_call x2, Pallas kernels, gather_rows(): pl.pallas_call(functools.partial(gather_kernel, chips, downward, paired,...  293 us
    ppermute x15, waiting for transfers between devices, swap_pairs(): return lax.ppermute(value, axis, [(i, i ^ distance) for i in range(count)])  214 us
    pallas_call x2, Pallas kernels, scatter_rows(): pl.pallas_call(functools.partial(scatter_kernel, chips, upward, paired, p...  151 us
    reduce_scatter x1, waiting for transfers between devices, body(): lax.psum_scatter(jnp.swapaxes(spread, 1, 2).reshape(ctx_count, 2, tokens,...  134 us
    reduce_scatter x4, waiting for transfers between devices, reduced(): lax.psum_scatter(grad.astype(jnp.bfloat16), 'wt', scatter_dimension=0, ti...  77.3 us
    pallas_call x1, Pallas kernels, gather_weights(): pl.pallas_call(functools.partial(weights_kernel, count, len(slabs)), out_...  66.1 us
    pallas_call x1, Pallas kernels, run_experts(): pl.pallas_call(functools.partial(expert_kernel, blocks), grid=(local,), o...  57.8 us
    another operation x9, other arithmetic, in_order(): return jnp.stack([first, second])  28.5 us
  transfers between devices with their start and end apart: 23, of which 12 were waited for; matrix products, arithmetic and copies ran while one was open for 14% of the time, Pallas kernels for 30%

profile of v2, /device:TPU:0, one launch (start us, length us, event | category | flops | bytes accessed | tf_op | source)
XLA Modules:
  0.0 1395.3 jit_solution(13826419132134276688)
XLA Ops:
  13.2 66.1 %gather_weights.1 = (bf16[4,384,2560]{2,1,0:T(8,128)(2,1)}, bf16[4,32,384]{2,1,0:T(8,128)(2,1)}, s32[8,128]{1,0:T(8,128)}) custom-call(bf16[384,2560]{1,0:T(8,128)(2,1)} %pad_maximum_fusion.4.refs_0_, bf16[32,384]{1,0:T(8,128)(2,1)} %maximum_maximum_fusion.refs_1_), custom_call_target="tpu_custom_call" | custom-call | bytes 4096 | tf_op jit(solution)/shard_map/gather_weights/pallas_call | solution.py:280
  88.8 129.1 %gather_keys.1 = (bf16[4,1,2,256,1024]{4,3,2,1,0:T(8,128)(2,1)}, bf16[4,384,1536]{2,1,0:T(8,128)(2,1)}, bf16[4,384,2048]{2,1,0:T(8,128)(2,1)}, bf16[4,256,1536]{2,1,0:T(8,128)(2,1)}, s32[8,128]{1,0:T(8,128)}) custom-call(bf16[256,1024]{1,0:T(8,128)(2,1)} %slice.127.rows_ref, bf16[384,1536]{1,0:T(8,128)(2,1)} %refs_0_.1, ...), custom_call_target="tpu_custom_call" | custom-call | bytes 2000000000 | tf_op jit(solution)/shard_map/gather_keys/pallas_call | solution.py:434
  222.0 18.3 %collective-permute-done.7 = bf16[256,1536]{1,0:T(8,128)(2,1)} collective-permute-done((bf16[256,1536]{1,0:T(8,128)(2,1)S(1)}, bf16[256,1536]{1,0:T(8,128)(2,1)}, u32[]{:S(2)}, u32[]{:S(2)}) %collective-permute-start.7) | collective-permute-done | bytes 786464 | tf_op jit(solution)/shard_map/ppermute | solution.py:803
  258.0 28.0 %collective-permute-done.5.refs_10_ = bf16[4,512,384]{2,1,0:T(8,128)(2,1)S(1)} collective-permute-done((bf16[4,512,384]{2,1,0:T(8,128)(2,1)S(1)}, bf16[4,512,384]{2,1,0:T(8,128)(2,1)S(1)}, u32[]{:S(2)}, u32[]{:S(2)}) %collective-permute-start.5) | collective-permute-done | bytes 1572896 | tf_op jit(solution)/shard_map/ppermute | solution.py:803
  300.9 12.5 while.33
  319.8 31.1 %collective-permute-done.1.refs_2_ = bf16[4,384,512]{2,1,0:T(8,128)(2,1)} collective-permute-done((bf16[4,384,512]{2,1,0:T(8,128)(2,1)}, bf16[4,384,512]{2,1,0:T(8,128)(2,1)}, u32[]{:S(2)}, u32[]{:S(2)}) %collective-permute-start.1) | collective-permute-done | bytes 1572896 | tf_op jit(solution)/shard_map/ppermute | solution.py:803
  381.6 14.2 %all-gather = f32[16,12,256]{2,1,0:T(8,128)S(1)} all-gather(f32[2,12,256]{2,1,0:T(8,128)S(1)} %pad_maximum_fusion.13), channel_id=2, replica_groups=mesh['ctx'=8,'wt'=4] {'ctx'}, dimensions={0}, use_global_device_ids=true | all-gather | bytes 221184 | tf_op jit(solution)/shard_map/all_gather | solution.py:857
  399.7 164.4 %gather_tokens.1 = (bf16[4,2,2,256,1536]{4,3,2,1,0:T(8,128)(2,1)}, bf16[4,384,512]{2,1,0:T(8,128)(2,1)}, bf16[4,384,512]{2,1,0:T(8,128)(2,1)}, bf16[4,512,384]{2,1,0:T(8,128)(2,1)}, s32[8,128]{1,0:T(8,128)}) custom-call(bf16[256,1536]{1,0:T(8,128)(2,1)} %copy-done.15, bf16[4,384,512]{2,1,0:T(8,128)(2,1)} %collective-permute-done.refs_0_.refs_1_, ...), custom_call_target="tpu_custom_call" | custom-call | bytes 2000000000 | tf_op jit(solution)/shard_map/gather_tokens/pallas_call | solution.py:434
  564.1 12.8 pick_tokens.1.x_ref
  576.9 12.6 pick_grads.1
  589.6 57.8 %experts.1 = (bf16[4,2,4,80,1536]{4,3,2,1,0:T(8,128)(2,1)}, bf16[4,2,4,80,1536]{4,3,2,1,0:T(8,128)(2,1)}, bf16[4,4,384,512]{3,2,1,0:T(8,128)(2,1)}, bf16[4,4,384...) custom-call(bf16[4,2,4,80,1536]{4,3,2,1,0:T(8,128)(2,1)} %pick_tokens.1.x_ref, ...), custom_call_target="tpu_custom_call" | custom-call | bytes 4096 | tf_op jit(solution)/shard_map/experts/pallas_call | solution.py:783
  647.3 13.2 spread_grads.1.partial_ref
  660.6 86.1 %scatter_grads.1 = f32[256,1536]{1,0:T(8,128)} custom-call(bf16[4,2,2,256,1536]{4,3,2,1,0:T(8,128)(2,1)} %spread_grads.1.partial_ref), custom_call_target="tpu_custom_call" | custom-call | bytes 2000000000 | tf_op jit(solution)/shard_map/scatter_grads/pallas_call | solution.py:610
  779.5 21.0 %while.34 = (s32[]{:T(128)}, f32[256,4,3,128]{0,3,2,1:T(8,128)S(1)}, bf16[4,512,512]{1,2,0:T(8,128)(2,1)}, bf16[4,512,512]{1,2,0:T(8,128)(2,1)}, s32[4]{0:T(128)...) while((s32[]{:T(128)}, ...), condition=%wide.region_16.17_spmd.clone, body=%wide.region_13.16_spmd.clone.sunk | while | flops 2030699264 | bytes 41865064 | solution.py:156
  780.8 11.3 conditional.7
  813.6 65.2 %scatter_keys.1 = f32[256,1024]{1,0:T(8,128)} custom-call(bf16[4,1,2,256,1024]{4,3,2,1,0:T(8,128)(2,1)} %pad_maximum_fusion.3.partial_ref), custom_call_target="tpu_custom_call" | custom-call | bytes 2000000000 | tf_op jit(solution)/shard_map/scatter_keys/pallas_call | solution.py:610
  881.0 57.0 %collective-permute-done.11 = bf16[2,4,512,384]{3,2,1,0:T(8,128)(2,1)} collective-permute-done((bf16[2,4,512,384]{3,2,1,0:T(8,128)(2,1)}, bf16[2,4,512,384]{3,2,1,0:T(8,128)(2,1)}, u32[]{:S(2)}, u32[]{:S(2)}) %collective-permute-start.11) | collective-permute-done | bytes 3145760 | tf_op jit(solution)/shard_map/ppermute | solution.py:803
  937.9 66.5 %collective-permute-done.9 = bf16[2,4,384,512]{3,2,1,0:T(8,128)(2,1)} collective-permute-done((bf16[2,4,384,512]{3,2,1,0:T(8,128)(2,1)}, bf16[2,4,384,512]{3,2,1,0:T(8,128)(2,1)}, u32[]{:S(2)}, u32[]{:S(2)}) %collective-permute-start.9) | collective-permute-done | bytes 3145760 | tf_op jit(solution)/shard_map/ppermute | solution.py:803
  1019.2 13.3 spread_results.1
  1065.6 77.2 %reduce-scatter.11.cloned.1.call-done = bf16[384,2560]{1,0:T(8,128)(2,1)} async-done(((bf16[1536,2560]{1,0:T(8,128)(2,1)}), bf16[384,2560]{1,0:T(8,128)(2,1)}) %reduce-scatter.11.cloned.1.call-update) | async-done | bytes 1966096 | tf_op jit(solution)/shard_map/reduce_scatter | solution.py:1116
  1147.3 25.0 %reduce-scatter.19.cloned.1.call-done = bf16[384,2]{1,0:T(8,128)(2,1)} async-done(((bf16[1536,2]{1,0:T(8,128)(2,1)}), bf16[384,2]{1,0:T(8,128)(2,1)}) %reduce-scatter.19.cloned.1.call-update) | async-done | bytes 1552
  1173.2 17.7 %psum.35 = bf16[384,2]{0,1:T(2,128)(2,1)S(1)} all-reduce(bf16[384,2]{0,1:T(2,128)(2,1)S(1)} %copy.147), channel_id=1, replica_groups=mesh['ctx'=8,'wt'=4] {'ctx'}, use_global_device_ids=true, to_apply=%region_21.22 | all-reduce | flops 768 | bytes 3072 | tf_op jit(solution)/shard_map/psum | solution.py:1117
  1212.5 133.7 %reduce-scatter.9.cloned.1.call-done = bf16[1,2,256,1536]{3,2,1,0:T(8,128)(2,1)} async-done(((bf16[8,2,256,1536]{3,2,1,0:T(8,128)(2,1)}), bf16[1,2,256,1536]{3,2,1,0:T(8,128)(2,1)}) %reduce-scatter.9.cloned.1.call-update) | async-done | bytes 1572880 | tf_op jit(solution)/shard_map/reduce_scatter | solution.py:1014
  1357.1 16.4 %all-reduce.3.cloned.1.call-done = (bf16[384,2560]{1,0:T(8,128)(2,1)}, bf16[384,1536]{1,0:T(8,128)(2,1)}, bf16[384,2048]{1,0:T(8,128)(2,1)}, bf16[256,1536]{1,0:T(8,128)(2,1)}) async-done(((bf16[384,2560]{1,0:T(8,128)(2,1)}, bf16[384,1536]{1,0:T(8,128)(2,1)}, bf16[384,2048]{1,0:T(8,128)(2,1)}, bf16[256,1536]{1,0:T(8,128)(2,1)}), (bf16[384,2560]{1,0:T(8,128)(2,1)}, bf16[384,1536]{1,0:T(8,128)(2,1)}, ...) | async-done | bytes 5505040 | tf_op jit(solution)/shard_map/psum | solution.py:1117
  (308 shorter events, 271.8 us)
Async XLA Ops:
  8.0 568.9 %all-gather.4.cloned.1.call-start = ((), (), s32[]{:S(2)}) async-start(), calls=%async_computation.11 | async-start | bytes 14155776 | tf_op jit(solution)/shard_map/all_gather | solution.py:857
  221.4 18.9 %collective-permute-start.7 = (bf16[256,1536]{1,0:T(8,128)(2,1)S(1)}, bf16[256,1536]{1,0:T(8,128)(2,1)}, u32[]{:S(2)}, u32[]{:S(2)}) collective-permute-start(bf16[256,1536]{1,0:T(8,128)(2,1)S(1)} %fusion.63), channel_id=1, source_target_pairs={{0,1},{1,0},{2,3},{3,2},{4,5},{5,4},{6,7},{7,6},{8,9},{9,8},{10,11... | collective-permute-start | bytes 2359304 | tf_op jit(solution)/shard_map/ppermute | solution.py:803
  243.0 822.6 %reduce-scatter.17.cloned.1.call-start = ((), (), s32[]{:S(2)}) async-start(), calls=%async_computation.10 | async-start | bytes 3932160 | tf_op jit(solution)/shard_map/reduce_scatter | solution.py:1116
  248.7 37.3 %collective-permute-start.5 = (bf16[4,512,384]{2,1,0:T(8,128)(2,1)S(1)}, bf16[4,512,384]{2,1,0:T(8,128)(2,1)S(1)}, u32[]{:S(2)}, u32[]{:S(2)}) collective-permute-start(bf16[4,512,384]{2,1,0:T(8,128)(2,1)S(1)} %get-tuple-element.291.refs_8_), channel_id=1, source_target_pairs={{0,2},{1,3},{2,0},{3,1},{4,6},{5,7},{6,4},{7,5},{8,10},{9,11},{10,... | collective-permute-start | bytes 4718600 | tf_op jit(solution)/shard_map/ppermute | solution.py:803
  251.1 68.7 %collective-permute-start.3 = (bf16[4,384,512]{2,1,0:T(8,128)(2,1)}, bf16[4,384,512]{2,1,0:T(8,128)(2,1)}, u32[]{:S(2)}, u32[]{:S(2)}) collective-permute-start(bf16[4,384,512]{2,1,0:T(8,128)(2,1)} %get-tuple-element.288.refs_4_), channel_id=1, source_target_pairs={{0,2},{1,3},{2,0},{3,1},{4,6},{5,7},{6,4},{7,5},{8,10},{9,11},{10,... | collective-permute-start | bytes 4718600 | tf_op jit(solution)/shard_map/ppermute | solution.py:803
  254.8 96.0 %collective-permute-start.1 = (bf16[4,384,512]{2,1,0:T(8,128)(2,1)}, bf16[4,384,512]{2,1,0:T(8,128)(2,1)}, u32[]{:S(2)}, u32[]{:S(2)}) collective-permute-start(bf16[4,384,512]{2,1,0:T(8,128)(2,1)} %get-tuple-element.285.refs_0_), channel_id=1, source_target_pairs={{0,2},{1,3},{2,0},{3,1},{4,6},{5,7},{6,4},{7,5},{8,10},{9,11},{10,... | collective-permute-start | bytes 4718600 | tf_op jit(solution)/shard_map/ppermute | solution.py:803
  256.0 94.9 %collective-permute-start.4 = (bf16[4,512,384]{2,1,0:T(8,128)(2,1)}, bf16[4,512,384]{2,1,0:T(8,128)(2,1)}, u32[]{:S(2)}, u32[]{:S(2)}) collective-permute-start(bf16[4,512,384]{2,1,0:T(8,128)(2,1)} %get-tuple-element.528), channel_id=1, source_target_pairs={{0,1},{1,0},{2,3},{3,2},{4,5},{5,4},{6,7},{7,6},{8,9},{9,8},{10,11... | collective-permute-start | bytes 4718600 | tf_op jit(solution)/shard_map/ppermute | solution.py:803
  256.5 94.4 %collective-permute-start.2 = (bf16[4,384,512]{2,1,0:T(8,128)(2,1)}, bf16[4,384,512]{2,1,0:T(8,128)(2,1)}, u32[]{:S(2)}, u32[]{:S(2)}) collective-permute-start(bf16[4,384,512]{2,1,0:T(8,128)(2,1)} %get-tuple-element.530), channel_id=1, source_target_pairs={{0,1},{1,0},{2,3},{3,2},{4,5},{5,4},{6,7},{7,6},{8,9},{9,8},{10,11... | collective-permute-start | bytes 4718600 | tf_op jit(solution)/shard_map/ppermute | solution.py:803
  287.2 70.6 %collective-permute-start = (bf16[4,384,512]{2,1,0:T(8,128)(2,1)}, bf16[4,384,512]{2,1,0:T(8,128)(2,1)}, u32[]{:S(2)}, u32[]{:S(2)}) collective-permute-start(bf16[4,384,512]{2,1,0:T(8,128)(2,1)} %get-tuple-element.532), channel_id=1, source_target_pairs={{0,1},{1,0},{2,3},{3,2},{4,5},{5,4},{6,7},{7,6},{8,9},{9,8},{10,11... | collective-permute-start | bytes 4718600 | tf_op jit(solution)/shard_map/ppermute | solution.py:803
  362.0 390.2 %copy-start = (f32[256,1536]{1,0:T(8,128)}, f32[256,1536]{1,0:T(8,128)S(1)}, u32[]{:S(2)}) copy-start(f32[256,1536]{1,0:T(8,128)S(1)} %get-tuple-element.550) | copy-start | bytes 4718596
  370.7 694.9 %reduce-scatter.15.cloned.1.call-start = ((), (), s32[]{:S(2)}) async-start(), calls=%async_computation.9 | async-start | bytes 7864320 | tf_op jit(solution)/shard_map/reduce_scatter | solution.py:1116
  376.7 688.9 %reduce-scatter.13.cloned.1.call-start = ((), (), s32[]{:S(2)}) async-start(), calls=%async_computation.8 | async-start | bytes 5898240 | tf_op jit(solution)/shard_map/reduce_scatter | solution.py:1116
  377.4 4.1 collective-permute-start.6
  757.3 385.5 %reduce-scatter.11.cloned.1.call-start = ((), (), s32[]{:S(2)}) async-start(), calls=%async_computation.7 | async-start | bytes 9830400 | tf_op jit(solution)/shard_map/reduce_scatter | solution.py:1116
  761.3 119.6 %collective-permute-start.10 = (bf16[2,4,384,512]{3,2,1,0:T(8,128)(2,1)}, bf16[2,4,384,512]{3,2,1,0:T(8,128)(2,1)}, u32[]{:S(2)}, u32[]{:S(2)}) collective-permute-start(bf16[2,4,384,512]{3,2,1,0:T(8,128)(2,1)} %slice.109), channel_id=1, source_target_pairs={{0,2},{1,3},{2,0},{3,1},{4,6},{5,7},{6,4},{7,5},{8,10},{9,11},{10,... | collective-permute-start | bytes 9437192 | tf_op jit(solution)/shard_map/ppermute | solution.py:803
  765.9 172.1 %collective-permute-start.11 = (bf16[2,4,512,384]{3,2,1,0:T(8,128)(2,1)}, bf16[2,4,512,384]{3,2,1,0:T(8,128)(2,1)}, u32[]{:S(2)}, u32[]{:S(2)}) collective-permute-start(bf16[2,4,512,384]{3,2,1,0:T(8,128)(2,1)} %slice.110), channel_id=1, source_target_pairs={{0,2},{1,3},{2,0},{3,1},{4,6},{5,7},{6,4},{7,5},{8,10},{9,11},{10,... | collective-permute-start | bytes 9437192 | tf_op jit(solution)/shard_map/ppermute | solution.py:803
  771.2 233.2 %collective-permute-start.9 = (bf16[2,4,384,512]{3,2,1,0:T(8,128)(2,1)}, bf16[2,4,384,512]{3,2,1,0:T(8,128)(2,1)}, u32[]{:S(2)}, u32[]{:S(2)}) collective-permute-start(bf16[2,4,384,512]{3,2,1,0:T(8,128)(2,1)} %slice.108), channel_id=1, source_target_pairs={{0,2},{1,3},{2,0},{3,1},{4,6},{5,7},{6,4},{7,5},{8,10},{9,11},{10,... | collective-permute-start | bytes 9437192 | tf_op jit(solution)/shard_map/ppermute | solution.py:803
  1011.3 160.9 %reduce-scatter.19.cloned.1.call-start = ((), (), s32[]{:S(2)}) async-start(), calls=%async_computation.12 | async-start | bytes 491520
  1019.1 327.1 %reduce-scatter.9.cloned.1.call-start = ((), (), s32[]{:S(2)}) async-start(), calls=%async_computation.6 | async-start | bytes 14155776 | tf_op jit(solution)/shard_map/reduce_scatter | solution.py:1014
  1043.4 330.1 %all-reduce.3.cloned.1.call-start = ((), (), s32[]{:S(2)}) async-start(), calls=%async_computation.13 | async-start | bytes 11010048 | tf_op jit(solution)/shard_map/psum | solution.py:1117
  1051.7 139.8 %collective-permute-start.14 = (bf16[4,512,384]{2,1,0:T(8,128)(2,1)}, bf16[4,512,384]{2,1,0:T(8,128)(2,1)}, u32[]{:S(2)}, u32[]{:S(2)}) collective-permute-start(bf16[4,512,384]{2,1,0:T(8,128)(2,1)} %fusion.52), channel_id=1, source_target_pairs={{0,1},{1,0},{2,3},{3,2},{4,5},{5,4},{6,7},{7,6},{8,9},{9,8},{10,11... | collective-permute-start | bytes 4718600 | tf_op jit(solution)/shard_map/ppermute | solution.py:803
  1057.6 140.3 %collective-permute-start.13 = (bf16[4,384,512]{2,1,0:T(8,128)(2,1)}, bf16[4,384,512]{2,1,0:T(8,128)(2,1)}, u32[]{:S(2)}, u32[]{:S(2)}) collective-permute-start(bf16[4,384,512]{2,1,0:T(8,128)(2,1)} %fusion.51), channel_id=1, source_target_pairs={{0,1},{1,0},{2,3},{3,2},{4,5},{5,4},{6,7},{7,6},{8,9},{9,8},{10,11... | collective-permute-start | bytes 4718600 | tf_op jit(solution)/shard_map/ppermute | solution.py:803
  1064.7 133.2 %collective-permute-start.12 = (bf16[4,384,512]{2,1,0:T(8,128)(2,1)}, bf16[4,384,512]{2,1,0:T(8,128)(2,1)}, u32[]{:S(2)}, u32[]{:S(2)}) collective-permute-start(bf16[4,384,512]{2,1,0:T(8,128)(2,1)} %fusion.50), channel_id=1, source_target_pairs={{0,1},{1,0},{2,3},{3,2},{4,5},{5,4},{6,7},{7,6},{8,9},{9,8},{10,11... | collective-permute-start | bytes 4718600 | tf_op jit(solution)/shard_map/ppermute | solution.py:803
  1347.4 36.3 %collective-permute-start.8 = (bf16[256,1536]{1,0:T(8,128)(2,1)S(1)}, bf16[256,1536]{1,0:T(8,128)(2,1)S(1)}, u32[]{:S(2)}, u32[]{:S(2)}) collective-permute-start(bf16[256,1536]{1,0:T(8,128)(2,1)S(1)} %dynamic-slice_bitcast_fusion.6), channel_id=1, source_target_pairs={{0,1},{1,0},{2,3},{3,2},{4,5},{5,4},{6,7},{7,6},{8,9},{9,8},{10,11... | collective-permute-start | bytes 2359304 | tf_op jit(solution)/shard_map/ppermute | solution.py:803
  (48 other events, 949.8 us)
Sparse Core Ops, SparseCore 0:
  243.2 114.8 all-gather.3
  1143.0 230.4 all-reduce.2
Sparse Core Ops, SparseCore 1:
  370.8 50.2 reduce-scatter.16
  423.9 120.6 reduce-scatter.14
  757.4 103.5 reduce-scatter.12
  1011.4 131.4 reduce-scatter.10
  1146.3 25.9 reduce-scatter.18
  1174.6 171.6 reduce-scatter.8

commit v3 on v2

--- a/solution.py
+++ b/solution.py
@@ -27,138 +27,6 @@
 def silu_slope(gate_part):
     sigmoid = jax.nn.sigmoid(gate_part)
     return sigmoid * (1.0 + gate_part * (1.0 - sigmoid))
-
-
-def block_mask(begin, width, query_pos, query_seg, seg_all):
-    key_pos = begin + jnp.arange(width, dtype=jnp.int32)
-    key_seg = lax.dynamic_slice_in_dim(seg_all, begin, width)
-    return (key_pos[None, :] <= query_pos[:, None]) & (key_seg[None, :] == query_seg[:, None])
-
-
-def forward_piece(state, piece, grouped, query_pos, query_seg, seg_all, last_query):
-    piece_keys, piece_values = piece
-    count = piece_keys.shape[0]
-    width = math.gcd(count, 512)
-    scale = HEAD_DIM ** (-0.5)
-
-    def forward_inner(carry, index):
-        begin = index * width
-
-        def forward_compute(current):
-            best, total, accum = current
-            block_keys = lax.dynamic_slice_in_dim(piece_keys, begin, width).reshape(
-                width, KV_HEADS, HEAD_DIM
-            )
-            block_values = lax.dynamic_slice_in_dim(piece_values, begin, width).reshape(
-                width, KV_HEADS, HEAD_DIM
-            )
-            allowed = block_mask(begin, width, query_pos, query_seg, seg_all)
-            scores = (
-                jnp.einsum(
-                    "qkgd,skd->kgqs", grouped, block_keys, preferred_element_type=jnp.float32
-                )
-                * scale
-            )
-            scores = jnp.where(allowed[None, None], scores, masked_value)
-            newest = jnp.maximum(best, jnp.max(scores, axis=-1))
-            factor = jnp.exp(best - newest)
-            weights = jnp.exp(scores - newest[..., None])
-            total = total * factor + jnp.sum(weights, axis=-1)
-            accum = accum * factor[..., None] + jnp.einsum(
-                "kgqs,skd->kgqd",
-                weights.astype(jnp.bfloat16),
-                block_values,
-                preferred_element_type=jnp.float32,
-            )
-            return (newest, total, accum)
-
-        def forward_keep(current):
-            return current
-
-        return (lax.cond(begin <= last_query, forward_compute, forward_keep, carry), None)
-
-    state, _ = lax.scan(forward_inner, state, jnp.arange(count // width, dtype=jnp.int32))
-    return state
-
-
-def backward_piece(
-    state,
-    piece,
-    grouped,
-    grad_grouped,
-    log_totals,
-    deltas,
-    query_pos,
-    query_seg,
-    seg_all,
-    last_query,
-):
-    piece_keys, piece_values = piece
-    count = piece_keys.shape[0]
-    width = math.gcd(count, 512)
-    scale = HEAD_DIM ** (-0.5)
-    grad_queries, keys_grad, values_grad = state
-    kv_width = piece_keys.shape[1]
-
-    def backward_inner(carry, index):
-        begin = index * width
-
-        def backward_compute(current):
-            block_keys = lax.dynamic_slice_in_dim(piece_keys, begin, width).reshape(
-                width, KV_HEADS, HEAD_DIM
-            )
-            block_values = lax.dynamic_slice_in_dim(piece_values, begin, width).reshape(
-                width, KV_HEADS, HEAD_DIM
-            )
-            allowed = block_mask(begin, width, query_pos, query_seg, seg_all)
-            scores = (
-                jnp.einsum(
-                    "qkgd,skd->kgqs", grouped, block_keys, preferred_element_type=jnp.float32
-                )
-                * scale
-            )
-            scores = jnp.where(allowed[None, None], scores, masked_value)
-            probs = jnp.exp(scores - log_totals[..., None])
-            grad_probs = jnp.einsum(
-                "qkgd,skd->kgqs", grad_grouped, block_values, preferred_element_type=jnp.float32
-            )
-            grad_scores = (probs * (grad_probs - deltas[..., None])).astype(jnp.bfloat16)
-            updated = (
-                current
-                + jnp.einsum(
-                    "kgqs,skd->qkgd", grad_scores, block_keys, preferred_element_type=jnp.float32
-                )
-                * scale
-            )
-            key_term = (
-                jnp.einsum(
-                    "kgqs,qkgd->skd", grad_scores, grouped, preferred_element_type=jnp.float32
-                )
-                * scale
-            )
-            value_term = jnp.einsum(
-                "kgqs,qkgd->skd",
-                probs.astype(jnp.bfloat16),
-                grad_grouped,
-                preferred_element_type=jnp.float32,
-            )
-            return (updated, key_term.reshape(width, kv_width), value_term.reshape(width, kv_width))
-
-        def backward_keep(current):
-            empty = jnp.zeros((width, kv_width), jnp.float32)
-            return (current, empty, empty)
-
-        updated, key_term, value_term = lax.cond(
-            begin <= last_query, backward_compute, backward_keep, carry
-        )
-        return (updated, (key_term, value_term))
-
-    grad_queries, (key_terms, value_terms) = lax.scan(
-        backward_inner, grad_queries, jnp.arange(count // width, dtype=jnp.int32)
-    )
-    keys_grad = key_terms.reshape(count, -1)
-    values_grad = value_terms.reshape(count, -1)
-    return (grad_queries, keys_grad, values_grad)
 
 
 MESH = pl.DeviceIdType.MESH
@@ -196,13 +64,14 @@
 
 
 class Slabs:
-    def __init__(self, count, sources, targets, here, send, recv, near_send, near_recv):
+    def __init__(self, count, sources, targets, here, there, send, recv, near_send, near_recv, *stages):
         self.c, self.w = lax.axis_index("ctx"), lax.axis_index("wt")
         self.core = lax.rem(self.c, 2)
         self.near = (flip(self.c, 1), self.w)
         self.peers = [flip(self.w, d) for d in range(1, count)]
         self.pairs = list(zip(sources, targets))
-        self.here, self.send, self.recv = here, send, recv
+        self.here, self.there, self.send, self.recv = here, there, send, recv
+        self.stages = stages
         self.near_send, self.near_recv = near_send, near_recv
 
     def devices(self):
@@ -229,9 +98,11 @@
         spot = target.at[self.peers[i], self.half(source, core)]
         return remote(spot, spot, self.near_send.at[s, i], self.near_recv.at[s, i], self.near)
 
+    def load(self, s):
+        return pltpu.make_async_copy(self.pairs[s][0], self.stages[s], self.here.at[s])
+
     def keep(self, s):
-        source, target = self.pairs[s]
-        return pltpu.make_async_copy(source, target.at[self.w], self.here.at[s])
+        return pltpu.make_async_copy(self.stages[s], self.pairs[s][1].at[self.w], self.there.at[s])
 
     def every(self):
         return [(i, s) for s in range(len(self.pairs)) for i in range(len(self.peers))]
@@ -240,9 +111,12 @@
         for i, s in self.every():
             self.push(i, s).start()
         for s in range(len(self.pairs)):
+            self.load(s).start()
+
+    def relay(self):
+        for s in range(len(self.pairs)):
+            self.load(s).wait()
             self.keep(s).start()
-
-    def relay(self):
         for i, s in self.every():
             self.arrival(i, s).wait_recv()
             self.hand(i, s, self.core).start()
@@ -258,41 +132,19 @@
     @staticmethod
     def scratch(slabs, count):
         dma = pltpu.SemaphoreType.DMA
-        return [dma((slabs,))] + [dma((slabs, count - 1))] * 4
+        number = len(slabs)
+        return (
+            [dma((number,))] * 2
+            + [dma((number, count - 1))] * 4
+            + [pltpu.VMEM(s.shape, s.dtype) for s in slabs]
+        )
 
     @staticmethod
     def shapes(slabs, count):
         return tuple(jax.ShapeDtypeStruct((count,) + s.shape, s.dtype) for s in slabs)
 
 
-def weights_kernel(count, slabs, *refs):
-    sources, targets, zero_ref = refs[:slabs], refs[slabs : 2 * slabs], refs[2 * slabs]
-    plan = Slabs(count, sources, targets, *refs[2 * slabs + 1 :])
-    greet(plan.devices() + [plan.near])
-    plan.start()
-    zero_ref[...] = jnp.zeros_like(zero_ref)
-    plan.relay()
-    plan.finish()
-
-
-def gather_weights(slabs):
-    count = lax.axis_size("wt")
-    return pl.pallas_call(
-        functools.partial(weights_kernel, count, len(slabs)),
-        out_shape=Slabs.shapes(slabs, count) + (jax.ShapeDtypeStruct((8, 128), jnp.int32),),
-        in_specs=[pl.BlockSpec(memory_space=pl.ANY)] * len(slabs),
-        out_specs=(pl.BlockSpec(memory_space=pl.ANY),) * len(slabs)
-        + (pl.BlockSpec(memory_space=pltpu.VMEM),),
-        scratch_shapes=Slabs.scratch(len(slabs), count),
-        compiler_params=pltpu.CompilerParams(
-            collective_id=1, has_side_effects=True, vmem_limit_bytes=WIDE
-        ),
-        cost_estimate=CHEAP,
-        name="gather_weights",
-    )(*slabs)
-
-
-def gather_kernel(chips, downward, paired, count, slabs, passed, rows_ref, *refs):
+def weights_kernel(count, slabs, swaps, *refs):
     refs = list(refs)
 
     def take(number):
@@ -300,11 +152,76 @@
         del refs[:number]
         return taken
 
+    sources, given = take(slabs), take(swaps)
+    targets, paired, (zero_ref,) = take(slabs), take(swaps), take(1)
+    stages = take(swaps)
+    load_sem, keep_sem, swap_send, swap_recv = take(4)
+    plan = Slabs(count, sources, targets, *refs)
+    c, w = lax.axis_index("ctx"), lax.axis_index("wt")
+    side = lax.rem(w, 2)
+    partner = (c, flip(w, 1))
+    greet(plan.devices() + [plan.near])
+
+    def swap(i):
+        return remote(given[i], paired[i].at[side], swap_send.at[i], swap_recv.at[i], partner)
+
+    def load(i):
+        return pltpu.make_async_copy(given[i], stages[i], load_sem.at[i])
+
+    def keep(i):
+        return pltpu.make_async_copy(stages[i], paired[i].at[side], keep_sem.at[i])
+
+    plan.start()
+    for i in range(swaps):
+        swap(i).start()
+        load(i).start()
+    zero_ref[...] = jnp.zeros_like(zero_ref)
+    for i in range(swaps):
+        load(i).wait()
+        keep(i).start()
+    plan.relay()
+    plan.finish()
+    for i in range(swaps):
+        keep(i).wait()
+        swap(i).wait()
+
+
+def gather_weights(slabs, swaps):
+    count = lax.axis_size("wt")
+    dma = pltpu.SemaphoreType.DMA((len(swaps),))
+    pairs = tuple(jax.ShapeDtypeStruct((2,) + s.shape, s.dtype) for s in swaps)
+    shapes = Slabs.shapes(slabs, count) + pairs
+    return pl.pallas_call(
+        functools.partial(weights_kernel, count, len(slabs), len(swaps)),
+        out_shape=shapes + (jax.ShapeDtypeStruct((8, 128), jnp.int32),),
+        in_specs=[pl.BlockSpec(memory_space=pl.ANY)] * (len(slabs) + len(swaps)),
+        out_specs=(pl.BlockSpec(memory_space=pl.ANY),) * len(shapes)
+        + (pl.BlockSpec(memory_space=pltpu.VMEM),),
+        scratch_shapes=[pltpu.VMEM(s.shape, s.dtype) for s in swaps]
+        + [dma] * 4
+        + Slabs.scratch(slabs, count),
+        compiler_params=pltpu.CompilerParams(
+            collective_id=1, has_side_effects=True, vmem_limit_bytes=WIDE
+        ),
+        cost_estimate=LONG,
+        name="gather_weights",
+    )(*slabs, *swaps)
+
+
+def gather_kernel(chips, downward, paired, count, slabs, passed, rows_ref, *refs):
+    refs = list(refs)
+
+    def take(number):
+        taken = refs[:number]
+        del refs[:number]
+        return taken
+
     hops = count // 2 - 1
     sources, moved = take(slabs), take(passed)
     (out_ref,), targets, landed, (zero_ref,) = take(1), take(slabs), take(passed * hops), take(1)
+    (stage,) = take(1)
     here, up_send, up_recv, down_send, down_recv, pair_send, pair_recv, near_send, near_recv = take(9)
-    plan = Slabs(count, sources, targets, *take(5)) if slabs else None
+    plan = Slabs(count, sources, targets, *take(6 + slabs)) if slabs else None
     pass_send, pass_recv = take(2) if passed else (None, None)
     zero_ref[...] = jnp.zeros_like(zero_ref)
     c, w = lax.axis_index("ctx"), lax.axis_index("wt")
@@ -350,8 +267,9 @@
         taken(chip).wait_recv()
         hand(chip, 1 - side, spot(chip, 1 - side, core)).start()
 
-    keep = pltpu.make_async_copy(rows_ref, spot(z, side, core), here)
-    keep.start()
+    load = pltpu.make_async_copy(rows_ref, stage, here.at[0])
+    keep = pltpu.make_async_copy(stage, spot(z, side, core), here.at[1])
+    load.start()
     pl.when(z < chips - 1)(lambda: lift(z, rows_ref).start())
     if downward:
         pl.when(z > 0)(lambda: drop(z, rows_ref).start())
@@ -363,6 +281,8 @@
     for d in range(hops):
         for i in range(passed):
             onward(i, d).start()
+    load.wait()
+    keep.start()
     for step in range(1, chips):
         low, high = z - step, z + step
 
@@ -437,10 +357,10 @@
         in_specs=[pl.BlockSpec(memory_space=pl.ANY)] * (1 + len(slabs) + len(moved)),
         out_specs=(pl.BlockSpec(memory_space=pl.ANY),) * len(shapes)
         + (pl.BlockSpec(memory_space=pltpu.VMEM),),
-        scratch_shapes=[pltpu.SemaphoreType.DMA]
+        scratch_shapes=[pltpu.VMEM(rows.shape, rows.dtype), pltpu.SemaphoreType.DMA((2,))]
         + [line] * 6
         + [both] * 2
-        + (Slabs.scratch(len(slabs), count) if slabs else [])
+        + (Slabs.scratch(slabs, count) if slabs else [])
         + ([pltpu.SemaphoreType.DMA((len(moved), hops))] * 2 if moved else []),
         compiler_params=pltpu.CompilerParams(
             collective_id=collective_id, has_side_effects=True, vmem_limit_bytes=WIDE
@@ -522,7 +442,7 @@
 
     def add_into(chip, which, piece, other):
         spot = own.at[chip, which, cut(piece)]
-        spot[...] = (spot[...].astype(jnp.float32) + other[...].astype(jnp.float32)).astype(spot.dtype)
+        spot[...] = spot[...] + other[...]
 
     for chip in order:
 
@@ -631,6 +551,337 @@
     )(partial)
 
 
+def dense_kernel(chips, count, matrices, pieces, *refs):
+    refs = list(refs)
+
+    def take(number):
+        taken = refs[:number]
+        del refs[:number]
+        return taken
+
+    grads, outs = take(matrices), take(matrices)
+    own, sib, mates, low, final = (take(matrices) for _ in range(5))
+    (load, near_send, near_recv, send, recv, low_send, low_recv, back_send, back_recv, last_send, last_recv, keep) = refs
+    c, w = lax.axis_index("ctx"), lax.axis_index("wt")
+    z = c // 2
+    core = lax.rem(c, 2)
+    near = (flip(c, 1), w)
+    above = (lax.rem(c + 2, 2 * chips), w)
+    below = (lax.rem(c + 2 * chips - 2, 2 * chips), w)
+    peers = [flip(w, d) for d in range(1, count)]
+    greet([near, above, below] + [(c, p) for p in peers])
+
+    def span(j, parity=None):
+        m, first, rows = pieces[j]
+        if parity is None:
+            return pl.ds(first, rows)
+        half = grads[m].shape[1] // 2
+        return pl.ds(pl.multiple_of(parity * half + first, 16), rows)
+
+    def fetch(j):
+        m = pieces[j][0]
+        return pltpu.make_async_copy(grads[m].at[:, span(j, core)], own[m].at[:, span(j)], load.at[j])
+
+    def hand(j):
+        m = pieces[j][0]
+        return remote(
+            grads[m].at[:, span(j, 1 - core)], sib[m].at[:, span(j)], near_send.at[j], near_recv.at[j], near
+        )
+
+    def give(j, d):
+        m = pieces[j][0]
+        return remote(
+            own[m].at[peers[d], span(j)], mates[m].at[d, span(j)], send.at[j, d], recv.at[j, d], (c, peers[d])
+        )
+
+    def total(j):
+        return own[pieces[j][0]].at[w, span(j)]
+
+    def add(spot, other):
+        spot[...] = spot[...] + other[...]
+
+    def start(j):
+        hand(j).start()
+        fetch(j).start()
+
+    def share(j):
+        m = pieces[j][0]
+        fetch(j).wait()
+        hand(j).wait_recv()
+        for d in range(count - 1):
+            add(own[m].at[peers[d], span(j)], sib[m].at[peers[d], span(j)])
+            give(j, d).start()
+        add(total(j), sib[m].at[w, span(j)])
+
+    def collect(j):
+        m = pieces[j][0]
+        value = total(j)[...].astype(jnp.float32)
+        for d in range(count - 1):
+            give(j, d).wait_recv()
+            value = value + mates[m][d, span(j), :].astype(jnp.float32)
+        total(j)[...] = value.astype(jnp.bfloat16)
+
+    def line(j):
+        return (z, above, below) if j % 2 == 0 else (chips - 1 - z, below, above)
+
+    def onward(j):
+        m = pieces[j][0]
+        return remote(total(j), low[m].at[span(j)], low_send.at[j], low_recv.at[j], line(j)[1])
+
+    def backward(j):
+        spot = final[pieces[j][0]].at[span(j)]
+        return remote(spot, spot, back_send.at[j], back_recv.at[j], line(j)[2])
+
+    def across(j, parity):
+        m = pieces[j][0]
+        return remote(
+            final[m].at[span(j)], outs[m].at[span(j, parity)], last_send.at[j], last_recv.at[j], near
+        )
+
+    def store(j):
+        m = pieces[j][0]
+        return pltpu.make_async_copy(final[m].at[span(j)], outs[m].at[span(j, core)], keep.at[j])
+
+    def accumulate(j):
+        place = line(j)[0]
+        m = pieces[j][0]
+
+        @pl.when(place > 0)
+        def _():
+            onward(j).wait_recv()
+            add(total(j), low[m].at[span(j)])
+
+        @pl.when(place < chips - 1)
+        def _():
+            onward(j).start()
+
+        @pl.when(place == chips - 1)
+        def _():
+            final[m][span(j), :] = total(j)[...]
+            backward(j).start()
+            across(j, core).start()
+            store(j).start()
+
+    def spread(j):
+        place = line(j)[0]
+
+        @pl.when(place < chips - 1)
+        def _():
+            backward(j).wait_recv()
+            pl.when(place > 0)(lambda: backward(j).start())
+            across(j, core).start()
+            store(j).start()
+
+    number = len(pieces)
+    for j in range(number):
+        start(j)
+    for j in range(number):
+        share(j)
+    last = chips - 1
+    for t in range(number + 2 * last):
+        if t < number:
+            collect(t)
+        for hop in range(2 * last, -1, -1):
+            j = t - hop
+            if not 0 <= j < number:
+                continue
+            if hop <= last:
+                pl.when(line(j)[0] == hop)(lambda: accumulate(j))
+            if hop > last:
+                pl.when(line(j)[0] == 2 * last - hop)(lambda: spread(j))
+    for j in range(number):
+        place = line(j)[0]
+        hand(j).wait_send()
+        for d in range(count - 1):
+            give(j, d).wait_send()
+        pl.when(place < chips - 1)(lambda: onward(j).wait_send())
+        pl.when(place > 0)(lambda: backward(j).wait_send())
+        across(j, core).wait_send()
+        across(j, 1 - core).wait_recv()
+        store(j).wait()
+
+
+def reduce_dense(grads):
+    count = lax.axis_size("wt")
+    chips = lax.axis_size("ctx") // 2
+    shapes = [(g.shape[0] // count, g.shape[1]) for g in grads]
+    pieces = []
+    for m, (rows, _) in enumerate(shapes):
+        half, width = rows // 2, shapes[m][1]
+        cuts = max(n for n in range(1, 5) if half % (16 * n) == 0 and (n == 1 or half * width > 120000 * (n - 1)))
+        for i in range(cuts):
+            pieces.append((m, i * (rows // 2 // cuts), rows // 2 // cuts))
+    halves = [(rows // 2, width) for rows, width in shapes]
+    dma = pltpu.SemaphoreType.DMA
+    one, many = dma((len(pieces),)), dma((len(pieces), count - 1))
+    return pl.pallas_call(
+        functools.partial(dense_kernel, chips, count, len(grads), tuple(pieces)),
+        out_shape=[jax.ShapeDtypeStruct(s, jnp.bfloat16) for s in shapes],
+        in_specs=[pl.BlockSpec(memory_space=pl.ANY)] * len(grads),
+        out_specs=[pl.BlockSpec(memory_space=pl.ANY)] * len(grads),
+        scratch_shapes=[pltpu.VMEM((count,) + h, jnp.bfloat16) for h in halves]
+        + [pltpu.VMEM((count,) + h, jnp.bfloat16) for h in halves]
+        + [pltpu.VMEM((count - 1,) + h, jnp.bfloat16) for h in halves]
+        + [pltpu.VMEM(h, jnp.bfloat16) for h in halves]
+        + [pltpu.VMEM(h, jnp.bfloat16) for h in halves]
+        + [one, one, one, many, many, one, one, one, one, one, one, one],
+        compiler_params=pltpu.CompilerParams(
+            collective_id=7, has_side_effects=True, vmem_limit_bytes=WIDE
+        ),
+        cost_estimate=LONG,
+        name="reduce_dense",
+    )(*[g.reshape((count,) + s) for g, s in zip(grads, shapes)])
+
+
+def dot_of(a, b, left, right):
+    return lax.dot_general(
+        a, b, (((left,), (right,)), ((), ())), preferred_element_type=jnp.float32
+    )
+
+
+def stacked_heads(ref):
+    return jnp.concatenate(
+        [ref[:, h * HEAD_DIM : (h + 1) * HEAD_DIM] for h in range(ref.shape[1] // HEAD_DIM)], axis=0
+    )
+
+
+exponent_scale = HEAD_DIM ** (-0.5) * math.log2(math.e)
+
+
+def attend_kernel(place_ref, query_ref, both_ref, row_ref, column_ref, out_ref, log_ref, best, total, accum):
+    tokens = query_ref.shape[0]
+    group = query_ref.shape[1] // HEAD_DIM
+    width = 2 * tokens
+    place = place_ref[0]
+    queries = stacked_heads(query_ref)
+    best[...] = jnp.full_like(best, masked_value)
+    total[...] = jnp.zeros_like(total)
+    accum[...] = jnp.zeros_like(accum)
+    query_pos = place * tokens + lax.broadcasted_iota(jnp.int32, (tokens, width), 0)
+    key_pos = lax.broadcasted_iota(jnp.int32, (tokens, width), 1)
+
+    def step(j, carry):
+        span = pl.ds(pl.multiple_of(j * width, width), width)
+        allowed = (key_pos + j * width <= query_pos) & (row_ref[0:1, span] == column_ref[:, 0:1])
+        bias = jnp.where(allowed, 0.0, masked_value)
+        scores = dot_of(queries, both_ref[span, :HEAD_DIM], 1, 1)
+        scores = (scores.reshape(group, tokens, width) + bias[None]).reshape(group * tokens, width)
+        newest = jnp.maximum(best[...], jnp.max(scores, axis=1, keepdims=True))
+        factor = jnp.exp2((best[...] - newest) * exponent_scale)
+        weights = jnp.exp2((scores - newest[:, :1]) * exponent_scale)
+        total[...] = total[...] * factor + jnp.sum(weights, axis=1, keepdims=True)
+        accum[...] = accum[...] * factor + dot_of(
+            weights.astype(jnp.bfloat16), both_ref[span, HEAD_DIM:], 1, 0
+        )
+        best[...] = newest
+        return carry
+
+    lax.fori_loop(0, place // 2 + 1, step, 0)
+    heads = accum[...] / total[...]
+    for h in range(group):
+        out_ref[:, h * HEAD_DIM : (h + 1) * HEAD_DIM] = heads[h * tokens : (h + 1) * tokens]
+    logs = best[...] * exponent_scale + jnp.log2(total[...])
+    log_ref[0] = jnp.transpose(logs)[:8]
+
+
+def attend(place, projected, both, seg_row, seg_column):
+    tokens = projected.shape[0]
+    group = HEADS // KV_HEADS
+    rows, span = group * tokens, both.shape[0]
+    stat = pltpu.VMEM((rows, HEAD_DIM), jnp.float32)
+    return pl.pallas_call(
+        attend_kernel,
+        grid=(KV_HEADS,),
+        out_shape=(
+            jax.ShapeDtypeStruct((tokens, HEADS * HEAD_DIM), jnp.float32),
+            jax.ShapeDtypeStruct((KV_HEADS, 8, rows), jnp.float32),
+        ),
+        in_specs=[
+            pl.BlockSpec(memory_space=pltpu.SMEM),
+            pl.BlockSpec((tokens, group * HEAD_DIM), lambda g: (0, g)),
+            pl.BlockSpec((span, 2 * HEAD_DIM), lambda g: (0, g)),
+            pl.BlockSpec((1, span), lambda g: (0, 0)),
+            pl.BlockSpec((tokens, 1), lambda g: (0, 0)),
+        ],
+        out_specs=(
+            pl.BlockSpec((tokens, group * HEAD_DIM), lambda g: (0, g)),
+            pl.BlockSpec((1, 8, rows), lambda g: (g, 0, 0)),
+        ),
+        scratch_shapes=[stat, stat, stat],
+        compiler_params=pltpu.CompilerParams(vmem_limit_bytes=WIDE),
+        cost_estimate=CHEAP,
+        name="attend",
+    )(place, projected, both, seg_row, seg_column)
+
+
+def attend_back_kernel(place_ref, query_ref, both_ref, row_ref, column_ref, heads_ref, grad_ref, log_ref, grad_query_ref, grad_both_ref, accum):
+    tokens = query_ref.shape[0]
+    group = query_ref.shape[1] // HEAD_DIM
+    width = 2 * tokens
+    rows = group * tokens
+    scale = HEAD_DIM ** (-0.5)
+    place = place_ref[0]
+    queries, grads = stacked_heads(query_ref), stacked_heads(grad_ref)
+    product = grads.astype(jnp.float32) * stacked_heads(heads_ref)
+    delta = jnp.sum(product, axis=1, keepdims=True)
+    delta = jnp.transpose(jnp.broadcast_to(delta, (rows, HEAD_DIM)))[0:1]
+    logs = log_ref[0, 0:1, :]
+    accum[...] = jnp.zeros_like(accum)
+    grad_both_ref[...] = jnp.zeros_like(grad_both_ref)
+    query_pos = place * tokens + lax.broadcasted_iota(jnp.int32, (width, tokens), 1)
+    key_pos = lax.broadcasted_iota(jnp.int32, (width, tokens), 0)
+
+    def step(j, carry):
+        span = pl.ds(pl.multiple_of(j * width, width), width)
+        allowed = (key_pos + j * width <= query_pos) & (column_ref[span, 0:1] == row_ref[0:1, :])
+        bias = jnp.where(allowed, 0.0, masked_value)
+        bias = jnp.concatenate([bias] * group, axis=1)
+        keys, values = both_ref[span, :HEAD_DIM], both_ref[span, HEAD_DIM:]
+        scores = dot_of(keys, queries, 1, 1)
+        probs = jnp.exp2(scores * exponent_scale + bias - logs)
+        grad_probs = dot_of(values, grads, 1, 1)
+        grad_scores = (probs * (grad_probs - delta)).astype(jnp.bfloat16)
+        accum[...] += dot_of(grad_scores, keys, 0, 0)
+        grad_both_ref[span, :HEAD_DIM] = (dot_of(grad_scores, queries, 1, 0) * scale).astype(jnp.bfloat16)
+        grad_both_ref[span, HEAD_DIM:] = dot_of(probs.astype(jnp.bfloat16), grads, 1, 0).astype(jnp.bfloat16)
+        return carry
+
+    lax.fori_loop(0, place // 2 + 1, step, 0)
+    grad_queries = (accum[...] * scale).astype(jnp.bfloat16)
+    for h in range(group):
+        grad_query_ref[:, h * HEAD_DIM : (h + 1) * HEAD_DIM] = grad_queries[h * tokens : (h + 1) * tokens]
+
+
+def attend_back(place, projected, both, query_seg_row, seg_column, heads_out, grad_attended, logs):
+    tokens = projected.shape[0]
+    group = HEADS // KV_HEADS
+    rows, span = group * tokens, both.shape[0]
+    per_group = pl.BlockSpec((tokens, group * HEAD_DIM), lambda g: (0, g))
+    return pl.pallas_call(
+        attend_back_kernel,
+        grid=(KV_HEADS,),
+        out_shape=(
+            jax.ShapeDtypeStruct((tokens, HEADS * HEAD_DIM), jnp.bfloat16),
+            jax.ShapeDtypeStruct(both.shape, jnp.bfloat16),
+        ),
+        in_specs=[
+            pl.BlockSpec(memory_space=pltpu.SMEM),
+            per_group,
+            pl.BlockSpec((span, 2 * HEAD_DIM), lambda g: (0, g)),
+            pl.BlockSpec((1, tokens), lambda g: (0, 0)),
+            pl.BlockSpec((span, 1), lambda g: (0, 0)),
+            per_group,
+            per_group,
+            pl.BlockSpec((1, 8, rows), lambda g: (g, 0, 0)),
+        ],
+        out_specs=(per_group, pl.BlockSpec((span, 2 * HEAD_DIM), lambda g: (0, g))),
+        scratch_shapes=[pltpu.VMEM((rows, HEAD_DIM), jnp.float32)],
+        compiler_params=pltpu.CompilerParams(vmem_limit_bytes=WIDE),
+        cost_estimate=CHEAP,
+        name="attend_back",
+    )(place, projected, both, query_seg_row, seg_column, heads_out, grad_attended, logs)
+
+
 def pick_kernel(scaled, slot_ref, gate_ref, rows_ref, out_ref, scale_ref=None):
     local, depth = out_ref.shape[2], out_ref.shape[3]
     tokens = rows_ref.shape[3]
@@ -718,12 +969,12 @@
 
 
 def expert_kernel(blocks, x_ref, g_ref, scale_ref, *refs):
-    gate_refs, up_refs, down_refs = refs[:blocks], refs[blocks : 2 * blocks], refs[2 * blocks : 3 * blocks]
-    result_ref, back_ref, grad_gate_ref, grad_up_ref, grad_down_ref = refs[3 * blocks :]
+    tall_refs, down_refs = refs[:blocks], refs[blocks : 2 * blocks]
+    result_ref, back_ref, grad_tall_ref, grad_down_ref = refs[2 * blocks :]
     w = lax.axis_index("wt")
     chips, sides, _, depth, width = x_ref.shape
     rows = chips * sides * depth
-    part = gate_refs[0].shape[1]
+    part = tall_refs[0].shape[2]
     nn, nt, tn = (((1,), (0,)), ((), ())), (((1,), (1,)), ((), ())), (((0,), (0,)), ((), ()))
 
     def dot(a, b, dims):
@@ -741,7 +992,7 @@
     gate, up, grad_inner = None, None, None
     for q in range(blocks):
         x = piece(x_ref, q)
-        more_gate, more_up = dot(x, gate_refs[q][0], nn), dot(x, up_refs[q][0], nn)
+        more_gate, more_up = dot(x, tall_refs[q][0, 0], nn), dot(x, tall_refs[q][0, 1], nn)
         gate, up = (more_gate, more_up) if q == 0 else (gate + more_gate, up + more_up)
     for q in range(blocks):
         more = dot(piece(g_ref, q), down_refs[q][0], nt)
@@ -755,18 +1006,18 @@
     for q in range(blocks):
         result = dot(inner, down_refs[q][0], nn) * scale
         columns(result_ref, q)[...] = result.astype(jnp.bfloat16).reshape(chips, sides, depth, part)
-        back = dot(grad_gate, gate_refs[q][0], nt) + dot(grad_up, up_refs[q][0], nt)
+        back = dot(grad_gate, tall_refs[q][0, 0], nt) + dot(grad_up, tall_refs[q][0, 1], nt)
         columns(back_ref, q)[...] = back.astype(jnp.bfloat16).reshape(chips, sides, depth, part)
         grad_down_ref[q, 0] = dot(inner, piece(g_ref, q), tn).astype(jnp.bfloat16)
         x = piece(x_ref, q)
-        grad_gate_ref[q, 0] = dot(x, grad_gate, tn).astype(jnp.bfloat16)
-        grad_up_ref[q, 0] = dot(x, grad_up, tn).astype(jnp.bfloat16)
-
-
-def run_experts(x, g, scale, gates, ups, downs):
+        grad_tall_ref[q, 0, 0] = dot(x, grad_gate, tn).astype(jnp.bfloat16)
+        grad_tall_ref[q, 0, 1] = dot(x, grad_up, tn).astype(jnp.bfloat16)
+
+
+def run_experts(x, g, scale, talls, downs):
     chips, sides, local, depth, width = x.shape
-    blocks = len(gates)
-    part, inner = gates[0].shape[1:]
+    blocks = len(talls)
+    part, inner = talls[0].shape[2:]
     large = chips * sides * depth > 1024
     rows = pl.BlockSpec((chips, sides, 1, depth, width), lambda e: (0, 0, e, 0, 0))
     sources = pl.BlockSpec(
@@ -775,9 +1026,9 @@
         pipeline_mode=pl.Buffered(1 if large else 2),
     )
     scales = pl.BlockSpec((chips, sides, 1, depth, 128), lambda e: (0, 0, e, 0, 0))
-    tall = pl.BlockSpec((1, part, inner), lambda e: (e, 0, 0))
+    tall = pl.BlockSpec((1, 2, part, inner), lambda e: (e, 0, 0, 0))
     flat = pl.BlockSpec((1, inner, part), lambda e: (e, 0, 0))
-    tall_out = pl.BlockSpec((blocks, 1, part, inner), lambda e: (0, e, 0, 0))
+    tall_out = pl.BlockSpec((blocks, 1, 2, part, inner), lambda e: (0, e, 0, 0, 0))
     flat_out = pl.BlockSpec((blocks, 1, inner, part), lambda e: (0, e, 0, 0))
     total = chips * sides * local * depth
     return pl.pallas_call(
@@ -786,16 +1037,15 @@
         out_shape=(
             jax.ShapeDtypeStruct(x.shape, jnp.bfloat16),
             jax.ShapeDtypeStruct(x.shape, jnp.bfloat16),
-            jax.ShapeDtypeStruct((blocks, local, part, inner), jnp.bfloat16),
-            jax.ShapeDtypeStruct((blocks, local, part, inner), jnp.bfloat16),
+            jax.ShapeDtypeStruct((blocks, local, 2, part, inner), jnp.bfloat16),
             jax.ShapeDtypeStruct((blocks, local, inner, part), jnp.bfloat16),
         ),
-        in_specs=[sources, sources, scales] + [tall] * (2 * blocks) + [flat] * blocks,
-        out_specs=(rows, rows, tall_out, tall_out, flat_out),
+        in_specs=[sources, sources, scales] + [tall] * blocks + [flat] * blocks,
+        out_specs=(rows, rows, tall_out, flat_out),
         compiler_params=pltpu.CompilerParams(vmem_limit_bytes=60 * 2**20),
         cost_estimate=CHEAP,
         name="experts",
-    )(x, g, scale, *gates, *ups, *downs)
+    )(x, g, scale, *talls, *downs)
 
 
 def swap_pairs(value, axis, distance):
@@ -850,11 +1100,6 @@
     other = swap_pairs(total[1].astype(jnp.bfloat16), "wt", 1).astype(jnp.float32)
     both = in_order(total[0], other, side)
     return both.reshape((-1,) + both.shape[2:])
-
-
-def gather_side(rows, side):
-    both = in_order(rows, swap_pairs(rows, "wt", 1), side)
-    return lax.all_gather(both, "ctx", axis=0)
 
 
 def body(
@@ -884,9 +1129,22 @@
     tokens, width_model = hidden.shape[1:]
     wide, kv_width = w_query.shape[1], w_key.shape[1]
     shared_width = shared_gate.shape[1]
-    slab, gains, zero = gather_weights(
+    tables = jnp.concatenate(
+        [
+            jnp.swapaxes(routes[0], 0, 1).astype(jnp.float32),
+            jnp.zeros((8 - TOPK, tokens), jnp.float32),
+            jnp.swapaxes(gates[0], 0, 1),
+            jnp.zeros((8 - TOPK, tokens), jnp.float32),
+        ],
+        axis=0,
+    )
+    grad_rows = cotangent[0]
+    key_parts = jnp.stack(
+        [w_key.reshape(-1, KV_HEADS, HEAD_DIM), w_value.reshape(-1, KV_HEADS, HEAD_DIM)], axis=2
+    ).reshape(-1, 2 * kv_width)
+    slab, gains, table_pair, grad_pair, zero = gather_weights(
         (
-            jnp.concatenate([w_query, w_key, w_value], axis=1),
+            jnp.concatenate([w_query, key_parts], axis=1),
             jnp.concatenate(
                 [
                     norm_one_gain[None],
@@ -894,32 +1152,26 @@
                     jnp.zeros((30, norm_one_gain.shape[0]), jnp.bfloat16),
                 ]
             ),
-        )
-    )
+        ),
+        (tables, grad_rows),
+    )
+    all_tables = lax.all_gather(table_pair, "ctx", axis=0)
+    all_grads = lax.all_gather(grad_pair, "ctx", axis=0).reshape(chips, 2, 2, tokens, width_model)
+    zero = zero[0, 0]
     side = lax.rem(wt_index, 2)
-    later = side + zero[0, 0]
     slab = slab.reshape(-1, slab.shape[2])
     gain_one, gain_two = gains[:, 0].reshape(-1), gains[:, 1].reshape(-1)
-    tables = jnp.concatenate(
-        [jnp.swapaxes(routes[0], 0, 1).astype(jnp.float32), jnp.swapaxes(gates[0], 0, 1)], axis=0
-    )
-    all_tables = gather_side(tables, side)
-    collected = [collect_expert(e, later, pairs) for e in (expert_gate, expert_up, expert_down)]
     local = expert_gate.shape[0] // 2
     first_expert = (lax.axis_index("ctx") * 2 + side) * local
 
     inputs = hidden[0].astype(jnp.float32)
     offset = lax.axis_index("ctx") * tokens
-    query_pos = offset + jnp.arange(tokens, dtype=jnp.int32)
-    last_query = offset + tokens - 1
     seg_all = segment_ids[0]
     query_seg = lax.dynamic_slice_in_dim(seg_all, offset, tokens)
-    group = HEADS // KV_HEADS
     scale_one = inverse_rms(inputs)
     gain_one_full = gain_one.astype(jnp.float32)
     normed = (inputs * scale_one * gain_one_full).astype(jnp.bfloat16)
     projected = jnp.dot(normed, slab, preferred_element_type=jnp.float32).astype(jnp.bfloat16)
-    queries = projected[:, :wide]
     both, out_weight, both_weight, down_weight, zero = gather_rows(
         projected[:, wide:],
         2,
@@ -932,40 +1184,29 @@
     both_weight = both_weight.reshape(-1, both_weight.shape[2])
     down_weight = down_weight.reshape(-1, down_weight.shape[2])
     both = both.reshape(-1, 2 * kv_width)
-    all_keys, all_values = both[:, :kv_width], both[:, kv_width:]
-
-    table_shape = (chips, 2, 2, 2 * TOPK, tokens)
+    later = side + zero
+    collected = [
+        collect_expert(jnp.stack([expert_gate, expert_up], axis=1), later, pairs),
+        collect_expert(expert_down, later, pairs),
+    ]
+
+    table_shape = (chips, 2, 2, 16, tokens)
     ordered_tables = jnp.transpose(all_tables.reshape(table_shape), (0, 2, 3, 1, 4)).reshape(
-        chips, 2, 2 * TOPK, 2 * tokens
+        chips, 2, 16, 2 * tokens
     )
     experts_here = (first_expert + jnp.arange(local, dtype=jnp.int32)).astype(jnp.float32)
     named = ordered_tables[:, :, None, :TOPK] == experts_here[None, None, :, None, None]
     member = jnp.any(named, axis=3)
-    slot_gates = jnp.sum(jnp.where(named, ordered_tables[:, :, None, TOPK:], 0.0), axis=3)
+    slot_gates = jnp.sum(jnp.where(named, ordered_tables[:, :, None, 8 : 8 + TOPK], 0.0), axis=3)
     earlier = (
         jnp.arange(2 * tokens)[:, None] < jnp.arange(2 * tokens)[None, :]
     ).astype(jnp.bfloat16)
     rank = jnp.dot(member.astype(jnp.bfloat16), earlier, preferred_element_type=jnp.float32)
     slots = jnp.where(member, rank.astype(jnp.int32), -1)
 
-    grad_rows = cotangent[0]
-    all_grads = gather_side(
-        lax.dynamic_index_in_dim(jnp.stack([grad_rows, grad_rows]), zero, 0, False), side
-    ).reshape(chips, 2, 2, tokens, width_model)
-
-    grouped = queries.reshape(tokens, KV_HEADS, group, HEAD_DIM)
-    start_state = (
-        jnp.full((KV_HEADS, group, tokens), masked_value, jnp.float32),
-        jnp.zeros((KV_HEADS, group, tokens), jnp.float32),
-        jnp.zeros((KV_HEADS, group, tokens, HEAD_DIM), jnp.float32),
-    )
-    best, total, accum = forward_piece(
-        start_state, (all_keys, all_values), grouped, query_pos, query_seg, seg_all, last_query
-    )
-    log_totals = best + jnp.log(total)
-    attended_full = jnp.transpose(accum / total[..., None], (2, 0, 1, 3)).reshape(
-        tokens, HEADS * HEAD_DIM
-    )
+    place = lax.axis_index("ctx").astype(jnp.int32).reshape(1)
+    seg_row, seg_column = seg_all[None, :], seg_all[:, None]
+    attended_full, logs = attend(place, projected, both, seg_row, query_seg[:, None])
     attended = attended_full.astype(jnp.bfloat16)
     attended, collected = lax.optimization_barrier((attended, collected))
     middle = inputs + jnp.dot(attended, out_weight, preferred_element_type=jnp.float32)
@@ -984,26 +1225,24 @@
             blocks += [straight[d], landed[i * (pairs - 1) + d]]
         return blocks
 
-    gate_blocks, up_blocks, down_blocks = blocks_of(0), blocks_of(1), blocks_of(2)
+    tall_blocks, down_blocks = blocks_of(0), blocks_of(1)
     (received_rows,) = pick_rows(all_rows, slots, slot_gates, False)
     grad_received, row_gates = pick_rows(all_grads, slots, slot_gates, True)
-    if gate_blocks[0].shape[1] % 128:
-        results, backs, grads_gate, grads_up, grads_down = run_experts(
+    if down_blocks[0].shape[2] % 128:
+        results, backs, grads_tall, grads_down = run_experts(
             received_rows,
             grad_received,
             row_gates,
-            [settle_blocks(gate_blocks, wt_index, 1)],
-            [settle_blocks(up_blocks, wt_index, 1)],
+            [settle_blocks(tall_blocks, wt_index, 2)],
             [settle_blocks(down_blocks, wt_index, 2)],
         )
-        grads_gate = split_blocks(grads_gate[0], wt_index, wt_count, 1)
-        grads_up = split_blocks(grads_up[0], wt_index, wt_count, 1)
+        grads_tall = split_blocks(grads_tall[0], wt_index, wt_count, 2)
         grads_down = split_blocks(grads_down[0], wt_index, wt_count, 2)
     else:
-        results, backs, grads_gate, grads_up, grads_down = run_experts(
-            received_rows, grad_received, row_gates, gate_blocks, up_blocks, down_blocks
-        )
-    expert_grads = (grads_gate, grads_up, grads_down)
+        results, backs, grads_tall, grads_down = run_experts(
+            received_rows, grad_received, row_gates, tall_blocks, down_blocks
+        )
+    expert_grads = (grads_tall, grads_down)
     arrived = [
         [swap_pairs(g[2 * d : 2 * d + 2], "wt", 2 * d) for d in range(1, pairs)] for g in expert_grads
     ]
@@ -1058,47 +1297,21 @@
     grad_attended = jnp.einsum(
         "td,qd->tq", grad_branch, out_weight, preferred_element_type=jnp.float32
     ).astype(jnp.bfloat16)
-    grad_grouped = grad_attended.reshape(tokens, KV_HEADS, group, HEAD_DIM)
-    deltas = jnp.transpose(
-        jnp.sum(
-            grad_grouped.astype(jnp.float32)
-            * attended_full.reshape(tokens, KV_HEADS, group, HEAD_DIM),
-            axis=-1,
-        ),
-        (1, 2, 0),
-    )
-    pack_len = seg_all.shape[0]
-    back_state = (
-        jnp.zeros((tokens, KV_HEADS, group, HEAD_DIM), jnp.float32),
-        jnp.zeros((pack_len, kv_width), jnp.float32),
-        jnp.zeros((pack_len, kv_width), jnp.float32),
-    )
-    grad_queries_full, keys_terms, values_terms = backward_piece(
-        back_state,
-        (all_keys, all_values),
-        grouped,
-        grad_grouped,
-        log_totals,
-        deltas,
-        query_pos,
-        query_seg,
-        seg_all,
-        last_query,
+    grad_queries, grad_parts = attend_back(
+        place, projected, both, query_seg[None, :], seg_column, attended_full, grad_attended, logs
     )
     grad_both = scatter_rows(
-        jnp.concatenate([keys_terms, values_terms], axis=1)
-        .astype(jnp.bfloat16)
-        .reshape(chips, 1, 2, tokens, 2 * kv_width),
+        grad_parts.reshape(chips, 1, 2, tokens, 2 * kv_width),
         6,
         False,
         False,
         "scatter_keys",
     ).astype(jnp.bfloat16)
     grad_both, arrived = lax.optimization_barrier((grad_both, arrived))
-    sum_experts_gate, sum_experts_up, sum_experts_down = [
+    sum_tall, sum_experts_down = [
         scatter_expert(g, a, side) for g, a in zip(expert_grads, arrived)
     ]
-    grad_queries = grad_queries_full.reshape(tokens, HEADS * HEAD_DIM).astype(jnp.bfloat16)
+    sum_experts_gate, sum_experts_up = sum_tall[:, 0], sum_tall[:, 1]
     grad_projected = jnp.concatenate([grad_queries, grad_both], axis=1)
     grad_slab = jnp.einsum("tc,tq->cq", normed, grad_projected, preferred_element_type=jnp.float32)
     grad_normed = jnp.einsum(
@@ -1112,20 +1325,28 @@
         - inputs * scale_one**3 * jnp.mean(scaled_one * inputs, axis=-1, keepdims=True)
     )
 
-    def reduced(grad):
-        part = lax.psum_scatter(grad.astype(jnp.bfloat16), "wt", scatter_dimension=0, tiled=True)
-        return lax.psum(part, "ctx").astype(jnp.float32)
-
-    final_shared = reduced(grad_shared_both)
+    depth = norm_one_gain.shape[0]
+    gain_grads = jnp.stack([grad_gain_one, grad_gain_two]).reshape(2, wt_count, 1, depth)
+    gain_grads = jnp.pad(gain_grads.astype(jnp.bfloat16), ((0, 0), (0, 0), (0, 15), (0, 0)))
+    gain_grads = jnp.swapaxes(gain_grads, 0, 1).reshape(wt_count * 32, depth)
+    final_slab, final_shared, final_out, final_down, final_gains = [
+        total.astype(jnp.float32)
+        for total in reduce_dense(
+            [
+                grad_slab.astype(jnp.bfloat16),
+                grad_shared_both.astype(jnp.bfloat16),
+                grad_out_weight.astype(jnp.bfloat16),
+                grad_shared_down.astype(jnp.bfloat16),
+                gain_grads,
+            ]
+        )
+    ]
     final_gate, final_up = final_shared[:, :shared_width], final_shared[:, shared_width:]
-    final_down = reduced(grad_shared_down)
-    final_out = reduced(grad_out_weight)
-    final_slab = reduced(grad_slab)
     final_query = final_slab[:, :wide]
-    final_key = final_slab[:, wide : wide + kv_width]
-    final_value = final_slab[:, wide + kv_width :]
-    final_gains = reduced(jnp.stack([grad_gain_one, grad_gain_two], axis=1))
-    final_gain_one, final_gain_two = final_gains[:, 0], final_gains[:, 1]
+    final_parts = final_slab[:, wide:].reshape(-1, KV_HEADS, 2, HEAD_DIM)
+    final_key = final_parts[:, :, 0].reshape(-1, kv_width)
+    final_value = final_parts[:, :, 1].reshape(-1, kv_width)
+    final_gain_one, final_gain_two = final_gains[0], final_gains[16]
     return (
         output[None],
         grad_inputs[None],

time: 1400 us -> 1170 us (0.84)
  waiting for transfers between devices: 467 us -> 17.6 us
  Pallas kernels: 621 us -> 837 us
  blocking collectives: 31.9 us -> 88.7 us
  local copies, waits for them, and re-layouts: 105 us -> 77.2 us
    pallas_call x1 -> x4, Pallas kernels: 66.1 us -> 296 us  [the longest x1 212 us: reduce_dense(): pl.pallas_call(functools.partial(dense_kernel, chips, count, len(grads),...]
    ppermute x15 -> x9, waiting for transfers between devices: 214 us -> 17.5 us  [swap_pairs(): return lax.ppermute(value, axis, [(i, i ^ distance) for i in range(count)])]
    reduce_scatter x1, waiting for transfers between devices: 134 us -> 0.01 us  [body(): lax.psum_scatter(jnp.swapaxes(spread, 1, 2).reshape(ctx_count, 2, tokens,...]
    reduce_scatter x4 -> x0, waiting for transfers between devices: 77.3 us -> none  [reduced(): lax.psum_scatter(grad.astype(jnp.bfloat16), 'wt', scatter_dimension=0, ti...]
    all_gather x1, blocking collectives: 14.2 us -> 88.7 us  [body(): all_tables = lax.all_gather(table_pair, 'ctx', axis=0)]
    pallas_call x2, Pallas kernels: 293 us -> 246 us  [gather_rows(): pl.pallas_call(functools.partial(gather_kernel, chips, downward, paired,...]
    pallas_call x2, Pallas kernels: 151 us -> 186 us  [scatter_rows(): pl.pallas_call(functools.partial(scatter_kernel, chips, upward, paired, p...]
    unnamed x9 -> x2, waiting for transfers between devices: 25.1 us -> 0.03 us
  transfers between devices with their start and end apart: 23 -> 11, of which waited for: 12 -> 1; matrix products, arithmetic and copies ran while one was open for 14% -> 14% of each run, Pallas kernels for 30% -> 59%
where the time goes in v3:
time: 1170 us; the launch traced here: 1160 us
  Pallas kernels  837 us (72%)
  blocking collectives  88.7 us (8%)
  local copies, waits for them, and re-layouts  77.2 us (7%)
  other arithmetic  64 us (5%)
  matrix products  54.4 us (5%)
  waiting for transfers between devices  17.6 us (2%)
  between operations  15.5 us (1%)
    pallas_call x2, Pallas kernels, gather_rows(): pl.pallas_call(functools.partial(gather_kernel, chips, downward, paired,...  246 us
    pallas_call x1, Pallas kernels, reduce_dense(): pl.pallas_call(functools.partial(dense_kernel, chips, count, len(grads),...  212 us
    pallas_call x2, Pallas kernels, scatter_rows(): pl.pallas_call(functools.partial(scatter_kernel, chips, upward, paired, p...  186 us
    all_gather x1, blocking collectives, body(): all_tables = lax.all_gather(table_pair, 'ctx', axis=0)  88.7 us
    pallas_call x1, Pallas kernels, gather_weights(): pl.pallas_call(functools.partial(weights_kernel, count, len(slabs), len(s...  66 us
    pallas_call x1, Pallas kernels, run_experts(): pl.pallas_call(functools.partial(expert_kernel, blocks), grid=(local,), o...  57.8 us
    pallas_call x2, Pallas kernels, spread_rows(): pl.pallas_call(spread_kernel, grid=(chips, sides), out_shape=jax.ShapeDty...  26.2 us
    another operation x4, other arithmetic, in_order(): return jnp.stack([first, second])  25.5 us
  transfers between devices with their start and end apart: 11, of which 1 were waited for; matrix products, arithmetic and copies ran while one was open for 14% of the time, Pallas kernels for 59%

profile of v3, /device:TPU:0, one launch (start us, length us, event | category | flops | bytes accessed | tf_op | source)
XLA Modules:
  0.0 1164.1 jit_solution(14939857554571201902)
XLA Ops:
  19.1 66.0 %gather_weights.1 = (bf16[4,384,2560]{2,1,0:T(8,128)(2,1)}, bf16[4,32,384]{2,1,0:T(8,128)(2,1)}, f32[2,16,256]{2,1,0:T(8,128)}, bf16[2,256,1536]{2,1,0:T(8,128)(2,1)}, s32[8,128]{1,0:T(8,128)}) custom-call(bf16[384,2560]{1,0:T(8,128)(2,1)} %pad_maximum_fusion.2.refs_0_, bf16[32,384]{1,0:T(8,128)(2,1)} %maximum_maximum_fusion.refs_1_, ...), custom_call_target="tpu_custom_call" | custom-call | bytes 2000000000 | tf_op jit(solution)/shard_map/gather_weights/pallas_call | solution.py:194
  86.3 5.6 convolution_convert_fusion.3.query_ref
  95.2 83.8 %gather_keys.1 = (bf16[4,1,2,256,1024]{4,3,2,1,0:T(8,128)(2,1)}, bf16[4,384,1536]{2,1,0:T(8,128)(2,1)}, bf16[4,384,2048]{2,1,0:T(8,128)(2,1)}, bf16[4,256,1536]{2,1,0:T(8,128)(2,1)}, s32[8,128]{1,0:T(8,128)}) custom-call(bf16[256,1024]{1,0:T(8,128)(2,1)} %slice.106.rows_ref, bf16[384,1536]{1,0:T(8,128)(2,1)} %refs_0_.1, ...), custom_call_target="tpu_custom_call" | custom-call | bytes 2000000000 | tf_op jit(solution)/shard_map/gather_keys/pallas_call | solution.py:354
  192.8 8.1 attend.1
  203.3 88.7 %all-gather = f32[16,16,256]{2,1,0:T(8,128)S(1)} all-gather(f32[2,16,256]{2,1,0:T(8,128)S(1)} %copy-done.25), channel_id=2, replica_groups=mesh['ctx'=8,'wt'=4] {'ctx'}, dimensions={0}, use_global_device_ids=true | all-gather | bytes 294912 | tf_op jit(solution)/shard_map/all_gather | solution.py:1158
  301.5 161.8 %gather_tokens.1 = (bf16[4,2,2,256,1536]{4,3,2,1,0:T(8,128)(2,1)}, bf16[4,2,384,512]{3,2,1,0:T(8,128)(2,1)}, bf16[4,512,384]{2,1,0:T(8,128)(2,1)}, s32[8,128]{1,0:T(8,128)}) custom-call(bf16[256,1536]{1,0:T(8,128)(2,1)} %multiply_convert_fusion.rows_ref, bf16[4,2,384,512]{3,2,1,0:T(8,128)(2,1)} %collective-permute-done.refs_0_.refs_1_, ...), custom_call_target="tpu_custom_call" | custom-call | bytes 2000000000 | tf_op jit(solution)/shard_map/gather_tokens/pallas_call | solution.py:354
  463.3 12.3 %pick_tokens.1.x_ref = bf16[4,2,4,80,1536]{4,3,2,1,0:T(8,128)(2,1)} custom-call(s32[4,2,4,512]{3,2,1,0:T(4,128)} %fusion.28.slot_ref, f32[4,2,4,512]{3,2,1,0:T(4,128)} %fusion.40.gate_ref, bf16[4,2,2,256,1536]{4,3,2,1,0:T(8,128)(2,1)} %get-tuple-element.63.rows_ref), custom_call_target="tpu_custom_call" | custom-call | bytes 4096 | tf_op jit(solution)/shard_map/pick_tokens/pallas_call | solution.py:925
  475.6 12.6 %pick_grads.1 = (bf16[4,2,4,80,1536]{4,3,2,1,0:T(8,128)(2,1)}, f32[4,2,4,80,128]{4,3,2,1,0:T(8,128)}) custom-call(s32[4,2,4,512]{3,2,1,0:T(4,128)} %fusion.28.slot_ref, f32[4,2,4,512]{3,2,1,0:T(4,128)} %fusion.40.gate_ref, bf16[4,2,2,256,1536]{4,3,2,1,0:T(8,128)(2,1)} %bitcast.179), custom_call_target="tpu_custom_call" | custom-call | bytes 4096 | tf_op jit(solution)/shard_map/pick_grads/pallas_call | solution.py:925
  488.2 57.8 %experts.1 = (bf16[4,2,4,80,1536]{4,3,2,1,0:T(8,128)(2,1)}, bf16[4,2,4,80,1536]{4,3,2,1,0:T(8,128)(2,1)}, bf16[4,4,2,384,512]{4,3,2,1,0:T(8,128)(2,1)}, bf16[4,4,512,384]{3,2,1,0:T(8,128)(2,1)}) custom-call(bf16[4,2,4,80,1536]{4,3,2,1,0:T(8,128)(2,1)} %pick_tokens.1.x_ref, bf16[4,2,4,80,1536]{4,3,2,1,0:T(8,128)(2,1)} %get-tuple-element.65.g_ref, ...), custom_call_target="tpu_custom_call" | custom-call | bytes 4096 | tf_op jit(solution)/shard_map/experts/pallas_call | solution.py:1034
  546.0 13.1 %spread_results.1 = bf16[4,2,2,256,1536]{4,3,2,1,0:T(8,128)(2,1)} custom-call(s32[4,2,4,512]{3,2,1,0:T(4,128)} %fusion.28.slot_ref, bf16[4,2,4,80,1536]{4,3,2,1,0:T(8,128)(2,1)} %get-tuple-element.73.rows_ref), custom_call_target="tpu_custom_call" | custom-call | bytes 4096 | tf_op jit(solution)/shard_map/spread_results/pallas_call | solution.py:956
  559.1 10.6 copy.73
  569.8 6.1 slice.88
  595.6 13.1 %spread_grads.1.partial_ref = bf16[4,2,2,256,1536]{4,3,2,1,0:T(8,128)(2,1)} custom-call(s32[4,2,4,512]{3,2,1,0:T(4,128)} %fusion.28.slot_ref, bf16[4,2,4,80,1536]{4,3,2,1,0:T(8,128)(2,1)} %get-tuple-element.74.rows_ref), custom_call_target="tpu_custom_call" | custom-call | bytes 4096 | tf_op jit(solution)/shard_map/spread_grads/pallas_call | solution.py:956
  608.7 122.3 %scatter_grads.1 = f32[256,1536]{1,0:T(8,128)} custom-call(bf16[4,2,2,256,1536]{4,3,2,1,0:T(8,128)(2,1)} %spread_grads.1.partial_ref), custom_call_target="tpu_custom_call" | custom-call | bytes 2000000000 | tf_op jit(solution)/shard_map/scatter_grads/pallas_call | solution.py:530
  741.5 10.2 attend_back.1
  751.6 64.2 %scatter_keys.1 = f32[256,1024]{1,0:T(8,128)} custom-call(bf16[4,1,2,256,1024]{4,3,2,1,0:T(8,128)(2,1)} %bitcast.184), custom_call_target="tpu_custom_call" | custom-call | bytes 2000000000 | tf_op jit(solution)/shard_map/scatter_keys/pallas_call | solution.py:530
  822.0 11.4 convert_add_fusion
  838.7 7.2 fusion.22
  845.9 6.7 convolution_convert_fusion
  856.9 211.9 %reduce_dense.1 = (bf16[384,2560]{1,0:T(8,128)(2,1)}, bf16[384,2048]{1,0:T(8,128)(2,1)}, bf16[384,1536]{1,0:T(8,128)(2,1)}, bf16[256,1536]{1,0:T(8,128)(2,1)}, bf16[32,384]{1,0:T(8,128)(2,1)}) custom-call(bf16[4,384,2560]{2,1,0:T(8,128)(2,1)} %bitcast.169, bf16[4,384,2048]{2,1,0:T(8,128)(2,1)} %bitcast.172, bf16[4,384,1536]{2,1,0:T(8,128)(2,1)} %bitcast.173, ...), custom_call_target="tpu_custom_call" | custom-call | bytes 2000000000 | tf_op jit(solution)/shard_map/reduce_dense/pallas_call | solution.py:717
  1093.9 17.5 %collective-permute-done.8 = bf16[4,512,384]{2,1,0:T(8,128)(2,1)} collective-permute-done((bf16[4,512,384]{2,1,0:T(8,128)(2,1)}, bf16[4,512,384]{2,1,0:T(8,128)(2,1)}, u32[]{:S(2)}, u32[]{:S(2)}) %collective-permute-start.8) | collective-permute-done | bytes 1572896 | tf_op jit(solution)/shard_map/ppermute | solution.py:1053
  1119.0 8.6 fusion
  1131.2 11.2 pad_maximum_fusion
  1142.4 11.6 slice_bitcast_fusion
  (173 shorter events, 126.3 us)
Async XLA Ops:
  7.2 468.5 %all-gather.4.cloned.1.call-start = ((), (), s32[]{:S(2)}) async-start(), calls=%async_computation.2 | async-start | bytes 14155776 | tf_op jit(solution)/shard_map/all_gather | solution.py:1159
  19.1 67.0 %copy-start.4 = (bf16[1,256,1536]{2,1,0:T(8,128)(2,1)S(1)}, bf16[1,256,1536]{2,1,0:T(8,128)(2,1)}, u32[]{:S(2)}) copy-start(bf16[1,256,1536]{2,1,0:T(8,128)(2,1)} %param.17) | copy-start | bytes 2359300
  85.1 1042.5 %reduce-scatter.2.cloned.1.call-start = ((), (), s32[]{:S(2)}) async-start(), calls=%async_computation.1 | async-start | bytes 14155776 | tf_op jit(solution)/shard_map/reduce_scatter | solution.py:1253
  86.3 7.6 copy-start.21
  86.3 7.6 copy-start.22
  185.2 110.8 %collective-permute-start = (bf16[4,2,384,512]{3,2,1,0:T(8,128)(2,1)}, bf16[4,2,384,512]{3,2,1,0:T(8,128)(2,1)}, u32[]{:S(2)}, u32[]{:S(2)}) collective-permute-start(bf16[4,2,384,512]{3,2,1,0:T(8,128)(2,1)} %get-tuple-element.104), channel_id=1, source_target_pairs={{0,1},{1,0},{2,3},{3,2},{4,5},{5,4},{6,7},{7,6},{8,9},{9,8},{10,11... | collective-permute-start | bytes 9437192 | tf_op jit(solution)/shard_map/ppermute | solution.py:1053
  186.7 109.3 %collective-permute-start.1 = (bf16[4,2,384,512]{3,2,1,0:T(8,128)(2,1)S(1)}, bf16[4,2,384,512]{3,2,1,0:T(8,128)(2,1)}, u32[]{:S(2)}, u32[]{:S(2)}) collective-permute-start(bf16[4,2,384,512]{3,2,1,0:T(8,128)(2,1)S(1)} %get-tuple-element.67.refs_0_), channel_id=1, source_target_pairs={{0,2},{1,3},{2,0},{3,1},{4,6},{5,7},{6,4},{7,5},{8,10},{9,11},{10,... | collective-permute-start | bytes 9437192 | tf_op jit(solution)/shard_map/ppermute | solution.py:1053
  189.3 106.7 %collective-permute-start.2 = (bf16[4,512,384]{2,1,0:T(8,128)(2,1)}, bf16[4,512,384]{2,1,0:T(8,128)(2,1)}, u32[]{:S(2)}, u32[]{:S(2)}) collective-permute-start(bf16[4,512,384]{2,1,0:T(8,128)(2,1)} %get-tuple-element.108), channel_id=1, source_target_pairs={{0,1},{1,0},{2,3},{3,2},{4,5},{5,4},{6,7},{7,6},{8,9},{9,8},{10,11... | collective-permute-start | bytes 4718600 | tf_op jit(solution)/shard_map/ppermute | solution.py:1053
  190.7 105.3 %collective-permute-start.3 = (bf16[4,512,384]{2,1,0:T(8,128)(2,1)}, bf16[4,512,384]{2,1,0:T(8,128)(2,1)}, u32[]{:S(2)}, u32[]{:S(2)}) collective-permute-start(bf16[4,512,384]{2,1,0:T(8,128)(2,1)} %get-tuple-element.70.refs_4_), channel_id=1, source_target_pairs={{0,2},{1,3},{2,0},{3,1},{4,6},{5,7},{6,4},{7,5},{8,10},{9,11},{10,... | collective-permute-start | bytes 4718600 | tf_op jit(solution)/shard_map/ppermute | solution.py:1053
  300.3 436.1 %copy-start.1 = (f32[256,1536]{1,0:T(8,128)}, f32[256,1536]{1,0:T(8,128)S(1)}, u32[]{:S(2)}) copy-start(f32[256,1536]{1,0:T(8,128)S(1)} %get-tuple-element.120) | copy-start | bytes 4718596
  569.7 7.2 copy-start.24
  569.8 9.1 copy-start.7
  575.9 246.1 %collective-permute-start.5 = (bf16[2,4,2,384,512]{4,3,2,1,0:T(8,128)(2,1)}, bf16[2,4,2,384,512]{4,3,2,1,0:T(8,128)(2,1)}, u32[]{:S(2)}, u32[]{:S(2)}) collective-permute-start(bf16[2,4,2,384,512]{4,3,2,1,0:T(8,128)(2,1)} %slice.88), channel_id=1, source_target_pairs={{0,2},{1,3},{2,0},{3,1},{4,6},{5,7},{6,4},{7,5},{8,10},{9,11},{10,... | collective-permute-start | bytes 18874376 | tf_op jit(solution)/shard_map/ppermute | solution.py:1053
  587.4 234.6 %collective-permute-start.6 = (bf16[2,4,512,384]{3,2,1,0:T(8,128)(2,1)}, bf16[2,4,512,384]{3,2,1,0:T(8,128)(2,1)}, u32[]{:S(2)}, u32[]{:S(2)}) collective-permute-start(bf16[2,4,512,384]{3,2,1,0:T(8,128)(2,1)} %slice.89), channel_id=1, source_target_pairs={{0,2},{1,3},{2,0},{3,1},{4,6},{5,7},{6,4},{7,5},{8,10},{9,11},{10,... | collective-permute-start | bytes 9437192 | tf_op jit(solution)/shard_map/ppermute | solution.py:1053
  838.3 278.8 %collective-permute-start.7 = (bf16[4,2,384,512]{3,2,1,0:T(8,128)(2,1)}, bf16[4,2,384,512]{3,2,1,0:T(8,128)(2,1)}, u32[]{:S(2)}, u32[]{:S(2)}) collective-permute-start(bf16[4,2,384,512]{3,2,1,0:T(8,128)(2,1)} %fusion.4), channel_id=1, source_target_pairs={{0,1},{1,0},{2,3},{3,2},{4,5},{5,4},{6,7},{7,6},{8,9},{9,8},{10,11... | collective-permute-start | bytes 9437192 | tf_op jit(solution)/shard_map/ppermute | solution.py:1053
  856.1 217.0 %copy-start = (f32[2,4,512,384]{3,2,1,0:T(8,128)}, f32[2,4,512,384]{3,2,1,0:T(8,128)S(1)}, u32[]{:S(2)}) copy-start(f32[2,4,512,384]{3,2,1,0:T(8,128)S(1)} %convert_add_fusion.1) | copy-start | bytes 18874372
  1074.4 37.0 %collective-permute-start.8 = (bf16[4,512,384]{2,1,0:T(8,128)(2,1)}, bf16[4,512,384]{2,1,0:T(8,128)(2,1)}, u32[]{:S(2)}, u32[]{:S(2)}) collective-permute-start(bf16[4,512,384]{2,1,0:T(8,128)(2,1)} %fusion.25), channel_id=1, source_target_pairs={{0,1},{1,0},{2,3},{3,2},{4,5},{5,4},{6,7},{7,6},{8,9},{9,8},{10,11... | collective-permute-start | bytes 4718600 | tf_op jit(solution)/shard_map/ppermute | solution.py:1053
  1083.7 8.5 copy-start.19
  1088.2 23.1 %slice-start.3 = ((s8[6291456]{0:T(1024)(128)(4,1)}), s8[4194304]{0:T(1024)(128)(4,1)S(1)}, s32[]{:S(2)}) async-start(s8[6291456]{0:T(1024)(128)(4,1)} %bitcast.175), calls=%async_computation.6 | async-start | bytes 8388608
  1090.2 21.2 %slice-start.4 = ((s8[6291456]{0:T(1024)(128)(4,1)}), s8[2097152]{0:T(1024)(128)(4,1)S(1)}, s32[]{:S(2)}) async-start(s8[6291456]{0:T(1024)(128)(4,1)} %bitcast.175), calls=%async_computation.7 | async-start | bytes 4194304
  1129.7 24.4 %collective-permute-start.4 = (bf16[256,1536]{1,0:T(8,128)(2,1)}, bf16[256,1536]{1,0:T(8,128)(2,1)S(1)}, u32[]{:S(2)}, u32[]{:S(2)}) collective-permute-start(bf16[256,1536]{1,0:T(8,128)(2,1)} %dynamic-slice_bitcast_fusion.2), channel_id=1, source_target_pairs={{0,1},{1,0},{2,3},{3,2},{4,5},{5,4},{6,7},{7,6},{8,9},{9,8},{10,11... | collective-permute-start | bytes 2359304 | tf_op jit(solution)/shard_map/ppermute | solution.py:1053
  1142.4 11.6 copy-start.2
  1142.4 11.6 copy-start.15
  1142.4 11.6 copy-start.18
  (23 other events, 89.5 us)
Sparse Core Ops, SparseCore 0:
  85.2 122.5 all-gather.3
  569.9 177.1 reduce-scatter.1

commit v4 on v3

--- a/solution.py
+++ b/solution.py
@@ -546,7 +546,7 @@
         compiler_params=pltpu.CompilerParams(
             collective_id=collective_id, has_side_effects=True, vmem_limit_bytes=WIDE
         ),
-        cost_estimate=LONG,
+        cost_estimate=LONG if paired else CHEAP,
         name=name,
     )(partial)
 
@@ -884,7 +884,7 @@
 
 def pick_kernel(scaled, slot_ref, gate_ref, rows_ref, out_ref, scale_ref=None):
     local, depth = out_ref.shape[2], out_ref.shape[3]
-    tokens = rows_ref.shape[3]
+    tokens = slot_ref.shape[3] // 2
     place = lax.broadcasted_iota(jnp.int32, (depth, tokens), 0)
     total, weight = None, None
     for core in range(2):
@@ -934,7 +934,7 @@
     )(slots, gates, rows)
 
 
-def spread_kernel(slot_ref, rows_ref, out_ref):
+def spread_kernel(apart, slot_ref, rows_ref, out_ref):
     local, depth, width = rows_ref.shape[2:]
     tokens = out_ref.shape[3]
     place = lax.broadcasted_iota(jnp.int32, (depth, tokens), 0)
@@ -944,24 +944,29 @@
         ones = jnp.concatenate(
             [(slot_ref[0, 0, e : e + 1, span] == place).astype(jnp.float32) for e in range(local)], axis=0
         ).astype(jnp.bfloat16)
-        out_ref[0, 0, core] = lax.dot_general(
+        spot = out_ref.at[0, core, 0] if apart else out_ref.at[0, 0, core]
+        spot[...] = lax.dot_general(
             ones, rows, (((0,), (0,)), ((), ())), preferred_element_type=jnp.float32
         ).astype(jnp.bfloat16)
 
 
-def spread_rows(rows, slots, name):
+def spread_rows(rows, slots, name, apart):
     chips, sides, local, both = slots.shape
     depth, width = rows.shape[3:]
     tokens = both // 2
     return pl.pallas_call(
-        spread_kernel,
+        functools.partial(spread_kernel, apart),
         grid=(chips, sides),
-        out_shape=jax.ShapeDtypeStruct((chips, sides, 2, tokens, width), jnp.bfloat16),
+        out_shape=jax.ShapeDtypeStruct(
+            (chips, 2, sides, tokens, width) if apart else (chips, sides, 2, tokens, width), jnp.bfloat16
+        ),
         in_specs=[
             pl.BlockSpec((1, 1, local, both), lambda z, s: (z, s, 0, 0)),
             pl.BlockSpec((1, 1, local, depth, width), lambda z, s: (z, s, 0, 0, 0)),
         ],
-        out_specs=pl.BlockSpec((1, 1, 2, tokens, width), lambda z, s: (z, s, 0, 0, 0)),
+        out_specs=pl.BlockSpec((1, 2, 1, tokens, width), lambda z, s: (z, 0, s, 0, 0))
+        if apart
+        else pl.BlockSpec((1, 1, 2, tokens, width), lambda z, s: (z, s, 0, 0, 0)),
         compiler_params=pltpu.CompilerParams(vmem_limit_bytes=WIDE),
         cost_estimate=CHEAP,
         name=name,
@@ -970,7 +975,10 @@
 
 def expert_kernel(blocks, x_ref, g_ref, scale_ref, *refs):
     tall_refs, down_refs = refs[:blocks], refs[blocks : 2 * blocks]
-    result_ref, back_ref, grad_tall_ref, grad_down_ref = refs[2 * blocks :]
+    result_ref, back_ref, *grad_refs = refs[2 * blocks :]
+    hops = len(grad_refs) // 3
+    grad_gate_refs, grad_up_refs = grad_refs[:hops], grad_refs[hops : 2 * hops]
+    grad_down_refs = grad_refs[2 * hops :]
     w = lax.axis_index("wt")
     chips, sides, _, depth, width = x_ref.shape
     rows = chips * sides * depth
@@ -1008,10 +1016,10 @@
         columns(result_ref, q)[...] = result.astype(jnp.bfloat16).reshape(chips, sides, depth, part)
         back = dot(grad_gate, tall_refs[q][0, 0], nt) + dot(grad_up, tall_refs[q][0, 1], nt)
         columns(back_ref, q)[...] = back.astype(jnp.bfloat16).reshape(chips, sides, depth, part)
-        grad_down_ref[q, 0] = dot(inner, piece(g_ref, q), tn).astype(jnp.bfloat16)
+        grad_down_refs[q // 2][q % 2, 0] = dot(inner, piece(g_ref, q), tn).astype(jnp.bfloat16)
         x = piece(x_ref, q)
-        grad_tall_ref[q, 0, 0] = dot(x, grad_gate, tn).astype(jnp.bfloat16)
-        grad_tall_ref[q, 0, 1] = dot(x, grad_up, tn).astype(jnp.bfloat16)
+        grad_gate_refs[q // 2][q % 2, 0] = dot(x, grad_gate, tn).astype(jnp.bfloat16)
+        grad_up_refs[q // 2][q % 2, 0] = dot(x, grad_up, tn).astype(jnp.bfloat16)
 
 
 def run_experts(x, g, scale, talls, downs):
@@ -1028,26 +1036,65 @@
     scales = pl.BlockSpec((chips, sides, 1, depth, 128), lambda e: (0, 0, e, 0, 0))
     tall = pl.BlockSpec((1, 2, part, inner), lambda e: (e, 0, 0, 0))
     flat = pl.BlockSpec((1, inner, part), lambda e: (e, 0, 0))
-    tall_out = pl.BlockSpec((blocks, 1, 2, part, inner), lambda e: (0, e, 0, 0, 0))
-    flat_out = pl.BlockSpec((blocks, 1, inner, part), lambda e: (0, e, 0, 0))
-    total = chips * sides * local * depth
+    hops, each = max(blocks // 2, 1), min(blocks, 2)
+    tall_out = pl.BlockSpec((each, 1, part, inner), lambda e: (0, e, 0, 0))
+    flat_out = pl.BlockSpec((each, 1, inner, part), lambda e: (0, e, 0, 0))
     return pl.pallas_call(
         functools.partial(expert_kernel, blocks),
         grid=(local,),
         out_shape=(
             jax.ShapeDtypeStruct(x.shape, jnp.bfloat16),
             jax.ShapeDtypeStruct(x.shape, jnp.bfloat16),
-            jax.ShapeDtypeStruct((blocks, local, 2, part, inner), jnp.bfloat16),
-            jax.ShapeDtypeStruct((blocks, local, inner, part), jnp.bfloat16),
+            *[jax.ShapeDtypeStruct((each, local, part, inner), jnp.bfloat16)] * (2 * hops),
+            *[jax.ShapeDtypeStruct((each, local, inner, part), jnp.bfloat16)] * hops,
         ),
         in_specs=[sources, sources, scales] + [tall] * blocks + [flat] * blocks,
-        out_specs=(rows, rows, tall_out, flat_out),
+        out_specs=(rows, rows) + (tall_out,) * (2 * hops) + (flat_out,) * hops,
         compiler_params=pltpu.CompilerParams(vmem_limit_bytes=60 * 2**20),
         cost_estimate=CHEAP,
         name="experts",
     )(x, g, scale, *talls, *downs)
 
 
+def place_kernel(arrivals, side_ref, *refs):
+    own, other, more, outs = refs[:3], refs[3:6], refs[6 : 6 + 3 * arrivals], refs[6 + 3 * arrivals :]
+    mine = pl.program_id(0) == side_ref[0]
+
+    @pl.when(mine)
+    def _():
+        for i in range(3):
+            value = own[i][0, 0].astype(jnp.float32)
+            for m in more[i * arrivals : (i + 1) * arrivals]:
+                value = value + m[0, 0].astype(jnp.float32)
+            outs[i][0] = value
+
+    @pl.when(jnp.logical_not(mine))
+    def _():
+        for i in range(3):
+            outs[i][0] = other[i][0].astype(jnp.float32)
+
+
+def place_experts(side, own, more, other):
+    local = other[0].shape[0]
+    arrivals = len(more[0])
+    shapes = [o.shape[1:] for o in other]
+    paired = [pl.BlockSpec((1, 1) + s, lambda h, e: (0, e, 0, 0)) for s in shapes]
+    single = [pl.BlockSpec((1,) + s, lambda h, e: (e, 0, 0)) for s in shapes]
+    return pl.pallas_call(
+        functools.partial(place_kernel, arrivals),
+        grid=(2, local),
+        out_shape=[jax.ShapeDtypeStruct((2 * local,) + s, jnp.float32) for s in shapes],
+        in_specs=[pl.BlockSpec(memory_space=pltpu.SMEM)]
+        + paired
+        + single
+        + [p for p in paired for _ in range(arrivals)],
+        out_specs=[pl.BlockSpec((1,) + s, lambda h, e: (h * local + e, 0, 0)) for s in shapes],
+        compiler_params=pltpu.CompilerParams(vmem_limit_bytes=WIDE),
+        cost_estimate=CHEAP,
+        name="place_experts",
+    )(side, *own, *other, *[m for group in more for m in group])
+
+
 def swap_pairs(value, axis, distance):
     count = lax.axis_size(axis)
     return lax.ppermute(value, axis, [(i, i ^ distance) for i in range(count)])
@@ -1058,12 +1105,6 @@
         lax.dynamic_index_in_dim(stacked, mine, 0, keepdims=False),
         lax.dynamic_index_in_dim(stacked, 1 - mine, 0, keepdims=False),
     )
-
-
-def in_order(own, other, mine):
-    first = jnp.where(mine == 0, own, other)
-    second = jnp.where(mine == 0, other, own)
-    return jnp.stack([first, second])
 
 
 def collect_expert(shard, side, pairs):
@@ -1091,15 +1132,6 @@
             for q in range(count)
         ]
     )
-
-
-def scatter_expert(grads, arrived, side):
-    total = grads[:2].astype(jnp.float32)
-    for more in arrived:
-        total = total + more.astype(jnp.float32)
-    other = swap_pairs(total[1].astype(jnp.bfloat16), "wt", 1).astype(jnp.float32)
-    both = in_order(total[0], other, side)
-    return both.reshape((-1,) + both.shape[2:])
 
 
 def body(
@@ -1129,37 +1161,36 @@
     tokens, width_model = hidden.shape[1:]
     wide, kv_width = w_query.shape[1], w_key.shape[1]
     shared_width = shared_gate.shape[1]
-    tables = jnp.concatenate(
-        [
-            jnp.swapaxes(routes[0], 0, 1).astype(jnp.float32),
-            jnp.zeros((8 - TOPK, tokens), jnp.float32),
-            jnp.swapaxes(gates[0], 0, 1),
-            jnp.zeros((8 - TOPK, tokens), jnp.float32),
-        ],
-        axis=0,
+    gates_here = gates[0]
+    gate_high = gates_here.astype(jnp.bfloat16)
+    gate_rest = gates_here - gate_high.astype(jnp.float32)
+    gate_middle = gate_rest.astype(jnp.bfloat16)
+    gate_low = (gate_rest - gate_middle.astype(jnp.float32)).astype(jnp.bfloat16)
+    table = jnp.concatenate(
+        [routes[0].astype(jnp.bfloat16), gate_high, gate_middle, gate_low], axis=1
     )
     grad_rows = cotangent[0]
-    key_parts = jnp.stack(
-        [w_key.reshape(-1, KV_HEADS, HEAD_DIM), w_value.reshape(-1, KV_HEADS, HEAD_DIM)], axis=2
-    ).reshape(-1, 2 * kv_width)
-    slab, gains, table_pair, grad_pair, zero = gather_weights(
-        (
-            jnp.concatenate([w_query, key_parts], axis=1),
-            jnp.concatenate(
-                [
-                    norm_one_gain[None],
-                    norm_two_gain[None],
-                    jnp.zeros((30, norm_one_gain.shape[0]), jnp.bfloat16),
-                ]
-            ),
-        ),
-        (tables, grad_rows),
-    )
-    all_tables = lax.all_gather(table_pair, "ctx", axis=0)
-    all_grads = lax.all_gather(grad_pair, "ctx", axis=0).reshape(chips, 2, 2, tokens, width_model)
+    depth = norm_one_gain.shape[0]
+    extra_rows = 16
+    table_rows = extra_rows * width_model // tokens
+    packed = jnp.pad(jnp.swapaxes(table, 0, 1), ((0, table_rows - 4 * TOPK), (0, 0)))
+    extended = jnp.concatenate([grad_rows, packed.reshape(extra_rows, width_model)], axis=0)
+    gain_pair = jnp.concatenate(
+        [norm_one_gain[None], norm_two_gain[None], jnp.zeros((30, depth), jnp.bfloat16)]
+    )
+    query_weight, key_weight, value_weight, gains, grad_pair, zero = gather_weights(
+        (w_query, w_key, w_value, gain_pair), (extended,)
+    )
+    query_weight = query_weight.reshape(-1, wide)
+    key_weight = key_weight.reshape(-1, kv_width)
+    value_weight = value_weight.reshape(-1, kv_width)
     zero = zero[0, 0]
     side = lax.rem(wt_index, 2)
-    slab = slab.reshape(-1, slab.shape[2])
+    later = side + zero
+    collected = [
+        collect_expert(jnp.stack([expert_gate, expert_up], axis=1), later, pairs),
+        collect_expert(expert_down, later, pairs),
+    ]
     gain_one, gain_two = gains[:, 0].reshape(-1), gains[:, 1].reshape(-1)
     local = expert_gate.shape[0] // 2
     first_expert = (lax.axis_index("ctx") * 2 + side) * local
@@ -1171,9 +1202,20 @@
     scale_one = inverse_rms(inputs)
     gain_one_full = gain_one.astype(jnp.float32)
     normed = (inputs * scale_one * gain_one_full).astype(jnp.bfloat16)
-    projected = jnp.dot(normed, slab, preferred_element_type=jnp.float32).astype(jnp.bfloat16)
+
+    def project(weight):
+        return jnp.dot(normed, weight, preferred_element_type=jnp.float32).astype(jnp.bfloat16)
+
+    queries = project(query_weight)
+    fresh = jnp.stack(
+        [
+            project(key_weight).reshape(tokens, KV_HEADS, HEAD_DIM),
+            project(value_weight).reshape(tokens, KV_HEADS, HEAD_DIM),
+        ],
+        axis=2,
+    ).reshape(tokens, 2 * kv_width)
     both, out_weight, both_weight, down_weight, zero = gather_rows(
-        projected[:, wide:],
+        fresh,
         2,
         False,
         False,
@@ -1184,20 +1226,23 @@
     both_weight = both_weight.reshape(-1, both_weight.shape[2])
     down_weight = down_weight.reshape(-1, down_weight.shape[2])
     both = both.reshape(-1, 2 * kv_width)
-    later = side + zero
-    collected = [
-        collect_expert(jnp.stack([expert_gate, expert_up], axis=1), later, pairs),
-        collect_expert(expert_down, later, pairs),
-    ]
-
-    table_shape = (chips, 2, 2, 16, tokens)
-    ordered_tables = jnp.transpose(all_tables.reshape(table_shape), (0, 2, 3, 1, 4)).reshape(
-        chips, 2, 16, 2 * tokens
+
+    grad_pair = lax.dynamic_index_in_dim(jnp.stack([grad_pair, grad_pair]), zero, 0, False)
+    all_grads = lax.all_gather(grad_pair, "ctx", axis=0).reshape(
+        chips, 2, 2, tokens + extra_rows, width_model
+    )
+    tables = all_grads[:, :, :, tokens:].reshape(chips, 2, 2, table_rows, tokens)[:, :, :, : 4 * TOPK]
+    tables = jnp.transpose(tables.astype(jnp.float32), (0, 2, 3, 1, 4)).reshape(
+        chips, 2, 4 * TOPK, 2 * tokens
+    )
+    table_routes, gate_parts = tables[:, :, :TOPK], tables[:, :, TOPK:]
+    table_gates = (
+        gate_parts[:, :, :TOPK] + gate_parts[:, :, TOPK : 2 * TOPK] + gate_parts[:, :, 2 * TOPK :]
     )
     experts_here = (first_expert + jnp.arange(local, dtype=jnp.int32)).astype(jnp.float32)
-    named = ordered_tables[:, :, None, :TOPK] == experts_here[None, None, :, None, None]
+    named = table_routes[:, :, None] == experts_here[None, None, :, None, None]
     member = jnp.any(named, axis=3)
-    slot_gates = jnp.sum(jnp.where(named, ordered_tables[:, :, None, 8 : 8 + TOPK], 0.0), axis=3)
+    slot_gates = jnp.sum(jnp.where(named, table_gates[:, :, None], 0.0), axis=3)
     earlier = (
         jnp.arange(2 * tokens)[:, None] < jnp.arange(2 * tokens)[None, :]
     ).astype(jnp.bfloat16)
@@ -1206,7 +1251,7 @@
 
     place = lax.axis_index("ctx").astype(jnp.int32).reshape(1)
     seg_row, seg_column = seg_all[None, :], seg_all[:, None]
-    attended_full, logs = attend(place, projected, both, seg_row, query_seg[:, None])
+    attended_full, logs = attend(place, queries, both, seg_row, query_seg[:, None])
     attended = attended_full.astype(jnp.bfloat16)
     attended, collected = lax.optimization_barrier((attended, collected))
     middle = inputs + jnp.dot(attended, out_weight, preferred_element_type=jnp.float32)
@@ -1229,41 +1274,41 @@
     (received_rows,) = pick_rows(all_rows, slots, slot_gates, False)
     grad_received, row_gates = pick_rows(all_grads, slots, slot_gates, True)
     if down_blocks[0].shape[2] % 128:
-        results, backs, grads_tall, grads_down = run_experts(
+        results, backs, grads_gate, grads_up, grads_down = run_experts(
             received_rows,
             grad_received,
             row_gates,
             [settle_blocks(tall_blocks, wt_index, 2)],
             [settle_blocks(down_blocks, wt_index, 2)],
         )
-        grads_tall = split_blocks(grads_tall[0], wt_index, wt_count, 2)
-        grads_down = split_blocks(grads_down[0], wt_index, wt_count, 2)
+        wholes = [
+            split_blocks(grads_gate[0], wt_index, wt_count, 1),
+            split_blocks(grads_up[0], wt_index, wt_count, 1),
+            split_blocks(grads_down[0], wt_index, wt_count, 2),
+        ]
+        hop_grads = [[g[2 * d : 2 * d + 2] for d in range(pairs)] for g in wholes]
     else:
-        results, backs, grads_tall, grads_down = run_experts(
+        results, backs, *rest = run_experts(
             received_rows, grad_received, row_gates, tall_blocks, down_blocks
         )
-    expert_grads = (grads_tall, grads_down)
-    arrived = [
-        [swap_pairs(g[2 * d : 2 * d + 2], "wt", 2 * d) for d in range(1, pairs)] for g in expert_grads
-    ]
+        hop_grads = [rest[i * pairs : (i + 1) * pairs] for i in range(3)]
+    arrived = [[swap_pairs(g[d], "wt", 2 * d) for d in range(1, pairs)] for g in hop_grads]
+    first_arrived, later_arrived = arrived[:1], arrived[1:]
     routed_grad = scatter_rows(
-        spread_rows(backs, slots, "spread_grads"), 5, True, True, "scatter_grads"
-    )
-    spread = spread_rows(results, slots, "spread_results")
+        spread_rows(backs, slots, "spread_grads", False), 5, True, True, "scatter_grads"
+    )
+    routed_grad, results, first_arrived = lax.optimization_barrier(
+        (routed_grad, results, first_arrived)
+    )
+    spread = spread_rows(results, slots, "spread_results", True)
     partial = lax.psum_scatter(
-        jnp.swapaxes(spread, 1, 2).reshape(ctx_count, 2, tokens, width_model),
-        "ctx",
-        scatter_dimension=0,
-        tiled=True,
+        spread.reshape(ctx_count, 2, tokens, width_model), "ctx", scatter_dimension=0, tiled=True
     )[0]
-    kept, given = own_and_other(partial, side)
-    routed = kept.astype(jnp.float32) + swap_pairs(given, "wt", 1).astype(jnp.float32)
 
     shared_parts = jnp.dot(normed_two, both_weight, preferred_element_type=jnp.float32)
     shared_gate_part, shared_up_part = shared_parts[:, :shared_width], shared_parts[:, shared_width:]
     shared_inner = (jax.nn.silu(shared_gate_part) * shared_up_part).astype(jnp.bfloat16)
     shared_result = jnp.dot(shared_inner, down_weight, preferred_element_type=jnp.float32)
-    output = (middle + shared_result + routed).astype(jnp.bfloat16)
     grad_out = grad_rows.astype(jnp.float32)
     grad_shared_down = jnp.einsum(
         "tf,td->fd", shared_inner, grad_rows, preferred_element_type=jnp.float32
@@ -1298,7 +1343,7 @@
         "td,qd->tq", grad_branch, out_weight, preferred_element_type=jnp.float32
     ).astype(jnp.bfloat16)
     grad_queries, grad_parts = attend_back(
-        place, projected, both, query_seg[None, :], seg_column, attended_full, grad_attended, logs
+        place, queries, both, query_seg[None, :], seg_column, attended_full, grad_attended, logs
     )
     grad_both = scatter_rows(
         grad_parts.reshape(chips, 1, 2, tokens, 2 * kv_width),
@@ -1307,15 +1352,32 @@
         False,
         "scatter_keys",
     ).astype(jnp.bfloat16)
-    grad_both, arrived = lax.optimization_barrier((grad_both, arrived))
-    sum_tall, sum_experts_down = [
-        scatter_expert(g, a, side) for g, a in zip(expert_grads, arrived)
-    ]
-    sum_experts_gate, sum_experts_up = sum_tall[:, 0], sum_tall[:, 1]
-    grad_projected = jnp.concatenate([grad_queries, grad_both], axis=1)
-    grad_slab = jnp.einsum("tc,tq->cq", normed, grad_projected, preferred_element_type=jnp.float32)
-    grad_normed = jnp.einsum(
-        "tq,cq->tc", grad_projected, slab, preferred_element_type=jnp.float32
+    grad_both, later_arrived = lax.optimization_barrier((grad_both, later_arrived))
+    arrived = first_arrived + later_arrived
+
+    def crossed(own, more):
+        total = own[1].astype(jnp.float32)
+        for m in more:
+            total = total + m[1].astype(jnp.float32)
+        return swap_pairs(total.astype(jnp.bfloat16), "wt", 1)
+
+    others = [crossed(g[0], a) for g, a in zip(hop_grads, arrived)]
+    grad_both = grad_both.reshape(tokens, KV_HEADS, 2, HEAD_DIM)
+    grad_keys = grad_both[:, :, 0].reshape(tokens, kv_width)
+    grad_values = grad_both[:, :, 1].reshape(tokens, kv_width)
+
+    def weight_grad(grad):
+        return jnp.einsum("tc,tq->cq", normed, grad, preferred_element_type=jnp.float32).astype(
+            jnp.bfloat16
+        )
+
+    def input_grad(grad, weight):
+        return jnp.einsum("tq,cq->tc", grad, weight, preferred_element_type=jnp.float32)
+
+    grad_normed = (
+        input_grad(grad_queries, query_weight)
+        + input_grad(grad_keys, key_weight)
+        + input_grad(grad_values, value_weight)
     )
     grad_gain_one = jnp.sum(grad_normed * inputs * scale_one, axis=0)
     scaled_one = grad_normed * gain_one_full
@@ -1325,27 +1387,32 @@
         - inputs * scale_one**3 * jnp.mean(scaled_one * inputs, axis=-1, keepdims=True)
     )
 
-    depth = norm_one_gain.shape[0]
     gain_grads = jnp.stack([grad_gain_one, grad_gain_two]).reshape(2, wt_count, 1, depth)
     gain_grads = jnp.pad(gain_grads.astype(jnp.bfloat16), ((0, 0), (0, 0), (0, 15), (0, 0)))
     gain_grads = jnp.swapaxes(gain_grads, 0, 1).reshape(wt_count * 32, depth)
-    final_slab, final_shared, final_out, final_down, final_gains = [
-        total.astype(jnp.float32)
-        for total in reduce_dense(
-            [
-                grad_slab.astype(jnp.bfloat16),
-                grad_shared_both.astype(jnp.bfloat16),
-                grad_out_weight.astype(jnp.bfloat16),
-                grad_shared_down.astype(jnp.bfloat16),
-                gain_grads,
-            ]
-        )
+    dense_grads = [
+        weight_grad(grad_queries),
+        grad_shared_both.astype(jnp.bfloat16),
+        grad_out_weight.astype(jnp.bfloat16),
+        grad_shared_down.astype(jnp.bfloat16),
+        weight_grad(grad_keys),
+        weight_grad(grad_values),
+        gain_grads,
+    ]
+    dense_grads, partial = lax.optimization_barrier((dense_grads, partial))
+    kept, given = own_and_other(partial, side)
+    crossing = swap_pairs(given, "wt", 1)
+    totals = reduce_dense(dense_grads)
+    totals, others, crossing = lax.optimization_barrier((totals, others, crossing))
+    routed = kept.astype(jnp.float32) + crossing.astype(jnp.float32)
+    output = (middle + shared_result + routed).astype(jnp.bfloat16)
+    sum_experts_gate, sum_experts_up, sum_experts_down = place_experts(
+        side.astype(jnp.int32).reshape(1), [g[0] for g in hop_grads], arrived, others
+    )
+    final_query, final_shared, final_out, final_down, final_key, final_value, final_gains = [
+        total.astype(jnp.float32) for total in totals
     ]
     final_gate, final_up = final_shared[:, :shared_width], final_shared[:, shared_width:]
-    final_query = final_slab[:, :wide]
-    final_parts = final_slab[:, wide:].reshape(-1, KV_HEADS, 2, HEAD_DIM)
-    final_key = final_parts[:, :, 0].reshape(-1, kv_width)
-    final_value = final_parts[:, :, 1].reshape(-1, kv_width)
     final_gain_one, final_gain_two = final_gains[0], final_gains[16]
     return (
         output[None],

time: 1170 us -> 1090 us (0.932)
  waiting for transfers between devices: 17.6 us -> 114 us
  blocking collectives: 88.7 us -> 0 us
  local copies, waits for them, and re-layouts: 77.2 us -> 29.1 us
  other arithmetic: 64 us -> 41.7 us
  Pallas kernels: 837 us -> 821 us
    ppermute x9 -> x11, waiting for transfers between devices: 17.5 us -> 112 us  [swap_pairs(): return lax.ppermute(value, axis, [(i, i ^ distance) for i in range(count)])]
    all_gather x1 -> x0, blocking collectives: 88.7 us -> none  [body(): all_tables = lax.all_gather(table_pair, 'ctx', axis=0)]
    pallas_call x2, Pallas kernels: 246 us -> 188 us  [gather_rows(): pl.pallas_call(functools.partial(gather_kernel, chips, downward, paired,...]
    pallas_call x1, Pallas kernels: 212 us -> 254 us  [reduce_dense(): pl.pallas_call(functools.partial(dense_kernel, chips, count, len(grads),...]
    another operation x5 -> x2, other arithmetic: 27.3 us -> 2.97 us  [the longest x1 1.78 us: body(): jnp.stack([grad_pair, grad_pair])]
    pallas_call x2, Pallas kernels: 186 us -> 164 us  [scatter_rows(): pl.pallas_call(functools.partial(scatter_kernel, chips, upward, paired, p...]
    pallas_call x2 -> x3, Pallas kernels: 26.2 us -> 44.4 us  [the longest x2 27 us: spread_rows(): pl.pallas_call(functools.partial(spread_kernel, apart), grid=(chips, side...]
    add x2 -> x1, other arithmetic: 14.8 us -> 0.04 us  [body(): gate_parts[:, :, :TOPK] + gate_parts[:, :, TOPK:2 * TOPK]]
  transfers between devices with their start and end apart: 11 -> 13, of which waited for: 1 -> 4; matrix products, arithmetic and copies ran while one was open for 14% -> 7% of each run, Pallas kernels for 59% -> 51%
where the time goes in v4:
time: 1090 us
  Pallas kernels  821 us (75%)
  waiting for transfers between devices  114 us (10%)
  matrix products  51 us (5%)
  other arithmetic  41.7 us (4%)
  local copies, waits for them, and re-layouts  29.1 us (3%)
  between operations  17.7 us (2%)
  starting transfers between devices  13.2 us (1%)
    pallas_call x1, Pallas kernels, reduce_dense(): pl.pallas_call(functools.partial(dense_kernel, chips, count, len(grads),...  254 us
    pallas_call x2, Pallas kernels, gather_rows(): pl.pallas_call(functools.partial(gather_kernel, chips, downward, paired,...  188 us
    pallas_call x2, Pallas kernels, scatter_rows(): pl.pallas_call(functools.partial(scatter_kernel, chips, upward, paired, p...  164 us
    ppermute x11, waiting for transfers between devices, swap_pairs(): return lax.ppermute(value, axis, [(i, i ^ distance) for i in range(count)])  112 us
    pallas_call x1, Pallas kernels, gather_weights(): pl.pallas_call(functools.partial(weights_kernel, count, len(slabs), len(s...  67 us
    pallas_call x1, Pallas kernels, run_experts(): pl.pallas_call(functools.partial(expert_kernel, blocks), grid=(local,), o...  58.2 us
    pallas_call x2, Pallas kernels, spread_rows(): pl.pallas_call(functools.partial(spread_kernel, apart), grid=(chips, side...  27 us
    pallas_call x2, Pallas kernels, pick_rows(): pl.pallas_call(functools.partial(pick_kernel, scaled), grid=(chips, sides...  24.9 us
  transfers between devices with their start and end apart: 13, of which 4 were waited for; matrix products, arithmetic and copies ran while one was open for 7% of the time, Pallas kernels for 51%

profile of v4, /device:TPU:0, one launch (start us, length us, event | category | flops | bytes accessed | tf_op | source)
XLA Modules:
  0.0 1087.8 jit_solution(1501031147954943335)
XLA Ops:
  13.6 67.0 %gather_weights.1 = (bf16[4,384,1536]{2,1,0:T(8,128)(2,1)}, bf16[4,384,512]{2,1,0:T(8,128)(2,1)}, bf16[4,384,512]{2,1,0:T(8,128)(2,1)}, bf16[4,32,384]{2,1,0:T(8...) custom-call(bf16[384,1536]{1,0:T(8,128)(2,1)} %refs_0_.2, bf16[384,512]{1,0:T(8,128)(2,1)} %refs_1_.1, ...), custom_call_target="tpu_custom_call" | custom-call | bytes 2000000000 | tf_op jit(solution)/shard_map/gather_weights/pallas_call | solution.py:194
  89.7 83.8 %gather_keys.1 = (bf16[4,1,2,256,1024]{4,3,2,1,0:T(8,128)(2,1)}, bf16[4,384,1536]{2,1,0:T(8,128)(2,1)}, bf16[4,384,2048]{2,1,0:T(8,128)(2,1)}, bf16[4,256,1536]{2,1,0:T(8,128)(2,1)}, s32[8,128]{1,0:T(8,128)}) custom-call(bf16[256,1024]{1,0:T(8,128)(2,1)} %reshape.306.rows_ref, bf16[384,1536]{1,0:T(8,128)(2,1)} %refs_0_.3, ...), custom_call_target="tpu_custom_call" | custom-call | bytes 2000000000 | tf_op jit(solution)/shard_map/gather_keys/pallas_call | solution.py:354
  180.6 5.5 fusion.1
  193.8 4.8 convolution_convert_fusion.7.query_ref
  198.6 8.1 attend.1
  208.1 82.4 %collective-permute-done.3.refs_6_ = bf16[4,512,384]{2,1,0:T(8,128)(2,1)} collective-permute-done((bf16[4,512,384]{2,1,0:T(8,128)(2,1)}, bf16[4,512,384]{2,1,0:T(8,128)(2,1)}, u32[]{:S(2)}, u32[]{:S(2)}) %collective-permute-start.3) | collective-permute-done | bytes 1572896 | tf_op jit(solution)/shard_map/ppermute | solution.py:1100
  292.7 3.8 multiply_reduce_fusion.2
  297.8 104.6 %gather_tokens.1 = (bf16[4,2,2,256,1536]{4,3,2,1,0:T(8,128)(2,1)}, bf16[4,2,384,512]{3,2,1,0:T(8,128)(2,1)}, bf16[4,512,384]{2,1,0:T(8,128)(2,1)}, s32[8,128]{1,0:T(8,128)}) custom-call(bf16[256,1536]{1,0:T(8,128)(2,1)} %multiply_convert_fusion.rows_ref, bf16[4,2,384,512]{3,2,1,0:T(8,128)(2,1)} %collective-permute-done.refs_0_.refs_1_, ...), custom_call_target="tpu_custom_call" | custom-call | bytes 2000000000 | tf_op jit(solution)/shard_map/gather_tokens/pallas_call | solution.py:354
  408.7 12.5 %pick_grads.1 = (bf16[4,2,4,80,1536]{4,3,2,1,0:T(8,128)(2,1)}, f32[4,2,4,80,128]{4,3,2,1,0:T(8,128)}) custom-call(s32[4,2,4,512]{3,2,1,0:T(4,128)} %fusion.26.slot_ref, f32[4,2,4,512]{3,2,1,0:T(4,128)} %fusion.36.gate_ref, bf16[4,2,2,272,1536]{4,3,2,1,0:T(8,128)(2,1)} %bitcast.172), custom_call_target="tpu_custom_call" | custom-call | bytes 4096 | tf_op jit(solution)/shard_map/pick_grads/pallas_call | solution.py:925
  421.2 12.4 %pick_tokens.1.x_ref = bf16[4,2,4,80,1536]{4,3,2,1,0:T(8,128)(2,1)} custom-call(s32[4,2,4,512]{3,2,1,0:T(4,128)} %fusion.26.slot_ref, f32[4,2,4,512]{3,2,1,0:T(4,128)} %fusion.36.gate_ref, bf16[4,2,2,256,1536]{4,3,2,1,0:T(8,128)(2,1)} %get-tuple-element.99.rows_ref), custom_call_target="tpu_custom_call" | custom-call | bytes 4096 | tf_op jit(solution)/shard_map/pick_tokens/pallas_call | solution.py:925
  433.6 58.2 %experts.1 = (bf16[4,2,4,80,1536]{4,3,2,1,0:T(8,128)(2,1)}, bf16[4,2,4,80,1536]{4,3,2,1,0:T(8,128)(2,1)}, bf16[2,4,384,512]{3,2,1,0:T(8,128)(2,1)}, bf16[2,4,384...) custom-call(bf16[4,2,4,80,1536]{4,3,2,1,0:T(8,128)(2,1)} %pick_token, ...), custom_call_target="tpu_custom_call" | custom-call | bytes 4096 | tf_op jit(solution)/shard_map/experts/pallas_call | solution.py:1042
  493.2 13.1 %spread_grads.1.partial_ref = bf16[4,2,2,256,1536]{4,3,2,1,0:T(8,128)(2,1)} custom-call(s32[4,2,4,512]{3,2,1,0:T(4,128)} %fusion.26.slot_ref, bf16[4,2,4,80,1536]{4,3,2,1,0:T(8,128)(2,1)} %get-tuple-element.108.rows_ref), custom_call_target="tpu_custom_call" | custom-call | bytes 4096 | tf_op jit(solution)/shard_map/spread_grads/pallas_call | solution.py:957
  506.4 84.6 %scatter_grads.1 = f32[256,1536]{1,0:T(8,128)} custom-call(bf16[4,2,2,256,1536]{4,3,2,1,0:T(8,128)(2,1)} %spread_grads.1.partial_ref), custom_call_target="tpu_custom_call" | custom-call | bytes 2000000000 | tf_op jit(solution)/shard_map/scatter_grads/pallas_call | solution.py:530
  590.9 13.9 %spread_results.1 = bf16[4,2,2,256,1536]{4,3,2,1,0:T(8,128)(2,1)} custom-call(s32[4,2,4,512]{3,2,1,0:T(4,128)} %fusion.26.slot_ref, bf16[4,2,4,80,1536]{4,3,2,1,0:T(8,128)(2,1)} %get-tuple-element.118.rows_ref), custom_call_target="tpu_custom_call" | custom-call | bytes 4096 | tf_op jit(solution)/shard_map/spread_results/pallas_call | solution.py:957
  607.4 4.7 fusion.56
  618.4 4.6 convolution_convert_fusion
  629.6 11.3 %attend_back.1 = (bf16[256,1536]{1,0:T(8,128)(2,1)}, bf16[2048,1024]{1,0:T(8,128)(2,1)}) custom-call(s32[1]{0:T(128)} %bitcast.1.place_ref, bf16[256,1536]{1,0:T(8,128)(2,1)} %convolution_convert_fusion.7.query_ref, bf16[2048,1024]{1,0:T(8,128)(2,1)} %bitcast.170, s32[1,256]{1,0:T(1,128)} %constant_dynamic-slice_fusion.row_ref, s32[2048,1]{1,0:T(8,128)} %copy.80.column_ref, ...), custom_call_target="tpu_custom_call" | custom-call | bytes 4096 | tf_op jit(solution)/shard_map/attend_back/pallas_call | solution.py:860
  640.9 79.6 %scatter_keys.1 = f32[256,1024]{1,0:T(8,128)} custom-call(bf16[4,1,2,256,1024]{4,3,2,1,0:T(8,128)(2,1)} %bitcast.176), custom_call_target="tpu_custom_call" | custom-call | bytes 4096 | tf_op jit(solution)/shard_map/scatter_keys/pallas_call | solution.py:530
  721.8 28.7 %collective-permute-done.6.refs_8_ = bf16[2,4,512,384]{3,2,1,0:T(8,128)(2,1)} collective-permute-done((bf16[2,4,512,384]{3,2,1,0:T(8,128)(2,1)}, bf16[2,4,512,384]{3,2,1,0:T(8,128)(2,1)}, u32[]{:S(2)}, u32[]{:S(2)}) %collective-permute-start.6) | collective-permute-done | bytes 3145760 | tf_op jit(solution)/shard_map/ppermute | solution.py:1100
  768.7 3.9 fusion.57
  776.0 3.7 convolution_convert_fusion.2
  782.3 3.6 convolution_convert_fusion.1
  795.0 254.3 %reduce_dense.1 = (bf16[384,1536]{1,0:T(8,128)(2,1)}, bf16[384,2048]{1,0:T(8,128)(2,1)}, bf16[384,1536]{1,0:T(8,128)(2,1)}, bf16[256,1536]{1,0:T(8,128)(2,1)}, b...) custom-call(bf16[4,384,1536]{2,1,0:T(8,128)(2,1)} %bitcast.167, ...), custom_call_target="tpu_custom_call" | custom-call | bytes 2000000000 | tf_op jit(solution)/shard_map/reduce_dense/pallas_call | solution.py:717
  1060.2 17.4 %place_experts.1 = (f32[8,384,512]{2,1,0:T(8,128)}, f32[8,384,512]{2,1,0:T(8,128)}, f32[8,512,384]{2,1,0:T(8,128)}) custom-call(s32[1]{0:T(128)} %bitcast.53.side_ref, bf16[2,4,384,512]{3,2,1,0:T(8,128)(2,1)} %get-tuple-element.134.refs_0_, bf16[2,4,384,512]{3,2,1,0:T(8,128)(2,1)} %get-tuple-element.136.refs_1_, ...), custom_call_target="tpu_custom_call" | custom-call | bytes 4096 | tf_op jit(solution)/shard_map/place_experts/pallas_call | solution.py:1083
  (179 shorter events, 103.8 us)
Async XLA Ops:
  7.2 395.2 %all-gather.2.cloned.1.call-start = ((), (), s32[]{:S(2)}) async-start(), calls=%async_computation.1 | async-start | bytes 15040512 | tf_op jit(solution)/shard_map/all_gather | solution.py:1231
  12.9 68.6 %copy-start = (bf16[1,256,1536]{2,1,0:T(8,128)(2,1)S(1)}, bf16[1,256,1536]{2,1,0:T(8,128)(2,1)}, u32[]{:S(2)}) copy-start(bf16[1,256,1536]{2,1,0:T(8,128)(2,1)} %param.17) | copy-start | bytes 2359300
  89.7 87.0 %copy-start.18 = (bf16[2,272,1536]{2,1,0:T(8,128)(2,1)S(1)}, bf16[2,272,1536]{2,1,0:T(8,128)(2,1)}, u32[]{:S(2)}) copy-start(bf16[2,272,1536]{2,1,0:T(8,128)(2,1)} %get-tuple-element.95) | copy-start | bytes 5013508
  178.5 609.6 %reduce-scatter.2.cloned.1.call-start = ((), (), s32[]{:S(2)}) async-start(), calls=%async_computation.2 | async-start | bytes 14155776 | tf_op jit(solution)/shard_map/reduce_scatter | solution.py:1304
  180.6 7.4 copy-start.16
  186.1 105.5 %collective-permute-start.1 = (bf16[4,2,384,512]{3,2,1,0:T(8,128)(2,1)}, bf16[4,2,384,512]{3,2,1,0:T(8,128)(2,1)}, u32[]{:S(2)}, u32[]{:S(2)}) collective-permute-start(bf16[4,2,384,512]{3,2,1,0:T(8,128)(2,1)} %get-tuple-element.102.refs_0_), channel_id=1, source_target_pairs={{0,2},{1,3},{2,0},{3,1},{4,6},{5,7},{6,4},{7,5},{8,10},{9,11},{10,... | collective-permute-start | bytes 9437192 | tf_op jit(solution)/shard_map/ppermute | solution.py:1100
  187.6 104.0 %collective-permute-start = (bf16[4,2,384,512]{3,2,1,0:T(8,128)(2,1)}, bf16[4,2,384,512]{3,2,1,0:T(8,128)(2,1)}, u32[]{:S(2)}, u32[]{:S(2)}) collective-permute-start(bf16[4,2,384,512]{3,2,1,0:T(8,128)(2,1)} %get-tuple-element.162), channel_id=1, source_target_pairs={{0,1},{1,0},{2,3},{3,2},{4,5},{5,4},{6,7},{7,6},{8,9},{9,8},{10,11... | collective-permute-start | bytes 9437192 | tf_op jit(solution)/shard_map/ppermute | solution.py:1100
  190.0 100.5 %collective-permute-start.3 = (bf16[4,512,384]{2,1,0:T(8,128)(2,1)}, bf16[4,512,384]{2,1,0:T(8,128)(2,1)}, u32[]{:S(2)}, u32[]{:S(2)}) collective-permute-start(bf16[4,512,384]{2,1,0:T(8,128)(2,1)} %get-tuple-element.105.refs_4_), channel_id=1, source_target_pairs={{0,2},{1,3},{2,0},{3,1},{4,6},{5,7},{6,4},{7,5},{8,10},{9,11},{10,... | collective-permute-start | bytes 4718600 | tf_op jit(solution)/shard_map/ppermute | solution.py:1100
  191.5 100.1 %collective-permute-start.2 = (bf16[4,512,384]{2,1,0:T(8,128)(2,1)}, bf16[4,512,384]{2,1,0:T(8,128)(2,1)S(1)}, u32[]{:S(2)}, u32[]{:S(2)}) collective-permute-start(bf16[4,512,384]{2,1,0:T(8,128)(2,1)} %get-tuple-element.166), channel_id=1, source_target_pairs={{0,1},{1,0},{2,3},{3,2},{4,5},{5,4},{6,7},{7,6},{8,9},{9,8},{10,11... | collective-permute-start | bytes 4718600 | tf_op jit(solution)/shard_map/ppermute | solution.py:1100
  208.1 88.4 %copy-start.12 = (bf16[256,1536]{1,0:T(8,128)(2,1)}, bf16[256,1536]{1,0:T(8,128)(2,1)S(1)}, u32[]{:S(2)}) copy-start(bf16[256,1536]{1,0:T(8,128)(2,1)S(1)} %convert_element_type.238) | copy-start | bytes 2359300
  296.5 326.5 %copy-start.1 = (f32[256,1536]{1,0:T(8,128)}, f32[256,1536]{1,0:T(8,128)S(1)}, u32[]{:S(2)}) copy-start(f32[256,1536]{1,0:T(8,128)S(1)} %get-tuple-element.182) | copy-start | bytes 4718596
  491.8 99.2 %collective-permute-start.4 = (bf16[2,4,384,512]{3,2,1,0:T(8,128)(2,1)}, bf16[2,4,384,512]{3,2,1,0:T(8,128)(2,1)S(1)}, u32[]{:S(2)}, u32[]{:S(2)}) collective-permute-start(bf16[2,4,384,512]{3,2,1,0:T(8,128)(2,1)} %get-tuple-element.110), channel_id=1, source_target_pairs={{0,2},{1,3},{2,0},{3,1},{4,6},{5,7},{6,4},{7,5},{8,10},{9,11},{10,... | collective-permute-start | bytes 9437192 | tf_op jit(solution)/shard_map/ppermute | solution.py:1100
  590.9 13.9 %copy-start.7 = (bf16[2,4,384,512]{3,2,1,0:T(8,128)(2,1)}, bf16[2,4,384,512]{3,2,1,0:T(8,128)(2,1)S(1)}, u32[]{:S(2)}) copy-start(bf16[2,4,384,512]{3,2,1,0:T(8,128)(2,1)S(1)} %collective-permute-done.4.refs_6_) | copy-start | bytes 9437188
  612.2 109.7 %collective-permute-start.5 = (bf16[2,4,384,512]{3,2,1,0:T(8,128)(2,1)}, bf16[2,4,384,512]{3,2,1,0:T(8,128)(2,1)}, u32[]{:S(2)}, u32[]{:S(2)}) collective-permute-start(bf16[2,4,384,512]{3,2,1,0:T(8,128)(2,1)} %get-tuple-element.115), channel_id=1, source_target_pairs={{0,2},{1,3},{2,0},{3,1},{4,6},{5,7},{6,4},{7,5},{8,10},{9,11},{10,... | collective-permute-start | bytes 9437192 | tf_op jit(solution)/shard_map/ppermute | solution.py:1100
  613.7 136.9 %collective-permute-start.6 = (bf16[2,4,512,384]{3,2,1,0:T(8,128)(2,1)}, bf16[2,4,512,384]{3,2,1,0:T(8,128)(2,1)}, u32[]{:S(2)}, u32[]{:S(2)}) collective-permute-start(bf16[2,4,512,384]{3,2,1,0:T(8,128)(2,1)} %get-tuple-element.116), channel_id=1, source_target_pairs={{0,2},{1,3},{2,0},{3,1},{4,6},{5,7},{6,4},{7,5},{8,10},{9,11},{10,... | collective-permute-start | bytes 9437192 | tf_op jit(solution)/shard_map/ppermute | solution.py:1100
  618.4 8.8 slice-start.2
  640.9 109.7 %copy-start.6 = (bf16[2,4,512,384]{3,2,1,0:T(8,128)(2,1)S(1)}, bf16[2,4,512,384]{3,2,1,0:T(8,128)(2,1)}, u32[]{:S(2)}) copy-start(bf16[2,4,512,384]{3,2,1,0:T(8,128)(2,1)} %get-tuple-element.138.refs_2_) | copy-start | bytes 9437188
  750.5 8.3 copy-start.8
  753.7 295.6 %collective-permute-start.9 = (bf16[4,512,384]{2,1,0:T(8,128)(2,1)}, bf16[4,512,384]{2,1,0:T(8,128)(2,1)}, u32[]{:S(2)}, u32[]{:S(2)}) collective-permute-start(bf16[4,512,384]{2,1,0:T(8,128)(2,1)} %fusion.23), channel_id=1, source_target_pairs={{0,1},{1,0},{2,3},{3,2},{4,5},{5,4},{6,7},{7,6},{8,9},{9,8},{10,11... | collective-permute-start | bytes 4718600 | tf_op jit(solution)/shard_map/ppermute | solution.py:1100
  758.4 290.9 %collective-permute-start.8 = (bf16[4,384,512]{2,1,0:T(8,128)(2,1)}, bf16[4,384,512]{2,1,0:T(8,128)(2,1)}, u32[]{:S(2)}, u32[]{:S(2)}) collective-permute-start(bf16[4,384,512]{2,1,0:T(8,128)(2,1)} %fusion.22), channel_id=1, source_target_pairs={{0,1},{1,0},{2,3},{3,2},{4,5},{5,4},{6,7},{7,6},{8,9},{9,8},{10,11... | collective-permute-start | bytes 4718600 | tf_op jit(solution)/shard_map/ppermute | solution.py:1100
  760.5 288.9 %collective-permute-start.7 = (bf16[4,384,512]{2,1,0:T(8,128)(2,1)}, bf16[4,384,512]{2,1,0:T(8,128)(2,1)}, u32[]{:S(2)}, u32[]{:S(2)}) collective-permute-start(bf16[4,384,512]{2,1,0:T(8,128)(2,1)} %fusion.21), channel_id=1, source_target_pairs={{0,1},{1,0},{2,3},{3,2},{4,5},{5,4},{6,7},{7,6},{8,9},{9,8},{10,11... | collective-permute-start | bytes 4718600 | tf_op jit(solution)/shard_map/ppermute | solution.py:1100
  790.2 259.2 %collective-permute-start.10 = (bf16[256,1536]{1,0:T(8,128)(2,1)}, bf16[256,1536]{1,0:T(8,128)(2,1)}, u32[]{:S(2)}, u32[]{:S(2)}) collective-permute-start(bf16[256,1536]{1,0:T(8,128)(2,1)} %dynamic-slice_bitcast_fusion.2), channel_id=1, source_target_pairs={{0,1},{1,0},{2,3},{3,2},{4,5},{5,4},{6,7},{7,6},{8,9},{9,8},{10,11... | collective-permute-start | bytes 2359304 | tf_op jit(solution)/shard_map/ppermute | solution.py:1100
  1060.2 17.4 %copy-start.11 = (f32[256,1536]{1,0:T(8,128)S(1)}, f32[256,1536]{1,0:T(8,128)}, u32[]{:S(2)}) copy-start(f32[256,1536]{1,0:T(8,128)} %get-tuple-element.184) | copy-start | bytes 4718596
  1060.2 17.4 %copy-start.20 = (bf16[1,2,256,1536]{3,2,1,0:T(8,128)(2,1)S(1)}, bf16[1,2,256,1536]{3,2,1,0:T(8,128)(2,1)}, u32[]{:S(2)}) copy-start(bf16[1,2,256,1536]{3,2,1,0:T(8,128)(2,1)} %reduce-scatter.2.cloned.1.call-done) | copy-start | bytes 4718596
  (25 other events, 82.9 us)
Sparse Core Ops, SparseCore 0:
  178.6 122.1 all-gather.1
  605.0 183.0 reduce-scatter.1

commit v5 on v4

--- a/solution.py
+++ b/solution.py
@@ -1253,12 +1253,40 @@
     seg_row, seg_column = seg_all[None, :], seg_all[:, None]
     attended_full, logs = attend(place, queries, both, seg_row, query_seg[:, None])
     attended = attended_full.astype(jnp.bfloat16)
-    attended, collected = lax.optimization_barrier((attended, collected))
     middle = inputs + jnp.dot(attended, out_weight, preferred_element_type=jnp.float32)
     scale_two = inverse_rms(middle)
     gain_two_full = gain_two.astype(jnp.float32)
     normed_two = (middle * scale_two * gain_two_full).astype(jnp.bfloat16)
 
+    shared_parts = jnp.dot(normed_two, both_weight, preferred_element_type=jnp.float32)
+    shared_gate_part, shared_up_part = shared_parts[:, :shared_width], shared_parts[:, shared_width:]
+    shared_inner = (jax.nn.silu(shared_gate_part) * shared_up_part).astype(jnp.bfloat16)
+    shared_result = jnp.dot(shared_inner, down_weight, preferred_element_type=jnp.float32)
+    grad_out = grad_rows.astype(jnp.float32)
+    grad_shared_down = jnp.einsum(
+        "tf,td->fd", shared_inner, grad_rows, preferred_element_type=jnp.float32
+    )
+    grad_shared_inner = jnp.einsum(
+        "td,fd->tf", grad_rows, down_weight, preferred_element_type=jnp.float32
+    )
+    grad_shared_gate_part = (
+        grad_shared_inner * shared_up_part * silu_slope(shared_gate_part)
+    ).astype(jnp.bfloat16)
+    grad_shared_up_part = (grad_shared_inner * jax.nn.silu(shared_gate_part)).astype(jnp.bfloat16)
+    grad_shared_parts = jnp.concatenate([grad_shared_gate_part, grad_shared_up_part], axis=1)
+    grad_shared_both = jnp.einsum(
+        "td,tf->df", normed_two, grad_shared_parts, preferred_element_type=jnp.float32
+    )
+    grad_shared_rows = jnp.einsum(
+        "tf,df->td", grad_shared_parts, both_weight, preferred_element_type=jnp.float32
+    )
+    grad_shared_both = grad_shared_both.astype(jnp.bfloat16)
+    grad_shared_down = grad_shared_down.astype(jnp.bfloat16)
+    normed_two, collected, shared_result, grad_shared_both, grad_shared_down, grad_shared_rows = (
+        lax.optimization_barrier(
+            (normed_two, collected, shared_result, grad_shared_both, grad_shared_down, grad_shared_rows)
+        )
+    )
     all_rows, *landed, zero = gather_rows(
         normed_two, 3, True, True, "gather_tokens", (), [c[1] for c in collected]
     )
@@ -1297,37 +1325,16 @@
     routed_grad = scatter_rows(
         spread_rows(backs, slots, "spread_grads", False), 5, True, True, "scatter_grads"
     )
-    routed_grad, results, first_arrived = lax.optimization_barrier(
-        (routed_grad, results, first_arrived)
-    )
-    spread = spread_rows(results, slots, "spread_results", True)
-    partial = lax.psum_scatter(
-        spread.reshape(ctx_count, 2, tokens, width_model), "ctx", scatter_dimension=0, tiled=True
-    )[0]
-
-    shared_parts = jnp.dot(normed_two, both_weight, preferred_element_type=jnp.float32)
-    shared_gate_part, shared_up_part = shared_parts[:, :shared_width], shared_parts[:, shared_width:]
-    shared_inner = (jax.nn.silu(shared_gate_part) * shared_up_part).astype(jnp.bfloat16)
-    shared_result = jnp.dot(shared_inner, down_weight, preferred_element_type=jnp.float32)
-    grad_out = grad_rows.astype(jnp.float32)
-    grad_shared_down = jnp.einsum(
-        "tf,td->fd", shared_inner, grad_rows, preferred_element_type=jnp.float32
-    )
-    grad_shared_inner = jnp.einsum(
-        "td,fd->tf", grad_rows, down_weight, preferred_element_type=jnp.float32
-    )
-    grad_shared_gate_part = (
-        grad_shared_inner * shared_up_part * silu_slope(shared_gate_part)
-    ).astype(jnp.bfloat16)
-    grad_shared_up_part = (grad_shared_inner * jax.nn.silu(shared_gate_part)).astype(jnp.bfloat16)
-    grad_shared_parts = jnp.concatenate([grad_shared_gate_part, grad_shared_up_part], axis=1)
-    grad_shared_both = jnp.einsum(
-        "td,tf->df", normed_two, grad_shared_parts, preferred_element_type=jnp.float32
-    )
-    grad_normed_two = (
-        jnp.einsum("tf,df->td", grad_shared_parts, both_weight, preferred_element_type=jnp.float32)
-        + routed_grad
-    )
+    routed_grad, first_arrived = lax.optimization_barrier((routed_grad, first_arrived))
+
+    def crossed(own, more):
+        total = own[1].astype(jnp.float32)
+        for m in more:
+            total = total + m[1].astype(jnp.float32)
+        return swap_pairs(total.astype(jnp.bfloat16), "wt", 1)
+
+    gate_other = crossed(hop_grads[0][0], first_arrived[0])
+    grad_normed_two = grad_shared_rows + routed_grad
     grad_gain_two = jnp.sum(grad_normed_two * middle * scale_two, axis=0)
     scaled_two = grad_normed_two * gain_two_full
     grad_middle = (
@@ -1342,6 +1349,8 @@
     grad_attended = jnp.einsum(
         "td,qd->tq", grad_branch, out_weight, preferred_element_type=jnp.float32
     ).astype(jnp.bfloat16)
+    grad_attended, up_arrived = lax.optimization_barrier((grad_attended, later_arrived[0]))
+    up_other = crossed(hop_grads[1][0], up_arrived)
     grad_queries, grad_parts = attend_back(
         place, queries, both, query_seg[None, :], seg_column, attended_full, grad_attended, logs
     )
@@ -1352,16 +1361,17 @@
         False,
         "scatter_keys",
     ).astype(jnp.bfloat16)
-    grad_both, later_arrived = lax.optimization_barrier((grad_both, later_arrived))
-    arrived = first_arrived + later_arrived
-
-    def crossed(own, more):
-        total = own[1].astype(jnp.float32)
-        for m in more:
-            total = total + m[1].astype(jnp.float32)
-        return swap_pairs(total.astype(jnp.bfloat16), "wt", 1)
-
-    others = [crossed(g[0], a) for g, a in zip(hop_grads, arrived)]
+    grad_both, down_arrived, gate_other, up_other, results = lax.optimization_barrier(
+        (grad_both, later_arrived[1], gate_other, up_other, results)
+    )
+    arrived = [first_arrived[0], up_arrived, down_arrived]
+    down_other = crossed(hop_grads[2][0], down_arrived)
+    partial = lax.psum_scatter(
+        spread_rows(results, slots, "spread_results", True).reshape(ctx_count, 2, tokens, width_model),
+        "ctx",
+        scatter_dimension=0,
+        tiled=True,
+    )[0]
     grad_both = grad_both.reshape(tokens, KV_HEADS, 2, HEAD_DIM)
     grad_keys = grad_both[:, :, 0].reshape(tokens, kv_width)
     grad_values = grad_both[:, :, 1].reshape(tokens, kv_width)
@@ -1392,18 +1402,18 @@
     gain_grads = jnp.swapaxes(gain_grads, 0, 1).reshape(wt_count * 32, depth)
     dense_grads = [
         weight_grad(grad_queries),
-        grad_shared_both.astype(jnp.bfloat16),
+        grad_shared_both,
         grad_out_weight.astype(jnp.bfloat16),
-        grad_shared_down.astype(jnp.bfloat16),
+        grad_shared_down,
         weight_grad(grad_keys),
         weight_grad(grad_values),
         gain_grads,
     ]
-    dense_grads, partial = lax.optimization_barrier((dense_grads, partial))
+    totals = reduce_dense(dense_grads)
+    totals, down_other, partial = lax.optimization_barrier((totals, down_other, partial))
+    others = [gate_other, up_other, down_other]
     kept, given = own_and_other(partial, side)
     crossing = swap_pairs(given, "wt", 1)
-    totals = reduce_dense(dense_grads)
-    totals, others, crossing = lax.optimization_barrier((totals, others, crossing))
     routed = kept.astype(jnp.float32) + crossing.astype(jnp.float32)
     output = (middle + shared_result + routed).astype(jnp.bfloat16)
     sum_experts_gate, sum_experts_up, sum_experts_down = place_experts(

time: 1090 us -> 997 us (0.915)
  Pallas kernels: 821 us -> 731 us
  waiting for transfers between devices: 114 us -> 99.2 us
    pallas_call x1, Pallas kernels: 254 us -> 202 us  [reduce_dense(): pl.pallas_call(functools.partial(dense_kernel, chips, count, len(grads),...]
    pallas_call x2, Pallas kernels: 164 us -> 129 us  [scatter_rows(): pl.pallas_call(functools.partial(scatter_kernel, chips, upward, paired, p...]
    ppermute x11, waiting for transfers between devices: 112 us -> 99.1 us  [swap_pairs(): return lax.ppermute(value, axis, [(i, i ^ distance) for i in range(count)])]
  transfers between devices with their start and end apart: 13 -> 13, of which waited for: 4 -> 5; matrix products, arithmetic and copies ran while one was open for 7% -> 9% of each run, Pallas kernels for 51% -> 49%
where the time goes in v5:
time: 997 us; the launch traced here: 990 us
  Pallas kernels  731 us (73%)
  waiting for transfers between devices  99.2 us (10%)
  matrix products  53.2 us (5%)
  other arithmetic  44.9 us (5%)
  local copies, waits for them, and re-layouts  31.7 us (3%)
  between operations  17.6 us (2%)
  starting transfers between devices  12.1 us (1%)
    pallas_call x1, Pallas kernels, reduce_dense(): pl.pallas_call(functools.partial(dense_kernel, chips, count, len(grads),...  202 us
    pallas_call x2, Pallas kernels, gather_rows(): pl.pallas_call(functools.partial(gather_kernel, chips, downward, paired,...  188 us
    pallas_call x2, Pallas kernels, scatter_rows(): pl.pallas_call(functools.partial(scatter_kernel, chips, upward, paired, p...  129 us
    ppermute x11, waiting for transfers between devices, swap_pairs(): return lax.ppermute(value, axis, [(i, i ^ distance) for i in range(count)])  99.1 us
    pallas_call x1, Pallas kernels, gather_weights(): pl.pallas_call(functools.partial(weights_kernel, count, len(slabs), len(s...  67 us
    pallas_call x1, Pallas kernels, run_experts(): pl.pallas_call(functools.partial(expert_kernel, blocks), grid=(local,), o...  58.1 us
    pallas_call x2, Pallas kernels, spread_rows(): pl.pallas_call(functools.partial(spread_kernel, apart), grid=(chips, side...  26.5 us
    pallas_call x2, Pallas kernels, pick_rows(): pl.pallas_call(functools.partial(pick_kernel, scaled), grid=(chips, sides...  24.9 us
  transfers between devices with their start and end apart: 13, of which 5 were waited for; matrix products, arithmetic and copies ran while one was open for 9% of the time, Pallas kernels for 49%

profile of v5, /device:TPU:0, one launch (start us, length us, event | category | flops | bytes accessed | tf_op | source)
XLA Modules:
  0.0 990.0 jit_solution(16898482402467226747)
XLA Ops:
  13.6 67.0 %gather_weights.1 = (bf16[4,384,1536]{2,1,0:T(8,128)(2,1)}, bf16[4,384,512]{2,1,0:T(8,128)(2,1)}, bf16[4,384,512]{2,1,0:T(8,128)(2,1)}, bf16[4,32,384]{2,1,0:T(8...) custom-call(bf16[384,1536]{1,0:T(8,128)(2,1)} %refs_0_.2, bf16[384,512]{1,0:T(8,128)(2,1)} %refs_1_.1, ...), custom_call_target="tpu_custom_call" | custom-call | bytes 2000000000 | tf_op jit(solution)/shard_map/gather_weights/pallas_call | solution.py:194
  91.5 83.8 %gather_keys.1 = (bf16[4,1,2,256,1024]{4,3,2,1,0:T(8,128)(2,1)}, bf16[4,384,1536]{2,1,0:T(8,128)(2,1)}, bf16[4,384,2048]{2,1,0:T(8,128)(2,1)}, bf16[4,256,1536]{2,1,0:T(8,128)(2,1)}, s32[8,128]{1,0:T(8,128)}) custom-call(bf16[256,1024]{1,0:T(8,128)(2,1)} %reshape.300.rows_ref, bf16[384,1536]{1,0:T(8,128)(2,1)} %refs_0_.3, ...), custom_call_target="tpu_custom_call" | custom-call | bytes 2000000000 | tf_op jit(solution)/shard_map/gather_keys/pallas_call | solution.py:354
  183.7 4.0 dynamic-slice_bitcast_fusion
  189.2 3.7 fusion.1
  197.3 4.9 convolution_convert_fusion.7.query_ref
  202.2 8.0 attend.1
  223.3 4.5 convolution_convert_fusion
  231.4 60.8 %collective-permute-done.1.refs_2_ = bf16[4,2,384,512]{3,2,1,0:T(8,128)(2,1)} collective-permute-done((bf16[4,2,384,512]{3,2,1,0:T(8,128)(2,1)}, bf16[4,2,384,512]{3,2,1,0:T(8,128)(2,1)}, u32[]{:S(2)}, u32[]{:S(2)}) %collective-permute-start.1) | collective-permute-done | bytes 3145760 | tf_op jit(solution)/shard_map/ppermute | solution.py:1100
  292.1 5.9 collective-permute-done.refs_0_.refs_1_
  298.0 104.6 %gather_tokens.1 = (bf16[4,2,2,256,1536]{4,3,2,1,0:T(8,128)(2,1)}, bf16[4,2,384,512]{3,2,1,0:T(8,128)(2,1)}, bf16[4,512,384]{2,1,0:T(8,128)(2,1)}, s32[8,128]{1,0:T(8,128)}) custom-call(bf16[256,1536]{1,0:T(8,128)(2,1)} %copy-done.6, bf16[4,2,384,512]{3,2,1,0:T(8,128)(2,1)} %collective-permute-done.refs_0_.refs_1_, ...), custom_call_target="tpu_custom_call" | custom-call | bytes 2000000000 | tf_op jit(solution)/shard_map/gather_tokens/pallas_call | solution.py:354
  414.0 12.5 %pick_grads.1 = (bf16[4,2,4,80,1536]{4,3,2,1,0:T(8,128)(2,1)}, f32[4,2,4,80,128]{4,3,2,1,0:T(8,128)}) custom-call(s32[4,2,4,512]{3,2,1,0:T(4,128)} %fusion.26.slot_ref, f32[4,2,4,512]{3,2,1,0:T(4,128)} %fusion.36.gate_ref, bf16[4,2,2,272,1536]{4,3,2,1,0:T(8,128)(2,1)} %bitcast.169), custom_call_target="tpu_custom_call" | custom-call | bytes 4096 | tf_op jit(solution)/shard_map/pick_grads/pallas_call | solution.py:925
  426.5 12.4 %pick_tokens.1.x_ref = bf16[4,2,4,80,1536]{4,3,2,1,0:T(8,128)(2,1)} custom-call(s32[4,2,4,512]{3,2,1,0:T(4,128)} %fusion.26.slot_ref, f32[4,2,4,512]{3,2,1,0:T(4,128)} %fusion.36.gate_ref, bf16[4,2,2,256,1536]{4,3,2,1,0:T(8,128)(2,1)} %get-tuple-element.98.rows_ref), custom_call_target="tpu_custom_call" | custom-call | bytes 4096 | tf_op jit(solution)/shard_map/pick_tokens/pallas_call | solution.py:925
  438.9 58.1 %experts.1 = (bf16[4,2,4,80,1536]{4,3,2,1,0:T(8,128)(2,1)}, bf16[4,2,4,80,1536]{4,3,2,1,0:T(8,128)(2,1)}, bf16[2,4,384,512]{3,2,1,0:T(8,128)(2,1)}, bf16[2,4,384...) custom-call(bf16[4,2,4,80,1536]{4,3,2,1,0:T(8,128)(2,1)} %pick_token, ...), custom_call_target="tpu_custom_call" | custom-call | bytes 4096 | tf_op jit(solution)/shard_map/experts/pallas_call | solution.py:1042
  499.1 13.2 %spread_grads.1.partial_ref = bf16[4,2,2,256,1536]{4,3,2,1,0:T(8,128)(2,1)} custom-call(s32[4,2,4,512]{3,2,1,0:T(4,128)} %fusion.26.slot_ref, bf16[4,2,4,80,1536]{4,3,2,1,0:T(8,128)(2,1)} %get-tuple-element.107.rows_ref), custom_call_target="tpu_custom_call" | custom-call | bytes 4096 | tf_op jit(solution)/shard_map/spread_grads/pallas_call | solution.py:957
  512.2 82.3 %scatter_grads.1 = f32[256,1536]{1,0:T(8,128)} custom-call(bf16[4,2,2,256,1536]{4,3,2,1,0:T(8,128)(2,1)} %spread_grads.1.partial_ref), custom_call_target="tpu_custom_call" | custom-call | bytes 2000000000 | tf_op jit(solution)/shard_map/scatter_grads/pallas_call | solution.py:530
  599.9 5.2 convolution_convert_fusion.6.grad_ref
  605.1 30.7 %collective-permute-done.5.refs_7_ = bf16[2,4,384,512]{3,2,1,0:T(8,128)(2,1)} collective-permute-done((bf16[2,4,384,512]{3,2,1,0:T(8,128)(2,1)}, bf16[2,4,384,512]{3,2,1,0:T(8,128)(2,1)}, u32[]{:S(2)}, u32[]{:S(2)}) %collective-permute-start.5) | collective-permute-done | bytes 3145760 | tf_op jit(solution)/shard_map/ppermute | solution.py:1100
  644.5 10.4 %attend_back.1 = (bf16[256,1536]{1,0:T(8,128)(2,1)}, bf16[2048,1024]{1,0:T(8,128)(2,1)}) custom-call(s32[1]{0:T(128)} %bitcast.1.place_ref, bf16[256,1536]{1,0:T(8,128)(2,1)} %convolution_convert_fusion.7.query_ref, bf16[2048,1024]{1,0:T(8,128)(2,1)} %bitcast.167, s32[1,256]{1,0:T(1,128)} %constant_dynamic-slice_fusion.row_ref, s32[2048,1]{1,0:T(8,128)} %copy.69.column_ref, ...), custom_call_target="tpu_custom_call" | custom-call | bytes 4096 | tf_op jit(solution)/shard_map/attend_back/pallas_call | solution.py:860
  655.0 46.9 %scatter_keys.1 = f32[256,1024]{1,0:T(8,128)} custom-call(bf16[4,1,2,256,1024]{4,3,2,1,0:T(8,128)(2,1)} %bitcast.173), custom_call_target="tpu_custom_call" | custom-call | bytes 4096 | tf_op jit(solution)/shard_map/scatter_keys/pallas_call | solution.py:530
  704.4 13.3 %spread_results.1 = bf16[4,2,2,256,1536]{4,3,2,1,0:T(8,128)(2,1)} custom-call(s32[4,2,4,512]{3,2,1,0:T(4,128)} %fusion.26.slot_ref, bf16[4,2,4,80,1536]{4,3,2,1,0:T(8,128)(2,1)} %get-tuple-element.133.rows_ref), custom_call_target="tpu_custom_call" | custom-call | bytes 4096 | tf_op jit(solution)/shard_map/spread_results/pallas_call | solution.py:957
  718.4 5.0 convolution_convert_fusion.2
  723.4 3.6 convolution_convert_fusion.1
  747.6 201.9 %reduce_dense.1 = (bf16[384,1536]{1,0:T(8,128)(2,1)}, bf16[384,2048]{1,0:T(8,128)(2,1)}, bf16[384,1536]{1,0:T(8,128)(2,1)}, bf16[256,1536]{1,0:T(8,128)(2,1)}, b...) custom-call(bf16[4,384,1536]{2,1,0:T(8,128)(2,1)} %bitcast.164, ...), custom_call_target="tpu_custom_call" | custom-call | bytes 2000000000 | tf_op jit(solution)/shard_map/reduce_dense/pallas_call | solution.py:717
  961.1 16.7 %place_experts.1 = (f32[8,384,512]{2,1,0:T(8,128)}, f32[8,384,512]{2,1,0:T(8,128)}, f32[8,512,384]{2,1,0:T(8,128)}) custom-call(s32[1]{0:T(128)} %bitcast.52.side_ref, bf16[2,4,384,512]{3,2,1,0:T(8,128)(2,1)} %get-tuple-element.118.refs_0_, bf16[2,4,384,512]{3,2,1,0:T(8,128)(2,1)} %get-tuple-element.120.refs_1_, ...), custom_call_target="tpu_custom_call" | custom-call | bytes 4096 | tf_op jit(solution)/shard_map/place_experts/pallas_call | solution.py:1083
  (191 shorter events, 112.9 us)
Async XLA Ops:
  7.2 395.4 %all-gather.2.cloned.1.call-start = ((), (), s32[]{:S(2)}) async-start(), calls=%async_computation.1 | async-start | bytes 15040512 | tf_op jit(solution)/shard_map/all_gather | solution.py:1231
  12.9 68.6 %copy-start = (bf16[1,256,1536]{2,1,0:T(8,128)(2,1)S(1)}, bf16[1,256,1536]{2,1,0:T(8,128)(2,1)}, u32[]{:S(2)}) copy-start(bf16[1,256,1536]{2,1,0:T(8,128)(2,1)} %param.17) | copy-start | bytes 2359300
  82.3 115.0 %copy-start.27 = (f32[256]{0:T(256)}, f32[256]{0:T(256)S(1)}, u32[]{:S(2)}) copy-start(f32[256]{0:T(256)S(1)} %get-tuple-element.172) | copy-start | bytes 3076
  181.8 767.8 %reduce-scatter.2.cloned.1.call-start = ((), (), s32[]{:S(2)}) async-start(), calls=%async_computation.2 | async-start | bytes 14155776 | tf_op jit(solution)/shard_map/reduce_scatter | solution.py:1369
  187.7 43.1 %collective-permute-start.3 = (bf16[4,512,384]{2,1,0:T(8,128)(2,1)}, bf16[4,512,384]{2,1,0:T(8,128)(2,1)}, u32[]{:S(2)}, u32[]{:S(2)}) collective-permute-start(bf16[4,512,384]{2,1,0:T(8,128)(2,1)} %get-tuple-element.104.refs_4_), channel_id=1, source_target_pairs={{0,2},{1,3},{2,0},{3,1},{4,6},{5,7},{6,4},{7,5},{8,10},{9,11},{10,... | collective-permute-start | bytes 4718600 | tf_op jit(solution)/shard_map/ppermute | solution.py:1100
  189.2 21.5 %slice-start.4 = ((s8[4718592]{0:T(1024)(128)(4,1)}), s8[524288]{0:T(1024)(128)(4,1)S(1)}, s32[]{:S(2)}) async-start(s8[4718592]{0:T(1024)(128)(4,1)} %bitcast.203), calls=%async_computation.7 | async-start | bytes 1048576
  192.8 99.3 %collective-permute-start.1 = (bf16[4,2,384,512]{3,2,1,0:T(8,128)(2,1)}, bf16[4,2,384,512]{3,2,1,0:T(8,128)(2,1)}, u32[]{:S(2)}, u32[]{:S(2)}) collective-permute-start(bf16[4,2,384,512]{3,2,1,0:T(8,128)(2,1)} %get-tuple-element.101.refs_0_), channel_id=1, source_target_pairs={{0,2},{1,3},{2,0},{3,1},{4,6},{5,7},{6,4},{7,5},{8,10},{9,11},{10,... | collective-permute-start | bytes 9437192 | tf_op jit(solution)/shard_map/ppermute | solution.py:1100
  193.8 37.6 %collective-permute-start.2 = (bf16[4,512,384]{2,1,0:T(8,128)(2,1)}, bf16[4,512,384]{2,1,0:T(8,128)(2,1)}, u32[]{:S(2)}, u32[]{:S(2)}) collective-permute-start(bf16[4,512,384]{2,1,0:T(8,128)(2,1)} %get-tuple-element.160), channel_id=1, source_target_pairs={{0,1},{1,0},{2,3},{3,2},{4,5},{5,4},{6,7},{7,6},{8,9},{9,8},{10,11... | collective-permute-start | bytes 4718600 | tf_op jit(solution)/shard_map/ppermute | solution.py:1100
  194.9 103.0 %collective-permute-start = (bf16[4,2,384,512]{3,2,1,0:T(8,128)(2,1)}, bf16[4,2,384,512]{3,2,1,0:T(8,128)(2,1)}, u32[]{:S(2)}, u32[]{:S(2)}) collective-permute-start(bf16[4,2,384,512]{3,2,1,0:T(8,128)(2,1)} %get-tuple-element.156), channel_id=1, source_target_pairs={{0,1},{1,0},{2,3},{3,2},{4,5},{5,4},{6,7},{7,6},{8,9},{9,8},{10,11... | collective-permute-start | bytes 9437192 | tf_op jit(solution)/shard_map/ppermute | solution.py:1100
  197.3 13.4 %slice-start.5 = ((s8[4718592]{0:T(1024)(128)(4,1)}), s8[4194304]{0:T(1024)(128)(4,1)S(1)}, s32[]{:S(2)}) async-start(s8[4718592]{0:T(1024)(128)(4,1)} %bitcast.203), calls=%async_computation.8 | async-start | bytes 8388608
  214.6 8.8 copy-start.6
  497.0 99.2 %collective-permute-start.4 = (bf16[2,4,384,512]{3,2,1,0:T(8,128)(2,1)}, bf16[2,4,384,512]{3,2,1,0:T(8,128)(2,1)S(1)}, u32[]{:S(2)}, u32[]{:S(2)}) collective-permute-start(bf16[2,4,384,512]{3,2,1,0:T(8,128)(2,1)} %get-tuple-element.108), channel_id=1, source_target_pairs={{0,2},{1,3},{2,0},{3,1},{4,6},{5,7},{6,4},{7,5},{8,10},{9,11},{10,... | collective-permute-start | bytes 9437192 | tf_op jit(solution)/shard_map/ppermute | solution.py:1100
  498.2 137.6 %collective-permute-start.5 = (bf16[2,4,384,512]{3,2,1,0:T(8,128)(2,1)}, bf16[2,4,384,512]{3,2,1,0:T(8,128)(2,1)}, u32[]{:S(2)}, u32[]{:S(2)}) collective-permute-start(bf16[2,4,384,512]{3,2,1,0:T(8,128)(2,1)} %get-tuple-element.110), channel_id=1, source_target_pairs={{0,2},{1,3},{2,0},{3,1},{4,6},{5,7},{6,4},{7,5},{8,10},{9,11},{10,... | collective-permute-start | bytes 9437192 | tf_op jit(solution)/shard_map/ppermute | solution.py:1100
  512.2 84.0 %copy-start.12 = (f32[256,1536]{1,0:T(8,128)S(1)}, f32[256,1536]{1,0:T(8,128)}, u32[]{:S(2)}) copy-start(f32[256,1536]{1,0:T(8,128)} %fusion.35) | copy-start | bytes 4718596
  512.2 84.0 %copy-start.32 = (f32[256]{0:T(256)S(1)}, f32[256]{0:T(256)}, u32[]{:S(2)}) copy-start(f32[256]{0:T(256)} %copy-done.31) | copy-start | bytes 3076
  594.6 108.6 %collective-permute-start.6 = (bf16[2,4,512,384]{3,2,1,0:T(8,128)(2,1)}, bf16[2,4,512,384]{3,2,1,0:T(8,128)(2,1)}, u32[]{:S(2)}, u32[]{:S(2)}) collective-permute-start(bf16[2,4,512,384]{3,2,1,0:T(8,128)(2,1)} %get-tuple-element.117), channel_id=1, source_target_pairs={{0,2},{1,3},{2,0},{3,1},{4,6},{5,7},{6,4},{7,5},{8,10},{9,11},{10,... | collective-permute-start | bytes 9437192 | tf_op jit(solution)/shard_map/ppermute | solution.py:1100
  596.2 43.9 %copy-start.11 = (bf16[2,4,384,512]{3,2,1,0:T(8,128)(2,1)}, bf16[2,4,384,512]{3,2,1,0:T(8,128)(2,1)S(1)}, u32[]{:S(2)}) copy-start(bf16[2,4,384,512]{3,2,1,0:T(8,128)(2,1)S(1)} %collective-permute-done.4.refs_6_) | copy-start | bytes 9437188
  599.8 36.0 %copy-start.9 = (bf16[2,4,384,512]{3,2,1,0:T(8,128)(2,1)S(1)}, bf16[2,4,384,512]{3,2,1,0:T(8,128)(2,1)}, u32[]{:S(2)}) copy-start(bf16[2,4,384,512]{3,2,1,0:T(8,128)(2,1)} %get-tuple-element.120.refs_1_) | copy-start | bytes 9437188
  639.0 64.2 %collective-permute-start.8 = (bf16[4,384,512]{2,1,0:T(8,128)(2,1)}, bf16[4,384,512]{2,1,0:T(8,128)(2,1)}, u32[]{:S(2)}, u32[]{:S(2)}) collective-permute-start(bf16[4,384,512]{2,1,0:T(8,128)(2,1)} %fusion.22), channel_id=1, source_target_pairs={{0,1},{1,0},{2,3},{3,2},{4,5},{5,4},{6,7},{7,6},{8,9},{9,8},{10,11... | collective-permute-start | bytes 4718600 | tf_op jit(solution)/shard_map/ppermute | solution.py:1100
  641.7 62.7 %collective-permute-start.7 = (bf16[4,384,512]{2,1,0:T(8,128)(2,1)}, bf16[4,384,512]{2,1,0:T(8,128)(2,1)}, u32[]{:S(2)}, u32[]{:S(2)}) collective-permute-start(bf16[4,384,512]{2,1,0:T(8,128)(2,1)} %fusion.21), channel_id=1, source_target_pairs={{0,1},{1,0},{2,3},{3,2},{4,5},{5,4},{6,7},{7,6},{8,9},{9,8},{10,11... | collective-permute-start | bytes 4718600 | tf_op jit(solution)/shard_map/ppermute | solution.py:1100
  718.4 8.6 slice-start.2
  733.0 216.6 %collective-permute-start.9 = (bf16[4,512,384]{2,1,0:T(8,128)(2,1)}, bf16[4,512,384]{2,1,0:T(8,128)(2,1)}, u32[]{:S(2)}, u32[]{:S(2)}) collective-permute-start(bf16[4,512,384]{2,1,0:T(8,128)(2,1)} %fusion.23), channel_id=1, source_target_pairs={{0,1},{1,0},{2,3},{3,2},{4,5},{5,4},{6,7},{7,6},{8,9},{9,8},{10,11... | collective-permute-start | bytes 4718600 | tf_op jit(solution)/shard_map/ppermute | solution.py:1100
  950.9 29.5 %collective-permute-start.10 = (bf16[256,1536]{1,0:T(8,128)(2,1)S(1)}, bf16[256,1536]{1,0:T(8,128)(2,1)S(1)}, u32[]{:S(2)}, u32[]{:S(2)}) collective-permute-start(bf16[256,1536]{1,0:T(8,128)(2,1)S(1)} %dynamic-slice_bitcast_fusion.2), channel_id=1, source_target_pairs={{0,1},{1,0},{2,3},{3,2},{4,5},{5,4},{6,7},{7,6},{8,9},{9,8},{10,11... | collective-permute-start | bytes 2359304 | tf_op jit(solution)/shard_map/ppermute | solution.py:1100
  961.1 17.3 %copy-start.13 = (bf16[384,2048]{1,0:T(8,128)(2,1)S(1)}, bf16[384,2048]{1,0:T(8,128)(2,1)}, u32[]{:S(2)}) copy-start(bf16[384,2048]{1,0:T(8,128)(2,1)} %get-tuple-element.140) | copy-start | bytes 4718596
  (30 other events, 91.6 us)
Sparse Core Ops, SparseCore 0:
  181.9 123.1 all-gather.1
  717.9 159.4 reduce-scatter.1

commit v6 on v5

--- a/solution.py
+++ b/solution.py
@@ -68,35 +68,44 @@
         self.c, self.w = lax.axis_index("ctx"), lax.axis_index("wt")
         self.core = lax.rem(self.c, 2)
         self.near = (flip(self.c, 1), self.w)
-        self.peers = [flip(self.w, d) for d in range(1, count)]
+        self.count = count
         self.pairs = list(zip(sources, targets))
         self.here, self.there, self.send, self.recv = here, there, send, recv
+        self.near_send, self.near_recv = near_send, near_recv
         self.stages = stages
-        self.near_send, self.near_recv = near_send, near_recv
+        dims = [1 << i for i in range(count.bit_length() - 1)]
+        self.orders = [dims, dims[::-1]]
 
     def devices(self):
-        return [(self.c, p) for p in self.peers]
-
-    def half(self, source, core):
-        rows = source.shape[0] // 2
-        return pl.ds(pl.multiple_of(core * rows, 16), rows)
-
-    def push(self, i, s):
-        source, target = self.pairs[s]
-        part = self.half(source, self.core)
+        return [(self.c, flip(self.w, d)) for d in self.orders[0]]
+
+    def rows(self, s, p, core):
+        rows = self.pairs[s][0].shape[0] // 4
+        return pl.ds(pl.multiple_of((core * 2 + p) * rows, 16), rows)
+
+    def block(self, s, p, f, core):
+        return self.pairs[s][1].at[flip(self.w, f), self.rows(s, p, core)]
+
+    def push(self, s, p, stage, held):
+        step = self.orders[p][stage]
+        part = self.rows(s, p, self.core)
+        source = self.pairs[s][0].at[part] if held == 0 else self.block(s, p, held, self.core)
+        index = (s, p, (step ^ held) - 1)
         return remote(
-            source.at[part], target.at[self.w, part], self.send.at[s, i], self.recv.at[s, i], (self.c, self.peers[i])
-        )
-
-    def arrival(self, i, s):
-        source, target = self.pairs[s]
-        spot = target.at[self.peers[i], self.half(source, self.core)]
-        return remote(spot, spot, self.send.at[s, i], self.recv.at[s, i], (self.c, self.peers[i]))
-
-    def hand(self, i, s, core):
-        source, target = self.pairs[s]
-        spot = target.at[self.peers[i], self.half(source, core)]
-        return remote(spot, spot, self.near_send.at[s, i], self.near_recv.at[s, i], self.near)
+            source,
+            self.block(s, p, held, self.core),
+            self.send.at[index],
+            self.recv.at[index],
+            (self.c, flip(self.w, step)),
+        )
+
+    def arrival(self, s, p, f):
+        spot = self.block(s, p, f, self.core)
+        return remote(spot, spot, self.send.at[s, p, f - 1], self.recv.at[s, p, f - 1], self.near)
+
+    def hand(self, s, p, f, core):
+        spot = self.block(s, p, f, core)
+        return remote(spot, spot, self.near_send.at[s, p, f - 1], self.near_recv.at[s, p, f - 1], self.near)
 
     def load(self, s):
         return pltpu.make_async_copy(self.pairs[s][0], self.stages[s], self.here.at[s])
@@ -104,12 +113,16 @@
     def keep(self, s):
         return pltpu.make_async_copy(self.stages[s], self.pairs[s][1].at[self.w], self.there.at[s])
 
+    def last_stage(self, p, f):
+        return max(i for i, d in enumerate(self.orders[p]) if f & d)
+
     def every(self):
-        return [(i, s) for s in range(len(self.pairs)) for i in range(len(self.peers))]
+        return [(s, p) for s in range(len(self.pairs)) for p in range(2)]
 
     def start(self):
-        for i, s in self.every():
-            self.push(i, s).start()
+        for stage in range(len(self.orders[0])):
+            for s, p in self.every():
+                self.push(s, p, stage, 0).start()
         for s in range(len(self.pairs)):
             self.load(s).start()
 
@@ -117,15 +130,23 @@
         for s in range(len(self.pairs)):
             self.load(s).wait()
             self.keep(s).start()
-        for i, s in self.every():
-            self.arrival(i, s).wait_recv()
-            self.hand(i, s, self.core).start()
+        last = len(self.orders[0])
+        for stage in range(last):
+            for s, p in self.every():
+                for f in range(1, self.count):
+                    if self.last_stage(p, f) == stage:
+                        self.arrival(s, p, f).wait_recv()
+                        for onward in range(stage + 1, last):
+                            self.push(s, p, onward, f).start()
+                        self.hand(s, p, f, self.core).start()
 
     def finish(self):
-        for i, s in self.every():
-            self.hand(i, s, 1 - self.core).wait_recv()
-            self.hand(i, s, self.core).wait_send()
-            self.push(i, s).wait_send()
+        for s, p in self.every():
+            for f in range(1, self.count):
+                stage = self.last_stage(p, f)
+                self.hand(s, p, f, 1 - self.core).wait_recv()
+                self.hand(s, p, f, self.core).wait_send()
+                self.push(s, p, stage, f ^ self.orders[p][stage]).wait_send()
         for s in range(len(self.pairs)):
             self.keep(s).wait()
 
@@ -135,7 +156,7 @@
         number = len(slabs)
         return (
             [dma((number,))] * 2
-            + [dma((number, count - 1))] * 4
+            + [dma((number, 2, count - 1))] * 4
             + [pltpu.VMEM(s.shape, s.dtype) for s in slabs]
         )
 
@@ -882,56 +903,116 @@
     )(place, projected, both, query_seg_row, seg_column, heads_out, grad_attended, logs)
 
 
-def pick_kernel(scaled, slot_ref, gate_ref, rows_ref, out_ref, scale_ref=None):
-    local, depth = out_ref.shape[2], out_ref.shape[3]
+def pick_rows_of(slot_rows, rows_of, local, depth, tokens):
+    place = lax.broadcasted_iota(jnp.int32, (depth, tokens), 0)
+    total, masks = None, []
+    for core in range(2):
+        chosen = [slot_rows[core][e : e + 1] == place for e in range(local)]
+        ones = jnp.concatenate([c.astype(jnp.float32) for c in chosen], axis=0).astype(jnp.bfloat16)
+        term = jnp.dot(ones, rows_of(core), preferred_element_type=jnp.float32)
+        total = term if total is None else total + term
+        masks.append(chosen)
+    return total, masks
+
+
+def pick_grads_kernel(local, first_ref, earlier_ref, rows_ref, out_ref, scale_ref, slot_ref):
+    depth = out_ref.shape[3]
     tokens = slot_ref.shape[3] // 2
-    place = lax.broadcasted_iota(jnp.int32, (depth, tokens), 0)
-    total, weight = None, None
+    slot_rows, gate_rows, count = [], [], None
     for core in range(2):
-        span = slice(core * tokens, (core + 1) * tokens)
-        chosen = [slot_ref[0, 0, e : e + 1, span] == place for e in range(local)]
-        ones = jnp.concatenate([c.astype(jnp.float32) for c in chosen], axis=0).astype(jnp.bfloat16)
-        rows = rows_ref[0, core, 0] if scaled else rows_ref[0, 0, core]
-        term = jnp.dot(ones, rows, preferred_element_type=jnp.float32)
-        total = term if total is None else total + term
-        if scaled:
-            gates = jnp.concatenate(
-                [
-                    jnp.sum(jnp.where(c, gate_ref[0, 0, e : e + 1, span], 0.0), axis=1, keepdims=True)
-                    for e, c in enumerate(chosen)
-                ],
-                axis=0,
-            )
-            weight = gates if weight is None else weight + gates
-    if scaled:
-        total = total * weight
-        scale_ref[0, 0] = jnp.broadcast_to(weight, (local * depth, 128)).reshape(local, depth, 128)
-    out_ref[0, 0] = total.astype(jnp.bfloat16).reshape(local, depth, total.shape[1])
-
-
-def pick_rows(rows, slots, gates, scaled):
-    chips, sides, local, both = slots.shape
-    tokens, width = both // 2, rows.shape[4]
+        table = rows_ref[0, core, 0, tokens : tokens + 16, :].astype(jnp.float32)
+        member, gate = [], []
+        for e in range(local):
+            expert = (first_ref[0] + e).astype(jnp.float32)
+            found, weight = None, None
+            for k in range(TOPK):
+                span = slice(k * tokens, (k + 1) * tokens)
+                named = table[0:1, span] == expert
+                value = jnp.where(named, table[1:2, span] + table[2:3, span] + table[3:4, span], 0.0)
+                mark = jnp.where(named, 1.0, 0.0)
+                found = mark if k == 0 else found + mark
+                weight = value if k == 0 else weight + value
+            member.append(found)
+            gate.append(weight)
+        member = jnp.concatenate(member + [jnp.zeros((8 - local, tokens), jnp.float32)], axis=0)
+        rank = jnp.dot(member.astype(jnp.bfloat16), earlier_ref[...], preferred_element_type=jnp.float32)
+        if core:
+            rank = rank + count
+        count = jnp.sum(member, axis=1, keepdims=True)
+        slots = jnp.where(member > 0.5, rank.astype(jnp.int32), -1)[:local]
+        slot_ref[0, 0, :, core * tokens : (core + 1) * tokens] = slots
+        slot_rows.append(slots)
+        gate_rows.append(gate)
+    total, masks = pick_rows_of(
+        slot_rows, lambda core: rows_ref[0, core, 0, :tokens, :], local, depth, tokens
+    )
+    weight = None
+    for core in range(2):
+        gates = jnp.concatenate(
+            [
+                jnp.sum(jnp.where(masks[core][e], gate_rows[core][e], 0.0), axis=1, keepdims=True)
+                for e in range(local)
+            ],
+            axis=0,
+        )
+        weight = gates if core == 0 else weight + gates
+    scale_ref[0, 0] = jnp.broadcast_to(weight, (local * depth, 128)).reshape(local, depth, 128)
+    out_ref[0, 0] = (total * weight).astype(jnp.bfloat16).reshape(local, depth, total.shape[1])
+
+
+def pick_grads(rows, first, local, tokens):
+    chips, _, sides, long, width = rows.shape
     depth = 2 * CAP
-    table = pl.BlockSpec((1, 1, local, both), lambda z, s: (z, s, 0, 0))
-    shapes = [jax.ShapeDtypeStruct((chips, sides, local, depth, width), jnp.bfloat16)]
-    specs = [pl.BlockSpec((1, 1, local, depth, width), lambda z, s: (z, s, 0, 0, 0))]
-    if scaled:
-        shapes.append(jax.ShapeDtypeStruct((chips, sides, local, depth, 128), jnp.float32))
-        specs.append(pl.BlockSpec((1, 1, local, depth, 128), lambda z, s: (z, s, 0, 0, 0)))
-        source = pl.BlockSpec((1, 2, 1, tokens, width), lambda z, s: (z, 0, s, 0, 0))
-    else:
-        source = pl.BlockSpec((1, 1, 2, tokens, width), lambda z, s: (z, s, 0, 0, 0))
+    earlier = jnp.arange(tokens)[:, None] < jnp.arange(tokens)[None, :]
     return pl.pallas_call(
-        functools.partial(pick_kernel, scaled),
+        functools.partial(pick_grads_kernel, local),
         grid=(chips, sides),
-        out_shape=shapes,
-        in_specs=[table, table, source],
-        out_specs=specs,
+        out_shape=(
+            jax.ShapeDtypeStruct((chips, sides, local, depth, width), jnp.bfloat16),
+            jax.ShapeDtypeStruct((chips, sides, local, depth, 128), jnp.float32),
+            jax.ShapeDtypeStruct((chips, sides, local, 2 * tokens), jnp.int32),
+        ),
+        in_specs=[
+            pl.BlockSpec(memory_space=pltpu.SMEM),
+            pl.BlockSpec((tokens, tokens), lambda z, s: (0, 0)),
+            pl.BlockSpec((1, 2, 1, long, width), lambda z, s: (z, 0, s, 0, 0)),
+        ],
+        out_specs=(
+            pl.BlockSpec((1, 1, local, depth, width), lambda z, s: (z, s, 0, 0, 0)),
+            pl.BlockSpec((1, 1, local, depth, 128), lambda z, s: (z, s, 0, 0, 0)),
+            pl.BlockSpec((1, 1, local, 2 * tokens), lambda z, s: (z, s, 0, 0)),
+        ),
         compiler_params=pltpu.CompilerParams(vmem_limit_bytes=WIDE),
         cost_estimate=CHEAP,
-        name="pick_grads" if scaled else "pick_tokens",
-    )(slots, gates, rows)
+        name="pick_grads",
+    )(first, earlier.astype(jnp.bfloat16), rows)
+
+
+def pick_tokens_kernel(slot_ref, rows_ref, out_ref):
+    local, depth = out_ref.shape[2], out_ref.shape[3]
+    tokens = rows_ref.shape[3]
+    slot_rows = [slot_ref[0, 0, :, core * tokens : (core + 1) * tokens] for core in range(2)]
+    total, _ = pick_rows_of(slot_rows, lambda core: rows_ref[0, 0, core], local, depth, tokens)
+    out_ref[0, 0] = total.astype(jnp.bfloat16).reshape(local, depth, total.shape[1])
+
+
+def pick_tokens(rows, slots):
+    chips, sides, local, both = slots.shape
+    tokens, width = rows.shape[3:]
+    depth = 2 * CAP
+    return pl.pallas_call(
+        pick_tokens_kernel,
+        grid=(chips, sides),
+        out_shape=jax.ShapeDtypeStruct((chips, sides, local, depth, width), jnp.bfloat16),
+        in_specs=[
+            pl.BlockSpec((1, 1, local, both), lambda z, s: (z, s, 0, 0)),
+            pl.BlockSpec((1, 1, 2, tokens, width), lambda z, s: (z, s, 0, 0, 0)),
+        ],
+        out_specs=pl.BlockSpec((1, 1, local, depth, width), lambda z, s: (z, s, 0, 0, 0)),
+        compiler_params=pltpu.CompilerParams(vmem_limit_bytes=WIDE),
+        cost_estimate=CHEAP,
+        name="pick_tokens",
+    )(slots, rows)
 
 
 def spread_kernel(apart, slot_ref, rows_ref, out_ref):
@@ -1172,11 +1253,12 @@
     grad_rows = cotangent[0]
     depth = norm_one_gain.shape[0]
     extra_rows = 16
-    table_rows = extra_rows * width_model // tokens
-    packed = jnp.pad(jnp.swapaxes(table, 0, 1), ((0, table_rows - 4 * TOPK), (0, 0)))
-    extended = jnp.concatenate([grad_rows, packed.reshape(extra_rows, width_model)], axis=0)
+    packed = jnp.pad(
+        jnp.swapaxes(table, 0, 1).reshape(4, width_model), ((0, extra_rows - 4), (0, 0))
+    )
+    extended = jnp.concatenate([grad_rows, packed], axis=0)
     gain_pair = jnp.concatenate(
-        [norm_one_gain[None], norm_two_gain[None], jnp.zeros((30, depth), jnp.bfloat16)]
+        [norm_one_gain[None], norm_two_gain[None], jnp.zeros((62, depth), jnp.bfloat16)]
     )
     query_weight, key_weight, value_weight, gains, grad_pair, zero = gather_weights(
         (w_query, w_key, w_value, gain_pair), (extended,)
@@ -1227,27 +1309,10 @@
     down_weight = down_weight.reshape(-1, down_weight.shape[2])
     both = both.reshape(-1, 2 * kv_width)
 
-    grad_pair = lax.dynamic_index_in_dim(jnp.stack([grad_pair, grad_pair]), zero, 0, False)
+    grad_pair, both = lax.optimization_barrier((grad_pair, both))
     all_grads = lax.all_gather(grad_pair, "ctx", axis=0).reshape(
         chips, 2, 2, tokens + extra_rows, width_model
     )
-    tables = all_grads[:, :, :, tokens:].reshape(chips, 2, 2, table_rows, tokens)[:, :, :, : 4 * TOPK]
-    tables = jnp.transpose(tables.astype(jnp.float32), (0, 2, 3, 1, 4)).reshape(
-        chips, 2, 4 * TOPK, 2 * tokens
-    )
-    table_routes, gate_parts = tables[:, :, :TOPK], tables[:, :, TOPK:]
-    table_gates = (
-        gate_parts[:, :, :TOPK] + gate_parts[:, :, TOPK : 2 * TOPK] + gate_parts[:, :, 2 * TOPK :]
-    )
-    experts_here = (first_expert + jnp.arange(local, dtype=jnp.int32)).astype(jnp.float32)
-    named = table_routes[:, :, None] == experts_here[None, None, :, None, None]
-    member = jnp.any(named, axis=3)
-    slot_gates = jnp.sum(jnp.where(named, table_gates[:, :, None], 0.0), axis=3)
-    earlier = (
-        jnp.arange(2 * tokens)[:, None] < jnp.arange(2 * tokens)[None, :]
-    ).astype(jnp.bfloat16)
-    rank = jnp.dot(member.astype(jnp.bfloat16), earlier, preferred_element_type=jnp.float32)
-    slots = jnp.where(member, rank.astype(jnp.int32), -1)
 
     place = lax.axis_index("ctx").astype(jnp.int32).reshape(1)
     seg_row, seg_column = seg_all[None, :], seg_all[:, None]
@@ -1299,8 +1364,10 @@
         return blocks
 
     tall_blocks, down_blocks = blocks_of(0), blocks_of(1)
-    (received_rows,) = pick_rows(all_rows, slots, slot_gates, False)
-    grad_received, row_gates = pick_rows(all_grads, slots, slot_gates, True)
+    grad_received, row_gates, slots = pick_grads(
+        all_grads, first_expert.astype(jnp.int32).reshape(1), local, tokens
+    )
+    received_rows = pick_tokens(all_rows, slots)
     if down_blocks[0].shape[2] % 128:
         results, backs, grads_gate, grads_up, grads_down = run_experts(
             received_rows,
@@ -1349,11 +1416,11 @@
     grad_attended = jnp.einsum(
         "td,qd->tq", grad_branch, out_weight, preferred_element_type=jnp.float32
     ).astype(jnp.bfloat16)
-    grad_attended, up_arrived = lax.optimization_barrier((grad_attended, later_arrived[0]))
-    up_other = crossed(hop_grads[1][0], up_arrived)
     grad_queries, grad_parts = attend_back(
         place, queries, both, query_seg[None, :], seg_column, attended_full, grad_attended, logs
     )
+    grad_parts, up_arrived = lax.optimization_barrier((grad_parts, later_arrived[0]))
+    up_other = crossed(hop_grads[1][0], up_arrived)
     grad_both = scatter_rows(
         grad_parts.reshape(chips, 1, 2, tokens, 2 * kv_width),
         6,

time: 997 us -> 954 us (0.957)
  Pallas kernels: 731 us -> 698 us
  waiting for transfers between devices: 99.2 us -> 111 us
    pallas_call x2, Pallas kernels: 188 us -> 171 us  [gather_rows(): pl.pallas_call(functools.partial(gather_kernel, chips, downward, paired,...]
    ppermute x11, waiting for transfers between devices: 99.1 us -> 111 us  [swap_pairs(): return lax.ppermute(value, axis, [(i, i ^ distance) for i in range(count)])]
    pallas_call x2, Pallas kernels: 129 us -> 118 us  [scatter_rows(): pl.pallas_call(functools.partial(scatter_kernel, chips, upward, paired, p...]
  transfers between devices with their start and end apart: 13 -> 13, of which waited for: 5 -> 6; matrix products, arithmetic and copies ran while one was open for 9% -> 9% of each run, Pallas kernels for 49% -> 50%
where the time goes in v6:
time: 954 us; the launch traced here: 947 us
  Pallas kernels  698 us (73%)
  waiting for transfers between devices  111 us (12%)
  matrix products  52.3 us (5%)
  other arithmetic  36.2 us (4%)
  local copies, waits for them, and re-layouts  23 us (2%)
  between operations  15.4 us (2%)
  starting transfers between devices  11.6 us (1%)
    pallas_call x1, Pallas kernels, reduce_dense(): pl.pallas_call(functools.partial(dense_kernel, chips, count, len(grads),...  205 us
    pallas_call x2, Pallas kernels, gather_rows(): pl.pallas_call(functools.partial(gather_kernel, chips, downward, paired,...  171 us
    pallas_call x2, Pallas kernels, scatter_rows(): pl.pallas_call(functools.partial(scatter_kernel, chips, upward, paired, p...  118 us
    ppermute x11, waiting for transfers between devices, swap_pairs(): return lax.ppermute(value, axis, [(i, i ^ distance) for i in range(count)])  111 us
    pallas_call x1, Pallas kernels, gather_weights(): pl.pallas_call(functools.partial(weights_kernel, count, len(slabs), len(s...  58.3 us
    pallas_call x1, Pallas kernels, run_experts(): pl.pallas_call(functools.partial(expert_kernel, blocks), grid=(local,), o...  57.8 us
    pallas_call x2, Pallas kernels, spread_rows(): pl.pallas_call(functools.partial(spread_kernel, apart), grid=(chips, side...  26.8 us
  transfers between devices with their start and end apart: 13, of which 6 were waited for; matrix products, arithmetic and copies ran while one was open for 9% of the time, Pallas kernels for 50%

profile of v6, /device:TPU:0, one launch (start us, length us, event | category | flops | bytes accessed | tf_op | source)
XLA Modules:
  0.0 947.3 jit_solution(12713082842951214691)
XLA Ops:
  13.6 58.3 %gather_weights.1 = (bf16[4,384,1536]{2,1,0:T(8,128)(2,1)}, bf16[4,384,512]{2,1,0:T(8,128)(2,1)}, bf16[4,384,512]{2,1,0:T(8,128)(2,1)}, bf16[4,64,384]{2,1,0:T(8...) custom-call(bf16[384,1536]{1,0:T(8,128)(2,1)} %refs_0_.2, bf16[384,512]{1,0:T(8,128)(2,1)} %refs_1_.1, ...), custom_call_target="tpu_custom_call" | custom-call | bytes 2000000000 | tf_op jit(solution)/shard_map/gather_weights/pallas_call | solution.py:215
  82.2 66.3 %gather_keys.1 = (bf16[4,1,2,256,1024]{4,3,2,1,0:T(8,128)(2,1)}, bf16[4,384,1536]{2,1,0:T(8,128)(2,1)}, bf16[4,384,2048]{2,1,0:T(8,128)(2,1)}, bf16[4,256,1536]{2,1,0:T(8,128)(2,1)}, s32[8,128]{1,0:T(8,128)}) custom-call(bf16[256,1024]{1,0:T(8,128)(2,1)} %reshape.287.rows_ref, bf16[384,1536]{1,0:T(8,128)(2,1)} %refs_0_.3, ...), custom_call_target="tpu_custom_call" | custom-call | bytes 2000000000 | tf_op jit(solution)/shard_map/gather_keys/pallas_call | solution.py:375
  150.5 4.1 dynamic-slice_bitcast_fusion
  163.9 4.8 convolution_convert_fusion.7.query_ref
  168.7 8.0 attend.1
  189.4 4.5 convolution_convert_fusion
  197.9 61.0 %collective-permute-done.1.refs_2_ = bf16[4,2,384,512]{3,2,1,0:T(8,128)(2,1)} collective-permute-done((bf16[4,2,384,512]{3,2,1,0:T(8,128)(2,1)}, bf16[4,2,384,512]{3,2,1,0:T(8,128)(2,1)}, u32[]{:S(2)}, u32[]{:S(2)}) %collective-permute-start.1) | collective-permute-done | bytes 3145760 | tf_op jit(solution)/shard_map/ppermute | solution.py:1181
  258.9 5.6 collective-permute-done.refs_0_.refs_1_
  264.5 104.7 %gather_tokens.1 = (bf16[4,2,2,256,1536]{4,3,2,1,0:T(8,128)(2,1)}, bf16[4,2,384,512]{3,2,1,0:T(8,128)(2,1)}, bf16[4,512,384]{2,1,0:T(8,128)(2,1)}, s32[8,128]{1,0:T(8,128)}) custom-call(bf16[256,1536]{1,0:T(8,128)(2,1)} %copy-done.6, bf16[4,2,384,512]{3,2,1,0:T(8,128)(2,1)} %collective-permute-done.refs_0_.refs_1_, ...), custom_call_target="tpu_custom_call" | custom-call | bytes 2000000000 | tf_op jit(solution)/shard_map/gather_tokens/pallas_call | solution.py:375
  369.2 13.3 %pick_grads.1 = (bf16[4,2,4,80,1536]{4,3,2,1,0:T(8,128)(2,1)}, f32[4,2,4,80,128]{4,3,2,1,0:T(8,128)}, s32[4,2,4,512]{3,2,1,0:T(4,128)}) custom-call(s32[1]{0:T(128)} %bitcast.26.first_ref, bf16[256,256]{1,0:T(8,128)(2,1)} %fusion.38.earlier_ref, bf16[4,2,2,272,1536]{4,3,2,1,0:T(8,128)(2,1)} %bitcast.156), custom_call_target="tpu_custom_call" | custom-call | bytes 4096 | tf_op jit(solution)/shard_map/pick_grads/pallas_call | solution.py:967
  382.5 12.3 %pick_tokens.1.x_ref = bf16[4,2,4,80,1536]{4,3,2,1,0:T(8,128)(2,1)} custom-call(s32[4,2,4,512]{3,2,1,0:T(4,128)} %get-tuple-element.98.slot_ref, bf16[4,2,2,256,1536]{4,3,2,1,0:T(8,128)(2,1)} %get-tuple-element.102.rows_ref), custom_call_target="tpu_custom_call" | custom-call | bytes 4096 | tf_op jit(solution)/shard_map/pick_tokens/pallas_call | solution.py:1003
  394.8 57.8 %experts.1 = (bf16[4,2,4,80,1536]{4,3,2,1,0:T(8,128)(2,1)}, bf16[4,2,4,80,1536]{4,3,2,1,0:T(8,128)(2,1)}, bf16[2,4,384,512]{3,2,1,0:T(8,128)(2,1)}, bf16[2,4,384...) custom-call(bf16[4,2,4,80,1536]{4,3,2,1,0:T(8,128)(2,1)} %pick_token, ...), custom_call_target="tpu_custom_call" | custom-call | bytes 4096 | tf_op jit(solution)/shard_map/experts/pallas_call | solution.py:1123
  456.6 13.2 %spread_grads.1.partial_ref = bf16[4,2,2,256,1536]{4,3,2,1,0:T(8,128)(2,1)} custom-call(s32[4,2,4,512]{3,2,1,0:T(4,128)} %get-tuple-element.98.slot_ref, bf16[4,2,4,80,1536]{4,3,2,1,0:T(8,128)(2,1)} %get-tuple-element.111.rows_ref), custom_call_target="tpu_custom_call" | custom-call | bytes 4096 | tf_op jit(solution)/shard_map/spread_grads/pallas_call | solution.py:1038
  469.8 82.4 %scatter_grads.1 = f32[256,1536]{1,0:T(8,128)} custom-call(bf16[4,2,2,256,1536]{4,3,2,1,0:T(8,128)(2,1)} %spread_grads.1.partial_ref), custom_call_target="tpu_custom_call" | custom-call | bytes 2000000000 | tf_op jit(solution)/shard_map/scatter_grads/pallas_call | solution.py:551
  555.9 5.2 convolution_convert_fusion.6.grad_ref
  561.1 10.6 %attend_back.1 = (bf16[256,1536]{1,0:T(8,128)(2,1)}, bf16[2048,1024]{1,0:T(8,128)(2,1)}) custom-call(s32[1]{0:T(128)} %bitcast.1.place_ref, bf16[256,1536]{1,0:T(8,128)(2,1)} %convolution_convert_fusion.7.query_ref, bf16[2048,1024]{1,0:T(8,128)(2,1)} %bitcast.155, s32[1,256]{1,0:T(1,128)} %constant_dynamic-slice_fusion.row_ref, s32[2048,1]{1,0:T(8,128)} %copy.55.column_ref, ...), custom_call_target="tpu_custom_call" | custom-call | bytes 4096 | tf_op jit(solution)/shard_map/attend_back/pallas_call | solution.py:881
  571.7 19.7 %collective-permute-done.5.refs_7_ = bf16[2,4,384,512]{3,2,1,0:T(8,128)(2,1)} collective-permute-done((bf16[2,4,384,512]{3,2,1,0:T(8,128)(2,1)}, bf16[2,4,384,512]{3,2,1,0:T(8,128)(2,1)}, u32[]{:S(2)}, u32[]{:S(2)}) %collective-permute-start.5) | collective-permute-done | bytes 3145760 | tf_op jit(solution)/shard_map/ppermute | solution.py:1181
  598.6 35.4 %scatter_keys.1 = f32[256,1024]{1,0:T(8,128)} custom-call(bf16[4,1,2,256,1024]{4,3,2,1,0:T(8,128)(2,1)} %bitcast.160), custom_call_target="tpu_custom_call" | custom-call | bytes 4096 | tf_op jit(solution)/shard_map/scatter_keys/pallas_call | solution.py:551
  635.3 21.3 %collective-permute-done.6.refs_8_ = bf16[2,4,512,384]{3,2,1,0:T(8,128)(2,1)} collective-permute-done((bf16[2,4,512,384]{3,2,1,0:T(8,128)(2,1)}, bf16[2,4,512,384]{3,2,1,0:T(8,128)(2,1)}, u32[]{:S(2)}, u32[]{:S(2)}) %collective-permute-start.6) | collective-permute-done | bytes 3145760 | tf_op jit(solution)/shard_map/ppermute | solution.py:1181
  659.1 13.7 %spread_results.1 = bf16[4,2,2,256,1536]{4,3,2,1,0:T(8,128)(2,1)} custom-call(s32[4,2,4,512]{3,2,1,0:T(4,128)} %get-tuple-element.98.slot_ref, bf16[4,2,4,80,1536]{4,3,2,1,0:T(8,128)(2,1)} %get-tuple-element.137.rows_ref), custom_call_target="tpu_custom_call" | custom-call | bytes 4096 | tf_op jit(solution)/shard_map/spread_results/pallas_call | solution.py:1038
  672.9 5.0 convolution_convert_fusion.2
  677.9 3.6 convolution_convert_fusion.1
  701.9 205.2 %reduce_dense.1 = (bf16[384,1536]{1,0:T(8,128)(2,1)}, bf16[384,2048]{1,0:T(8,128)(2,1)}, bf16[384,1536]{1,0:T(8,128)(2,1)}, bf16[256,1536]{1,0:T(8,128)(2,1)}, b...) custom-call(bf16[4,384,1536]{2,1,0:T(8,128)(2,1)} %bitcast.152, ...), custom_call_target="tpu_custom_call" | custom-call | bytes 2000000000 | tf_op jit(solution)/shard_map/reduce_dense/pallas_call | solution.py:738
  918.7 16.7 %place_experts.1 = (f32[8,384,512]{2,1,0:T(8,128)}, f32[8,384,512]{2,1,0:T(8,128)}, f32[8,512,384]{2,1,0:T(8,128)}) custom-call(s32[1]{0:T(128)} %bitcast.48.side_ref, bf16[2,4,384,512]{3,2,1,0:T(8,128)(2,1)} %get-tuple-element.122.refs_0_, bf16[2,4,384,512]{3,2,1,0:T(8,128)(2,1)} %get-tuple-element.124.refs_1_, ...), custom_call_target="tpu_custom_call" | custom-call | bytes 4096 | tf_op jit(solution)/shard_map/place_experts/pallas_call | solution.py:1164
  (169 shorter events, 99.4 us)
Async XLA Ops:
  7.2 362.0 %all-gather.3.cloned.1.call-start = ((), (), s32[]{:S(2)}) async-start(), calls=%async_computation.2 | async-start | bytes 15040512 | tf_op jit(solution)/shard_map/all_gather | solution.py:1313
  12.8 59.9 %copy-start = (bf16[1,256,1536]{2,1,0:T(8,128)(2,1)S(1)}, bf16[1,256,1536]{2,1,0:T(8,128)(2,1)}, u32[]{:S(2)}) copy-start(bf16[1,256,1536]{2,1,0:T(8,128)(2,1)} %param.17) | copy-start | bytes 2359300
  148.5 758.6 %reduce-scatter.2.cloned.1.call-start = ((), (), s32[]{:S(2)}) async-start(), calls=%async_computation.1 | async-start | bytes 14155776 | tf_op jit(solution)/shard_map/reduce_scatter | solution.py:1436
  154.5 42.4 %collective-permute-start.3 = (bf16[4,512,384]{2,1,0:T(8,128)(2,1)}, bf16[4,512,384]{2,1,0:T(8,128)(2,1)}, u32[]{:S(2)}, u32[]{:S(2)}) collective-permute-start(bf16[4,512,384]{2,1,0:T(8,128)(2,1)} %get-tuple-element.108.refs_4_), channel_id=1, source_target_pairs={{0,2},{1,3},{2,0},{3,1},{4,6},{5,7},{6,4},{7,5},{8,10},{9,11},{10,... | collective-permute-start | bytes 4718600 | tf_op jit(solution)/shard_map/ppermute | solution.py:1181
  155.9 21.4 %slice-start.4 = ((s8[4718592]{0:T(1024)(128)(4,1)}), s8[524288]{0:T(1024)(128)(4,1)S(1)}, s32[]{:S(2)}) async-start(s8[4718592]{0:T(1024)(128)(4,1)} %bitcast.188), calls=%async_computation.7 | async-start | bytes 1048576
  159.3 99.6 %collective-permute-start.1 = (bf16[4,2,384,512]{3,2,1,0:T(8,128)(2,1)}, bf16[4,2,384,512]{3,2,1,0:T(8,128)(2,1)}, u32[]{:S(2)}, u32[]{:S(2)}) collective-permute-start(bf16[4,2,384,512]{3,2,1,0:T(8,128)(2,1)} %get-tuple-element.105.refs_0_), channel_id=1, source_target_pairs={{0,2},{1,3},{2,0},{3,1},{4,6},{5,7},{6,4},{7,5},{8,10},{9,11},{10,... | collective-permute-start | bytes 9437192 | tf_op jit(solution)/shard_map/ppermute | solution.py:1181
  160.3 37.6 %collective-permute-start.2 = (bf16[4,512,384]{2,1,0:T(8,128)(2,1)}, bf16[4,512,384]{2,1,0:T(8,128)(2,1)}, u32[]{:S(2)}, u32[]{:S(2)}) collective-permute-start(bf16[4,512,384]{2,1,0:T(8,128)(2,1)} %get-tuple-element.164), channel_id=1, source_target_pairs={{0,1},{1,0},{2,3},{3,2},{4,5},{5,4},{6,7},{7,6},{8,9},{9,8},{10,11... | collective-permute-start | bytes 4718600 | tf_op jit(solution)/shard_map/ppermute | solution.py:1181
  161.4 103.1 %collective-permute-start = (bf16[4,2,384,512]{3,2,1,0:T(8,128)(2,1)}, bf16[4,2,384,512]{3,2,1,0:T(8,128)(2,1)}, u32[]{:S(2)}, u32[]{:S(2)}) collective-permute-start(bf16[4,2,384,512]{3,2,1,0:T(8,128)(2,1)} %get-tuple-element.160), channel_id=1, source_target_pairs={{0,1},{1,0},{2,3},{3,2},{4,5},{5,4},{6,7},{7,6},{8,9},{9,8},{10,11... | collective-permute-start | bytes 9437192 | tf_op jit(solution)/shard_map/ppermute | solution.py:1181
  163.9 13.5 %slice-start.5 = ((s8[4718592]{0:T(1024)(128)(4,1)}), s8[4194304]{0:T(1024)(128)(4,1)S(1)}, s32[]{:S(2)}) async-start(s8[4718592]{0:T(1024)(128)(4,1)} %bitcast.188), calls=%async_computation.8 | async-start | bytes 8388608
  180.7 8.7 copy-start.6
  394.8 59.9 %copy-start.28 = (s32[1,2048]{1,0:T(1,128)S(1)}, s32[1,2048]{1,0:T(1,128)}, u32[]{:S(2)}) copy-start(s32[1,2048]{1,0:T(1,128)} %row_ref.1) | copy-start | bytes 24580
  452.6 101.0 %collective-permute-start.4 = (bf16[2,4,384,512]{3,2,1,0:T(8,128)(2,1)}, bf16[2,4,384,512]{3,2,1,0:T(8,128)(2,1)}, u32[]{:S(2)}, u32[]{:S(2)}) collective-permute-start(bf16[2,4,384,512]{3,2,1,0:T(8,128)(2,1)} %get-tuple-element.112), channel_id=1, source_target_pairs={{0,2},{1,3},{2,0},{3,1},{4,6},{5,7},{6,4},{7,5},{8,10},{9,11},{10,... | collective-permute-start | bytes 9437192 | tf_op jit(solution)/shard_map/ppermute | solution.py:1181
  453.8 137.7 %collective-permute-start.5 = (bf16[2,4,384,512]{3,2,1,0:T(8,128)(2,1)}, bf16[2,4,384,512]{3,2,1,0:T(8,128)(2,1)}, u32[]{:S(2)}, u32[]{:S(2)}) collective-permute-start(bf16[2,4,384,512]{3,2,1,0:T(8,128)(2,1)} %get-tuple-element.119), channel_id=1, source_target_pairs={{0,2},{1,3},{2,0},{3,1},{4,6},{5,7},{6,4},{7,5},{8,10},{9,11},{10,... | collective-permute-start | bytes 9437192 | tf_op jit(solution)/shard_map/ppermute | solution.py:1181
  469.8 83.8 %copy-start.11 = (f32[256,1536]{1,0:T(8,128)S(1)}, f32[256,1536]{1,0:T(8,128)}, u32[]{:S(2)}) copy-start(f32[256,1536]{1,0:T(8,128)} %fusion.33) | copy-start | bytes 4718596
  552.2 104.5 %collective-permute-start.6 = (bf16[2,4,512,384]{3,2,1,0:T(8,128)(2,1)}, bf16[2,4,512,384]{3,2,1,0:T(8,128)(2,1)}, u32[]{:S(2)}, u32[]{:S(2)}) collective-permute-start(bf16[2,4,512,384]{3,2,1,0:T(8,128)(2,1)} %get-tuple-element.121), channel_id=1, source_target_pairs={{0,2},{1,3},{2,0},{3,1},{4,6},{5,7},{6,4},{7,5},{8,10},{9,11},{10,... | collective-permute-start | bytes 9437192 | tf_op jit(solution)/shard_map/ppermute | solution.py:1181
  561.1 30.3 %copy-start.9 = (bf16[2,4,384,512]{3,2,1,0:T(8,128)(2,1)S(1)}, bf16[2,4,384,512]{3,2,1,0:T(8,128)(2,1)}, u32[]{:S(2)}) copy-start(bf16[2,4,384,512]{3,2,1,0:T(8,128)(2,1)} %get-tuple-element.124.refs_1_) | copy-start | bytes 9437188
  593.5 63.1 %collective-permute-start.8 = (bf16[4,384,512]{2,1,0:T(8,128)(2,1)S(1)}, bf16[4,384,512]{2,1,0:T(8,128)(2,1)S(1)}, u32[]{:S(2)}, u32[]{:S(2)}) collective-permute-start(bf16[4,384,512]{2,1,0:T(8,128)(2,1)S(1)} %fusion.22), channel_id=1, source_target_pairs={{0,1},{1,0},{2,3},{3,2},{4,5},{5,4},{6,7},{7,6},{8,9},{9,8},{10,11... | collective-permute-start | bytes 4718600 | tf_op jit(solution)/shard_map/ppermute | solution.py:1181
  597.7 61.5 %collective-permute-start.7 = (bf16[4,384,512]{2,1,0:T(8,128)(2,1)}, bf16[4,384,512]{2,1,0:T(8,128)(2,1)S(1)}, u32[]{:S(2)}, u32[]{:S(2)}) collective-permute-start(bf16[4,384,512]{2,1,0:T(8,128)(2,1)} %fusion.21), channel_id=1, source_target_pairs={{0,1},{1,0},{2,3},{3,2},{4,5},{5,4},{6,7},{7,6},{8,9},{9,8},{10,11... | collective-permute-start | bytes 4718600 | tf_op jit(solution)/shard_map/ppermute | solution.py:1181
  656.6 16.2 %copy-start.17 = (bf16[4,384,512]{2,1,0:T(8,128)(2,1)}, bf16[4,384,512]{2,1,0:T(8,128)(2,1)S(1)}, u32[]{:S(2)}) copy-start(bf16[4,384,512]{2,1,0:T(8,128)(2,1)S(1)} %collective-permute-done.8.refs_4_) | copy-start | bytes 4718596
  659.1 13.7 %copy-start.18 = (bf16[4,384,512]{2,1,0:T(8,128)(2,1)}, bf16[4,384,512]{2,1,0:T(8,128)(2,1)S(1)}, u32[]{:S(2)}) copy-start(bf16[4,384,512]{2,1,0:T(8,128)(2,1)S(1)} %collective-permute-done.7.refs_3_) | copy-start | bytes 4718596
  672.9 8.6 slice-start.2
  687.4 219.8 %collective-permute-start.9 = (bf16[4,512,384]{2,1,0:T(8,128)(2,1)}, bf16[4,512,384]{2,1,0:T(8,128)(2,1)}, u32[]{:S(2)}, u32[]{:S(2)}) collective-permute-start(bf16[4,512,384]{2,1,0:T(8,128)(2,1)} %fusion.23), channel_id=1, source_target_pairs={{0,1},{1,0},{2,3},{3,2},{4,5},{5,4},{6,7},{7,6},{8,9},{9,8},{10,11... | collective-permute-start | bytes 4718600 | tf_op jit(solution)/shard_map/ppermute | solution.py:1181
  908.5 29.5 %collective-permute-start.10 = (bf16[256,1536]{1,0:T(8,128)(2,1)S(1)}, bf16[256,1536]{1,0:T(8,128)(2,1)S(1)}, u32[]{:S(2)}, u32[]{:S(2)}) collective-permute-start(bf16[256,1536]{1,0:T(8,128)(2,1)S(1)} %dynamic-slice_bitcast_fusion.2), channel_id=1, source_target_pairs={{0,1},{1,0},{2,3},{3,2},{4,5},{5,4},{6,7},{7,6},{8,9},{9,8},{10,11... | collective-permute-start | bytes 2359304 | tf_op jit(solution)/shard_map/ppermute | solution.py:1181
  918.6 17.3 %copy-start.12 = (bf16[384,2048]{1,0:T(8,128)(2,1)S(1)}, bf16[384,2048]{1,0:T(8,128)(2,1)}, u32[]{:S(2)}) copy-start(bf16[384,2048]{1,0:T(8,128)(2,1)} %get-tuple-element.144) | copy-start | bytes 4718596
  (25 other events, 77.4 us)
Sparse Core Ops, SparseCore 0:
  148.7 122.4 all-gather.2
  673.0 161.9 reduce-scatter.1

commit v7 on v6

--- a/solution.py
+++ b/solution.py
@@ -392,7 +392,14 @@
     return results + [zero[0, 0]]
 
 
-def scatter_kernel(chips, upward, paired, pieces, partial_ref, out_ref, own, sib, mate, low_in, high_in, load, near_send, near_recv, pair_send, pair_recv, up_send, up_recv, down_send, down_recv):
+def scatter_kernel(chips, upward, paired, pieces, fused, *refs):
+    if fused:
+        rows_ref, slot_ref, out_ref, built, *refs = refs
+        partial_ref = None
+    else:
+        partial_ref, out_ref, *refs = refs
+    own, sib, mate, low_in, high_in, load, near_send, near_recv, *refs = refs
+    pair_send, pair_recv, up_send, up_recv, down_send, down_recv = refs
     c, w = lax.axis_index("ctx"), lax.axis_index("wt")
     z = c // 2
     core = lax.rem(c, 2)
@@ -424,7 +431,7 @@
 
     def hand(chip, which):
         return remote(
-            partial_ref.at[chip, which, 1 - core],
+            built.at[chip, which] if fused else partial_ref.at[chip, which, 1 - core],
             sib.at[chip, which],
             near_send.at[chip, which],
             near_recv.at[chip, which],
@@ -465,18 +472,45 @@
         spot = own.at[chip, which, cut(piece)]
         spot[...] = spot[...] + other[...]
 
-    for chip in order:
-
-        def begin(chip=chip):
-            for which in range(sides):
-                hand(chip, which).start()
+    def spread(chip, which, parity, spot):
+        local, depth, width = rows_ref.shape[2:]
+        tokens = spot.shape[0]
+        span = pl.ds(pl.multiple_of(parity * tokens, tokens), tokens)
+        place = lax.broadcasted_iota(jnp.int32, (depth, tokens), 0)
+        ones = jnp.concatenate(
+            [
+                (slot_ref[chip, which, e : e + 1, span] == place).astype(jnp.float32)
+                for e in range(local)
+            ],
+            axis=0,
+        ).astype(jnp.bfloat16)
+        spot[...] = lax.dot_general(
+            ones,
+            rows_ref[chip, which].reshape(local * depth, width),
+            (((0,), (0,)), ((), ())),
+            preferred_element_type=jnp.float32,
+        ).astype(jnp.bfloat16)
+
+    def begin(chip):
+        for which in range(sides):
+            if fused:
+                spread(chip, which, 1 - core, built.at[chip, which])
+            hand(chip, which).start()
+            if fused:
+                spread(chip, which, core, own.at[chip, which])
+            else:
                 fetch(chip, which).start()
 
-        wanted(chip, begin)
+    if not fused:
+        for chip in order:
+            wanted(chip, lambda: begin(chip))
+    else:
+        begin(order[0])
 
     def meet(chip):
         for which in range(sides):
-            fetch(chip, which).wait()
+            if not fused:
+                fetch(chip, which).wait()
             hand(chip, which).wait_recv()
         for piece in range(pieces):
             if paired:
@@ -510,6 +544,8 @@
                 drop(chip, piece).start()
 
     for i, chip in enumerate(order):
+        if fused and i + 1 < len(order):
+            begin(order[i + 1])
         wanted(chip, lambda: meet(chip))
         if i >= 1:
             wanted(order[i - 1], lambda: travel(order[i - 1]))
@@ -543,19 +579,28 @@
         wanted(chip, lambda: finish(chip))
 
 
-def scatter_rows(partial, collective_id, upward, paired, name):
-    chips, sides, _, tokens, width = partial.shape
+def scatter_rows(partial, collective_id, upward, paired, name, slots=None):
+    fused = slots is not None
+    dma = pltpu.SemaphoreType.DMA
     pieces = 2
-    dma = pltpu.SemaphoreType.DMA
+    if fused:
+        chips, sides, _, _, width = partial.shape
+        tokens = slots.shape[3] // 2
+    else:
+        chips, sides, _, tokens, width = partial.shape
     block = (tokens, width)
+    several = pltpu.VMEM((chips, sides) + block, jnp.bfloat16)
     return pl.pallas_call(
-        functools.partial(scatter_kernel, chips, upward, paired, pieces),
+        functools.partial(scatter_kernel, chips, upward, paired, pieces, fused),
         out_shape=jax.ShapeDtypeStruct(block, jnp.float32),
-        in_specs=[pl.BlockSpec(memory_space=pl.ANY)],
+        in_specs=[pl.BlockSpec(memory_space=pltpu.VMEM)] * 2
+        if fused
+        else [pl.BlockSpec(memory_space=pl.ANY)],
         out_specs=pl.BlockSpec(memory_space=pltpu.VMEM),
-        scratch_shapes=[
-            pltpu.VMEM((chips, sides) + block, jnp.bfloat16),
-            pltpu.VMEM((chips, sides) + block, jnp.bfloat16),
+        scratch_shapes=([several] if fused else [])
+        + [
+            several,
+            several,
             pltpu.VMEM((chips if paired else 1,) + block, jnp.bfloat16),
             pltpu.VMEM((chips if upward else 1,) + block, jnp.bfloat16),
             pltpu.VMEM((chips,) + block, jnp.bfloat16),
@@ -569,7 +614,7 @@
         ),
         cost_estimate=LONG if paired else CHEAP,
         name=name,
-    )(partial)
+    )(*((partial, slots) if fused else (partial,)))
 
 
 def dense_kernel(chips, count, matrices, pieces, *refs):
@@ -589,11 +634,21 @@
     near = (flip(c, 1), w)
     above = (lax.rem(c + 2, 2 * chips), w)
     below = (lax.rem(c + 2 * chips - 2, 2 * chips), w)
-    peers = [flip(w, d) for d in range(1, count)]
-    greet([near, above, below] + [(c, p) for p in peers])
+    dims = [1 << i for i in range(count.bit_length() - 1)]
+    greet([near, above, below] + [(c, flip(w, d)) for d in dims])
+
+    def order(j):
+        return dims if pieces[j][3] else dims[::-1]
+
+    def sends(j, stage):
+        step, rest = order(j)[stage], order(j)[stage + 1 :]
+        offsets = [step]
+        for r in rest:
+            offsets += [o ^ r for o in offsets]
+        return offsets
 
     def span(j, parity=None):
-        m, first, rows = pieces[j]
+        m, first, rows, _ = pieces[j]
         if parity is None:
             return pl.ds(first, rows)
         half = grads[m].shape[1] // 2
@@ -609,10 +664,15 @@
             grads[m].at[:, span(j, 1 - core)], sib[m].at[:, span(j)], near_send.at[j], near_recv.at[j], near
         )
 
-    def give(j, d):
+    def give(j, stage, o):
         m = pieces[j][0]
+        step = order(j)[stage]
         return remote(
-            own[m].at[peers[d], span(j)], mates[m].at[d, span(j)], send.at[j, d], recv.at[j, d], (c, peers[d])
+            own[m].at[flip(w, o), span(j)],
+            mates[m].at[o - 1, span(j)],
+            send.at[j, o - 1],
+            recv.at[j, o - 1],
+            (c, flip(w, step)),
         )
 
     def total(j):
@@ -629,18 +689,29 @@
         m = pieces[j][0]
         fetch(j).wait()
         hand(j).wait_recv()
-        for d in range(count - 1):
-            add(own[m].at[peers[d], span(j)], sib[m].at[peers[d], span(j)])
-            give(j, d).start()
-        add(total(j), sib[m].at[w, span(j)])
-
-    def collect(j):
+        for o in sends(j, 0):
+            add(own[m].at[flip(w, o), span(j)], sib[m].at[flip(w, o), span(j)])
+            give(j, 0, o).start()
+        for o in range(count):
+            if o not in sends(j, 0):
+                add(own[m].at[flip(w, o), span(j)], sib[m].at[flip(w, o), span(j)])
+
+    def collect(j, stage):
         m = pieces[j][0]
-        value = total(j)[...].astype(jnp.float32)
-        for d in range(count - 1):
-            give(j, d).wait_recv()
-            value = value + mates[m][d, span(j), :].astype(jnp.float32)
-        total(j)[...] = value.astype(jnp.bfloat16)
+        step = order(j)[stage]
+        for o in sends(j, stage):
+            give(j, stage, o).wait_recv()
+        last = stage + 1 == len(dims)
+        onward_blocks = [] if last else sends(j, stage + 1)
+        for o in sends(j, stage):
+            kept = o ^ step
+            if kept in onward_blocks:
+                add(own[m].at[flip(w, kept), span(j)], mates[m].at[o - 1, span(j)])
+                give(j, stage + 1, kept).start()
+        for o in sends(j, stage):
+            kept = o ^ step
+            if kept not in onward_blocks:
+                add(own[m].at[flip(w, kept), span(j)], mates[m].at[o - 1, span(j)])
 
     def line(j):
         return (z, above, below) if j % 2 == 0 else (chips - 1 - z, below, above)
@@ -696,14 +767,17 @@
     number = len(pieces)
     for j in range(number):
         start(j)
-    for j in range(number):
-        share(j)
     last = chips - 1
-    for t in range(number + 2 * last):
+    lead, gap = 2, 1
+    behind = lead + gap * (len(dims) - 1)
+    for t in range(number + 2 * last + behind):
         if t < number:
-            collect(t)
+            share(t)
+        for stage in range(len(dims)):
+            if 0 <= t - lead - gap * stage < number:
+                collect(t - lead - gap * stage, stage)
         for hop in range(2 * last, -1, -1):
-            j = t - hop
+            j = t - hop - behind
             if not 0 <= j < number:
                 continue
             if hop <= last:
@@ -713,8 +787,9 @@
     for j in range(number):
         place = line(j)[0]
         hand(j).wait_send()
-        for d in range(count - 1):
-            give(j, d).wait_send()
+        for stage in range(len(dims)):
+            for o in sends(j, stage):
+                give(j, stage, o).wait_send()
         pl.when(place < chips - 1)(lambda: onward(j).wait_send())
         pl.when(place > 0)(lambda: backward(j).wait_send())
         across(j, core).wait_send()
@@ -729,9 +804,9 @@
     pieces = []
     for m, (rows, _) in enumerate(shapes):
         half, width = rows // 2, shapes[m][1]
-        cuts = max(n for n in range(1, 5) if half % (16 * n) == 0 and (n == 1 or half * width > 120000 * (n - 1)))
+        cuts = max(n for n in range(1, 9) if half % (16 * n) == 0 and (n == 1 or half * width > 60000 * (n - 1)))
         for i in range(cuts):
-            pieces.append((m, i * (rows // 2 // cuts), rows // 2 // cuts))
+            pieces.append((m, i * (rows // 2 // cuts), rows // 2 // cuts, len(pieces) % 2))
     halves = [(rows // 2, width) for rows, width in shapes]
     dma = pltpu.SemaphoreType.DMA
     one, many = dma((len(pieces),)), dma((len(pieces), count - 1))
@@ -1389,9 +1464,12 @@
         hop_grads = [rest[i * pairs : (i + 1) * pairs] for i in range(3)]
     arrived = [[swap_pairs(g[d], "wt", 2 * d) for d in range(1, pairs)] for g in hop_grads]
     first_arrived, later_arrived = arrived[:1], arrived[1:]
-    routed_grad = scatter_rows(
-        spread_rows(backs, slots, "spread_grads", False), 5, True, True, "scatter_grads"
-    )
+    if chips > 4:
+        routed_grad = scatter_rows(
+            spread_rows(backs, slots, "spread_grads", False), 5, True, True, "scatter_grads"
+        )
+    else:
+        routed_grad = scatter_rows(backs, 5, True, True, "scatter_grads", slots)
     routed_grad, first_arrived = lax.optimization_barrier((routed_grad, first_arrived))
 
     def crossed(own, more):

time: 954 us -> 961 us (level)
  waiting for transfers between devices: 111 us -> 121 us
    pallas_call x2 -> x1, Pallas kernels: 26.8 us -> 13.7 us  [spread_rows(): pl.pallas_call(functools.partial(spread_kernel, apart), grid=(chips, side...]
  transfers between devices with their start and end apart: 13 -> 13, of which waited for: 6 -> 5; matrix products, arithmetic and copies ran while one was open for 9% -> 10% of each run, Pallas kernels for 50% -> 49%
where the time goes in v7:
time: 961 us; the launch traced here: 955 us
  Pallas kernels  694 us (72%)
  waiting for transfers between devices  121 us (13%)
  matrix products  52.8 us (5%)
  other arithmetic  36.9 us (4%)
  local copies, waits for them, and re-layouts  22.6 us (2%)
  between operations  15.6 us (2%)
  starting transfers between devices  12.3 us (1%)
    pallas_call x1, Pallas kernels, reduce_dense(): pl.pallas_call(functools.partial(dense_kernel, chips, count, len(grads),...  211 us
    pallas_call x2, Pallas kernels, gather_rows(): pl.pallas_call(functools.partial(gather_kernel, chips, downward, paired,...  171 us
    pallas_call x2, Pallas kernels, scatter_rows(): pl.pallas_call(functools.partial(scatter_kernel, chips, upward, paired, p...  121 us
    ppermute x11, waiting for transfers between devices, swap_pairs(): return lax.ppermute(value, axis, [(i, i ^ distance) for i in range(count)])  121 us
    pallas_call x1, Pallas kernels, gather_weights(): pl.pallas_call(functools.partial(weights_kernel, count, len(slabs), len(s...  58.3 us
    pallas_call x1, Pallas kernels, run_experts(): pl.pallas_call(functools.partial(expert_kernel, blocks), grid=(local,), o...  58 us
  transfers between devices with their start and end apart: 13, of which 5 were waited for; matrix products, arithmetic and copies ran while one was open for 10% of the time, Pallas kernels for 49%

profile of v7, /device:TPU:0, one launch (start us, length us, event | category | flops | bytes accessed | tf_op | source)
XLA Modules:
  0.0 955.4 jit_solution(17203907282938805713)
XLA Ops:
  13.6 58.3 %gather_weights.1 = (bf16[4,384,1536]{2,1,0:T(8,128)(2,1)}, bf16[4,384,512]{2,1,0:T(8,128)(2,1)}, bf16[4,384,512]{2,1,0:T(8,128)(2,1)}, bf16[4,64,384]{2,1,0:T(8...) custom-call(bf16[384,1536]{1,0:T(8,128)(2,1)} %refs_0_.2, bf16[384,512]{1,0:T(8,128)(2,1)} %refs_1_.1, ...), custom_call_target="tpu_custom_call" | custom-call | bytes 2000000000 | tf_op jit(solution)/shard_map/gather_weights/pallas_call | solution.py:215
  80.9 66.3 %gather_keys.1 = (bf16[4,1,2,256,1024]{4,3,2,1,0:T(8,128)(2,1)}, bf16[4,384,1536]{2,1,0:T(8,128)(2,1)}, bf16[4,384,2048]{2,1,0:T(8,128)(2,1)}, bf16[4,256,1536]{2,1,0:T(8,128)(2,1)}, s32[8,128]{1,0:T(8,128)}) custom-call(bf16[256,1024]{1,0:T(8,128)(2,1)} %reshape.287.rows_ref, bf16[384,1536]{1,0:T(8,128)(2,1)} %refs_0_.3, ...), custom_call_target="tpu_custom_call" | custom-call | bytes 2000000000 | tf_op jit(solution)/shard_map/gather_keys/pallas_call | solution.py:375
  149.2 4.1 dynamic-slice_bitcast_fusion
  162.7 4.7 convolution_convert_fusion.7.query_ref
  167.3 8.0 attend.1
  176.0 4.5 multiply_reduce_fusion.2
  189.4 4.5 convolution_convert_fusion
  196.9 60.7 %collective-permute-done.1.refs_2_ = bf16[4,2,384,512]{3,2,1,0:T(8,128)(2,1)} collective-permute-done((bf16[4,2,384,512]{3,2,1,0:T(8,128)(2,1)}, bf16[4,2,384,512]{3,2,1,0:T(8,128)(2,1)}, u32[]{:S(2)}, u32[]{:S(2)}) %collective-permute-start.1) | collective-permute-done | bytes 3145760 | tf_op jit(solution)/shard_map/ppermute | solution.py:1256
  257.7 5.6 collective-permute-done.refs_0_.refs_1_
  263.2 104.7 %gather_tokens.1 = (bf16[4,2,2,256,1536]{4,3,2,1,0:T(8,128)(2,1)}, bf16[4,2,384,512]{3,2,1,0:T(8,128)(2,1)}, bf16[4,512,384]{2,1,0:T(8,128)(2,1)}, s32[8,128]{1,0:T(8,128)}) custom-call(bf16[256,1536]{1,0:T(8,128)(2,1)} %copy-done.6, bf16[4,2,384,512]{3,2,1,0:T(8,128)(2,1)} %collective-permute-done.refs_0_.refs_1_, ...), custom_call_target="tpu_custom_call" | custom-call | bytes 2000000000 | tf_op jit(solution)/shard_map/gather_tokens/pallas_call | solution.py:375
  368.0 13.5 %pick_grads.1 = (bf16[4,2,4,80,1536]{4,3,2,1,0:T(8,128)(2,1)}, f32[4,2,4,80,128]{4,3,2,1,0:T(8,128)}, s32[4,2,4,512]{3,2,1,0:T(4,128)}) custom-call(s32[1]{0:T(128)} %bitcast.26.first_ref, bf16[256,256]{1,0:T(8,128)(2,1)} %fusion.38.earlier_ref, bf16[4,2,2,272,1536]{4,3,2,1,0:T(8,128)(2,1)} %bitcast.156), custom_call_target="tpu_custom_call" | custom-call | bytes 4096 | tf_op jit(solution)/shard_map/pick_grads/pallas_call | solution.py:1042
  381.5 12.3 %pick_tokens.1.x_ref = bf16[4,2,4,80,1536]{4,3,2,1,0:T(8,128)(2,1)} custom-call(s32[4,2,4,512]{3,2,1,0:T(4,128)} %get-tuple-element.98.slot_ref.refs_1_, bf16[4,2,2,256,1536]{4,3,2,1,0:T(8,128)(2,1)} %get-tuple-element.102.rows_ref), custom_call_target="tpu_custom_call" | custom-call | bytes 4096 | tf_op jit(solution)/shard_map/pick_tokens/pallas_call | solution.py:1078
  393.8 58.0 %experts.1 = (bf16[4,2,4,80,1536]{4,3,2,1,0:T(8,128)(2,1)}, bf16[4,2,4,80,1536]{4,3,2,1,0:T(8,128)(2,1)}, bf16[2,4,384,512]{3,2,1,0:T(8,128)(2,1)}, bf16[2,4,384...) custom-call(bf16[4,2,4,80,1536]{4,3,2,1,0:T(8,128)(2,1)} %pick_token, ...), custom_call_target="tpu_custom_call" | custom-call | bytes 4096 | tf_op jit(solution)/shard_map/experts/pallas_call | solution.py:1198
  455.8 89.1 %scatter_grads.1 = f32[256,1536]{1,0:T(8,128)} custom-call(bf16[4,2,4,80,1536]{4,3,2,1,0:T(8,128)(2,1)} %get-tuple-element.111.refs_0_, s32[4,2,4,512]{3,2,1,0:T(4,128)} %get-tuple-element.98.slot_ref.refs_1_), custom_call_target="tpu_custom_call" | custom-call | bytes 2000000000 | tf_op jit(solution)/shard_map/scatter_grads/pallas_call | solution.py:593
  547.7 5.2 convolution_convert_fusion.6.grad_ref
  552.9 10.6 %attend_back.1 = (bf16[256,1536]{1,0:T(8,128)(2,1)}, bf16[2048,1024]{1,0:T(8,128)(2,1)}) custom-call(s32[1]{0:T(128)} %bitcast.1.place_ref, bf16[256,1536]{1,0:T(8,128)(2,1)} %convolution_convert_fusion.7.query_ref, bf16[2048,1024]{1,0:T(8,128)(2,1)} %bitcast.155, s32[1,256]{1,0:T(1,128)} %constant_dynamic-slice_fusion.row_ref, s32[2048,1]{1,0:T(8,128)} %copy.55.column_ref, ...), custom_call_target="tpu_custom_call" | custom-call | bytes 4096 | tf_op jit(solution)/shard_map/attend_back/pallas_call | solution.py:956
  563.5 27.1 %collective-permute-done.5.refs_7_ = bf16[2,4,384,512]{3,2,1,0:T(8,128)(2,1)} collective-permute-done((bf16[2,4,384,512]{3,2,1,0:T(8,128)(2,1)}, bf16[2,4,384,512]{3,2,1,0:T(8,128)(2,1)}, u32[]{:S(2)}, u32[]{:S(2)}) %collective-permute-start.5) | collective-permute-done | bytes 3145760 | tf_op jit(solution)/shard_map/ppermute | solution.py:1256
  597.7 32.1 %scatter_keys.1 = f32[256,1024]{1,0:T(8,128)} custom-call(bf16[4,1,2,256,1024]{4,3,2,1,0:T(8,128)(2,1)} %bitcast.160), custom_call_target="tpu_custom_call" | custom-call | bytes 4096 | tf_op jit(solution)/shard_map/scatter_keys/pallas_call | solution.py:593
  631.1 24.6 %collective-permute-done.6.refs_8_ = bf16[2,4,512,384]{3,2,1,0:T(8,128)(2,1)} collective-permute-done((bf16[2,4,512,384]{3,2,1,0:T(8,128)(2,1)}, bf16[2,4,512,384]{3,2,1,0:T(8,128)(2,1)}, u32[]{:S(2)}, u32[]{:S(2)}) %collective-permute-start.6) | collective-permute-done | bytes 3145760 | tf_op jit(solution)/shard_map/ppermute | solution.py:1256
  658.2 13.7 %spread_results.1 = bf16[4,2,2,256,1536]{4,3,2,1,0:T(8,128)(2,1)} custom-call(s32[4,2,4,512]{3,2,1,0:T(4,128)} %get-tuple-element.98.slot_ref.refs_1_, bf16[4,2,4,80,1536]{4,3,2,1,0:T(8,128)(2,1)} %get-tuple-element.137.rows_ref), custom_call_target="tpu_custom_call" | custom-call | bytes 4096 | tf_op jit(solution)/shard_map/spread_results/pallas_call | solution.py:1113
  672.0 5.5 convolution_convert_fusion.2
  677.5 3.6 convolution_convert_fusion.1
  701.1 211.3 %reduce_dense.1 = (bf16[384,1536]{1,0:T(8,128)(2,1)}, bf16[384,2048]{1,0:T(8,128)(2,1)}, bf16[384,1536]{1,0:T(8,128)(2,1)}, bf16[256,1536]{1,0:T(8,128)(2,1)}, b...) custom-call(bf16[4,384,1536]{2,1,0:T(8,128)(2,1)} %bitcast.152, ...), custom_call_target="tpu_custom_call" | custom-call | bytes 2000000000 | tf_op jit(solution)/shard_map/reduce_dense/pallas_call | solution.py:813
  925.3 16.7 %place_experts.1 = (f32[8,384,512]{2,1,0:T(8,128)}, f32[8,384,512]{2,1,0:T(8,128)}, f32[8,512,384]{2,1,0:T(8,128)}) custom-call(s32[1]{0:T(128)} %bitcast.48.side_ref, bf16[2,4,384,512]{3,2,1,0:T(8,128)(2,1)} %get-tuple-element.122.refs_0_, bf16[2,4,384,512]{3,2,1,0:T(8,128)(2,1)} %get-tuple-element.124.refs_1_, ...), custom_call_target="tpu_custom_call" | custom-call | bytes 4096 | tf_op jit(solution)/shard_map/place_experts/pallas_call | solution.py:1239
  (165 shorter events, 95.1 us)
Async XLA Ops:
  7.2 360.8 %all-gather.3.cloned.1.call-start = ((), (), s32[]{:S(2)}) async-start(), calls=%async_computation.2 | async-start | bytes 15040512 | tf_op jit(solution)/shard_map/all_gather | solution.py:1388
  12.8 59.9 %copy-start = (bf16[1,256,1536]{2,1,0:T(8,128)(2,1)S(1)}, bf16[1,256,1536]{2,1,0:T(8,128)(2,1)}, u32[]{:S(2)}) copy-start(bf16[1,256,1536]{2,1,0:T(8,128)(2,1)} %param.17) | copy-start | bytes 2359300
  147.3 765.2 %reduce-scatter.2.cloned.1.call-start = ((), (), s32[]{:S(2)}) async-start(), calls=%async_computation.1 | async-start | bytes 14155776 | tf_op jit(solution)/shard_map/reduce_scatter | solution.py:1514
  153.3 43.7 %collective-permute-start.3 = (bf16[4,512,384]{2,1,0:T(8,128)(2,1)}, bf16[4,512,384]{2,1,0:T(8,128)(2,1)}, u32[]{:S(2)}, u32[]{:S(2)}) collective-permute-start(bf16[4,512,384]{2,1,0:T(8,128)(2,1)} %get-tuple-element.108.refs_4_), channel_id=1, source_target_pairs={{0,2},{1,3},{2,0},{3,1},{4,6},{5,7},{6,4},{7,5},{8,10},{9,11},{10,... | collective-permute-start | bytes 4718600 | tf_op jit(solution)/shard_map/ppermute | solution.py:1256
  158.0 99.6 %collective-permute-start.1 = (bf16[4,2,384,512]{3,2,1,0:T(8,128)(2,1)}, bf16[4,2,384,512]{3,2,1,0:T(8,128)(2,1)}, u32[]{:S(2)}, u32[]{:S(2)}) collective-permute-start(bf16[4,2,384,512]{3,2,1,0:T(8,128)(2,1)} %get-tuple-element.105.refs_0_), channel_id=1, source_target_pairs={{0,2},{1,3},{2,0},{3,1},{4,6},{5,7},{6,4},{7,5},{8,10},{9,11},{10,... | collective-permute-start | bytes 9437192 | tf_op jit(solution)/shard_map/ppermute | solution.py:1256
  159.1 37.8 %collective-permute-start.2 = (bf16[4,512,384]{2,1,0:T(8,128)(2,1)}, bf16[4,512,384]{2,1,0:T(8,128)(2,1)}, u32[]{:S(2)}, u32[]{:S(2)}) collective-permute-start(bf16[4,512,384]{2,1,0:T(8,128)(2,1)} %get-tuple-element.164), channel_id=1, source_target_pairs={{0,1},{1,0},{2,3},{3,2},{4,5},{5,4},{6,7},{7,6},{8,9},{9,8},{10,11... | collective-permute-start | bytes 4718600 | tf_op jit(solution)/shard_map/ppermute | solution.py:1256
  160.2 103.1 %collective-permute-start = (bf16[4,2,384,512]{3,2,1,0:T(8,128)(2,1)}, bf16[4,2,384,512]{3,2,1,0:T(8,128)(2,1)}, u32[]{:S(2)}, u32[]{:S(2)}) collective-permute-start(bf16[4,2,384,512]{3,2,1,0:T(8,128)(2,1)} %get-tuple-element.160), channel_id=1, source_target_pairs={{0,1},{1,0},{2,3},{3,2},{4,5},{5,4},{6,7},{7,6},{8,9},{9,8},{10,11... | collective-permute-start | bytes 9437192 | tf_op jit(solution)/shard_map/ppermute | solution.py:1256
  180.8 8.6 copy-start.6
  393.8 60.1 %copy-start.29 = (s32[1,2048]{1,0:T(1,128)S(1)}, s32[1,2048]{1,0:T(1,128)}, u32[]{:S(2)}) copy-start(s32[1,2048]{1,0:T(1,128)} %row_ref.1) | copy-start | bytes 24580
  451.8 93.6 %collective-permute-start.4 = (bf16[2,4,384,512]{3,2,1,0:T(8,128)(2,1)}, bf16[2,4,384,512]{3,2,1,0:T(8,128)(2,1)}, u32[]{:S(2)}, u32[]{:S(2)}) collective-permute-start(bf16[2,4,384,512]{3,2,1,0:T(8,128)(2,1)} %get-tuple-element.112), channel_id=1, source_target_pairs={{0,2},{1,3},{2,0},{3,1},{4,6},{5,7},{6,4},{7,5},{8,10},{9,11},{10,... | collective-permute-start | bytes 9437192 | tf_op jit(solution)/shard_map/ppermute | solution.py:1256
  452.9 137.7 %collective-permute-start.5 = (bf16[2,4,384,512]{3,2,1,0:T(8,128)(2,1)}, bf16[2,4,384,512]{3,2,1,0:T(8,128)(2,1)}, u32[]{:S(2)}, u32[]{:S(2)}) collective-permute-start(bf16[2,4,384,512]{3,2,1,0:T(8,128)(2,1)} %get-tuple-element.119), channel_id=1, source_target_pairs={{0,2},{1,3},{2,0},{3,1},{4,6},{5,7},{6,4},{7,5},{8,10},{9,11},{10,... | collective-permute-start | bytes 9437192 | tf_op jit(solution)/shard_map/ppermute | solution.py:1256
  455.8 89.6 %copy-start.11 = (f32[256,1536]{1,0:T(8,128)S(1)}, f32[256,1536]{1,0:T(8,128)}, u32[]{:S(2)}) copy-start(f32[256,1536]{1,0:T(8,128)} %fusion.33) | copy-start | bytes 4718596
  544.9 110.8 %collective-permute-start.6 = (bf16[2,4,512,384]{3,2,1,0:T(8,128)(2,1)}, bf16[2,4,512,384]{3,2,1,0:T(8,128)(2,1)}, u32[]{:S(2)}, u32[]{:S(2)}) collective-permute-start(bf16[2,4,512,384]{3,2,1,0:T(8,128)(2,1)} %get-tuple-element.121), channel_id=1, source_target_pairs={{0,2},{1,3},{2,0},{3,1},{4,6},{5,7},{6,4},{7,5},{8,10},{9,11},{10,... | collective-permute-start | bytes 9437192 | tf_op jit(solution)/shard_map/ppermute | solution.py:1256
  552.9 37.7 %copy-start.9 = (bf16[2,4,384,512]{3,2,1,0:T(8,128)(2,1)S(1)}, bf16[2,4,384,512]{3,2,1,0:T(8,128)(2,1)}, u32[]{:S(2)}) copy-start(bf16[2,4,384,512]{3,2,1,0:T(8,128)(2,1)} %get-tuple-element.124.refs_1_) | copy-start | bytes 9437188
  592.6 63.1 %collective-permute-start.8 = (bf16[4,384,512]{2,1,0:T(8,128)(2,1)S(1)}, bf16[4,384,512]{2,1,0:T(8,128)(2,1)S(1)}, u32[]{:S(2)}, u32[]{:S(2)}) collective-permute-start(bf16[4,384,512]{2,1,0:T(8,128)(2,1)S(1)} %fusion.22), channel_id=1, source_target_pairs={{0,1},{1,0},{2,3},{3,2},{4,5},{5,4},{6,7},{7,6},{8,9},{9,8},{10,11... | collective-permute-start | bytes 4718600 | tf_op jit(solution)/shard_map/ppermute | solution.py:1256
  596.8 61.4 %collective-permute-start.7 = (bf16[4,384,512]{2,1,0:T(8,128)(2,1)}, bf16[4,384,512]{2,1,0:T(8,128)(2,1)S(1)}, u32[]{:S(2)}, u32[]{:S(2)}) collective-permute-start(bf16[4,384,512]{2,1,0:T(8,128)(2,1)} %fusion.21), channel_id=1, source_target_pairs={{0,1},{1,0},{2,3},{3,2},{4,5},{5,4},{6,7},{7,6},{8,9},{9,8},{10,11... | collective-permute-start | bytes 4718600 | tf_op jit(solution)/shard_map/ppermute | solution.py:1256
  655.7 16.2 %copy-start.17 = (bf16[4,384,512]{2,1,0:T(8,128)(2,1)}, bf16[4,384,512]{2,1,0:T(8,128)(2,1)S(1)}, u32[]{:S(2)}) copy-start(bf16[4,384,512]{2,1,0:T(8,128)(2,1)S(1)} %collective-permute-done.8.refs_4_) | copy-start | bytes 4718596
  658.2 13.7 %copy-start.18 = (bf16[4,384,512]{2,1,0:T(8,128)(2,1)}, bf16[4,384,512]{2,1,0:T(8,128)(2,1)S(1)}, u32[]{:S(2)}) copy-start(bf16[4,384,512]{2,1,0:T(8,128)(2,1)S(1)} %collective-permute-done.7.refs_3_) | copy-start | bytes 4718596
  671.9 5.5 copy-start.3
  671.9 5.5 copy-start.5
  672.0 9.1 slice-start.2
  686.6 225.9 %collective-permute-start.9 = (bf16[4,512,384]{2,1,0:T(8,128)(2,1)}, bf16[4,512,384]{2,1,0:T(8,128)(2,1)}, u32[]{:S(2)}, u32[]{:S(2)}) collective-permute-start(bf16[4,512,384]{2,1,0:T(8,128)(2,1)} %fusion.23), channel_id=1, source_target_pairs={{0,1},{1,0},{2,3},{3,2},{4,5},{5,4},{6,7},{7,6},{8,9},{9,8},{10,11... | collective-permute-start | bytes 4718600 | tf_op jit(solution)/shard_map/ppermute | solution.py:1256
  913.8 30.9 %collective-permute-start.10 = (bf16[256,1536]{1,0:T(8,128)(2,1)S(1)}, bf16[256,1536]{1,0:T(8,128)(2,1)}, u32[]{:S(2)}, u32[]{:S(2)}) collective-permute-start(bf16[256,1536]{1,0:T(8,128)(2,1)S(1)} %dynamic-slice_bitcast_fusion.2), channel_id=1, source_target_pairs={{0,1},{1,0},{2,3},{3,2},{4,5},{5,4},{6,7},{7,6},{8,9},{9,8},{10,11... | collective-permute-start | bytes 2359304 | tf_op jit(solution)/shard_map/ppermute | solution.py:1256
  925.3 17.3 %copy-start.12 = (bf16[384,2048]{1,0:T(8,128)(2,1)S(1)}, bf16[384,2048]{1,0:T(8,128)(2,1)}, u32[]{:S(2)}) copy-start(bf16[384,2048]{1,0:T(8,128)(2,1)} %get-tuple-element.144) | copy-start | bytes 4718596
  (24 other events, 72.8 us)
Sparse Core Ops, SparseCore 0:
  147.4 122.4 all-gather.2
  672.0 150.7 reduce-scatter.1

commit v8 on v7

--- a/solution.py
+++ b/solution.py
@@ -1131,7 +1131,8 @@
 
 def expert_kernel(blocks, x_ref, g_ref, scale_ref, *refs):
     tall_refs, down_refs = refs[:blocks], refs[blocks : 2 * blocks]
-    result_ref, back_ref, *grad_refs = refs[2 * blocks :]
+    result_ref, back_ref, *grad_refs = refs[2 * blocks : -3]
+    tall_all, flat_all, flat_grad = refs[-3:]
     hops = len(grad_refs) // 3
     grad_gate_refs, grad_up_refs = grad_refs[:hops], grad_refs[hops : 2 * hops]
     grad_down_refs = grad_refs[2 * hops :]
@@ -1153,29 +1154,40 @@
     def piece(ref, q):
         return columns(ref, q)[...].reshape(rows, part)
 
-    gate, up, grad_inner = None, None, None
+    def offset(q):
+        return 0 if blocks == 1 else pl.multiple_of(flip(w, q) * part, 128)
+
+    inner_width = tall_refs[0].shape[3]
     for q in range(blocks):
-        x = piece(x_ref, q)
-        more_gate, more_up = dot(x, tall_refs[q][0, 0], nn), dot(x, tall_refs[q][0, 1], nn)
-        gate, up = (more_gate, more_up) if q == 0 else (gate + more_gate, up + more_up)
-    for q in range(blocks):
-        more = dot(piece(g_ref, q), down_refs[q][0], nt)
-        grad_inner = more if q == 0 else grad_inner + more
+        span = pl.ds(offset(q), part)
+        tall_all[span, :inner_width] = tall_refs[q][0, 0]
+        tall_all[span, inner_width:] = tall_refs[q][0, 1]
+        flat_all[:, span] = down_refs[q][0]
+    x = x_ref[...].reshape(rows, width)
+    g = g_ref[...].reshape(rows, width)
+    gate = dot(x, tall_all[:, :inner_width], nn)
+    up = dot(x, tall_all[:, inner_width:], nn)
+    grad_inner = dot(g, flat_all[...], nt)
     sigmoid = jax.nn.sigmoid(gate)
     activated = gate * sigmoid
     inner = (activated * up).astype(jnp.bfloat16)
     grad_gate = (grad_inner * up * (sigmoid * (1.0 + gate * (1.0 - sigmoid)))).astype(jnp.bfloat16)
     grad_up = (grad_inner * activated).astype(jnp.bfloat16)
+    grad_both = jnp.concatenate([grad_gate, grad_up], axis=1)
     scale = scale_ref[...].reshape(rows, 128)[:, :1]
+    chunk = 512
+    for first in range(0, width, chunk):
+        span = slice(first, first + chunk)
+        result = dot(inner, flat_all[:, span], nn) * scale
+        result_ref[:, :, 0, :, span] = result.astype(jnp.bfloat16).reshape(chips, sides, depth, chunk)
+        back = dot(grad_both, tall_all[span, :], nt)
+        back_ref[:, :, 0, :, span] = back.astype(jnp.bfloat16).reshape(chips, sides, depth, chunk)
+        flat_grad[:, span] = dot(inner, g[:, span], tn).astype(jnp.bfloat16)
     for q in range(blocks):
-        result = dot(inner, down_refs[q][0], nn) * scale
-        columns(result_ref, q)[...] = result.astype(jnp.bfloat16).reshape(chips, sides, depth, part)
-        back = dot(grad_gate, tall_refs[q][0, 0], nt) + dot(grad_up, tall_refs[q][0, 1], nt)
-        columns(back_ref, q)[...] = back.astype(jnp.bfloat16).reshape(chips, sides, depth, part)
-        grad_down_refs[q // 2][q % 2, 0] = dot(inner, piece(g_ref, q), tn).astype(jnp.bfloat16)
-        x = piece(x_ref, q)
-        grad_gate_refs[q // 2][q % 2, 0] = dot(x, grad_gate, tn).astype(jnp.bfloat16)
-        grad_up_refs[q // 2][q % 2, 0] = dot(x, grad_up, tn).astype(jnp.bfloat16)
+        more = dot(piece(x_ref, q), grad_both, tn).astype(jnp.bfloat16)
+        grad_gate_refs[q // 2][q % 2, 0] = more[:, :inner_width]
+        grad_up_refs[q // 2][q % 2, 0] = more[:, inner_width:]
+        grad_down_refs[q // 2][q % 2, 0] = flat_grad[:, pl.ds(offset(q), part)]
 
 
 def run_experts(x, g, scale, talls, downs):
@@ -1206,6 +1218,11 @@
         ),
         in_specs=[sources, sources, scales] + [tall] * blocks + [flat] * blocks,
         out_specs=(rows, rows) + (tall_out,) * (2 * hops) + (flat_out,) * hops,
+        scratch_shapes=[
+            pltpu.VMEM((width, 2 * inner), jnp.bfloat16),
+            pltpu.VMEM((inner, width), jnp.bfloat16),
+            pltpu.VMEM((inner, width), jnp.bfloat16),
+        ],
         compiler_params=pltpu.CompilerParams(vmem_limit_bytes=60 * 2**20),
         cost_estimate=CHEAP,
         name="experts",
@@ -1470,7 +1487,15 @@
         )
     else:
         routed_grad = scatter_rows(backs, 5, True, True, "scatter_grads", slots)
-    routed_grad, first_arrived = lax.optimization_barrier((routed_grad, first_arrived))
+    routed_grad, first_arrived, results = lax.optimization_barrier(
+        (routed_grad, first_arrived, results)
+    )
+    partial = lax.psum_scatter(
+        spread_rows(results, slots, "spread_results", True).reshape(ctx_count, 2, tokens, width_model),
+        "ctx",
+        scatter_dimension=0,
+        tiled=True,
+    )[0]
 
     def crossed(own, more):
         total = own[1].astype(jnp.float32)
@@ -1506,17 +1531,11 @@
         False,
         "scatter_keys",
     ).astype(jnp.bfloat16)
-    grad_both, down_arrived, gate_other, up_other, results = lax.optimization_barrier(
-        (grad_both, later_arrived[1], gate_other, up_other, results)
+    grad_both, down_arrived, gate_other, up_other = lax.optimization_barrier(
+        (grad_both, later_arrived[1], gate_other, up_other)
     )
     arrived = [first_arrived[0], up_arrived, down_arrived]
     down_other = crossed(hop_grads[2][0], down_arrived)
-    partial = lax.psum_scatter(
-        spread_rows(results, slots, "spread_results", True).reshape(ctx_count, 2, tokens, width_model),
-        "ctx",
-        scatter_dimension=0,
-        tiled=True,
-    )[0]
     grad_both = grad_both.reshape(tokens, KV_HEADS, 2, HEAD_DIM)
     grad_keys = grad_both[:, :, 0].reshape(tokens, kv_width)
     grad_values = grad_both[:, :, 1].reshape(tokens, kv_width)

time: 961 us -> 959 us (level)
    pallas_call x2, Pallas kernels: 121 us -> 150 us  [scatter_rows(): pl.pallas_call(functools.partial(scatter_kernel, chips, upward, paired, p...]
    pallas_call x1, Pallas kernels: 211 us -> 191 us  [reduce_dense(): pl.pallas_call(functools.partial(dense_kernel, chips, count, len(grads),...]
  transfers between devices with their start and end apart: 13 -> 13, of which waited for: 5 -> 3; matrix products, arithmetic and copies ran while one was open for 10% -> 10% of each run, Pallas kernels for 49% -> 51%
where the time goes in v8:
time: 959 us; the launch traced here: 952 us
  Pallas kernels  696 us (73%)
  waiting for transfers between devices  114 us (12%)
  matrix products  52.2 us (5%)
  other arithmetic  38.9 us (4%)
  local copies, waits for them, and re-layouts  22.6 us (2%)
  between operations  15.4 us (2%)
  starting transfers between devices  12.2 us (1%)
    pallas_call x1, Pallas kernels, reduce_dense(): pl.pallas_call(functools.partial(dense_kernel, chips, count, len(grads),...  191 us
    pallas_call x2, Pallas kernels, gather_rows(): pl.pallas_call(functools.partial(gather_kernel, chips, downward, paired,...  171 us
    pallas_call x2, Pallas kernels, scatter_rows(): pl.pallas_call(functools.partial(scatter_kernel, chips, upward, paired, p...  150 us
    ppermute x11, waiting for transfers between devices, swap_pairs(): return lax.ppermute(value, axis, [(i, i ^ distance) for i in range(count)])  114 us
    pallas_call x1, Pallas kernels, gather_weights(): pl.pallas_call(functools.partial(weights_kernel, count, len(slabs), len(s...  58.3 us
    pallas_call x1, Pallas kernels, run_experts(): pl.pallas_call(functools.partial(expert_kernel, blocks), grid=(local,), o...  50.7 us
  transfers between devices with their start and end apart: 13, of which 3 were waited for; matrix products, arithmetic and copies ran while one was open for 10% of the time, Pallas kernels for 51%

profile of v8, /device:TPU:0, one launch (start us, length us, event | category | flops | bytes accessed | tf_op | source)
XLA Modules:
  0.0 952.0 jit_solution(12084470880401541808)
XLA Ops:
  13.6 58.3 %gather_weights.1 = (bf16[4,384,1536]{2,1,0:T(8,128)(2,1)}, bf16[4,384,512]{2,1,0:T(8,128)(2,1)}, bf16[4,384,512]{2,1,0:T(8,128)(2,1)}, bf16[4,64,384]{2,1,0:T(8...) custom-call(bf16[384,1536]{1,0:T(8,128)(2,1)} %refs_0_.2, bf16[384,512]{1,0:T(8,128)(2,1)} %refs_1_.1, ...), custom_call_target="tpu_custom_call" | custom-call | bytes 2000000000 | tf_op jit(solution)/shard_map/gather_weights/pallas_call | solution.py:215
  80.9 66.3 %gather_keys.1 = (bf16[4,1,2,256,1024]{4,3,2,1,0:T(8,128)(2,1)}, bf16[4,384,1536]{2,1,0:T(8,128)(2,1)}, bf16[4,384,2048]{2,1,0:T(8,128)(2,1)}, bf16[4,256,1536]{2,1,0:T(8,128)(2,1)}, s32[8,128]{1,0:T(8,128)}) custom-call(bf16[256,1024]{1,0:T(8,128)(2,1)} %reshape.287.rows_ref, bf16[384,1536]{1,0:T(8,128)(2,1)} %refs_0_.3, ...), custom_call_target="tpu_custom_call" | custom-call | bytes 2000000000 | tf_op jit(solution)/shard_map/gather_keys/pallas_call | solution.py:375
  149.2 4.1 dynamic-slice_bitcast_fusion
  154.7 3.3 fusion.1
  162.6 4.7 convolution_convert_fusion.7.query_ref
  167.3 8.0 attend.1
  176.0 4.5 multiply_reduce_fusion.2
  189.4 4.5 convolution_convert_fusion
  196.9 60.8 %collective-permute-done.1.refs_2_ = bf16[4,2,384,512]{3,2,1,0:T(8,128)(2,1)} collective-permute-done((bf16[4,2,384,512]{3,2,1,0:T(8,128)(2,1)}, bf16[4,2,384,512]{3,2,1,0:T(8,128)(2,1)}, u32[]{:S(2)}, u32[]{:S(2)}) %collective-permute-start.1) | collective-permute-done | bytes 3145760 | tf_op jit(solution)/shard_map/ppermute | solution.py:1273
  257.7 5.6 collective-permute-done.refs_0_.refs_1_
  263.3 104.7 %gather_tokens.1 = (bf16[4,2,2,256,1536]{4,3,2,1,0:T(8,128)(2,1)}, bf16[4,2,384,512]{3,2,1,0:T(8,128)(2,1)}, bf16[4,512,384]{2,1,0:T(8,128)(2,1)}, s32[8,128]{1,0:T(8,128)}) custom-call(bf16[256,1536]{1,0:T(8,128)(2,1)} %copy-done.6, bf16[4,2,384,512]{3,2,1,0:T(8,128)(2,1)} %collective-permute-done.refs_0_.refs_1_, ...), custom_call_target="tpu_custom_call" | custom-call | bytes 2000000000 | tf_op jit(solution)/shard_map/gather_tokens/pallas_call | solution.py:375
  368.0 13.3 %pick_grads.1 = (bf16[4,2,4,80,1536]{4,3,2,1,0:T(8,128)(2,1)}, f32[4,2,4,80,128]{4,3,2,1,0:T(8,128)}, s32[4,2,4,512]{3,2,1,0:T(4,128)}) custom-call(s32[1]{0:T(128)} %bitcast.26.first_ref, bf16[256,256]{1,0:T(8,128)(2,1)} %fusion.38.earlier_ref, bf16[4,2,2,272,1536]{4,3,2,1,0:T(8,128)(2,1)} %bitcast.156), custom_call_target="tpu_custom_call" | custom-call | bytes 4096 | tf_op jit(solution)/shard_map/pick_grads/pallas_call | solution.py:1042
  381.3 12.2 %pick_tokens.1.x_ref = bf16[4,2,4,80,1536]{4,3,2,1,0:T(8,128)(2,1)} custom-call(s32[4,2,4,512]{3,2,1,0:T(4,128)} %get-tuple-element.98.slot_ref.refs_1_, bf16[4,2,2,256,1536]{4,3,2,1,0:T(8,128)(2,1)} %get-tuple-element.102.rows_ref), custom_call_target="tpu_custom_call" | custom-call | bytes 4096 | tf_op jit(solution)/shard_map/pick_tokens/pallas_call | solution.py:1078
  393.5 50.7 %experts.1 = (bf16[4,2,4,80,1536]{4,3,2,1,0:T(8,128)(2,1)}, bf16[4,2,4,80,1536]{4,3,2,1,0:T(8,128)(2,1)}, bf16[2,4,384,512]{3,2,1,0:T(8,128)(2,1)}, bf16[2,4,384...) custom-call(bf16[4,2,4,80,1536]{4,3,2,1,0:T(8,128)(2,1)} %pick_token, ...), custom_call_target="tpu_custom_call" | custom-call | bytes 4096 | tf_op jit(solution)/shard_map/experts/pallas_call | solution.py:1210
  445.2 88.3 %scatter_grads.1 = f32[256,1536]{1,0:T(8,128)} custom-call(bf16[4,2,4,80,1536]{4,3,2,1,0:T(8,128)(2,1)} %get-tuple-element.111.refs_0_, s32[4,2,4,512]{3,2,1,0:T(4,128)} %get-tuple-element.98.slot_ref.refs_1_), custom_call_target="tpu_custom_call" | custom-call | bytes 2000000000 | tf_op jit(solution)/shard_map/scatter_grads/pallas_call | solution.py:593
  533.6 14.2 %spread_results.1 = bf16[4,2,2,256,1536]{4,3,2,1,0:T(8,128)(2,1)} custom-call(s32[4,2,4,512]{3,2,1,0:T(4,128)} %get-tuple-element.98.slot_ref.refs_1_, bf16[4,2,4,80,1536]{4,3,2,1,0:T(8,128)(2,1)} %get-tuple-element.137.rows_ref), custom_call_target="tpu_custom_call" | custom-call | bytes 4096 | tf_op jit(solution)/shard_map/spread_results/pallas_call | solution.py:1113
  555.0 5.2 convolution_convert_fusion.6.grad_ref
  560.2 11.3 %attend_back.1 = (bf16[256,1536]{1,0:T(8,128)(2,1)}, bf16[2048,1024]{1,0:T(8,128)(2,1)}) custom-call(s32[1]{0:T(128)} %bitcast.1.place_ref, bf16[256,1536]{1,0:T(8,128)(2,1)} %convolution_convert_fusion.7.query_ref, bf16[2048,1024]{1,0:T(8,128)(2,1)} %bitcast.155, s32[1,256]{1,0:T(1,128)} %constant_dynamic-slice_fusion.row_ref, s32[2048,1]{1,0:T(8,128)} %copy.55.column_ref, ...), custom_call_target="tpu_custom_call" | custom-call | bytes 4096 | tf_op jit(solution)/shard_map/attend_back/pallas_call | solution.py:956
  571.4 47.8 %collective-permute-done.5.refs_7_ = bf16[2,4,384,512]{3,2,1,0:T(8,128)(2,1)} collective-permute-done((bf16[2,4,384,512]{3,2,1,0:T(8,128)(2,1)}, bf16[2,4,384,512]{3,2,1,0:T(8,128)(2,1)}, u32[]{:S(2)}, u32[]{:S(2)}) %collective-permute-start.5) | collective-permute-done | bytes 3145760 | tf_op jit(solution)/shard_map/ppermute | solution.py:1273
  627.4 61.7 %scatter_keys.1 = f32[256,1024]{1,0:T(8,128)} custom-call(bf16[4,1,2,256,1024]{4,3,2,1,0:T(8,128)(2,1)} %bitcast.160), custom_call_target="tpu_custom_call" | custom-call | bytes 4096 | tf_op jit(solution)/shard_map/scatter_keys/pallas_call | solution.py:593
  690.4 5.0 convolution_convert_fusion.2
  695.4 3.6 convolution_convert_fusion.1
  718.5 190.8 %reduce_dense.1 = (bf16[384,1536]{1,0:T(8,128)(2,1)}, bf16[384,2048]{1,0:T(8,128)(2,1)}, bf16[384,1536]{1,0:T(8,128)(2,1)}, bf16[256,1536]{1,0:T(8,128)(2,1)}, b...) custom-call(bf16[4,384,1536]{2,1,0:T(8,128)(2,1)} %bitcast.152, ...), custom_call_target="tpu_custom_call" | custom-call | bytes 2000000000 | tf_op jit(solution)/shard_map/reduce_dense/pallas_call | solution.py:813
  922.2 16.7 %place_experts.1 = (f32[8,384,512]{2,1,0:T(8,128)}, f32[8,384,512]{2,1,0:T(8,128)}, f32[8,512,384]{2,1,0:T(8,128)}) custom-call(s32[1]{0:T(128)} %bitcast.48.side_ref, bf16[2,4,384,512]{3,2,1,0:T(8,128)(2,1)} %get-tuple-element.123.refs_0_, bf16[2,4,384,512]{3,2,1,0:T(8,128)(2,1)} %get-tuple-element.125.refs_1_, ...), custom_call_target="tpu_custom_call" | custom-call | bytes 4096 | tf_op jit(solution)/shard_map/place_experts/pallas_call | solution.py:1256
  (163 shorter events, 91.2 us)
Async XLA Ops:
  7.2 360.8 %all-gather.3.cloned.1.call-start = ((), (), s32[]{:S(2)}) async-start(), calls=%async_computation.2 | async-start | bytes 15040512 | tf_op jit(solution)/shard_map/all_gather | solution.py:1405
  12.8 59.9 %copy-start = (bf16[1,256,1536]{2,1,0:T(8,128)(2,1)S(1)}, bf16[1,256,1536]{2,1,0:T(8,128)(2,1)}, u32[]{:S(2)}) copy-start(bf16[1,256,1536]{2,1,0:T(8,128)(2,1)} %param.17) | copy-start | bytes 2359300
  147.3 762.0 %reduce-scatter.2.cloned.1.call-start = ((), (), s32[]{:S(2)}) async-start(), calls=%async_computation.1 | async-start | bytes 14155776 | tf_op jit(solution)/shard_map/reduce_scatter | solution.py:1493
  149.2 5.1 copy-start.16
  149.2 5.5 copy-start.17
  153.3 43.6 %collective-permute-start.3 = (bf16[4,512,384]{2,1,0:T(8,128)(2,1)}, bf16[4,512,384]{2,1,0:T(8,128)(2,1)}, u32[]{:S(2)}, u32[]{:S(2)}) collective-permute-start(bf16[4,512,384]{2,1,0:T(8,128)(2,1)} %get-tuple-element.108.refs_4_), channel_id=1, source_target_pairs={{0,2},{1,3},{2,0},{3,1},{4,6},{5,7},{6,4},{7,5},{8,10},{9,11},{10,... | collective-permute-start | bytes 4718600 | tf_op jit(solution)/shard_map/ppermute | solution.py:1273
  158.0 99.6 %collective-permute-start.1 = (bf16[4,2,384,512]{3,2,1,0:T(8,128)(2,1)}, bf16[4,2,384,512]{3,2,1,0:T(8,128)(2,1)}, u32[]{:S(2)}, u32[]{:S(2)}) collective-permute-start(bf16[4,2,384,512]{3,2,1,0:T(8,128)(2,1)} %get-tuple-element.105.refs_0_), channel_id=1, source_target_pairs={{0,2},{1,3},{2,0},{3,1},{4,6},{5,7},{6,4},{7,5},{8,10},{9,11},{10,... | collective-permute-start | bytes 9437192 | tf_op jit(solution)/shard_map/ppermute | solution.py:1273
  159.1 37.8 %collective-permute-start.2 = (bf16[4,512,384]{2,1,0:T(8,128)(2,1)}, bf16[4,512,384]{2,1,0:T(8,128)(2,1)}, u32[]{:S(2)}, u32[]{:S(2)}) collective-permute-start(bf16[4,512,384]{2,1,0:T(8,128)(2,1)} %get-tuple-element.164), channel_id=1, source_target_pairs={{0,1},{1,0},{2,3},{3,2},{4,5},{5,4},{6,7},{7,6},{8,9},{9,8},{10,11... | collective-permute-start | bytes 4718600 | tf_op jit(solution)/shard_map/ppermute | solution.py:1273
  160.1 103.1 %collective-permute-start = (bf16[4,2,384,512]{3,2,1,0:T(8,128)(2,1)}, bf16[4,2,384,512]{3,2,1,0:T(8,128)(2,1)}, u32[]{:S(2)}, u32[]{:S(2)}) collective-permute-start(bf16[4,2,384,512]{3,2,1,0:T(8,128)(2,1)} %get-tuple-element.160), channel_id=1, source_target_pairs={{0,1},{1,0},{2,3},{3,2},{4,5},{5,4},{6,7},{7,6},{8,9},{9,8},{10,11... | collective-permute-start | bytes 9437192 | tf_op jit(solution)/shard_map/ppermute | solution.py:1273
  180.7 8.6 copy-start.6
  444.2 89.4 %collective-permute-start.4 = (bf16[2,4,384,512]{3,2,1,0:T(8,128)(2,1)}, bf16[2,4,384,512]{3,2,1,0:T(8,128)(2,1)S(1)}, u32[]{:S(2)}, u32[]{:S(2)}) collective-permute-start(bf16[2,4,384,512]{3,2,1,0:T(8,128)(2,1)} %get-tuple-element.112), channel_id=1, source_target_pairs={{0,2},{1,3},{2,0},{3,1},{4,6},{5,7},{6,4},{7,5},{8,10},{9,11},{10,... | collective-permute-start | bytes 9437192 | tf_op jit(solution)/shard_map/ppermute | solution.py:1273
  533.6 14.2 %copy-start.11 = (bf16[2,4,384,512]{3,2,1,0:T(8,128)(2,1)}, bf16[2,4,384,512]{3,2,1,0:T(8,128)(2,1)S(1)}, u32[]{:S(2)}) copy-start(bf16[2,4,384,512]{3,2,1,0:T(8,128)(2,1)S(1)} %collective-permute-done.4.refs_6_) | copy-start | bytes 9437188
  547.8 71.4 %collective-permute-start.5 = (bf16[2,4,384,512]{3,2,1,0:T(8,128)(2,1)}, bf16[2,4,384,512]{3,2,1,0:T(8,128)(2,1)}, u32[]{:S(2)}, u32[]{:S(2)}) collective-permute-start(bf16[2,4,384,512]{3,2,1,0:T(8,128)(2,1)} %get-tuple-element.120), channel_id=1, source_target_pairs={{0,2},{1,3},{2,0},{3,1},{4,6},{5,7},{6,4},{7,5},{8,10},{9,11},{10,... | collective-permute-start | bytes 9437192 | tf_op jit(solution)/shard_map/ppermute | solution.py:1273
  551.2 150.5 %collective-permute-start.6 = (bf16[2,4,512,384]{3,2,1,0:T(8,128)(2,1)}, bf16[2,4,512,384]{3,2,1,0:T(8,128)(2,1)}, u32[]{:S(2)}, u32[]{:S(2)}) collective-permute-start(bf16[2,4,512,384]{3,2,1,0:T(8,128)(2,1)} %get-tuple-element.122), channel_id=1, source_target_pairs={{0,2},{1,3},{2,0},{3,1},{4,6},{5,7},{6,4},{7,5},{8,10},{9,11},{10,... | collective-permute-start | bytes 9437192 | tf_op jit(solution)/shard_map/ppermute | solution.py:1273
  554.9 5.2 copy-start.2
  560.2 59.0 %copy-start.9 = (bf16[2,4,384,512]{3,2,1,0:T(8,128)(2,1)S(1)}, bf16[2,4,384,512]{3,2,1,0:T(8,128)(2,1)}, u32[]{:S(2)}) copy-start(bf16[2,4,384,512]{3,2,1,0:T(8,128)(2,1)} %get-tuple-element.125.refs_1_) | copy-start | bytes 9437188
  622.3 79.3 %collective-permute-start.8 = (bf16[4,384,512]{2,1,0:T(8,128)(2,1)}, bf16[4,384,512]{2,1,0:T(8,128)(2,1)}, u32[]{:S(2)}, u32[]{:S(2)}) collective-permute-start(bf16[4,384,512]{2,1,0:T(8,128)(2,1)} %fusion.22), channel_id=1, source_target_pairs={{0,1},{1,0},{2,3},{3,2},{4,5},{5,4},{6,7},{7,6},{8,9},{9,8},{10,11... | collective-permute-start | bytes 4718600 | tf_op jit(solution)/shard_map/ppermute | solution.py:1273
  626.8 74.8 %collective-permute-start.7 = (bf16[4,384,512]{2,1,0:T(8,128)(2,1)}, bf16[4,384,512]{2,1,0:T(8,128)(2,1)}, u32[]{:S(2)}, u32[]{:S(2)}) collective-permute-start(bf16[4,384,512]{2,1,0:T(8,128)(2,1)} %fusion.21), channel_id=1, source_target_pairs={{0,1},{1,0},{2,3},{3,2},{4,5},{5,4},{6,7},{7,6},{8,9},{9,8},{10,11... | collective-permute-start | bytes 4718600 | tf_op jit(solution)/shard_map/ppermute | solution.py:1273
  690.4 5.0 copy-start.3
  690.4 5.0 copy-start.5
  690.4 8.6 slice-start.2
  704.6 204.7 %collective-permute-start.9 = (bf16[4,512,384]{2,1,0:T(8,128)(2,1)}, bf16[4,512,384]{2,1,0:T(8,128)(2,1)}, u32[]{:S(2)}, u32[]{:S(2)}) collective-permute-start(bf16[4,512,384]{2,1,0:T(8,128)(2,1)} %fusion.23), channel_id=1, source_target_pairs={{0,1},{1,0},{2,3},{3,2},{4,5},{5,4},{6,7},{7,6},{8,9},{9,8},{10,11... | collective-permute-start | bytes 4718600 | tf_op jit(solution)/shard_map/ppermute | solution.py:1273
  910.7 30.9 %collective-permute-start.10 = (bf16[256,1536]{1,0:T(8,128)(2,1)S(1)}, bf16[256,1536]{1,0:T(8,128)(2,1)}, u32[]{:S(2)}, u32[]{:S(2)}) collective-permute-start(bf16[256,1536]{1,0:T(8,128)(2,1)S(1)} %dynamic-slice_bitcast_fusion.2), channel_id=1, source_target_pairs={{0,1},{1,0},{2,3},{3,2},{4,5},{5,4},{6,7},{7,6},{8,9},{9,8},{10,11... | collective-permute-start | bytes 2359304 | tf_op jit(solution)/shard_map/ppermute | solution.py:1273
  922.2 17.3 %copy-start.13 = (bf16[384,2048]{1,0:T(8,128)(2,1)S(1)}, bf16[384,2048]{1,0:T(8,128)(2,1)}, u32[]{:S(2)}) copy-start(bf16[384,2048]{1,0:T(8,128)(2,1)} %get-tuple-element.144) | copy-start | bytes 4718596
  (23 other events, 64.0 us)
Sparse Core Ops, SparseCore 0:
  147.4 122.4 all-gather.2
  547.9 171.1 reduce-scatter.1

commit v9 on v8

--- a/solution.py
+++ b/solution.py
@@ -392,12 +392,24 @@
     return results + [zero[0, 0]]
 
 
-def scatter_kernel(chips, upward, paired, pieces, fused, *refs):
+def scatter_kernel(chips, upward, paired, pieces, fused, passed, *refs):
+    refs = list(refs)
+
+    def take(number):
+        taken = refs[:number]
+        del refs[:number]
+        return taken
+
     if fused:
-        rows_ref, slot_ref, out_ref, built, *refs = refs
+        rows_ref, slot_ref = take(2)
         partial_ref = None
     else:
-        partial_ref, out_ref, *refs = refs
+        (partial_ref,) = take(1)
+    moved = take(passed)
+    (out_ref,) = take(1)
+    landed = take(passed)
+    (built,) = take(1) if fused else (None,)
+    pass_send, pass_recv = take(2) if passed else (None, None)
     own, sib, mate, low_in, high_in, load, near_send, near_recv, *refs = refs
     pair_send, pair_recv, up_send, up_recv, down_send, down_recv = refs
     c, w = lax.axis_index("ctx"), lax.axis_index("wt")
@@ -409,7 +421,12 @@
     above = (lax.rem(c + 2, 2 * chips), w)
     below = (lax.rem(c + 2 * chips - 2, 2 * chips), w)
     rows = own.shape[2] // pieces
-    greet([near, above, below] + ([partner] if paired else []))
+    far = [(c, flip(w, 2 * d + 2)) for d in range(passed)]
+    greet([near, above, below] + ([partner] if paired else []) + far)
+
+    def onward(d):
+        return remote(moved[d], landed[d], pass_send.at[d], pass_recv.at[d], far[d])
+
     order = []
     for i in range(chips // 2):
         order += [chips - 1 - i, i]
@@ -506,6 +523,8 @@
             wanted(chip, lambda: begin(chip))
     else:
         begin(order[0])
+    for d in range(passed):
+        onward(d).start()
 
     def meet(chip):
         for which in range(sides):
@@ -577,9 +596,11 @@
 
     for chip in order:
         wanted(chip, lambda: finish(chip))
-
-
-def scatter_rows(partial, collective_id, upward, paired, name, slots=None):
+    for d in range(passed):
+        onward(d).wait()
+
+
+def scatter_rows(partial, collective_id, upward, paired, name, slots=None, moved=()):
     fused = slots is not None
     dma = pltpu.SemaphoreType.DMA
     pieces = 2
@@ -591,13 +612,17 @@
     block = (tokens, width)
     several = pltpu.VMEM((chips, sides) + block, jnp.bfloat16)
     return pl.pallas_call(
-        functools.partial(scatter_kernel, chips, upward, paired, pieces, fused),
-        out_shape=jax.ShapeDtypeStruct(block, jnp.float32),
-        in_specs=[pl.BlockSpec(memory_space=pltpu.VMEM)] * 2
-        if fused
-        else [pl.BlockSpec(memory_space=pl.ANY)],
-        out_specs=pl.BlockSpec(memory_space=pltpu.VMEM),
+        functools.partial(scatter_kernel, chips, upward, paired, pieces, fused, len(moved)),
+        out_shape=[jax.ShapeDtypeStruct(block, jnp.float32)]
+        + [jax.ShapeDtypeStruct(m.shape, m.dtype) for m in moved],
+        in_specs=(
+            [pl.BlockSpec(memory_space=pltpu.VMEM)] * 2 if fused else [pl.BlockSpec(memory_space=pl.ANY)]
+        )
+        + [pl.BlockSpec(memory_space=pl.ANY)] * len(moved),
+        out_specs=[pl.BlockSpec(memory_space=pltpu.VMEM)]
+        + [pl.BlockSpec(memory_space=pl.ANY)] * len(moved),
         scratch_shapes=([several] if fused else [])
+        + ([dma((len(moved),))] * 2 if moved else [])
         + [
             several,
             several,
@@ -614,7 +639,7 @@
         ),
         cost_estimate=LONG if paired else CHEAP,
         name=name,
-    )(*((partial, slots) if fused else (partial,)))
+    )(*((partial, slots) if fused else (partial,)), *moved)
 
 
 def dense_kernel(chips, count, matrices, pieces, *refs):
@@ -1479,17 +1504,21 @@
             received_rows, grad_received, row_gates, tall_blocks, down_blocks
         )
         hop_grads = [rest[i * pairs : (i + 1) * pairs] for i in range(3)]
-    arrived = [[swap_pairs(g[d], "wt", 2 * d) for d in range(1, pairs)] for g in hop_grads]
-    first_arrived, later_arrived = arrived[:1], arrived[1:]
+    later_arrived = [[swap_pairs(g[d], "wt", 2 * d) for d in range(1, pairs)] for g in hop_grads[1:]]
     if chips > 4:
-        routed_grad = scatter_rows(
-            spread_rows(backs, slots, "spread_grads", False), 5, True, True, "scatter_grads"
+        routed_grad, *gate_arrived = scatter_rows(
+            spread_rows(backs, slots, "spread_grads", False),
+            5,
+            True,
+            True,
+            "scatter_grads",
+            moved=hop_grads[0][1:],
         )
     else:
-        routed_grad = scatter_rows(backs, 5, True, True, "scatter_grads", slots)
-    routed_grad, first_arrived, results = lax.optimization_barrier(
-        (routed_grad, first_arrived, results)
-    )
+        routed_grad, *gate_arrived = scatter_rows(
+            backs, 5, True, True, "scatter_grads", slots, hop_grads[0][1:]
+        )
+    routed_grad, results = lax.optimization_barrier((routed_grad, results))
     partial = lax.psum_scatter(
         spread_rows(results, slots, "spread_results", True).reshape(ctx_count, 2, tokens, width_model),
         "ctx",
@@ -1503,7 +1532,7 @@
             total = total + m[1].astype(jnp.float32)
         return swap_pairs(total.astype(jnp.bfloat16), "wt", 1)
 
-    gate_other = crossed(hop_grads[0][0], first_arrived[0])
+    gate_other = crossed(hop_grads[0][0], gate_arrived)
     grad_normed_two = grad_shared_rows + routed_grad
     grad_gain_two = jnp.sum(grad_normed_two * middle * scale_two, axis=0)
     scaled_two = grad_normed_two * gain_two_full
@@ -1522,20 +1551,18 @@
     grad_queries, grad_parts = attend_back(
         place, queries, both, query_seg[None, :], seg_column, attended_full, grad_attended, logs
     )
-    grad_parts, up_arrived = lax.optimization_barrier((grad_parts, later_arrived[0]))
-    up_other = crossed(hop_grads[1][0], up_arrived)
-    grad_both = scatter_rows(
+    (grad_both,) = scatter_rows(
         grad_parts.reshape(chips, 1, 2, tokens, 2 * kv_width),
         6,
         False,
         False,
         "scatter_keys",
-    ).astype(jnp.bfloat16)
-    grad_both, down_arrived, gate_other, up_other = lax.optimization_barrier(
-        (grad_both, later_arrived[1], gate_other, up_other)
-    )
-    arrived = [first_arrived[0], up_arrived, down_arrived]
-    down_other = crossed(hop_grads[2][0], down_arrived)
+    )
+    grad_both = grad_both.astype(jnp.bfloat16)
+    grad_both, gate_other, up_arrived = lax.optimization_barrier(
+        (grad_both, gate_other, later_arrived[0])
+    )
+    up_other = crossed(hop_grads[1][0], up_arrived)
     grad_both = grad_both.reshape(tokens, KV_HEADS, 2, HEAD_DIM)
     grad_keys = grad_both[:, :, 0].reshape(tokens, kv_width)
     grad_values = grad_both[:, :, 1].reshape(tokens, kv_width)
@@ -1573,8 +1600,13 @@
         weight_grad(grad_values),
         gain_grads,
     ]
+    dense_grads, down_arrived = lax.optimization_barrier((dense_grads, later_arrived[1]))
+    arrived = [gate_arrived, up_arrived, down_arrived]
+    down_other = crossed(hop_grads[2][0], down_arrived)
     totals = reduce_dense(dense_grads)
-    totals, down_other, partial = lax.optimization_barrier((totals, down_other, partial))
+    totals, up_other, down_other, partial = lax.optimization_barrier(
+        (totals, up_other, down_other, partial)
+    )
     others = [gate_other, up_other, down_other]
     kept, given = own_and_other(partial, side)
     crossing = swap_pairs(given, "wt", 1)

time: 959 us -> 962 us (level)
  Pallas kernels: 696 us -> 738 us
  waiting for transfers between devices: 114 us -> 82.1 us
    ppermute x11 -> x10, waiting for transfers between devices: 114 us -> 82 us  [swap_pairs(): return lax.ppermute(value, axis, [(i, i ^ distance) for i in range(count)])]
    pallas_call x1, Pallas kernels: 191 us -> 220 us  [reduce_dense(): pl.pallas_call(functools.partial(dense_kernel, chips, count, len(grads),...]
    pallas_call x2, Pallas kernels: 150 us -> 163 us  [scatter_rows(): pl.pallas_call(functools.partial(scatter_kernel, chips, upward, paired, p...]
  transfers between devices with their start and end apart: 13 -> 12, of which waited for: 3 -> 4; matrix products, arithmetic and copies ran while one was open for 10% -> 9% of each run, Pallas kernels for 51% -> 46%
where the time goes in v9:
time: 962 us; the launch traced here: 956 us
  Pallas kernels  738 us (77%)
  waiting for transfers between devices  82.1 us (9%)
  matrix products  49.3 us (5%)
  other arithmetic  36.3 us (4%)
  local copies, waits for them, and re-layouts  23.6 us (2%)
  between operations  15.4 us (2%)
  starting transfers between devices  11.1 us (1%)
    pallas_call x1, Pallas kernels, reduce_dense(): pl.pallas_call(functools.partial(dense_kernel, chips, count, len(grads),...  220 us
    pallas_call x2, Pallas kernels, gather_rows(): pl.pallas_call(functools.partial(gather_kernel, chips, downward, paired,...  171 us
    pallas_call x2, Pallas kernels, scatter_rows(): pl.pallas_call(functools.partial(scatter_kernel, chips, upward, paired, p...  163 us
    ppermute x10, waiting for transfers between devices, swap_pairs(): return lax.ppermute(value, axis, [(i, i ^ distance) for i in range(count)])  82 us
    pallas_call x1, Pallas kernels, gather_weights(): pl.pallas_call(functools.partial(weights_kernel, count, len(slabs), len(s...  58.3 us
    pallas_call x1, Pallas kernels, run_experts(): pl.pallas_call(functools.partial(expert_kernel, blocks), grid=(local,), o...  50.9 us
  transfers between devices with their start and end apart: 12, of which 4 were waited for; matrix products, arithmetic and copies ran while one was open for 9% of the time, Pallas kernels for 46%

profile of v9, /device:TPU:0, one launch (start us, length us, event | category | flops | bytes accessed | tf_op | source)
XLA Modules:
  0.0 956.1 jit_solution(1150569072011129346)
XLA Ops:
  13.6 58.3 %gather_weights.1 = (bf16[4,384,1536]{2,1,0:T(8,128)(2,1)}, bf16[4,384,512]{2,1,0:T(8,128)(2,1)}, bf16[4,384,512]{2,1,0:T(8,128)(2,1)}, bf16[4,64,384]{2,1,0:T(8...) custom-call(bf16[384,1536]{1,0:T(8,128)(2,1)} %refs_0_.2, bf16[384,512]{1,0:T(8,128)(2,1)} %refs_1_.1, ...), custom_call_target="tpu_custom_call" | custom-call | bytes 2000000000 | tf_op jit(solution)/shard_map/gather_weights/pallas_call | solution.py:215
  82.2 66.3 %gather_keys.1 = (bf16[4,1,2,256,1024]{4,3,2,1,0:T(8,128)(2,1)}, bf16[4,384,1536]{2,1,0:T(8,128)(2,1)}, bf16[4,384,2048]{2,1,0:T(8,128)(2,1)}, bf16[4,256,1536]{2,1,0:T(8,128)(2,1)}, s32[8,128]{1,0:T(8,128)}) custom-call(bf16[256,1024]{1,0:T(8,128)(2,1)} %reshape.293.rows_ref, bf16[384,1536]{1,0:T(8,128)(2,1)} %refs_0_.3, ...), custom_call_target="tpu_custom_call" | custom-call | bytes 2000000000 | tf_op jit(solution)/shard_map/gather_keys/pallas_call | solution.py:375
  150.5 4.1 dynamic-slice_bitcast_fusion
  155.9 3.4 fusion.1
  163.9 4.8 convolution_convert_fusion.7.query_ref
  168.7 8.0 attend.1
  189.4 4.5 convolution_convert_fusion
  197.9 61.0 %collective-permute-done.1.refs_2_ = bf16[4,2,384,512]{3,2,1,0:T(8,128)(2,1)} collective-permute-done((bf16[4,2,384,512]{3,2,1,0:T(8,128)(2,1)}, bf16[4,2,384,512]{3,2,1,0:T(8,128)(2,1)}, u32[]{:S(2)}, u32[]{:S(2)}) %collective-permute-start.1) | collective-permute-done | bytes 3145760 | tf_op jit(solution)/shard_map/ppermute | solution.py:1298
  258.9 5.6 collective-permute-done.refs_0_.refs_1_
  264.5 104.7 %gather_tokens.1 = (bf16[4,2,2,256,1536]{4,3,2,1,0:T(8,128)(2,1)}, bf16[4,2,384,512]{3,2,1,0:T(8,128)(2,1)}, bf16[4,512,384]{2,1,0:T(8,128)(2,1)}, s32[8,128]{1,0:T(8,128)}) custom-call(bf16[256,1536]{1,0:T(8,128)(2,1)} %copy-done.5, bf16[4,2,384,512]{3,2,1,0:T(8,128)(2,1)} %collective-permute-done.refs_0_.refs_1_, ...), custom_call_target="tpu_custom_call" | custom-call | bytes 2000000000 | tf_op jit(solution)/shard_map/gather_tokens/pallas_call | solution.py:375
  369.2 13.3 %pick_grads.1 = (bf16[4,2,4,80,1536]{4,3,2,1,0:T(8,128)(2,1)}, f32[4,2,4,80,128]{4,3,2,1,0:T(8,128)}, s32[4,2,4,512]{3,2,1,0:T(4,128)}) custom-call(s32[1]{0:T(128)} %bitcast.26.first_ref, bf16[256,256]{1,0:T(8,128)(2,1)} %fusion.38.earlier_ref, bf16[4,2,2,272,1536]{4,3,2,1,0:T(8,128)(2,1)} %bitcast.157), custom_call_target="tpu_custom_call" | custom-call | bytes 4096 | tf_op jit(solution)/shard_map/pick_grads/pallas_call | solution.py:1067
  382.5 12.3 %pick_tokens.1.x_ref = bf16[4,2,4,80,1536]{4,3,2,1,0:T(8,128)(2,1)} custom-call(s32[4,2,4,512]{3,2,1,0:T(4,128)} %get-tuple-element.105.slot_ref.refs_1_, bf16[4,2,2,256,1536]{4,3,2,1,0:T(8,128)(2,1)} %get-tuple-element.109.rows_ref), custom_call_target="tpu_custom_call" | custom-call | bytes 4096 | tf_op jit(solution)/shard_map/pick_tokens/pallas_call | solution.py:1103
  394.8 50.9 %experts.1 = (bf16[4,2,4,80,1536]{4,3,2,1,0:T(8,128)(2,1)}, bf16[4,2,4,80,1536]{4,3,2,1,0:T(8,128)(2,1)}, bf16[2,4,384,512]{3,2,1,0:T(8,128)(2,1)}, bf16[2,4,384...) custom-call(bf16[4,2,4,80,1536]{4,3,2,1,0:T(8,128)(2,1)} %pick_token, ...), custom_call_target="tpu_custom_call" | custom-call | bytes 4096 | tf_op jit(solution)/shard_map/experts/pallas_call | solution.py:1235
  445.8 88.6 %scatter_grads.1 = (f32[256,1536]{1,0:T(8,128)}, bf16[2,4,384,512]{3,2,1,0:T(8,128)(2,1)}) custom-call(bf16[4,2,4,80,1536]{4,3,2,1,0:T(8,128)(2,1)} %get-tuple-element.118.refs_0_, s32[4,2,4,512]{3,2,1,0:T(4,128)} %get-tuple-element.105.slot_ref.refs_1_, bf16[2,4,384,512]{3,2,1,0:T(8,128)(2,1)} %get-tuple-element.119.refs_2_), custom_call_target="tpu_custom_call" | custom-call | bytes 2000000000 | tf_op jit(solution)/shard_map/scatter_grads/pallas_call | solution.py:614
  534.4 13.3 %spread_results.1 = bf16[4,2,2,256,1536]{4,3,2,1,0:T(8,128)(2,1)} custom-call(s32[4,2,4,512]{3,2,1,0:T(4,128)} %get-tuple-element.105.slot_ref.refs_1_, bf16[4,2,4,80,1536]{4,3,2,1,0:T(8,128)(2,1)} %get-tuple-element.151.rows_ref), custom_call_target="tpu_custom_call" | custom-call | bytes 4096 | tf_op jit(solution)/shard_map/spread_results/pallas_call | solution.py:1138
  550.9 3.6 fusion.21
  560.3 11.6 %attend_back.1 = (bf16[256,1536]{1,0:T(8,128)(2,1)}, bf16[2048,1024]{1,0:T(8,128)(2,1)}) custom-call(s32[1]{0:T(128)} %bitcast.1.place_ref, bf16[256,1536]{1,0:T(8,128)(2,1)} %convolution_convert_fusion.7.query_ref, bf16[2048,1024]{1,0:T(8,128)(2,1)} %bitcast.156, s32[1,256]{1,0:T(1,128)} %constant_dynamic-slice_fusion.row_ref, s32[2048,1]{1,0:T(8,128)} %copy.65.column_ref, ...), custom_call_target="tpu_custom_call" | custom-call | bytes 4096 | tf_op jit(solution)/shard_map/attend_back/pallas_call | solution.py:981
  571.9 74.7 %scatter_keys.1 = f32[256,1024]{1,0:T(8,128)} custom-call(bf16[4,1,2,256,1024]{4,3,2,1,0:T(8,128)(2,1)} %bitcast.161), custom_call_target="tpu_custom_call" | custom-call | bytes 4096 | tf_op jit(solution)/shard_map/scatter_keys/pallas_call | solution.py:614
  648.0 5.0 convolution_convert_fusion.2
  653.0 3.6 convolution_convert_fusion.1
  672.1 14.4 %collective-permute-done.6.refs_8_ = bf16[2,4,512,384]{3,2,1,0:T(8,128)(2,1)} collective-permute-done((bf16[2,4,512,384]{3,2,1,0:T(8,128)(2,1)}, bf16[2,4,512,384]{3,2,1,0:T(8,128)(2,1)}, u32[]{:S(2)}, u32[]{:S(2)}) %collective-permute-start.6) | collective-permute-done | bytes 3145760 | tf_op jit(solution)/shard_map/ppermute | solution.py:1298
  694.6 219.7 %reduce_dense.1 = (bf16[384,1536]{1,0:T(8,128)(2,1)}, bf16[384,2048]{1,0:T(8,128)(2,1)}, bf16[384,1536]{1,0:T(8,128)(2,1)}, bf16[256,1536]{1,0:T(8,128)(2,1)}, b...) custom-call(bf16[4,384,1536]{2,1,0:T(8,128)(2,1)} %bitcast.153, ...), custom_call_target="tpu_custom_call" | custom-call | bytes 2000000000 | tf_op jit(solution)/shard_map/reduce_dense/pallas_call | solution.py:838
  917.6 3.1 fusion.17
  927.4 16.7 %place_experts.1 = (f32[8,384,512]{2,1,0:T(8,128)}, f32[8,384,512]{2,1,0:T(8,128)}, f32[8,512,384]{2,1,0:T(8,128)}) custom-call(s32[1]{0:T(128)} %bitcast.49.side_ref, bf16[2,4,384,512]{3,2,1,0:T(8,128)(2,1)} %get-tuple-element.128.refs_0_, bf16[2,4,384,512]{3,2,1,0:T(8,128)(2,1)} %get-tuple-element.147.refs_1_, ...), custom_call_target="tpu_custom_call" | custom-call | bytes 4096 | tf_op jit(solution)/shard_map/place_experts/pallas_call | solution.py:1281
  (165 shorter events, 89.2 us)
Async XLA Ops:
  7.2 362.1 %all-gather.3.cloned.1.call-start = ((), (), s32[]{:S(2)}) async-start(), calls=%async_computation.2 | async-start | bytes 15040512 | tf_op jit(solution)/shard_map/all_gather | solution.py:1430
  12.8 59.9 %copy-start = (bf16[1,256,1536]{2,1,0:T(8,128)(2,1)S(1)}, bf16[1,256,1536]{2,1,0:T(8,128)(2,1)}, u32[]{:S(2)}) copy-start(bf16[1,256,1536]{2,1,0:T(8,128)(2,1)} %param.17) | copy-start | bytes 2359300
  148.5 765.8 %reduce-scatter.2.cloned.1.call-start = ((), (), s32[]{:S(2)}) async-start(), calls=%async_computation.1 | async-start | bytes 14155776 | tf_op jit(solution)/shard_map/reduce_scatter | solution.py:1522
  150.4 5.1 copy-start.14
  150.5 5.5 copy-start.15
  154.5 42.4 %collective-permute-start.3 = (bf16[4,512,384]{2,1,0:T(8,128)(2,1)}, bf16[4,512,384]{2,1,0:T(8,128)(2,1)}, u32[]{:S(2)}, u32[]{:S(2)}) collective-permute-start(bf16[4,512,384]{2,1,0:T(8,128)(2,1)} %get-tuple-element.115.refs_4_), channel_id=1, source_target_pairs={{0,2},{1,3},{2,0},{3,1},{4,6},{5,7},{6,4},{7,5},{8,10},{9,11},{10,... | collective-permute-start | bytes 4718600 | tf_op jit(solution)/shard_map/ppermute | solution.py:1298
  155.9 21.5 %slice-start.4 = ((s8[4718592]{0:T(1024)(128)(4,1)}), s8[524288]{0:T(1024)(128)(4,1)S(1)}, s32[]{:S(2)}) async-start(s8[4718592]{0:T(1024)(128)(4,1)} %bitcast.188), calls=%async_computation.7 | async-start | bytes 1048576
  159.3 99.6 %collective-permute-start.1 = (bf16[4,2,384,512]{3,2,1,0:T(8,128)(2,1)}, bf16[4,2,384,512]{3,2,1,0:T(8,128)(2,1)}, u32[]{:S(2)}, u32[]{:S(2)}) collective-permute-start(bf16[4,2,384,512]{3,2,1,0:T(8,128)(2,1)} %get-tuple-element.112.refs_0_), channel_id=1, source_target_pairs={{0,2},{1,3},{2,0},{3,1},{4,6},{5,7},{6,4},{7,5},{8,10},{9,11},{10,... | collective-permute-start | bytes 9437192 | tf_op jit(solution)/shard_map/ppermute | solution.py:1298
  160.3 37.6 %collective-permute-start.2 = (bf16[4,512,384]{2,1,0:T(8,128)(2,1)}, bf16[4,512,384]{2,1,0:T(8,128)(2,1)}, u32[]{:S(2)}, u32[]{:S(2)}) collective-permute-start(bf16[4,512,384]{2,1,0:T(8,128)(2,1)} %get-tuple-element.178), channel_id=1, source_target_pairs={{0,1},{1,0},{2,3},{3,2},{4,5},{5,4},{6,7},{7,6},{8,9},{9,8},{10,11... | collective-permute-start | bytes 4718600 | tf_op jit(solution)/shard_map/ppermute | solution.py:1298
  161.4 103.1 %collective-permute-start = (bf16[4,2,384,512]{3,2,1,0:T(8,128)(2,1)}, bf16[4,2,384,512]{3,2,1,0:T(8,128)(2,1)}, u32[]{:S(2)}, u32[]{:S(2)}) collective-permute-start(bf16[4,2,384,512]{3,2,1,0:T(8,128)(2,1)} %get-tuple-element.174), channel_id=1, source_target_pairs={{0,1},{1,0},{2,3},{3,2},{4,5},{5,4},{6,7},{7,6},{8,9},{9,8},{10,11... | collective-permute-start | bytes 9437192 | tf_op jit(solution)/shard_map/ppermute | solution.py:1298
  163.9 13.5 %slice-start.5 = ((s8[4718592]{0:T(1024)(128)(4,1)}), s8[4194304]{0:T(1024)(128)(4,1)S(1)}, s32[]{:S(2)}) async-start(s8[4718592]{0:T(1024)(128)(4,1)} %bitcast.188), calls=%async_computation.8 | async-start | bytes 8388608
  180.7 8.7 copy-start.5
  550.3 108.9 %collective-permute-start.5 = (bf16[2,4,384,512]{3,2,1,0:T(8,128)(2,1)}, bf16[2,4,384,512]{3,2,1,0:T(8,128)(2,1)}, u32[]{:S(2)}, u32[]{:S(2)}) collective-permute-start(bf16[2,4,384,512]{3,2,1,0:T(8,128)(2,1)} %get-tuple-element.130), channel_id=1, source_target_pairs={{0,2},{1,3},{2,0},{3,1},{4,6},{5,7},{6,4},{7,5},{8,10},{9,11},{10,... | collective-permute-start | bytes 9437192 | tf_op jit(solution)/shard_map/ppermute | solution.py:1298
  550.9 6.0 copy-start.9
  550.9 6.0 copy-start.10
  550.9 7.1 slice-start.6
  554.5 104.6 %collective-permute-start.4 = (bf16[4,384,512]{2,1,0:T(8,128)(2,1)}, bf16[4,384,512]{2,1,0:T(8,128)(2,1)}, u32[]{:S(2)}, u32[]{:S(2)}) collective-permute-start(bf16[4,384,512]{2,1,0:T(8,128)(2,1)} %fusion.21), channel_id=1, source_target_pairs={{0,1},{1,0},{2,3},{3,2},{4,5},{5,4},{6,7},{7,6},{8,9},{9,8},{10,11... | collective-permute-start | bytes 4718600 | tf_op jit(solution)/shard_map/ppermute | solution.py:1298
  556.0 130.5 %collective-permute-start.6 = (bf16[2,4,512,384]{3,2,1,0:T(8,128)(2,1)}, bf16[2,4,512,384]{3,2,1,0:T(8,128)(2,1)}, u32[]{:S(2)}, u32[]{:S(2)}) collective-permute-start(bf16[2,4,512,384]{3,2,1,0:T(8,128)(2,1)} %get-tuple-element.132), channel_id=1, source_target_pairs={{0,2},{1,3},{2,0},{3,1},{4,6},{5,7},{6,4},{7,5},{8,10},{9,11},{10,... | collective-permute-start | bytes 9437192 | tf_op jit(solution)/shard_map/ppermute | solution.py:1298
  647.9 8.6 slice-start.2
  668.4 18.1 %copy-start.8 = (bf16[2,4,512,384]{3,2,1,0:T(8,128)(2,1)S(1)}, bf16[2,4,512,384]{3,2,1,0:T(8,128)(2,1)}, u32[]{:S(2)}) copy-start(bf16[2,4,512,384]{3,2,1,0:T(8,128)(2,1)} %get-tuple-element.149.refs_2_) | copy-start | bytes 9437188
  689.6 224.7 %collective-permute-start.8 = (bf16[4,512,384]{2,1,0:T(8,128)(2,1)}, bf16[4,512,384]{2,1,0:T(8,128)(2,1)}, u32[]{:S(2)}, u32[]{:S(2)}) collective-permute-start(bf16[4,512,384]{2,1,0:T(8,128)(2,1)} %fusion.23), channel_id=1, source_target_pairs={{0,1},{1,0},{2,3},{3,2},{4,5},{5,4},{6,7},{7,6},{8,9},{9,8},{10,11... | collective-permute-start | bytes 4718600 | tf_op jit(solution)/shard_map/ppermute | solution.py:1298
  693.5 220.8 %collective-permute-start.7 = (bf16[4,384,512]{2,1,0:T(8,128)(2,1)}, bf16[4,384,512]{2,1,0:T(8,128)(2,1)}, u32[]{:S(2)}, u32[]{:S(2)}) collective-permute-start(bf16[4,384,512]{2,1,0:T(8,128)(2,1)} %fusion.22), channel_id=1, source_target_pairs={{0,1},{1,0},{2,3},{3,2},{4,5},{5,4},{6,7},{7,6},{8,9},{9,8},{10,11... | collective-permute-start | bytes 4718600 | tf_op jit(solution)/shard_map/ppermute | solution.py:1298
  915.7 31.1 %collective-permute-start.9 = (bf16[256,1536]{1,0:T(8,128)(2,1)S(1)}, bf16[256,1536]{1,0:T(8,128)(2,1)S(1)}, u32[]{:S(2)}, u32[]{:S(2)}) collective-permute-start(bf16[256,1536]{1,0:T(8,128)(2,1)S(1)} %dynamic-slice_bitcast_fusion.2), channel_id=1, source_target_pairs={{0,1},{1,0},{2,3},{3,2},{4,5},{5,4},{6,7},{7,6},{8,9},{9,8},{10,11... | collective-permute-start | bytes 2359304 | tf_op jit(solution)/shard_map/ppermute | solution.py:1298
  927.4 17.3 %copy-start.11 = (bf16[384,2048]{1,0:T(8,128)(2,1)S(1)}, bf16[384,2048]{1,0:T(8,128)(2,1)}, u32[]{:S(2)}) copy-start(bf16[384,2048]{1,0:T(8,128)(2,1)} %get-tuple-element.158) | copy-start | bytes 4718596
  (23 other events, 63.0 us)
Sparse Core Ops, SparseCore 0:
  148.7 122.4 all-gather.2
  547.8 170.5 reduce-scatter.1

commit v10 on v9

--- a/solution.py
+++ b/solution.py
@@ -392,7 +392,7 @@
     return results + [zero[0, 0]]
 
 
-def scatter_kernel(chips, upward, paired, pieces, fused, passed, *refs):
+def scatter_kernel(chips, upward, paired, pieces, fused, passed, extra, *refs):
     refs = list(refs)
 
     def take(number):
@@ -406,9 +406,13 @@
     else:
         (partial_ref,) = take(1)
     moved = take(passed)
+    (extra_ref,) = take(1) if extra else (None,)
     (out_ref,) = take(1)
     landed = take(passed)
+    (spread_ref, extra_stage, extra_sem) = take(1) + [None, None] if extra else (None, None, None)
     (built,) = take(1) if fused else (None,)
+    if extra:
+        extra_stage, extra_sem = take(2)
     pass_send, pass_recv = take(2) if passed else (None, None)
     own, sib, mate, low_in, high_in, load, near_send, near_recv, *refs = refs
     pair_send, pair_recv, up_send, up_recv, down_send, down_recv = refs
@@ -489,8 +493,9 @@
         spot = own.at[chip, which, cut(piece)]
         spot[...] = spot[...] + other[...]
 
-    def spread(chip, which, parity, spot):
-        local, depth, width = rows_ref.shape[2:]
+    def spread(chip, which, parity, spot, source=None):
+        source = rows_ref if source is None else source
+        local, depth, width = source.shape[2:]
         tokens = spot.shape[0]
         span = pl.ds(pl.multiple_of(parity * tokens, tokens), tokens)
         place = lax.broadcasted_iota(jnp.int32, (depth, tokens), 0)
@@ -503,10 +508,24 @@
         ).astype(jnp.bfloat16)
         spot[...] = lax.dot_general(
             ones,
-            rows_ref[chip, which].reshape(local * depth, width),
+            source[chip, which].reshape(local * depth, width),
             (((0,), (0,)), ((), ())),
             preferred_element_type=jnp.float32,
         ).astype(jnp.bfloat16)
+
+    def aside(chip, which, parity):
+        slot = which * 2 + parity
+        return pltpu.make_async_copy(
+            extra_stage.at[slot], spread_ref.at[chip, parity, which], extra_sem.at[slot]
+        )
+
+    def put_aside(i, chip):
+        for which in range(sides):
+            for parity in range(2):
+                if i > 0:
+                    aside(order[i - 1], which, parity).wait()
+                spread(chip, which, parity, extra_stage.at[which * 2 + parity], extra_ref)
+                aside(chip, which, parity).start()
 
     def begin(chip):
         for which in range(sides):
@@ -568,6 +587,8 @@
         wanted(chip, lambda: meet(chip))
         if i >= 1:
             wanted(order[i - 1], lambda: travel(order[i - 1]))
+        if extra:
+            put_aside(i, chip)
     wanted(order[-1], lambda: travel(order[-1]))
     for piece in range(pieces):
         out_ref[cut(piece), :] = own.at[z, side, cut(piece)][...].astype(jnp.float32)
@@ -598,9 +619,13 @@
         wanted(chip, lambda: finish(chip))
     for d in range(passed):
         onward(d).wait()
-
-
-def scatter_rows(partial, collective_id, upward, paired, name, slots=None, moved=()):
+    if extra:
+        for which in range(sides):
+            for parity in range(2):
+                aside(order[-1], which, parity).wait()
+
+
+def scatter_rows(partial, collective_id, upward, paired, name, slots=None, moved=(), extra=None):
     fused = slots is not None
     dma = pltpu.SemaphoreType.DMA
     pieces = 2
@@ -610,18 +635,22 @@
     else:
         chips, sides, _, tokens, width = partial.shape
     block = (tokens, width)
+    has_extra = int(extra is not None)
     several = pltpu.VMEM((chips, sides) + block, jnp.bfloat16)
     return pl.pallas_call(
-        functools.partial(scatter_kernel, chips, upward, paired, pieces, fused, len(moved)),
+        functools.partial(scatter_kernel, chips, upward, paired, pieces, fused, len(moved), extra is not None),
         out_shape=[jax.ShapeDtypeStruct(block, jnp.float32)]
-        + [jax.ShapeDtypeStruct(m.shape, m.dtype) for m in moved],
+        + [jax.ShapeDtypeStruct(m.shape, m.dtype) for m in moved]
+        + ([jax.ShapeDtypeStruct((chips, 2, sides) + block, jnp.bfloat16)] if has_extra else []),
         in_specs=(
             [pl.BlockSpec(memory_space=pltpu.VMEM)] * 2 if fused else [pl.BlockSpec(memory_space=pl.ANY)]
         )
-        + [pl.BlockSpec(memory_space=pl.ANY)] * len(moved),
+        + [pl.BlockSpec(memory_space=pl.ANY)] * len(moved)
+        + [pl.BlockSpec(memory_space=pltpu.VMEM)] * has_extra,
         out_specs=[pl.BlockSpec(memory_space=pltpu.VMEM)]
-        + [pl.BlockSpec(memory_space=pl.ANY)] * len(moved),
+        + [pl.BlockSpec(memory_space=pl.ANY)] * (len(moved) + has_extra),
         scratch_shapes=([several] if fused else [])
+        + ([pltpu.VMEM((2 * sides,) + block, jnp.bfloat16), dma((2 * sides,))] if has_extra else [])
         + ([dma((len(moved),))] * 2 if moved else [])
         + [
             several,
@@ -639,10 +668,10 @@
         ),
         cost_estimate=LONG if paired else CHEAP,
         name=name,
-    )(*((partial, slots) if fused else (partial,)), *moved)
-
-
-def dense_kernel(chips, count, matrices, pieces, *refs):
+    )(*((partial, slots) if fused else (partial,)), *moved, *([extra] if has_extra else []))
+
+
+def dense_kernel(chips, count, matrices, pieces, crossings, *refs):
     refs = list(refs)
 
     def take(number):
@@ -650,7 +679,8 @@
         del refs[:number]
         return taken
 
-    grads, outs = take(matrices), take(matrices)
+    grads, moved, outs, landed = take(matrices), take(crossings), take(matrices), take(crossings)
+    cross_send, cross_recv = take(2)
     own, sib, mates, low, final = (take(matrices) for _ in range(5))
     (load, near_send, near_recv, send, recv, low_send, low_recv, back_send, back_recv, last_send, last_recv, keep) = refs
     c, w = lax.axis_index("ctx"), lax.axis_index("wt")
@@ -671,6 +701,11 @@
         for r in rest:
             offsets += [o ^ r for o in offsets]
         return offsets
+
+    def cross(i):
+        return remote(
+            moved[i], landed[i], cross_send.at[i], cross_recv.at[i], (c, flip(w, 1))
+        )
 
     def span(j, parity=None):
         m, first, rows, _ = pieces[j]
@@ -798,6 +833,9 @@
     for t in range(number + 2 * last + behind):
         if t < number:
             share(t)
+        if t == number:
+            for i in range(crossings):
+                cross(i).start()
         for stage in range(len(dims)):
             if 0 <= t - lead - gap * stage < number:
                 collect(t - lead - gap * stage, stage)
@@ -809,6 +847,8 @@
                 pl.when(line(j)[0] == hop)(lambda: accumulate(j))
             if hop > last:
                 pl.when(line(j)[0] == 2 * last - hop)(lambda: spread(j))
+    for i in range(crossings):
+        cross(i).wait()
     for j in range(number):
         place = line(j)[0]
         hand(j).wait_send()
@@ -822,7 +862,7 @@
         store(j).wait()
 
 
-def reduce_dense(grads):
+def reduce_dense(grads, moved):
     count = lax.axis_size("wt")
     chips = lax.axis_size("ctx") // 2
     shapes = [(g.shape[0] // count, g.shape[1]) for g in grads]
@@ -836,11 +876,13 @@
     dma = pltpu.SemaphoreType.DMA
     one, many = dma((len(pieces),)), dma((len(pieces), count - 1))
     return pl.pallas_call(
-        functools.partial(dense_kernel, chips, count, len(grads), tuple(pieces)),
-        out_shape=[jax.ShapeDtypeStruct(s, jnp.bfloat16) for s in shapes],
-        in_specs=[pl.BlockSpec(memory_space=pl.ANY)] * len(grads),
-        out_specs=[pl.BlockSpec(memory_space=pl.ANY)] * len(grads),
-        scratch_shapes=[pltpu.VMEM((count,) + h, jnp.bfloat16) for h in halves]
+        functools.partial(dense_kernel, chips, count, len(grads), tuple(pieces), len(moved)),
+        out_shape=[jax.ShapeDtypeStruct(s, jnp.bfloat16) for s in shapes]
+        + [jax.ShapeDtypeStruct(m.shape, m.dtype) for m in moved],
+        in_specs=[pl.BlockSpec(memory_space=pl.ANY)] * (len(grads) + len(moved)),
+        out_specs=[pl.BlockSpec(memory_space=pl.ANY)] * (len(grads) + len(moved)),
+        scratch_shapes=[dma((len(moved),))] * 2
+        + [pltpu.VMEM((count,) + h, jnp.bfloat16) for h in halves]
         + [pltpu.VMEM((count,) + h, jnp.bfloat16) for h in halves]
         + [pltpu.VMEM((count - 1,) + h, jnp.bfloat16) for h in halves]
         + [pltpu.VMEM(h, jnp.bfloat16) for h in halves]
@@ -851,7 +893,7 @@
         ),
         cost_estimate=LONG,
         name="reduce_dense",
-    )(*[g.reshape((count,) + s) for g, s in zip(grads, shapes)])
+    )(*[g.reshape((count,) + s) for g, s in zip(grads, shapes)], *moved)
 
 
 def dot_of(a, b, left, right):
@@ -1514,25 +1556,26 @@
             "scatter_grads",
             moved=hop_grads[0][1:],
         )
+        routed_grad, results = lax.optimization_barrier((routed_grad, results))
+        spread = spread_rows(results, slots, "spread_results", True)
     else:
-        routed_grad, *gate_arrived = scatter_rows(
-            backs, 5, True, True, "scatter_grads", slots, hop_grads[0][1:]
-        )
-    routed_grad, results = lax.optimization_barrier((routed_grad, results))
+        routed_grad, *gate_arrived, spread = scatter_rows(
+            backs, 5, True, True, "scatter_grads", slots, hop_grads[0][1:], results
+        )
     partial = lax.psum_scatter(
-        spread_rows(results, slots, "spread_results", True).reshape(ctx_count, 2, tokens, width_model),
+        spread.reshape(ctx_count, 2, tokens, width_model),
         "ctx",
         scatter_dimension=0,
         tiled=True,
     )[0]
 
-    def crossed(own, more):
+    def across(own, more):
         total = own[1].astype(jnp.float32)
         for m in more:
             total = total + m[1].astype(jnp.float32)
-        return swap_pairs(total.astype(jnp.bfloat16), "wt", 1)
-
-    gate_other = crossed(hop_grads[0][0], gate_arrived)
+        return total.astype(jnp.bfloat16)
+
+    gate_other = swap_pairs(across(hop_grads[0][0], gate_arrived), "wt", 1)
     grad_normed_two = grad_shared_rows + routed_grad
     grad_gain_two = jnp.sum(grad_normed_two * middle * scale_two, axis=0)
     scaled_two = grad_normed_two * gain_two_full
@@ -1562,7 +1605,7 @@
     grad_both, gate_other, up_arrived = lax.optimization_barrier(
         (grad_both, gate_other, later_arrived[0])
     )
-    up_other = crossed(hop_grads[1][0], up_arrived)
+    up_given = across(hop_grads[1][0], up_arrived)
     grad_both = grad_both.reshape(tokens, KV_HEADS, 2, HEAD_DIM)
     grad_keys = grad_both[:, :, 0].reshape(tokens, kv_width)
     grad_values = grad_both[:, :, 1].reshape(tokens, kv_width)
@@ -1602,11 +1645,9 @@
     ]
     dense_grads, down_arrived = lax.optimization_barrier((dense_grads, later_arrived[1]))
     arrived = [gate_arrived, up_arrived, down_arrived]
-    down_other = crossed(hop_grads[2][0], down_arrived)
-    totals = reduce_dense(dense_grads)
-    totals, up_other, down_other, partial = lax.optimization_barrier(
-        (totals, up_other, down_other, partial)
-    )
+    down_given = across(hop_grads[2][0], down_arrived)
+    *totals, up_other, down_other = reduce_dense(dense_grads, [up_given, down_given])
+    totals, partial = lax.optimization_barrier((totals, partial))
     others = [gate_other, up_other, down_other]
     kept, given = own_and_other(partial, side)
     crossing = swap_pairs(given, "wt", 1)

time: 962 us -> 943 us (0.980)
  Pallas kernels: 738 us -> 718 us
    pallas_call x1 -> x0, Pallas kernels: 13.3 us -> none  [spread_rows(): pl.pallas_call(functools.partial(spread_kernel, apart), grid=(chips, side...]
    ppermute x10 -> x8, waiting for transfers between devices: 82 us -> 86.8 us  [swap_pairs(): return lax.ppermute(value, axis, [(i, i ^ distance) for i in range(count)])]
  transfers between devices with their start and end apart: 12 -> 10, of which waited for: 4 -> 4; matrix products, arithmetic and copies ran while one was open for 9% -> 9% of each run, Pallas kernels for 46% -> 46%
where the time goes in v10:
time: 943 us; the launch traced here: 937 us
  Pallas kernels  718 us (76%)
  waiting for transfers between devices  86.8 us (9%)
  matrix products  49.3 us (5%)
  other arithmetic  36.3 us (4%)
  local copies, waits for them, and re-layouts  22.4 us (2%)
  between operations  15.3 us (2%)
    pallas_call x1, Pallas kernels, reduce_dense(): pl.pallas_call(functools.partial(dense_kernel, chips, count, len(grads),...  211 us
    pallas_call x2, Pallas kernels, gather_rows(): pl.pallas_call(functools.partial(gather_kernel, chips, downward, paired,...  171 us
    pallas_call x2, Pallas kernels, scatter_rows(): pl.pallas_call(functools.partial(scatter_kernel, chips, upward, paired, p...  166 us
    ppermute x8, waiting for transfers between devices, swap_pairs(): return lax.ppermute(value, axis, [(i, i ^ distance) for i in range(count)])  86.8 us
    pallas_call x1, Pallas kernels, gather_weights(): pl.pallas_call(functools.partial(weights_kernel, count, len(slabs), len(s...  58.3 us
    pallas_call x1, Pallas kernels, run_experts(): pl.pallas_call(functools.partial(expert_kernel, blocks), grid=(local,), o...  50.6 us
  transfers between devices with their start and end apart: 10, of which 4 were waited for; matrix products, arithmetic and copies ran while one was open for 9% of the time, Pallas kernels for 46%

profile of v10, /device:TPU:0, one launch (start us, length us, event | category | flops | bytes accessed | tf_op | source)
XLA Modules:
  0.0 937.0 jit_solution(15586939681387933419)
XLA Ops:
  13.6 58.3 %gather_weights.1 = (bf16[4,384,1536]{2,1,0:T(8,128)(2,1)}, bf16[4,384,512]{2,1,0:T(8,128)(2,1)}, bf16[4,384,512]{2,1,0:T(8,128)(2,1)}, bf16[4,64,384]{2,1,0:T(8...) custom-call(bf16[384,1536]{1,0:T(8,128)(2,1)} %refs_0_.2, bf16[384,512]{1,0:T(8,128)(2,1)} %refs_1_.1, ...), custom_call_target="tpu_custom_call" | custom-call | bytes 2000000000 | tf_op jit(solution)/shard_map/gather_weights/pallas_call | solution.py:215
  80.9 66.3 %gather_keys.1 = (bf16[4,1,2,256,1024]{4,3,2,1,0:T(8,128)(2,1)}, bf16[4,384,1536]{2,1,0:T(8,128)(2,1)}, bf16[4,384,2048]{2,1,0:T(8,128)(2,1)}, bf16[4,256,1536]{2,1,0:T(8,128)(2,1)}, s32[8,128]{1,0:T(8,128)}) custom-call(bf16[256,1024]{1,0:T(8,128)(2,1)} %reshape.293.rows_ref, bf16[384,1536]{1,0:T(8,128)(2,1)} %refs_0_.3, ...), custom_call_target="tpu_custom_call" | custom-call | bytes 2000000000 | tf_op jit(solution)/shard_map/gather_keys/pallas_call | solution.py:375
  149.2 4.1 dynamic-slice_bitcast_fusion
  154.7 3.3 fusion.1
  162.7 4.7 convolution_convert_fusion.7.query_ref
  167.4 8.0 attend.1
  176.1 4.5 multiply_reduce_fusion.2
  189.5 4.5 convolution_convert_fusion
  197.0 60.7 %collective-permute-done.1.refs_2_ = bf16[4,2,384,512]{3,2,1,0:T(8,128)(2,1)} collective-permute-done((bf16[4,2,384,512]{3,2,1,0:T(8,128)(2,1)}, bf16[4,2,384,512]{3,2,1,0:T(8,128)(2,1)}, u32[]{:S(2)}, u32[]{:S(2)}) %collective-permute-start.1) | collective-permute-done | bytes 3145760 | tf_op jit(solution)/shard_map/ppermute | solution.py:1340
  257.7 5.6 collective-permute-done.refs_0_.refs_1_
  263.3 104.6 %gather_tokens.1 = (bf16[4,2,2,256,1536]{4,3,2,1,0:T(8,128)(2,1)}, bf16[4,2,384,512]{3,2,1,0:T(8,128)(2,1)}, bf16[4,512,384]{2,1,0:T(8,128)(2,1)}, s32[8,128]{1,0:T(8,128)}) custom-call(bf16[256,1536]{1,0:T(8,128)(2,1)} %copy-done.5, bf16[4,2,384,512]{3,2,1,0:T(8,128)(2,1)} %collective-permute-done.refs_0_.refs_1_, ...), custom_call_target="tpu_custom_call" | custom-call | bytes 2000000000 | tf_op jit(solution)/shard_map/gather_tokens/pallas_call | solution.py:375
  368.0 13.6 %pick_grads.1 = (bf16[4,2,4,80,1536]{4,3,2,1,0:T(8,128)(2,1)}, f32[4,2,4,80,128]{4,3,2,1,0:T(8,128)}, s32[4,2,4,512]{3,2,1,0:T(4,128)}) custom-call(s32[1]{0:T(128)} %bitcast.26.first_ref, bf16[256,256]{1,0:T(8,128)(2,1)} %fusion.38.earlier_ref, bf16[4,2,2,272,1536]{4,3,2,1,0:T(8,128)(2,1)} %bitcast.156), custom_call_target="tpu_custom_call" | custom-call | bytes 4096 | tf_op jit(solution)/shard_map/pick_grads/pallas_call | solution.py:1109
  381.6 12.3 %pick_tokens.1.x_ref = bf16[4,2,4,80,1536]{4,3,2,1,0:T(8,128)(2,1)} custom-call(s32[4,2,4,512]{3,2,1,0:T(4,128)} %get-tuple-element.104.slot_ref.refs_1_, bf16[4,2,2,256,1536]{4,3,2,1,0:T(8,128)(2,1)} %get-tuple-element.108.rows_ref), custom_call_target="tpu_custom_call" | custom-call | bytes 4096 | tf_op jit(solution)/shard_map/pick_tokens/pallas_call | solution.py:1145
  393.8 50.6 %experts.1 = (bf16[4,2,4,80,1536]{4,3,2,1,0:T(8,128)(2,1)}, bf16[4,2,4,80,1536]{4,3,2,1,0:T(8,128)(2,1)}, bf16[2,4,384,512]{3,2,1,0:T(8,128)(2,1)}, bf16[2,4,384...) custom-call(bf16[4,2,4,80,1536]{4,3,2,1,0:T(8,128)(2,1)} %pick_token, ...), custom_call_target="tpu_custom_call" | custom-call | bytes 4096 | tf_op jit(solution)/shard_map/experts/pallas_call | solution.py:1277
  444.4 90.9 %scatter_grads.1 = (f32[256,1536]{1,0:T(8,128)}, bf16[2,4,384,512]{3,2,1,0:T(8,128)(2,1)}, bf16[4,2,2,256,1536]{4,3,2,1,0:T(8,128)(2,1)}) custom-call(bf16[4,2,4,80,1536]{4,3,2,1,0:T(8,128)(2,1)} %get-tuple-element.117.refs_0_, s32[4,2,4,512]{3,2,1,0:T(4,128)} %get-tuple-element.104.slot_ref.refs_1_, bf16[2,4,384,512]{3,2,1,0:T(8,128)(2,1)} %get-tuple-element.118.refs_2_, ...), custom_call_target="tpu_custom_call" | custom-call | bytes 2000000000 | tf_op jit(solution)/shard_map/scatter_grads/pallas_call | solution.py:640
  538.8 3.6 fusion.21
  548.1 11.5 %attend_back.1 = (bf16[256,1536]{1,0:T(8,128)(2,1)}, bf16[2048,1024]{1,0:T(8,128)(2,1)}) custom-call(s32[1]{0:T(128)} %bitcast.1.place_ref, bf16[256,1536]{1,0:T(8,128)(2,1)} %convolution_convert_fusion.7.query_ref, bf16[2048,1024]{1,0:T(8,128)(2,1)} %bitcast.155, s32[1,256]{1,0:T(1,128)} %constant_dynamic-slice_fusion.row_ref, s32[2048,1]{1,0:T(8,128)} %copy.65.column_ref, ...), custom_call_target="tpu_custom_call" | custom-call | bytes 4096 | tf_op jit(solution)/shard_map/attend_back/pallas_call | solution.py:1023
  559.6 75.1 %scatter_keys.1 = f32[256,1024]{1,0:T(8,128)} custom-call(bf16[4,1,2,256,1024]{4,3,2,1,0:T(8,128)(2,1)} %bitcast.161), custom_call_target="tpu_custom_call" | custom-call | bytes 4096 | tf_op jit(solution)/shard_map/scatter_keys/pallas_call | solution.py:640
  636.1 5.0 convolution_convert_fusion.2
  641.1 3.6 convolution_convert_fusion.1
  660.0 14.2 %collective-permute-done.6.refs_8_ = bf16[2,4,512,384]{3,2,1,0:T(8,128)(2,1)} collective-permute-done((bf16[2,4,512,384]{3,2,1,0:T(8,128)(2,1)}, bf16[2,4,512,384]{3,2,1,0:T(8,128)(2,1)}, u32[]{:S(2)}, u32[]{:S(2)}) %collective-permute-start.6) | collective-permute-done | bytes 3145760 | tf_op jit(solution)/shard_map/ppermute | solution.py:1340
  680.3 210.5 %reduce_dense.1 = (bf16[384,1536]{1,0:T(8,128)(2,1)}, bf16[384,2048]{1,0:T(8,128)(2,1)}, bf16[384,1536]{1,0:T(8,128)(2,1)}, bf16[256,1536]{1,0:T(8,128)(2,1)}, b...) custom-call(bf16[4,384,1536]{2,1,0:T(8,128)(2,1)} %bitcast.152, ...), custom_call_target="tpu_custom_call" | custom-call | bytes 2000000000 | tf_op jit(solution)/shard_map/reduce_dense/pallas_call | solution.py:878
  890.8 16.6 %place_experts.1 = (f32[8,384,512]{2,1,0:T(8,128)}, f32[8,384,512]{2,1,0:T(8,128)}, f32[8,512,384]{2,1,0:T(8,128)}) custom-call(s32[1]{0:T(128)} %bitcast.49.side_ref, bf16[2,4,384,512]{3,2,1,0:T(8,128)(2,1)} %get-tuple-element.126.refs_0_, bf16[2,4,384,512]{3,2,1,0:T(8,128)(2,1)} %get-tuple-element.138.refs_1_, ...), custom_call_target="tpu_custom_call" | custom-call | bytes 4096 | tf_op jit(solution)/shard_map/place_experts/pallas_call | solution.py:1323
  922.3 6.3 collective-permute-done.7
  (157 shorter events, 83.1 us)
Async XLA Ops:
  7.2 360.8 %all-gather.3.cloned.1.call-start = ((), (), s32[]{:S(2)}) async-start(), calls=%async_computation.2 | async-start | bytes 15040512 | tf_op jit(solution)/shard_map/all_gather | solution.py:1472
  12.8 59.9 %copy-start = (bf16[1,256,1536]{2,1,0:T(8,128)(2,1)S(1)}, bf16[1,256,1536]{2,1,0:T(8,128)(2,1)}, u32[]{:S(2)}) copy-start(bf16[1,256,1536]{2,1,0:T(8,128)(2,1)} %param.17) | copy-start | bytes 2359300
  147.3 760.2 %reduce-scatter.2.cloned.1.call-start = ((), (), s32[]{:S(2)}) async-start(), calls=%async_computation.1 | async-start | bytes 14155776 | tf_op jit(solution)/shard_map/reduce_scatter | solution.py:1565
  149.2 5.1 copy-start.14
  149.2 5.5 copy-start.15
  153.3 43.7 %collective-permute-start.3 = (bf16[4,512,384]{2,1,0:T(8,128)(2,1)}, bf16[4,512,384]{2,1,0:T(8,128)(2,1)}, u32[]{:S(2)}, u32[]{:S(2)}) collective-permute-start(bf16[4,512,384]{2,1,0:T(8,128)(2,1)} %get-tuple-element.114.refs_4_), channel_id=1, source_target_pairs={{0,2},{1,3},{2,0},{3,1},{4,6},{5,7},{6,4},{7,5},{8,10},{9,11},{10,... | collective-permute-start | bytes 4718600 | tf_op jit(solution)/shard_map/ppermute | solution.py:1340
  158.0 99.7 %collective-permute-start.1 = (bf16[4,2,384,512]{3,2,1,0:T(8,128)(2,1)}, bf16[4,2,384,512]{3,2,1,0:T(8,128)(2,1)}, u32[]{:S(2)}, u32[]{:S(2)}) collective-permute-start(bf16[4,2,384,512]{3,2,1,0:T(8,128)(2,1)} %get-tuple-element.111.refs_0_), channel_id=1, source_target_pairs={{0,2},{1,3},{2,0},{3,1},{4,6},{5,7},{6,4},{7,5},{8,10},{9,11},{10,... | collective-permute-start | bytes 9437192 | tf_op jit(solution)/shard_map/ppermute | solution.py:1340
  159.2 37.8 %collective-permute-start.2 = (bf16[4,512,384]{2,1,0:T(8,128)(2,1)}, bf16[4,512,384]{2,1,0:T(8,128)(2,1)}, u32[]{:S(2)}, u32[]{:S(2)}) collective-permute-start(bf16[4,512,384]{2,1,0:T(8,128)(2,1)} %get-tuple-element.176), channel_id=1, source_target_pairs={{0,1},{1,0},{2,3},{3,2},{4,5},{5,4},{6,7},{7,6},{8,9},{9,8},{10,11... | collective-permute-start | bytes 4718600 | tf_op jit(solution)/shard_map/ppermute | solution.py:1340
  160.2 103.1 %collective-permute-start = (bf16[4,2,384,512]{3,2,1,0:T(8,128)(2,1)}, bf16[4,2,384,512]{3,2,1,0:T(8,128)(2,1)}, u32[]{:S(2)}, u32[]{:S(2)}) collective-permute-start(bf16[4,2,384,512]{3,2,1,0:T(8,128)(2,1)} %get-tuple-element.172), channel_id=1, source_target_pairs={{0,1},{1,0},{2,3},{3,2},{4,5},{5,4},{6,7},{7,6},{8,9},{9,8},{10,11... | collective-permute-start | bytes 9437192 | tf_op jit(solution)/shard_map/ppermute | solution.py:1340
  176.1 4.8 slice-start.1
  180.8 8.6 copy-start.5
  538.0 109.2 %collective-permute-start.5 = (bf16[2,4,384,512]{3,2,1,0:T(8,128)(2,1)}, bf16[2,4,384,512]{3,2,1,0:T(8,128)(2,1)}, u32[]{:S(2)}, u32[]{:S(2)}) collective-permute-start(bf16[2,4,384,512]{3,2,1,0:T(8,128)(2,1)} %get-tuple-element.128), channel_id=1, source_target_pairs={{0,2},{1,3},{2,0},{3,1},{4,6},{5,7},{6,4},{7,5},{8,10},{9,11},{10,... | collective-permute-start | bytes 9437192 | tf_op jit(solution)/shard_map/ppermute | solution.py:1340
  538.8 5.9 copy-start.9
  538.8 5.9 copy-start.10
  538.8 6.9 slice-start.4
  542.4 104.8 %collective-permute-start.4 = (bf16[4,384,512]{2,1,0:T(8,128)(2,1)}, bf16[4,384,512]{2,1,0:T(8,128)(2,1)}, u32[]{:S(2)}, u32[]{:S(2)}) collective-permute-start(bf16[4,384,512]{2,1,0:T(8,128)(2,1)} %fusion.21), channel_id=1, source_target_pairs={{0,1},{1,0},{2,3},{3,2},{4,5},{5,4},{6,7},{7,6},{8,9},{9,8},{10,11... | collective-permute-start | bytes 4718600 | tf_op jit(solution)/shard_map/ppermute | solution.py:1340
  543.7 130.5 %collective-permute-start.6 = (bf16[2,4,512,384]{3,2,1,0:T(8,128)(2,1)}, bf16[2,4,512,384]{3,2,1,0:T(8,128)(2,1)}, u32[]{:S(2)}, u32[]{:S(2)}) collective-permute-start(bf16[2,4,512,384]{3,2,1,0:T(8,128)(2,1)} %get-tuple-element.130), channel_id=1, source_target_pairs={{0,2},{1,3},{2,0},{3,1},{4,6},{5,7},{6,4},{7,5},{8,10},{9,11},{10,... | collective-permute-start | bytes 9437192 | tf_op jit(solution)/shard_map/ppermute | solution.py:1340
  636.0 5.0 copy-start.2
  636.0 5.0 copy-start.4
  636.1 8.6 slice-start.2
  656.3 17.9 %copy-start.8 = (bf16[2,4,512,384]{3,2,1,0:T(8,128)(2,1)S(1)}, bf16[2,4,512,384]{3,2,1,0:T(8,128)(2,1)}, u32[]{:S(2)}) copy-start(bf16[2,4,512,384]{3,2,1,0:T(8,128)(2,1)} %get-tuple-element.140.refs_2_) | copy-start | bytes 9437188
  908.8 19.9 %collective-permute-start.7 = (bf16[256,1536]{1,0:T(8,128)(2,1)S(1)}, bf16[256,1536]{1,0:T(8,128)(2,1)S(1)}, u32[]{:S(2)}, u32[]{:S(2)}) collective-permute-start(bf16[256,1536]{1,0:T(8,128)(2,1)S(1)} %dynamic-slice_bitcast_fusion.2), channel_id=1, source_target_pairs={{0,1},{1,0},{2,3},{3,2},{4,5},{5,4},{6,7},{7,6},{8,9},{9,8},{10,11... | collective-permute-start | bytes 2359304 | tf_op jit(solution)/shard_map/ppermute | solution.py:1340
  920.3 8.3 copy-start.12
  920.3 8.3 copy-start.18
  (20 other events, 48.0 us)
Sparse Core Ops, SparseCore 0:
  147.4 122.3 all-gather.2
  535.6 170.6 reduce-scatter.1
